TPU v7x, 32 devices: a whole 2x2x4 slice. The times are simulated.
32 devices in a mesh: group: 4 (over y, x), bulk: 8 (over z, core).
Axes of the slice: x: 2, y: 2, z: 4, core: 2. Of those that a mesh axis runs over, the one named last changes fastest.
Arguments:
- rhs: float32 [128, 64, 128], P(('group', 'bulk')), may hold values from -90 to 90, as said below
- diag_tiles: float32 [128, 128, 128], P(('group', 'bulk')), may hold values from -0.06 to 0.06
- offdiag_blocks: float32 [128, 11, 128, 128], P(('group', 'bulk')), may hold values from -0.026 to 0.026
- coupling: float32 [64, 4, 128, 128], P(('group', 'bulk')), may hold values from -0.05 to 0.05, as said below
- col_index: int32 [128, 11], replicated, may hold values from 0 to 127, as said below
- load: int32 [128], replicated, may hold values from 3 to 11
- new_slot: int32 [128], replicated, may hold values from 0 to 127, as said below
Outputs:
- solution_out: float32 [128, 64, 128], P(('group', 'bulk'))
- residual_out: float32 [128, 64, 128], P(('group', 'bulk'))
Inputs may be any that keep to these rules, and one draw needn't show every extreme that they name: `rhs`: made of random entries times scales of the rows and of the columns. `coupling`: entry [d * 2 + k, h] is the transpose of entry [(h * 8 + d % 8) * 2 + k, d // 8]. `col_index`: for each part g and each tile position t, the column t of the 32 block rows of part g is a permutation of that part's slots g * 32 to (g + 1) * 32 - 1. Of the 44 entries of the 4 block rows of one device (slots d * 4 to (d + 1) * 4 - 1), at most 6 name slots of any one device, and exactly 6 name slots of some device. `new_slot`: A permutation. On every device exactly one block row moves, from a slot k with 2 <= k % 4; it stays in its part, goes from owner b to owner b XOR m, where m (1 to 7) is one number for the whole part, and takes the slot that the moving row of that device leaves.
All inputs are finite; a program needn't handle non-finite values.
Results may differ from a plain program's by a relative error of at most 0.0003.
Values sent between devices are 32-bit elements; how exact they have to be, the bound alone decides.
No kernel may reach another device: no remote copies, remote signals or barrier semaphores. Data moves between devices by JAX's collectives and lax.ppermute only.
A program may use at most 64 MiB of HBM per device.

v0:
```python
import jax
import jax.numpy as jnp
from jax import lax
from jax.sharding import PartitionSpec as P

highest = lax.Precision.HIGHEST
diagonal_shift = 4.0


def from_partner(value, axis, bit):
    mask = 2**bit
    pairs = [(source, source ^ mask) for source in range(lax.axis_size(axis))]
    return lax.ppermute(value, axis, pairs)


def chol_apply(matrix, right):
    factor = jnp.linalg.cholesky(matrix)
    middle = lax.linalg.triangular_solve(factor, right, left_side=True, lower=True)
    return lax.linalg.triangular_solve(factor, middle, left_side=True, lower=True, transpose_a=True)


def global_gram(left, right):
    partial_gram = jnp.einsum("snt,smt->nm", left, right, precision=highest)
    total = lax.psum(partial_gram, ("group", "bulk"))
    return 0.5 * (total + total.T)


def operate(vectors, diag, masked, column_ids, coupling):
    row_count = vectors.shape[0]
    boundary_rows = coupling.shape[0]
    part_count = coupling.shape[1]
    group_rows = row_count * lax.axis_size("bulk")
    border = lax.all_gather(vectors[:boundary_rows], "group", axis=0, tiled=True)
    final_output = diagonal_shift * vectors + jnp.einsum(
        "rnj,rij->rni", vectors, diag, precision=highest
    )
    returned = jnp.einsum("rni,rkij->rknj", vectors, masked, precision=highest)
    flat_terms = returned.reshape((-1,) + vectors.shape[1:])
    panel = lax.all_gather(vectors, "bulk", axis=0, tiled=True)
    buffer = jax.ops.segment_sum(flat_terms, column_ids.reshape(-1), num_segments=group_rows)
    owed = lax.psum_scatter(buffer, "bulk", scatter_dimension=0, tiled=True)
    picked = panel[column_ids]
    final_output = (
        final_output + jnp.einsum("rknj,rkij->rni", picked, masked, precision=highest) + owed
    )
    border = border.reshape((part_count, boundary_rows) + vectors.shape[1:])
    crossed = jnp.einsum("khij,hknj->kni", coupling, border, precision=highest)
    return final_output.at[:boundary_rows].add(crossed)


def advance(state, diag, masked, column_ids, coupling, last_step):
    solution, resid, direction, gram_rr = state
    image = operate(direction, diag, masked, column_ids, coupling)
    gram_pq = global_gram(direction, image)
    alpha = chol_apply(gram_pq, gram_rr)
    solution = solution + jnp.einsum("mn,smt->snt", alpha, direction, precision=highest)
    resid = resid - jnp.einsum("mn,smt->snt", alpha, image, precision=highest)
    if not last_step:
        gram_new = global_gram(resid, resid)
        beta = chol_apply(gram_rr, gram_new)
        direction = resid + jnp.einsum("mn,smt->snt", beta, direction, precision=highest)
        gram_rr = gram_new
    return (solution, resid, direction, gram_rr)


def local(rhs, diag_tiles, offdiag_blocks, coupling, col_index, load, new_slot):
    row_count = rhs.shape[0]
    off_count = offdiag_blocks.shape[1]
    bulk_count = lax.axis_size("bulk")
    group_rows = row_count * bulk_count
    my_group = lax.axis_index("group")
    my_bulk = lax.axis_index("bulk")
    first_slot = (my_group * bulk_count + my_bulk) * row_count
    group_base = my_group * group_rows
    own_slots = first_slot + jnp.arange(row_count, dtype=jnp.int32)
    tile_ids = jnp.arange(off_count, dtype=jnp.int32)
    old_columns = col_index[own_slots] - group_base
    old_mask = (tile_ids[None, :] < load[own_slots][:, None]).astype(jnp.float32)
    old_masked = offdiag_blocks * old_mask[:, :, None, None]
    own_new = new_slot[own_slots]
    leaving = jnp.argmax((own_new != own_slots).astype(jnp.int32))
    target = own_new[leaving]
    target_bulk = target // row_count % bulk_count
    xor_mask = jnp.bitwise_xor(target_bulk, my_bulk)
    start_state = (jnp.zeros_like(rhs), rhs, rhs, global_gram(rhs, rhs))
    state = advance(start_state, diag_tiles, old_masked, old_columns, coupling, False)
    state = advance(state, diag_tiles, old_masked, old_columns, coupling, True)
    solution = state[0]
    resid = state[1]
    pieces = [solution[leaving], resid[leaving]]
    flat = jnp.concatenate([piece.reshape(-1) for piece in pieces])
    for bit_pos in range(bulk_count.bit_length() - 1):
        partner = from_partner(flat, "bulk", bit_pos)
        chosen = jnp.bitwise_and(jnp.right_shift(xor_mask, bit_pos), 1) == 1
        flat = jnp.where(chosen, partner, flat)
    outputs = []
    offset = 0
    for piece in pieces:
        outputs.append(flat[offset : offset + piece.size].reshape(piece.shape))
        offset = offset + piece.size
    return (solution.at[leaving].set(outputs[0]), resid.at[leaving].set(outputs[1]))


def solution(mesh):
    return jax.shard_map(
        local,
        mesh=mesh,
        in_specs=(
            P(("group", "bulk"), None, None),
            P(("group", "bulk"), None, None),
            P(("group", "bulk"), None, None, None),
            P(("group", "bulk"), None, None, None),
            P(),
            P(),
            P(),
        ),
        out_specs=(P(("group", "bulk"), None, None), P(("group", "bulk"), None, None)),
        check_vma=False,
    )
```

profile of v0, /device:TPU:0, one launch (start us, length us, event | category | flops | bytes accessed | tf_op | source)
XLA Modules:
  0.0 343.9 jit_solution(1690486080009741150)
XLA Ops:
  9.5 1.3 gather_fusion.2
  10.8 3.8 %fusion.4 = f32[4,11,128,64]{2,3,1,0:T(8,128)S(1)} fusion(f32[4,11,128,128]{3,2,1,0:T(8,128)} %param.22, f32[4,11]{1,0:T(4,128)S(1)} %fusion.59, f32[4,64,128]{2,1,0:T(8,128)} %param.20), kind=kOutput, calls=%fused_computation.11 | convolution fusion | flops 554369024 | bytes 4456624 | tf_op jit(solution)/shard_map/rni,rkij->rknj/dot_general | solution.py:37
  14.8 3.1 scatter_fusion
  19.0 11.1 %all_gather.13 = f32[8,64,128]{2,1,0:T(8,128)} all-gather(f32[2,64,128]{2,1,0:T(8,128)S(1)} %slice.127), channel_id=1, replica_groups=mesh['group'=4,'bulk'=8] {'group'}, dimensions={0}, use_global_device_ids=true | all-gather | bytes 327680 | tf_op jit(solution)/shard_map/all_gather | solution.py:33
  31.0 3.5 %all-gather.3.cloned.1.call-done = f32[32,64,128]{2,1,0:T(8,128)} async-done(((f32[4,64,128]{2,1,0:T(8,128)}), f32[32,64,128]{2,1,0:T(8,128)}) %all-gather.3.cloned.1.call-update) | async-done | bytes 1048592 | tf_op jit(solution)/shard_map/all_gather | solution.py:39
  34.5 3.0 gather_fusion.1
  37.5 5.4 %fusion.12 = f32[4,64,128]{2,1,0:T(8,128)} fusion(f32[4,11,64,128]{3,2,1,0:T(8,128)} %bitcast.188, f32[4,11,128,128]{3,2,1,0:T(8,128)S(1)} %copy-done.2, f32[4,11]{1,0:T(4,128)S(1)} %fusion.59), kind=kOutput, calls=%fused_computation.19 | convolution fusion | flops 554369024 | bytes 4456624 | tf_op jit(solution)/shard_map/rknj,rkij->rni/dot_general | solution.py:44
  42.9 25.7 %reduce-scatter.3.cloned.1.call-done = f32[4,64,128]{2,1,0:T(8,128)} async-done(((f32[32,64,128]{2,1,0:T(8,128)}), f32[4,64,128]{2,1,0:T(8,128)}) %reduce-scatter.3.cloned.1.call-update) | async-done | bytes 131088 | tf_op jit(solution)/shard_map/reduce_scatter | solution.py:41
  68.5 1.7 fusion.21
  70.2 1.6 fusion.29
  73.4 39.0 %all-reduce = (f32[64,64]{1,0:T(8,128)}, f32[64,64]{1,0:T(8,128)}) all-reduce(f32[64,64]{1,0:T(8,128)} %convolution_bitcast_fusion.12, f32[64,64]{1,0:T(8,128)} %convolution_bitcast_fusion.13), channel_id=1, replica_groups=mesh['group'=4,'bulk'=8] {'group','bulk'}, use_global_device_ids=true, to_apply=%region_5.7 | all-reduce | flops 8192 | bytes 65536 | tf_op jit(solution)/shard_map/psum | solution.py:24
  112.3 1.4 copy.41
  113.8 1.4 copy.43
  115.2 1.4 fusion.51
  116.6 1.4 copy.46
  118.1 1.4 fusion.50
  119.5 7.2 %cholesky.70 = f32[64,64]{1,0:T(8,128)} custom-call(f32[64,64]{1,0:T(8,128)} %fusion.50), custom_call_target="Cholesky" | custom-call | tf_op jit(solution)/shard_map/jit(cholesky)/cholesky | solution.py:17
  128.2 2.1 fusion.35
  130.2 6.3 %custom-call.15 = f32[1,64,64]{1,2,0:T(8,128)} custom-call(f32[1,64,64]{2,1,0:T(8,128)} %fusion.35), custom_call_target="InvertDiagBlocksLowerTriangular" | custom-call | tf_op jit(solution)/shard_map/triangular_solve/custom-call.2 | solution.py:19
  136.5 1.4 copy.42
  138.0 1.4 fusion.55
  139.3 7.2 %cholesky.59 = f32[64,64]{1,0:T(8,128)} custom-call(f32[64,64]{1,0:T(8,128)} %fusion.55), custom_call_target="Cholesky" | custom-call | tf_op jit(solution)/shard_map/jit(cholesky)/cholesky | solution.py:17
  148.0 2.0 fusion.34
  150.0 6.3 %custom-call.13 = f32[1,64,64]{1,2,0:T(8,128)} custom-call(f32[1,64,64]{2,1,0:T(8,128)} %fusion.34), custom_call_target="InvertDiagBlocksLowerTriangular" | custom-call | tf_op jit(solution)/shard_map/triangular_solve/custom-call.2 | solution.py:19
  158.9 1.2 fusion.25
  161.6 42.2 %psum.30 = f32[64,64]{1,0:T(8,128)} all-reduce(f32[64,64]{1,0:T(8,128)} %convolution_bitcast_fusion.10), channel_id=1, replica_groups=mesh['group'=4,'bulk'=8] {'group','bulk'}, use_global_device_ids=true, to_apply=%region_6.10 | all-reduce | flops 4096 | bytes 32768 | tf_op jit(solution)/shard_map/psum | solution.py:24
  203.8 1.4 copy.47
  205.3 1.0 fusion.47
  207.3 1.8 fusion.24
  209.2 4.0 %fusion = f32[4,11,128,64]{2,3,1,0:T(8,128)} fusion(f32[4,11,128,128]{3,2,1,0:T(8,128)S(1)} %copy-done.2, f32[4,11]{1,0:T(4,128)S(1)} %fusion.59, f32[4,64,128]{2,1,0:T(8,128)} %fusion.24), kind=kOutput, calls=%fused_computation.7 | convolution fusion | flops 554369024 | bytes 4456624 | tf_op jit(solution)/shard_map/rni,rkij->rknj/dot_general | solution.py:37
  213.2 1.1 broadcast.203
  214.3 8.1 %scatter_fusion.1 = f32[32,64,128]{2,1,0:T(8,128)} fusion(f32[32,64,128]{2,1,0:T(8,128)} %broadcast.203, s32[44]{0:T(128)} %copy-done.15, f32[44,64,128]{2,1,0:T(8,128)} %bitcast.185), kind=kCustom, calls=%fused_computation.6 | custom fusion | flops 360448 | bytes 4325552 | tf_op jit(solution)/shard_map/scatter-add | solution.py:40
  222.4 1.2 gather_fusion.4
  223.6 1.3 fusion.60
  227.6 10.8 %all_gather.15 = f32[8,64,128]{2,1,0:T(8,128)} all-gather(f32[2,64,128]{2,1,0:T(8,128)S(1)} %slice.146), channel_id=1, replica_groups=mesh['group'=4,'bulk'=8] {'group'}, dimensions={0}, use_global_device_ids=true | all-gather | bytes 327680 | tf_op jit(solution)/shard_map/all_gather | solution.py:33
  238.4 1.7 convolution_bitcast_fusion.4
  240.1 3.0 gather_fusion.3
  243.1 5.5 %fusion.15 = f32[4,64,128]{2,1,0:T(8,128)} fusion(f32[4,11,64,128]{3,2,1,0:T(8,128)} %bitcast.186, f32[4,11,128,128]{3,2,1,0:T(8,128)S(1)} %copy-done.2, f32[4,11]{1,0:T(4,128)S(1)} %fusion.59), kind=kOutput, calls=%fused_computation.20 | convolution fusion | flops 554369024 | bytes 4456624 | tf_op jit(solution)/shard_map/rknj,rkij->rni/dot_general | solution.py:44
  248.5 17.0 %reduce-scatter.5.cloned.1.call-done = f32[4,64,128]{2,1,0:T(8,128)} async-done(((f32[32,64,128]{2,1,0:T(8,128)}), f32[4,64,128]{2,1,0:T(8,128)}) %reduce-scatter.5.cloned.1.call-update) | async-done | bytes 131088 | tf_op jit(solution)/shard_map/reduce_scatter | solution.py:41
  265.5 1.7 fusion.19
  267.2 1.6 fusion.27
  269.1 38.0 %psum.31 = f32[64,64]{1,0:T(8,128)S(1)} all-reduce(f32[64,64]{1,0:T(8,128)S(1)} %convolution_bitcast_fusion.8), channel_id=1, replica_groups=mesh['group'=4,'bulk'=8] {'group','bulk'}, use_global_device_ids=true, to_apply=%region_9.13 | all-reduce | flops 4096 | bytes 32768 | tf_op jit(solution)/shard_map/psum | solution.py:24
  307.2 5.8 %cholesky.81 = f32[64,64]{1,0:T(8,128)S(1)} custom-call(f32[64,64]{1,0:T(8,128)S(1)} %fusion.44), custom_call_target="Cholesky" | custom-call | tf_op jit(solution)/shard_map/jit(cholesky)/cholesky | solution.py:17
  314.4 4.9 %custom-call.17 = f32[1,64,64]{1,2,0:T(8,128)S(1)} custom-call(f32[1,64,64]{2,1,0:T(8,128)S(1)} %fusion.36), custom_call_target="InvertDiagBlocksLowerTriangular" | custom-call | tf_op jit(solution)/shard_map/triangular_solve/custom-call.2 | solution.py:19
  323.8 2.9 collective-permute-start.1
  326.7 2.7 collective-permute-done.1
  329.5 1.9 collective-permute-start.2
  332.1 3.9 %collective-permute-done.2 = f32[16384]{0:T(1024)S(1)} collective-permute-done((f32[16384]{0:T(1024)S(1)}, f32[16384]{0:T(1024)S(1)}, u32[]{:S(2)}, u32[]{:S(2)}) %collective-permute-start.2) | collective-permute-done | bytes 65568 | tf_op jit(solution)/shard_map/ppermute | solution.py:13
  (90 shorter events, 20.5 us)
Async XLA Ops:
  7.2 63.0 %copy-start = (f32[2,4,128,128]{3,2,1,0:T(8,128)S(1)}, f32[2,4,128,128]{3,2,1,0:T(8,128)}, u32[]{:S(2)}) copy-start(f32[2,4,128,128]{3,2,1,0:T(8,128)} %param.23) | copy-start | bytes 1572868
  7.2 27.3 %all-gather.3.cloned.1.call-start = ((), (), s32[]{:S(2)}) async-start(), calls=%async_computation.2 | async-start | bytes 1179648 | tf_op jit(solution)/shard_map/all_gather | solution.py:39
  7.9 60.6 %reduce-scatter.3.cloned.1.call-start = ((), (), s32[]{:S(2)}) async-start(), calls=%async_computation.3 | async-start | bytes 1179648 | tf_op jit(solution)/shard_map/reduce_scatter | solution.py:41
  9.5 5.3 %copy-start.15 = (s32[44]{0:T(128)}, s32[44]{0:T(128)S(1)}, u32[]{:S(2)}) copy-start(s32[44]{0:T(128)S(1)} %reshape.290) | copy-start | bytes 532
  14.7 4.1 %copy-start.4 = (f32[4,64,128]{2,1,0:T(8,128)S(1)}, f32[4,64,128]{2,1,0:T(8,128)}, u32[]{:S(2)}) copy-start(f32[4,64,128]{2,1,0:T(8,128)} %param.20) | copy-start | bytes 393220
  17.8 1.0 copy-start.3
  18.8 221.2 %all-gather.5.cloned.1.call-start = ((), (), s32[]{:S(2)}) async-start(), calls=%async_computation.4 | async-start | bytes 1179648 | tf_op jit(solution)/shard_map/all_gather | solution.py:39
  31.0 6.5 %copy-start.2 = (f32[4,11,128,128]{3,2,1,0:T(8,128)S(1)}, f32[4,11,128,128]{3,2,1,0:T(8,128)}, u32[]{:S(2)}) copy-start(f32[4,11,128,128]{3,2,1,0:T(8,128)} %param.22) | copy-start | bytes 8650756
  71.8 0.7 copy-start.8
  158.3 0.6 copy-start.13
  160.0 0.7 copy-start.6
  209.2 56.3 %reduce-scatter.5.cloned.1.call-start = ((), (), s32[]{:S(2)}) async-start(), calls=%async_computation.5 | async-start | bytes 1179648 | tf_op jit(solution)/shard_map/reduce_scatter | solution.py:41
  214.3 8.1 %copy-start.1 = (s32[128]{0:T(128)S(1)}, s32[128]{0:T(128)}, u32[]{:S(2)}) copy-start(s32[128]{0:T(128)} %param.26) | copy-start | bytes 1540
  243.0 22.4 %copy-start.5 = (f32[4,64,128]{2,1,0:T(8,128)S(1)}, f32[4,64,128]{2,1,0:T(8,128)}, u32[]{:S(2)}) copy-start(f32[4,64,128]{2,1,0:T(8,128)} %fusion.24) | copy-start | bytes 393220
  248.5 70.8 %copy-start.10 = (f32[64,64]{1,0:T(8,128)S(1)}, f32[64,64]{1,0:T(8,128)}, u32[]{:S(2)}) copy-start(f32[64,64]{1,0:T(8,128)} %psum.30) | copy-start | bytes 49156
  248.5 70.8 %copy-start.14 = (f32[64,64]{0,1:T(8,128)S(1)}, f32[64,64]{0,1:T(8,128)}, u32[]{:S(2)}) copy-start(f32[64,64]{0,1:T(8,128)} %copy.47) | copy-start | bytes 49156
  248.5 71.3 %copy-start.7 = (f32[4,64,128]{2,1,0:T(8,128)S(1)}, f32[4,64,128]{2,1,0:T(8,128)}, u32[]{:S(2)}) copy-start(f32[4,64,128]{2,1,0:T(8,128)} %copy-done.6) | copy-start | bytes 393220
  248.5 71.6 %copy-start.9 = (f32[4,64,128]{2,1,0:T(8,128)S(1)}, f32[4,64,128]{2,1,0:T(8,128)}, u32[]{:S(2)}) copy-start(f32[4,64,128]{2,1,0:T(8,128)} %convolution_bitcast_fusion.4) | copy-start | bytes 393220
  267.2 53.4 %copy-start.16 = (s32[4]{0:T(128)S(1)}, s32[4]{0:T(128)}, u32[]{:S(2)}) copy-start(s32[4]{0:T(128)} %gather_fusion.4) | copy-start | bytes 52
  268.8 62.6 %copy-start.17 = (s32[3]{0:T(128)S(1)}, s32[3]{0:T(128)}, u32[]{:S(2)}) copy-start(s32[3]{0:T(128)} %constant.172.clone.1) | copy-start | bytes 40
  320.5 3.3 collective-permute-start
  323.8 5.7 %collective-permute-start.1 = (f32[16384]{0:T(1024)S(1)}, f32[16384]{0:T(1024)S(1)}, u32[]{:S(2)}, u32[]{:S(2)}) collective-permute-start(f32[16384]{0:T(1024)S(1)} %broadcast_select_fusion), channel_id=1, source_target_pairs={{0,2},{1,3},{2,0},{3,1},{4,6},{5,7},{6,4},{7,5},{8,10},{9,11},{10,... | collective-permute-start | bytes 196616 | tf_op jit(solution)/shard_map/ppermute | solution.py:13
  329.5 6.5 %collective-permute-start.2 = (f32[16384]{0:T(1024)S(1)}, f32[16384]{0:T(1024)S(1)}, u32[]{:S(2)}, u32[]{:S(2)}) collective-permute-start(f32[16384]{0:T(1024)S(1)} %broadcast_select_fusion.1), channel_id=1, source_target_pairs={{0,4},{1,5},{2,6},{3,7},{4,0},{5,1},{6,2},{7,3},{8,12},{9,13},{10,... | collective-permute-start | bytes 196616 | tf_op jit(solution)/shard_map/ppermute | solution.py:13
  336.7 0.7 copy-start.11
  336.7 0.7 copy-start.12
Sparse Core Ops, SparseCore 0:
  9.6 24.8 all-gather.2
  36.8 31.7 reduce-scatter.2
  209.3 21.9 all-gather.4
  233.4 32.0 reduce-scatter.4
where the time goes:
time: 346 us; the launch traced here: 344 us
  blocking collectives  141 us (41%)
  other arithmetic  64.2 us (19%)
  waiting for transfers between devices  53.5 us (15%)
  matrix products  37.7 us (11%)
  local copies, waits for them, and re-layouts  23.6 us (7%)
  between operations  18.7 us (5%)
  starting transfers between devices  5.05 us (1%)
    psum x3, blocking collectives, global_gram(): total = lax.psum(partial_gram, ('group', 'bulk'))  119 us
    reduce_scatter x2, waiting for transfers between devices, operate(): owed = lax.psum_scatter(buffer, 'bulk', scatter_dimension=0, tiled=True)  42.6 us
    another operation x9, other arithmetic, chol_apply(): factor = jnp.linalg.cholesky(matrix)  23.9 us
    another operation x6, other arithmetic, chol_apply(): lax.linalg.triangular_solve(factor, middle, left_side=True, lower=True, t...  22.1 us
    all_gather x2, blocking collectives, operate(): lax.all_gather(vectors[:boundary_rows], 'group', axis=0, tiled=True)  21.9 us
    scatter-add x2, other arithmetic, operate(): jax.ops.segment_sum(flat_terms, column_ids.reshape(-1), num_segments=grou...  11.1 us
    dot_general x2, matrix products, operate(): jnp.einsum('rknj,rkij->rni', picked, masked, precision=highest)  10.9 us
    dot_general x2, matrix products, operate(): returned = jnp.einsum('rni,rkij->rknj', vectors, masked, precision=highest)  7.8 us
  transfers between devices with their start and end apart: 7, of which 5 were waited for; matrix products, arithmetic and copies ran while one was open for 14% of the time, Pallas kernels for 0%

commit v1 on v0

--- a/solution.py
+++ b/solution.py
@@ -19,10 +19,16 @@
     return lax.linalg.triangular_solve(factor, middle, left_side=True, lower=True, transpose_a=True)
 
 
-def global_gram(left, right):
-    partial_gram = jnp.einsum("snt,smt->nm", left, right, precision=highest)
-    total = lax.psum(partial_gram, ("group", "bulk"))
-    return 0.5 * (total + total.T)
+def mm(left, right):
+    return jnp.dot(left, right, precision=highest)
+
+
+def sym(matrix):
+    return 0.5 * (matrix + matrix.T)
+
+
+def partial_gram(left, right):
+    return jnp.einsum("snt,smt->nm", left, right, precision=highest)
 
 
 def operate(vectors, diag, masked, column_ids, coupling):
@@ -31,9 +37,7 @@
     part_count = coupling.shape[1]
     group_rows = row_count * lax.axis_size("bulk")
     border = lax.all_gather(vectors[:boundary_rows], "group", axis=0, tiled=True)
-    final_output = diagonal_shift * vectors + jnp.einsum(
-        "rnj,rij->rni", vectors, diag, precision=highest
-    )
+    final_output = jnp.einsum("rnj,rij->rni", vectors, diag, precision=highest)
     returned = jnp.einsum("rni,rkij->rknj", vectors, masked, precision=highest)
     flat_terms = returned.reshape((-1,) + vectors.shape[1:])
     panel = lax.all_gather(vectors, "bulk", axis=0, tiled=True)
@@ -48,19 +52,8 @@
     return final_output.at[:boundary_rows].add(crossed)
 
 
-def advance(state, diag, masked, column_ids, coupling, last_step):
-    solution, resid, direction, gram_rr = state
-    image = operate(direction, diag, masked, column_ids, coupling)
-    gram_pq = global_gram(direction, image)
-    alpha = chol_apply(gram_pq, gram_rr)
-    solution = solution + jnp.einsum("mn,smt->snt", alpha, direction, precision=highest)
-    resid = resid - jnp.einsum("mn,smt->snt", alpha, image, precision=highest)
-    if not last_step:
-        gram_new = global_gram(resid, resid)
-        beta = chol_apply(gram_rr, gram_new)
-        direction = resid + jnp.einsum("mn,smt->snt", beta, direction, precision=highest)
-        gram_rr = gram_new
-    return (solution, resid, direction, gram_rr)
+def combine(vectors, matrix):
+    return jnp.einsum("mn,smt->snt", matrix, vectors, precision=highest)
 
 
 def local(rhs, diag_tiles, offdiag_blocks, coupling, col_index, load, new_slot):
@@ -82,11 +75,42 @@
     target = own_new[leaving]
     target_bulk = target // row_count % bulk_count
     xor_mask = jnp.bitwise_xor(target_bulk, my_bulk)
-    start_state = (jnp.zeros_like(rhs), rhs, rhs, global_gram(rhs, rhs))
-    state = advance(start_state, diag_tiles, old_masked, old_columns, coupling, False)
-    state = advance(state, diag_tiles, old_masked, old_columns, coupling, True)
-    solution = state[0]
-    resid = state[1]
+
+    first = operate(rhs, diag_tiles, old_masked, old_columns, coupling)
+    second = operate(first, diag_tiles, old_masked, old_columns, coupling)
+    grams = jnp.stack(
+        [
+            partial_gram(rhs, rhs),
+            partial_gram(rhs, first),
+            partial_gram(first, first),
+            partial_gram(first, second),
+        ]
+    )
+    grams = lax.psum(grams, ("group", "bulk"))
+    g0, g1, g2, g3 = (sym(grams[i]) for i in range(4))
+    eye = jnp.eye(g0.shape[0], dtype=jnp.float32)
+    a = chol_apply(diagonal_shift * g0 + g1, g0)
+    m = eye - diagonal_shift * a
+    cross = mm(m.T, mm(g1, a))
+    g_new = sym(mm(m.T, mm(g0, m)) - cross - cross.T + mm(a.T, mm(g2, a)))
+    b = chol_apply(g0, g_new)
+    c = m + b
+    cross = mm(c.T, mm(diagonal_shift * g1 + g2, a))
+    g_pq = (
+        mm(c.T, mm(diagonal_shift * g0 + g1, c))
+        - cross
+        - cross.T
+        + mm(a.T, mm(diagonal_shift * g2 + g3, a))
+    )
+    a1 = chol_apply(sym(g_pq), g_new)
+    aa1 = mm(a, a1)
+    ca1 = mm(c, a1)
+    solution = combine(rhs, a + ca1) - combine(first, aa1)
+    resid = (
+        combine(rhs, m - diagonal_shift * ca1)
+        - combine(first, a + ca1 - diagonal_shift * aa1)
+        + combine(second, aa1)
+    )
     pieces = [solution[leaving], resid[leaving]]
     flat = jnp.concatenate([piece.reshape(-1) for piece in pieces])
     for bit_pos in range(bulk_count.bit_length() - 1):

time: 346 us -> 323 us (0.934)
  waiting for transfers between devices: 53.5 us -> 175 us
  blocking collectives: 141 us -> 21.6 us
  other arithmetic: 64.2 us -> 50.8 us
  local copies, waits for them, and re-layouts: 23.6 us -> 16.9 us
    psum x0 -> x1, waiting for transfers between devices: none -> 120 us  [local(): grams = lax.psum(grams, ('group', 'bulk'))]
    psum x3 -> x0, blocking collectives: 119 us -> none  [global_gram(): total = lax.psum(partial_gram, ('group', 'bulk'))]
    another operation x6, other arithmetic: 22.1 us -> 16.6 us  [chol_apply(): lax.linalg.triangular_solve(factor, middle, left_side=True, lower=True, t...]
    psum x4 -> x0, local copies, waits for them, and re-layouts: 4.4 us -> none  [global_gram(): total = lax.psum(partial_gram, ('group', 'bulk'))]
    another operation x9, other arithmetic: 23.9 us -> 19.6 us  [chol_apply(): factor = jnp.linalg.cholesky(matrix)]
    dot_general x11 -> x25, matrix products: 11.4 us -> 12.7 us  [the longest x4 4.75 us: partial_gram(): return jnp.einsum('snt,smt->nm', left, right, precision=highest)]
  transfers between devices with their start and end apart: 7 -> 8, of which waited for: 5 -> 6; matrix products, arithmetic and copies ran while one was open for 14% -> 15% of each run, Pallas kernels for 0% -> 0%
where the time goes in v1:
time: 323 us; the launch traced here: 322 us
  waiting for transfers between devices  175 us (54%)
  other arithmetic  50.8 us (16%)
  matrix products  35.8 us (11%)
  blocking collectives  21.6 us (7%)
  between operations  18.7 us (6%)
  local copies, waits for them, and re-layouts  16.9 us (5%)
  starting transfers between devices  3.27 us (1%)
    psum x1, waiting for transfers between devices, local(): grams = lax.psum(grams, ('group', 'bulk'))  120 us
    reduce_scatter x2, waiting for transfers between devices, operate(): owed = lax.psum_scatter(buffer, 'bulk', scatter_dimension=0, tiled=True)  42.7 us
    all_gather x2, blocking collectives, operate(): lax.all_gather(vectors[:boundary_rows], 'group', axis=0, tiled=True)  21.6 us
    another operation x9, other arithmetic, chol_apply(): factor = jnp.linalg.cholesky(matrix)  19.6 us
    another operation x6, other arithmetic, chol_apply(): lax.linalg.triangular_solve(factor, middle, left_side=True, lower=True, t...  16.6 us
    scatter-add x2, other arithmetic, operate(): jax.ops.segment_sum(flat_terms, column_ids.reshape(-1), num_segments=grou...  10.9 us
    dot_general x2, matrix products, operate(): jnp.einsum('rknj,rkij->rni', picked, masked, precision=highest)  10.9 us
    dot_general x2, matrix products, operate(): returned = jnp.einsum('rni,rkij->rknj', vectors, masked, precision=highest)  7.8 us
  transfers between devices with their start and end apart: 8, of which 6 were waited for; matrix products, arithmetic and copies ran while one was open for 15% of the time, Pallas kernels for 0%

profile of v1, /device:TPU:0, one launch (start us, length us, event | category | flops | bytes accessed | tf_op | source)
XLA Modules:
  0.0 322.2 jit_solution(7602224859685870431)
XLA Ops:
  7.2 0.7 all-gather.3.cloned.1.call-update
  8.0 0.8 copy.72
  9.5 1.3 gather_fusion.2
  10.8 3.8 %fusion.4 = f32[4,11,128,64]{2,3,1,0:T(8,128)S(1)} fusion(f32[4,11,128,128]{3,2,1,0:T(8,128)} %param.22, f32[4,11]{1,0:T(4,128)S(1)} %fusion.99, f32[4,64,128]{2,1,0:T(8,128)} %param.20), kind=kOutput, calls=%fused_computation.11 | convolution fusion | flops 554369024 | bytes 4456624 | tf_op jit(solution)/shard_map/rni,rkij->rknj/dot_general | solution.py:41
  14.8 3.1 scatter_fusion
  17.8 1.0 copy-done.5
  19.0 11.1 %all_gather.13 = f32[8,64,128]{2,1,0:T(8,128)} all-gather(f32[2,64,128]{2,1,0:T(8,128)S(1)} %slice.137), channel_id=1, replica_groups=mesh['group'=4,'bulk'=8] {'group'}, dimensions={0}, use_global_device_ids=true | all-gather | bytes 327680 | tf_op jit(solution)/shard_map/all_gather | solution.py:39
  30.1 4.4 %all-gather.3.cloned.1.call-done = f32[32,64,128]{2,1,0:T(8,128)} async-done(((f32[4,64,128]{2,1,0:T(8,128)}), f32[32,64,128]{2,1,0:T(8,128)}) %all-gather.3.cloned.1.call-update) | async-done | bytes 1048592 | tf_op jit(solution)/shard_map/all_gather | solution.py:43
  34.5 3.0 gather_fusion.1
  37.5 5.4 %fusion.12 = f32[4,64,128]{2,1,0:T(8,128)} fusion(f32[4,11,64,128]{3,2,1,0:T(8,128)} %bitcast.276, f32[4,11,128,128]{3,2,1,0:T(8,128)S(1)} %copy-done.2, f32[4,11]{1,0:T(4,128)S(1)} %fusion.99), kind=kOutput, calls=%fused_computation.19 | convolution fusion | flops 554369024 | bytes 4456624 | tf_op jit(solution)/shard_map/rknj,rkij->rni/dot_general | solution.py:48
  42.9 25.9 %reduce-scatter.3.cloned.1.call-done = f32[4,64,128]{2,1,0:T(8,128)} async-done(((f32[32,64,128]{2,1,0:T(8,128)}), f32[4,64,128]{2,1,0:T(8,128)}) %reduce-scatter.3.cloned.1.call-update) | async-done | bytes 131088 | tf_op jit(solution)/shard_map/reduce_scatter | solution.py:45
  68.8 1.7 fusion.19
  70.5 1.6 fusion.25
  72.8 0.7 copy-done.3
  73.5 4.0 %fusion = f32[4,11,128,64]{2,3,1,0:T(8,128)} fusion(f32[4,11,128,128]{3,2,1,0:T(8,128)S(1)} %copy-done.2, f32[4,11]{1,0:T(4,128)S(1)} %fusion.99, f32[4,64,128]{2,1,0:T(8,128)} %copy-done.3), kind=kOutput, calls=%fused_computation.7 | convolution fusion | flops 554369024 | bytes 4456624 | tf_op jit(solution)/shard_map/rni,rkij->rknj/dot_general | solution.py:41
  77.5 1.1 broadcast.205
  78.6 7.8 %scatter_fusion.1 = f32[32,64,128]{2,1,0:T(8,128)} fusion(f32[32,64,128]{2,1,0:T(8,128)} %broadcast.205, s32[44]{0:T(128)S(1)} %copy-done.16, f32[44,64,128]{2,1,0:T(8,128)} %bitcast.273), kind=kCustom, calls=%fused_computation.6 | custom fusion | flops 360448 | bytes 4325552 | tf_op jit(solution)/shard_map/scatter-add | solution.py:44
  86.5 1.1 gather_fusion.4
  87.7 1.8 convolution_bitcast_fusion.10
  89.5 10.5 %all_gather.15 = f32[8,64,128]{2,1,0:T(8,128)} all-gather(f32[2,64,128]{2,1,0:T(8,128)} %copy-done.9), channel_id=1, replica_groups=mesh['group'=4,'bulk'=8] {'group'}, dimensions={0}, use_global_device_ids=true | all-gather | bytes 327680 | tf_op jit(solution)/shard_map/all_gather | solution.py:39
  100.1 0.9 convolution_bitcast_fusion.8
  100.9 1.8 convolution_bitcast_fusion.9
  102.7 3.0 gather_fusion.3
  105.7 5.4 %fusion.15 = f32[4,64,128]{2,1,0:T(8,128)} fusion(f32[4,11,64,128]{3,2,1,0:T(8,128)} %bitcast.274, f32[4,11,128,128]{3,2,1,0:T(8,128)S(1)} %copy-done.2, f32[4,11]{1,0:T(4,128)S(1)} %fusion.99), kind=kOutput, calls=%fused_computation.20 | convolution fusion | flops 554369024 | bytes 4456624 | tf_op jit(solution)/shard_map/rknj,rkij->rni/dot_general | solution.py:48
  111.1 16.8 %reduce-scatter.5.cloned.1.call-done = f32[4,64,128]{2,1,0:T(8,128)} async-done(((f32[32,64,128]{2,1,0:T(8,128)}), f32[4,64,128]{2,1,0:T(8,128)}) %reduce-scatter.5.cloned.1.call-update) | async-done | bytes 131088 | tf_op jit(solution)/shard_map/reduce_scatter | solution.py:45
  128.0 1.7 fusion.18
  129.6 1.6 fusion.24
  131.5 0.7 pad_maximum_fusion
  132.2 0.6 fusion.100
  134.6 120.1 %all-reduce.2.cloned.1.call-done = f32[4,64,64]{2,1,0:T(8,128)} async-done(((f32[4,64,64]{2,1,0:T(8,128)}), f32[4,64,64]{2,1,0:T(8,128)}) %all-reduce.2.cloned.1.call-update) | async-done | bytes 65552 | tf_op jit(solution)/shard_map/psum | solution.py:89
  254.7 0.9 slice_bitcast_fusion.2
  255.8 0.8 multiply_add_fusion
  256.9 5.9 %cholesky.59 = f32[64,64]{1,0:T(8,128)S(1)} custom-call(f32[64,64]{1,0:T(8,128)S(1)} %copy.82), custom_call_target="Cholesky" | custom-call | tf_op jit(solution)/shard_map/jit(cholesky)/cholesky | solution.py:17
  262.8 0.6 compare_reduce_fusion.2
  263.4 0.7 fusion.30
  264.1 4.9 %custom-call.13 = f32[1,64,64]{1,2,0:T(8,128)S(1)} custom-call(f32[1,64,64]{2,1,0:T(8,128)S(1)} %fusion.30), custom_call_target="InvertDiagBlocksLowerTriangular" | custom-call | tf_op jit(solution)/shard_map/triangular_solve/custom-call.2 | solution.py:19
  269.9 5.9 %cholesky.70 = f32[64,64]{1,0:T(8,128)S(1)} custom-call(f32[64,64]{1,0:T(8,128)S(1)} %copy.85), custom_call_target="Cholesky" | custom-call | tf_op jit(solution)/shard_map/jit(cholesky)/cholesky | solution.py:17
  276.4 0.7 fusion.31
  277.1 4.9 %custom-call.15 = f32[1,64,64]{1,2,0:T(8,128)S(1)} custom-call(f32[1,64,64]{2,1,0:T(8,128)S(1)} %fusion.31), custom_call_target="InvertDiagBlocksLowerTriangular" | custom-call | tf_op jit(solution)/shard_map/triangular_solve/custom-call.2 | solution.py:19
  285.6 5.8 %cholesky.81 = f32[64,64]{1,0:T(8,128)S(1)} custom-call(f32[64,64]{1,0:T(8,128)S(1)} %fusion.46), custom_call_target="Cholesky" | custom-call | tf_op jit(solution)/shard_map/jit(cholesky)/cholesky | solution.py:17
  292.1 0.7 fusion.32
  292.8 4.9 %custom-call.17 = f32[1,64,64]{1,2,0:T(8,128)S(1)} custom-call(f32[1,64,64]{2,1,0:T(8,128)S(1)} %fusion.32), custom_call_target="InvertDiagBlocksLowerTriangular" | custom-call | tf_op jit(solution)/shard_map/triangular_solve/custom-call.2 | solution.py:19
  303.5 1.5 collective-permute-start.1
  305.0 3.1 collective-permute-done.1
  308.0 1.5 collective-permute-start.2
  309.5 0.7 and_reduce_fusion
  310.3 4.0 %collective-permute-done.2 = f32[16384]{0:T(1024)S(1)} collective-permute-done((f32[16384]{0:T(1024)S(1)}, f32[16384]{0:T(1024)S(1)}, u32[]{:S(2)}, u32[]{:S(2)}) %collective-permute-start.2) | collective-permute-done | bytes 65568 | tf_op jit(solution)/shard_map/ppermute | solution.py:13
  314.3 0.7 fusion.34
  (118 shorter events, 12.1 us)
Async XLA Ops:
  7.2 63.4 %copy-start = (f32[2,4,128,128]{3,2,1,0:T(8,128)S(1)}, f32[2,4,128,128]{3,2,1,0:T(8,128)}, u32[]{:S(2)}) copy-start(f32[2,4,128,128]{3,2,1,0:T(8,128)} %param.23) | copy-start | bytes 1572868
  7.2 27.3 %all-gather.3.cloned.1.call-start = ((), (), s32[]{:S(2)}) async-start(), calls=%async_computation.2 | async-start | bytes 1179648 | tf_op jit(solution)/shard_map/all_gather | solution.py:43
  7.9 60.9 %reduce-scatter.3.cloned.1.call-start = ((), (), s32[]{:S(2)}) async-start(), calls=%async_computation.3 | async-start | bytes 1179648 | tf_op jit(solution)/shard_map/reduce_scatter | solution.py:45
  9.5 5.3 %copy-start.15 = (s32[44]{0:T(128)}, s32[44]{0:T(128)S(1)}, u32[]{:S(2)}) copy-start(s32[44]{0:T(128)S(1)} %reshape.290) | copy-start | bytes 532
  14.7 4.1 %copy-start.6 = (f32[4,64,128]{2,1,0:T(8,128)S(1)}, f32[4,64,128]{2,1,0:T(8,128)}, u32[]{:S(2)}) copy-start(f32[4,64,128]{2,1,0:T(8,128)} %param.20) | copy-start | bytes 393220
  17.8 1.0 copy-start.5
  18.8 83.9 %all-gather.5.cloned.1.call-start = ((), (), s32[]{:S(2)}) async-start(), calls=%async_computation.4 | async-start | bytes 1179648 | tf_op jit(solution)/shard_map/all_gather | solution.py:43
  30.1 7.3 %copy-start.2 = (f32[4,11,128,128]{3,2,1,0:T(8,128)S(1)}, f32[4,11,128,128]{3,2,1,0:T(8,128)}, u32[]{:S(2)}) copy-start(f32[4,11,128,128]{3,2,1,0:T(8,128)} %param.22) | copy-start | bytes 8650756
  72.1 0.6 copy-start.9
  72.8 0.7 copy-start.3
  73.5 5.2 %copy-start.16 = (s32[44]{0:T(128)S(1)}, s32[44]{0:T(128)}, u32[]{:S(2)}) copy-start(s32[44]{0:T(128)} %copy-done.15) | copy-start | bytes 532
  73.5 54.5 %reduce-scatter.5.cloned.1.call-start = ((), (), s32[]{:S(2)}) async-start(), calls=%async_computation.5 | async-start | bytes 1179648 | tf_op jit(solution)/shard_map/reduce_scatter | solution.py:45
  78.6 7.9 %copy-start.1 = (s32[128]{0:T(128)S(1)}, s32[128]{0:T(128)}, u32[]{:S(2)}) copy-start(s32[128]{0:T(128)} %param.26) | copy-start | bytes 1540
  86.5 13.6 %copy-start.4 = (f32[4,64,128]{2,1,0:T(8,128)S(1)}, f32[4,64,128]{2,1,0:T(8,128)}, u32[]{:S(2)}) copy-start(f32[4,64,128]{2,1,0:T(8,128)} %copy-done.3) | copy-start | bytes 393220
  86.5 168.2 %all-reduce.2.cloned.1.call-start = ((), (), s32[]{:S(2)}) async-start(), calls=%async_computation.6 | async-start | bytes 262144 | tf_op jit(solution)/shard_map/psum | solution.py:89
  111.1 20.4 %copy-start.12 = (f32[1,64,64]{2,1,0:T(8,128)S(1)}, f32[1,64,64]{2,1,0:T(8,128)}, u32[]{:S(2)}) copy-start(f32[1,64,64]{2,1,0:T(8,128)} %convolution_bitcast_fusion.10) | copy-start | bytes 49156
  111.1 20.4 %copy-start.13 = (f32[1,64,64]{2,1,0:T(8,128)S(1)}, f32[1,64,64]{2,1,0:T(8,128)}, u32[]{:S(2)}) copy-start(f32[1,64,64]{2,1,0:T(8,128)} %convolution_bitcast_fusion.8) | copy-start | bytes 49156
  111.1 20.4 %copy-start.14 = (f32[1,64,64]{2,1,0:T(8,128)S(1)}, f32[1,64,64]{2,1,0:T(8,128)}, u32[]{:S(2)}) copy-start(f32[1,64,64]{2,1,0:T(8,128)} %convolution_bitcast_fusion.9) | copy-start | bytes 49156
  111.1 21.1 %copy-start.17 = (s32[4]{0:T(128)S(1)}, s32[4]{0:T(128)}, u32[]{:S(2)}) copy-start(s32[4]{0:T(128)} %gather_fusion.4) | copy-start | bytes 52
  254.7 28.0 %copy-start.8 = (f32[4,64,64]{2,1,0:T(8,128)S(1)}, f32[4,64,64]{2,1,0:T(8,128)}, u32[]{:S(2)}) copy-start(f32[4,64,64]{2,1,0:T(8,128)} %all-reduce.2.cloned.1.call-done) | copy-start | bytes 196612
  282.3 16.1 %copy-start.7 = (f32[4,64,128]{2,1,0:T(8,128)S(1)}, f32[4,64,128]{2,1,0:T(8,128)}, u32[]{:S(2)}) copy-start(f32[4,64,128]{2,1,0:T(8,128)} %param.20) | copy-start | bytes 393220
  298.1 11.4 %copy-start.18 = (s32[3]{0:T(128)S(1)}, s32[3]{0:T(128)}, u32[]{:S(2)}) copy-start(s32[3]{0:T(128)} %constant.176.clone.1) | copy-start | bytes 40
  300.2 3.3 %collective-permute-start = (f32[16384]{0:T(1024)S(1)}, f32[16384]{0:T(1024)S(1)}, u32[]{:S(2)}, u32[]{:S(2)}) collective-permute-start(f32[16384]{0:T(1024)S(1)} %pad_maximum_fusion.1), channel_id=1, source_target_pairs={{0,1},{1,0},{2,3},{3,2},{4,5},{5,4},{6,7},{7,6},{8,9},{9,8},{10,11... | collective-permute-start | bytes 196616 | tf_op jit(solution)/shard_map/ppermute | solution.py:13
  303.5 4.6 %collective-permute-start.1 = (f32[16384]{0:T(1024)S(1)}, f32[16384]{0:T(1024)S(1)}, u32[]{:S(2)}, u32[]{:S(2)}) collective-permute-start(f32[16384]{0:T(1024)S(1)} %broadcast_select_fusion), channel_id=1, source_target_pairs={{0,2},{1,3},{2,0},{3,1},{4,6},{5,7},{6,4},{7,5},{8,10},{9,11},{10,... | collective-permute-start | bytes 196616 | tf_op jit(solution)/shard_map/ppermute | solution.py:13
  308.0 6.2 %collective-permute-start.2 = (f32[16384]{0:T(1024)S(1)}, f32[16384]{0:T(1024)S(1)}, u32[]{:S(2)}, u32[]{:S(2)}) collective-permute-start(f32[16384]{0:T(1024)S(1)} %broadcast_select_fusion.1), channel_id=1, source_target_pairs={{0,4},{1,5},{2,6},{3,7},{4,0},{5,1},{6,2},{7,3},{8,12},{9,13},{10,... | collective-permute-start | bytes 196616 | tf_op jit(solution)/shard_map/ppermute | solution.py:13
  315.0 0.7 copy-start.10
  315.0 0.7 copy-start.11
Sparse Core Ops, SparseCore 0:
  9.6 24.8 all-gather.2
  36.8 31.9 reduce-scatter.2
  73.6 20.2 all-gather.4
  96.0 31.8 reduce-scatter.4
  133.9 120.7 all-reduce.1

commit v2 on v0

v2 whole, which is shorter than its diff:
```python
import functools

import jax
import jax.numpy as jnp
from jax import lax
from jax.experimental import pallas as pl
from jax.experimental.pallas import tpu as pltpu
from jax.sharding import PartitionSpec as P

shift = 4.0
f32 = jnp.float32
bf16 = jnp.bfloat16
normal = (((1,), (0,)), ((), ()))
right_t = (((1,), (1,)), ((), ()))
left_t = (((0,), (0,)), ((), ()))
vmem = pl.BlockSpec(memory_space=pltpu.VMEM)
smem = pl.BlockSpec(memory_space=pltpu.SMEM)
vmem_bytes = 32 * 2**20


def params():
    return pltpu.CompilerParams(vmem_limit_bytes=vmem_bytes)


def swap(value, axis, mask):
    pairs = [(source, source ^ mask) for source in range(lax.axis_size(axis))]
    return lax.ppermute(value, axis, pairs)


def split(value):
    high = value.astype(bf16)
    return high, (value - high.astype(f32)).astype(bf16)


def dot16(left, right, dims):
    return lax.dot_general(left, right, dims, preferred_element_type=f32)


def dot32(left, right, dims=normal):
    return lax.dot_general(
        left, right, dims, preferred_element_type=f32, precision=lax.Precision.HIGHEST
    )


def split_rows(vectors):
    high, low = split(vectors)
    return jnp.concatenate([high, low], axis=0)


def times_tile(rows, tile, dims):
    count = rows.shape[0] // 2
    high, low = split(tile)
    both = dot16(rows, high, dims)
    return both[:count] + both[count:] + dot16(rows[:count], low, dims)


def pack(gram):
    half = gram.shape[0] // 2
    return jnp.concatenate([gram[:half], gram[half:]], axis=1)


def unpack(packed):
    half = packed.shape[1] // 2
    return jnp.concatenate([packed[:, :half], packed[:, half:]], axis=0)


def sym(gram):
    return 0.5 * (gram + gram.T)


def first_slot(row_count):
    device = lax.axis_index("group") * lax.axis_size("bulk") + lax.axis_index("bulk")
    return device * row_count


def live(load_ref, slot, tile):
    return jnp.where(tile < load_ref[slot], 1.0, 0.0)


def returned_kernel(bulk_count, moved, vectors, tiles, col, load, new_slot, *outs):
    row_count, count = vectors.shape[:2]
    me = lax.axis_index("bulk")
    base = lax.axis_index("group") * bulk_count * row_count
    total = outs[-1]
    s = pl.program_id(0)
    slot = first_slot(row_count) + s

    @pl.when(s == 0)
    def _():
        total[...] = jnp.zeros_like(total)

    rows = split_rows(vectors[s])
    for t in range(tiles.shape[1]):
        product = times_tile(rows, tiles[0, t], normal)
        target = col[slot, t]
        if moved:
            place = new_slot[target] - base
        else:
            target = target - base
            owner = target // row_count
            rel = owner ^ me
            order = (rel & 1) * (bulk_count // 2) + (rel >> 1)
            place = order * row_count + target - owner * row_count
        total[place] += live(load, slot, t) * product

    if not moved:

        @pl.when(s == row_count - 1)
        def _():
            half = total.shape[0] // 2
            outs[0][...] = total[:half]
            outs[1][...] = total[half:]


def returned(vectors, tiles, col, load, new_slot, bulk_count, moved):
    row_count, count, order = vectors.shape
    tile_count = tiles.shape[1]
    whole = (bulk_count * row_count, count, order)
    half = (bulk_count * row_count // 2, count, order)
    out_shapes = [whole] if moved else [half, half]
    return pl.pallas_call(
        functools.partial(returned_kernel, bulk_count, moved),
        grid=(row_count,),
        out_shape=[jax.ShapeDtypeStruct(shape, f32) for shape in out_shapes],
        in_specs=[
            vmem,
            pl.BlockSpec((1, tile_count, order, order), lambda s: (s, 0, 0, 0)),
            smem,
            smem,
            smem,
        ],
        out_specs=[vmem for _ in out_shapes],
        scratch_shapes=[] if moved else [pltpu.VMEM(whole, f32)],
        compiler_params=params(),
        name="returned_moved" if moved else "returned",
    )(vectors, tiles, col, load, new_slot)


def near_kernel(bulk_count, pieces, second, *refs):
    refs = list(refs)
    panel = [refs.pop(0) for _ in range(pieces)]
    vectors, tiles, diag, coupling = refs[:4]
    part_count = coupling.shape[1]
    border = refs[4 : 3 + part_count]
    col, load, new_slot, near, moving, extra, rows_of, gram = refs[3 + part_count :]
    row_count, count, order = near.shape[0], near.shape[1], near.shape[2]
    row_count = vectors.shape[0] if not second else row_count
    me = lax.axis_index("bulk")
    mine = lax.axis_index("group")
    base = mine * bulk_count * row_count
    s = pl.program_id(0)
    slot = first_slot(row_count) + s
    per_piece = bulk_count * row_count // pieces

    def place_of(target):
        target = target - base
        owner = target // row_count
        if second:
            return (owner ^ me) * row_count + target - owner * row_count
        return target

    @pl.when(s == 0)
    def _():
        for index, piece in enumerate(panel):
            for k in range(per_piece):
                value = piece[k * count : (k + 1) * count] if second else piece[k]
                rows_of[index * per_piece + k] = split_rows(value)
        gram[...] = jnp.zeros_like(gram)

    def own(k):
        return vectors[k]

    direct = None
    for t in range(tiles.shape[1]):
        rows = rows_of[place_of(col[slot, t])]
        high, low = split(tiles[0, t])
        alive = live(load, slot, t)
        both = alive * dot16(rows, high, right_t)
        rest = alive * dot16(rows[:count], low, right_t)
        direct = (both, rest) if direct is None else (direct[0] + both, direct[1] + rest)
    direct = direct[0][:count] + direct[0][count:] + direct[1]
    value = vectors[s]
    near_value = times_tile(split_rows(value), diag[0], right_t)
    near[s] = near_value + direct
    if second:
        gram[...] += dot32(value, near_value + 2.0 * direct, right_t)
    else:
        gram[...] += dot32(value, value, right_t)

    @pl.when(s < coupling.shape[0])
    def _():
        k = jnp.minimum(s, coupling.shape[0] - 1)
        crossed = times_tile(split_rows(value), coupling[k, mine], right_t)
        for index, ref in enumerate(border):
            tile = coupling[k, mine ^ (index + 1)]
            crossed = crossed + times_tile(split_rows(ref[k]), tile, right_t)
        near[s] += crossed
        if second:
            gram[...] += dot32(value, crossed, right_t)

    arriving = new_slot[slot]
    if second:
        incoming = place_of(arriving)
        for index, piece in enumerate(panel):

            @pl.when(incoming // row_count == index)
            def _(piece=piece):
                start = pl.multiple_of(incoming % row_count * count, count)
                moving[s] = piece[pl.ds(start, count)]

        @pl.when(arriving != slot)
        def _():
            extra[count // 2 :] = near[s]

    else:
        moving[s] = panel[0][place_of(arriving)]

    @pl.when(s == row_count - 1)
    def _():
        extra[: count // 2] = pack(gram[...])


def near_part(panel, vectors, tiles, diag, coupling, border, col, load, new_slot, bulk_count, second):
    row_count, count, order = vectors.shape
    tile_count = tiles.shape[1]
    extra_rows = count // 2 + (count if second else 0)
    shapes = [vectors.shape, vectors.shape, (extra_rows, order)]
    return pl.pallas_call(
        functools.partial(near_kernel, bulk_count, len(panel), second),
        grid=(row_count,),
        out_shape=[jax.ShapeDtypeStruct(shape, f32) for shape in shapes],
        in_specs=[vmem] * len(panel)
        + [
            vmem,
            pl.BlockSpec((1, tile_count, order, order), lambda s: (s, 0, 0, 0)),
            pl.BlockSpec((1, order, order), lambda s: (s, 0, 0)),
            vmem,
        ]
        + [vmem] * len(border)
        + [smem] * 3,
        out_specs=[vmem] * 3,
        scratch_shapes=[
            pltpu.VMEM((bulk_count * row_count, 2 * count, order), bf16),
            pltpu.VMEM((count, count), f32),
        ],
        compiler_params=params(),
        name="near_second" if second else "near_first",
    )(*panel, vectors, tiles, diag, coupling, *border, col, load, new_slot)


def gather_first_kernel(vectors, near, keep, *refs):
    received = refs[:-4]
    packed, first, flat, edge = refs[-4:]
    row_count, count = vectors.shape[:2]
    grams = [None, None]
    for k in range(row_count):
        value = near[k] + keep[k]
        for ref in received:
            value = value + ref[k]
        first[k] = value
        flat[k * count : (k + 1) * count] = value
        if k < edge.shape[0]:
            edge[k] = value
        terms = (dot32(vectors[k], value, right_t), dot32(value, value, right_t))
        grams = [term if old is None else old + term for old, term in zip(grams, terms)]
    start = row_count * count
    half = count // 2
    flat[start : start + half] = packed[...]
    flat[start + half : start + 2 * half] = pack(grams[0])
    flat[start + 2 * half :] = pack(grams[1])


def gather_first(vectors, near, keep, received, packed, edge_rows):
    row_count, count, order = vectors.shape
    shapes = [
        vectors.shape,
        (row_count * count + 3 * (count // 2), order),
        (edge_rows, count, order),
    ]
    specs = [pl.BlockSpec((row_count, count, order), lambda s: (0, 0, 0))] * (3 + len(received))
    return pl.pallas_call(
        gather_first_kernel,
        grid=(1,),
        out_shape=[jax.ShapeDtypeStruct(shape, f32) for shape in shapes],
        in_specs=specs + [vmem],
        out_specs=[vmem] * 3,
        compiler_params=params(),
        name="gather_first",
    )(vectors, near, keep, *received, packed)


def inverse_factors(matrices):
    count = matrices[0].shape[0]
    blocks = count // 8
    row_ids = lax.broadcasted_iota(jnp.int32, (count, count), 0)
    col_ids = lax.broadcasted_iota(jnp.int32, (count, count), 1)
    eye = (row_ids == col_ids).astype(f32)
    sub = lax.broadcasted_iota(jnp.int32, (8, 2 * count), 0)
    work = []
    for matrix in matrices:
        both = jnp.concatenate([matrix, eye], axis=1)
        work.append([both[8 * i : 8 * i + 8] for i in range(blocks)])
    for j in range(count):
        block, k = divmod(j, 8)
        for w in work:
            row = w[block][k : k + 1]
            scale = lax.rsqrt(row[:, j : j + 1])
            pivot = row * scale
            for i in range(block, blocks):
                changed = w[i] - w[i][:, j : j + 1] * scale * pivot
                if i == block:
                    changed = jnp.where(sub > k, changed, jnp.where(sub == k, pivot, w[i]))
                w[i] = changed
    return [jnp.concatenate(w, axis=0)[:, count:] for w in work]


def solve(inverse_factor, right):
    return dot32(inverse_factor, dot32(inverse_factor, right), left_t)


def early_kernel(packed, out):
    count = out.shape[1]
    half = count // 2
    g0, g1, g2 = (sym(unpack(packed[i * half : (i + 1) * half])) for i in range(3))
    eye = (
        lax.broadcasted_iota(jnp.int32, (count, count), 0)
        == lax.broadcasted_iota(jnp.int32, (count, count), 1)
    ).astype(f32)
    factor_pq, factor_rr = inverse_factors([shift * g0 + g1, g0])
    a = solve(factor_pq, g0)
    m = eye - shift * a
    cross = dot32(m, dot32(g1, a), left_t)
    g_new = dot32(m, dot32(g0, m), left_t) - cross - cross.T + dot32(a, dot32(g2, a), left_t)
    g_new = sym(g_new)
    c = m + solve(factor_rr, g_new)
    cross = dot32(c, dot32(shift * g1 + g2, a), left_t)
    g_pq = dot32(c, dot32(shift * g0 + g1, c), left_t) - cross - cross.T
    out[0] = a
    out[1] = c
    out[2] = g_new
    out[3] = g_pq + shift * dot32(a, dot32(g2, a), left_t)


def early(packed, count):
    return pl.pallas_call(
        early_kernel,
        out_shape=jax.ShapeDtypeStruct((4, count, count), f32),
        in_specs=[vmem],
        out_specs=vmem,
        compiler_params=params(),
        name="early_solves",
    )(packed)


def final_kernel(packed, small, moving, first, near, row, owed, new_slot, solution, resid):
    row_count, count = moving.shape[:2]
    a, c, g_new, g_pq = (small[i] for i in range(4))
    g3 = sym(unpack(packed[...]))
    g_pq = sym(g_pq + dot32(a, dot32(g3, a), left_t))
    (factor,) = inverse_factors([g_pq])
    a1 = solve(factor, g_new)
    aa1 = dot32(a, a1)
    ca1 = dot32(c, a1)
    eye = (
        lax.broadcasted_iota(jnp.int32, (count, count), 0)
        == lax.broadcasted_iota(jnp.int32, (count, count), 1)
    ).astype(f32)
    m = eye - shift * a
    zero = jnp.zeros_like(a)
    top = jnp.concatenate([a + ca1, -aa1, zero], axis=0)
    low = jnp.concatenate([m - shift * ca1, shift * aa1 - a - ca1, aa1], axis=0)
    coef = jnp.concatenate([top, low], axis=1)
    slot = first_slot(row_count)
    for k in range(row_count):
        stays = new_slot[slot + k] == slot + k
        second = jnp.where(stays, near[k], row[...]) + owed[k]
        basis = jnp.concatenate([moving[k], first[k], second], axis=0)
        both = dot32(coef, basis, left_t)
        solution[k] = both[:count]
        resid[k] = both[count:]


def final(packed, small, moving, first, near, row, owed, new_slot):
    return pl.pallas_call(
        final_kernel,
        out_shape=[jax.ShapeDtypeStruct(near.shape, f32)] * 2,
        in_specs=[vmem] * 7 + [smem],
        out_specs=[vmem] * 2,
        compiler_params=params(),
        name="final",
    )(packed, small, moving, first, near, row, owed, new_slot)


def local(rhs, diag_tiles, offdiag_blocks, coupling, col_index, load, new_slot):
    row_count, count, order = rhs.shape
    edge_rows, part_count = coupling.shape[:2]
    bulk_count = lax.axis_size("bulk")
    half = count // 2
    my_bulk = lax.axis_index("bulk")
    slot = first_slot(row_count)
    own_new = lax.dynamic_slice(new_slot, (slot,), (row_count,))
    own_slots = slot + jnp.arange(row_count, dtype=jnp.int32)
    target = jnp.max(jnp.where(own_new != own_slots, own_new, -1))
    xor_mask = (target // row_count % bulk_count) ^ my_bulk

    keep, send = returned(rhs, offdiag_blocks, col_index, load, new_slot, bulk_count, False)
    panel = lax.all_gather(rhs, "bulk", axis=0, tiled=True)
    border = [swap(rhs[:edge_rows], "group", mask) for mask in range(1, part_count)]
    from_core = swap(send, "bulk", 1)
    received = [from_core]
    for z in range(1, bulk_count // 2):
        rows = slice(z * row_count, (z + 1) * row_count)
        received.append(swap(keep[rows] + from_core[rows], "bulk", 2 * z))
    near, moving, packed = near_part(
        [panel], rhs, offdiag_blocks, diag_tiles, coupling, border, col_index, load, new_slot,
        bulk_count, False,
    )
    first, flat, edge = gather_first(rhs, near, keep, received, packed, edge_rows)

    far = [swap(flat, "bulk", 2 * z) for z in range(1, bulk_count // 2)]
    border = [swap(edge, "group", mask) for mask in range(1, part_count)]
    (owed,) = returned(first, offdiag_blocks, col_index, load, new_slot, bulk_count, True)
    owed = lax.psum_scatter(owed, "bulk", scatter_dimension=0, tiled=True)
    panel = []
    for piece in [flat] + far:
        panel += [piece, swap(piece, "bulk", 1)]
    grams = sum(piece[row_count * count :] for piece in panel)
    mask = 1
    while mask < part_count:
        grams = grams + swap(grams, "group", mask)
        mask *= 2
    near, first, extra = near_part(
        panel, first, offdiag_blocks, diag_tiles, coupling, border, col_index, load, new_slot,
        bulk_count, True,
    )
    small = early(grams, count)

    is_gram = lax.broadcasted_iota(jnp.int32, extra.shape, 0) < half
    mask = 1
    while mask < bulk_count:
        partner = swap(extra, "bulk", mask)
        chosen = jnp.bitwise_and(xor_mask, mask) != 0
        extra = jnp.where(is_gram, extra + partner, jnp.where(chosen, partner, extra))
        mask *= 2
    gram, row = extra[:half], extra[half:]
    mask = 1
    while mask < part_count:
        gram = gram + swap(gram, "group", mask)
        mask *= 2
    return tuple(final(gram, small, moving, first, near, row, owed, new_slot))


def solution(mesh):
    rows = P(("group", "bulk"))
    return jax.shard_map(
        local,
        mesh=mesh,
        in_specs=(rows, rows, rows, rows, P(), P(), P()),
        out_specs=(rows, rows),
        check_vma=False,
    )
```

time: 346 us -> 152 us (0.44)
  blocking collectives: 141 us -> 0 us
  other arithmetic: 64.2 us -> 2.8 us
  matrix products: 37.7 us -> 0 us
  Pallas kernels: 0 us -> 36.3 us
  starting transfers between devices: 5.05 us -> 28.5 us
  waiting for transfers between devices: 53.5 us -> 41.4 us
    psum x3 -> x0, blocking collectives: 119 us -> none  [global_gram(): total = lax.psum(partial_gram, ('group', 'bulk'))]
    another operation x17 -> x0, other arithmetic: 48 us -> none  [the longest x9 23.9 us: chol_apply(): factor = jnp.linalg.cholesky(matrix)]
    reduce_scatter x2 -> x1, waiting for transfers between devices: 42.6 us -> 0.02 us  [local(): owed = lax.psum_scatter(owed, 'bulk', scatter_dimension=0, tiled=True)]
    pallas_call x0 -> x7, Pallas kernels: none -> 36.3 us  [the longest x2 12.2 us: near_part(): pl.pallas_call(functools.partial(near_kernel, bulk_count, len(panel), sec...]
    dot_general x17 -> x0, matrix products: 33.3 us -> none  [the longest x2 10.9 us: operate(): jnp.einsum('rknj,rkij->rni', picked, masked, precision=highest)]
    ppermute x3 -> x24, waiting for transfers between devices: 6.68 us -> 33 us  [swap(): return lax.ppermute(value, axis, pairs)]
    ppermute x3 -> x24, starting transfers between devices: 4.89 us -> 28.5 us  [swap(): return lax.ppermute(value, axis, pairs)]
    all_gather x2 -> x0, blocking collectives: 21.9 us -> none  [operate(): lax.all_gather(vectors[:boundary_rows], 'group', axis=0, tiled=True)]
  transfers between devices with their start and end apart: 7 -> 26, of which waited for: 5 -> 12; matrix products, arithmetic and copies ran while one was open for 14% -> 3% of each run, Pallas kernels for 0% -> 15%
where the time goes in v2:
time: 152 us; the launch traced here: 151 us
  waiting for transfers between devices  41.4 us (27%)
  Pallas kernels  36.3 us (24%)
  starting transfers between devices  28.5 us (19%)
  local copies, waits for them, and re-layouts  25.5 us (17%)
  between operations  16.7 us (11%)
  other arithmetic  2.8 us (2%)
    ppermute x24, waiting for transfers between devices, swap(): return lax.ppermute(value, axis, pairs)  33 us
    ppermute x24, starting transfers between devices, swap(): return lax.ppermute(value, axis, pairs)  28.5 us
    unnamed x93, local copies, waits for them, and re-layouts  25.5 us
    pallas_call x2, Pallas kernels, near_part(): pl.pallas_call(functools.partial(near_kernel, bulk_count, len(panel), sec...  12.2 us
    pallas_call x1, Pallas kernels, final(): pl.pallas_call(final_kernel, out_shape=[jax.ShapeDtypeStruct(near.shape,...  8.36 us
    pallas_call x1, Pallas kernels, early(): pl.pallas_call(early_kernel, out_shape=jax.ShapeDtypeStruct((4, count, co...  7.72 us
    all_gather x1, waiting for transfers between devices, local(): panel = lax.all_gather(rhs, 'bulk', axis=0, tiled=True)  7.62 us
    pallas_call x2, Pallas kernels, returned(): pl.pallas_call(functools.partial(returned_kernel, bulk_count, moved), gri...  6.52 us
  transfers between devices with their start and end apart: 26, of which 12 were waited for; matrix products, arithmetic and copies ran while one was open for 3% of the time, Pallas kernels for 15%

profile of v2, /device:TPU:0, one launch (start us, length us, event | category | flops | bytes accessed | tf_op | source)
XLA Modules:
  0.0 151.3 jit_solution(4471978840328803453)
XLA Ops:
  8.0 1.4 copy.13.refs_8_.col.refs_15_
  9.4 1.8 %copy-done = f32[4,11,128,128]{3,2,1,0:T(8,128)S(1)} copy-done((f32[4,11,128,128]{3,2,1,0:T(8,128)S(1)}, f32[4,11,128,128]{3,2,1,0:T(8,128)}, u32[]{:S(2)}) %copy-start) | copy-done | bytes 2883608
  11.2 0.9 copy-done.3
  12.1 0.8 copy-done.6
  14.3 3.3 %returned.1 = (f32[16,64,128]{2,1,0:T(8,128)S(1)}, f32[16,64,128]{2,1,0:T(8,128)S(1)}) custom-call(f32[4,64,128]{2,1,0:T(8,128)S(1)} %copy-done.3, f32[4,11,128,128]{3,2,1,0:T(8,128)S(1)} %copy-done, s32[128,11]{1,0:T(8,128)S(1)} %copy-done.6, s32[128]{0:T(128)S(1)} %copy-done.42, s32[128]{0:T(128)S(1)} %copy-done.40), custom_call_target="tpu_custom_call" | custom-call | tf_op jit(solution)/shard_map/returned/pallas_call | solution.py:121
  18.1 2.6 %collective-permute-start = (f32[2,64,128]{2,1,0:T(8,128)S(1)}, f32[2,64,128]{2,1,0:T(8,128)S(1)}, u32[]{:S(2)}, u32[]{:S(2)}) collective-permute-start(f32[2,64,128]{2,1,0:T(8,128)S(1)} %slice.53), channel_id=1, source_target_pairs={{0,8},{8,0},{16,24},{24,16},{1,9},{9,1},{17,25},{25,17},{2,10},{10... | collective-permute-start | bytes 196616 | tf_op jit(solution)/shard_map/ppermute | solution.py:27
  20.7 0.8 slice_add_fusion
  21.6 0.8 copy-done.9
  22.4 1.9 %collective-permute-start.4 = (f32[4,64,128]{2,1,0:T(8,128)}, f32[4,64,128]{2,1,0:T(8,128)}, u32[]{:S(2)}, u32[]{:S(2)}) collective-permute-start(f32[4,64,128]{2,1,0:T(8,128)} %get-tuple-element.26), channel_id=1, source_target_pairs={{0,2},{1,3},{2,0},{3,1},{4,6},{5,7},{6,4},{7,5},{8,10},{9,11},{10,... | collective-permute-start | bytes 393224 | tf_op jit(solution)/shard_map/ppermute | solution.py:27
  24.3 2.6 %collective-permute-start.5 = (f32[4,64,128]{2,1,0:T(8,128)}, f32[4,64,128]{2,1,0:T(8,128)}, u32[]{:S(2)}, u32[]{:S(2)}) collective-permute-start(f32[4,64,128]{2,1,0:T(8,128)} %get-tuple-element.25), channel_id=1, source_target_pairs={{0,4},{1,5},{2,6},{3,7},{4,0},{5,1},{6,2},{7,3},{8,12},{9,13},{10,... | collective-permute-start | bytes 393224 | tf_op jit(solution)/shard_map/ppermute | solution.py:27
  26.9 1.7 %collective-permute-start.1 = (f32[2,64,128]{2,1,0:T(8,128)S(1)}, f32[2,64,128]{2,1,0:T(8,128)S(1)}, u32[]{:S(2)}, u32[]{:S(2)}) collective-permute-start(f32[2,64,128]{2,1,0:T(8,128)S(1)} %slice.53), channel_id=1, source_target_pairs={{0,16},{8,24},{16,0},{24,8},{1,17},{9,25},{17,1},{25,9},{2,18},{10... | collective-permute-start | bytes 196616 | tf_op jit(solution)/shard_map/ppermute | solution.py:27
  29.3 1.4 collective-permute-start.2
  31.8 2.6 %collective-permute-done.2.refs_7_ = f32[2,64,128]{2,1,0:T(8,128)S(1)} collective-permute-done((f32[2,64,128]{2,1,0:T(8,128)S(1)}, f32[2,64,128]{2,1,0:T(8,128)S(1)}, u32[]{:S(2)}, u32[]{:S(2)}) %collective-permute-start.2) | collective-permute-done | bytes 65568 | tf_op jit(solution)/shard_map/ppermute | solution.py:27
  35.1 7.6 %all-gather.2.cloned.1.call-done.refs_0_ = f32[32,64,128]{2,1,0:T(8,128)} async-done(((f32[4,64,128]{2,1,0:T(8,128)}), f32[32,64,128]{2,1,0:T(8,128)}) %all-gather.2.cloned.1.call-update) | async-done | bytes 1048592 | tf_op jit(solution)/shard_map/all_gather | solution.py:407
  42.7 0.8 copy-done.7
  43.6 0.9 copy-done.13
  44.5 1.2 copy-done.15
  45.7 0.8 copy-done.35
  46.6 0.8 copy-done.37
  47.4 0.8 copy-done.39
  48.3 5.3 %near_first.1 = (f32[4,64,128]{2,1,0:T(8,128)S(1)}, f32[4,64,128]{2,1,0:T(8,128)S(1)}, f32[32,128]{1,0:T(8,128)S(1)}) custom-call(f32[32,64,128]{2,1,0:T(8,128)S(1)} %copy-done.15, f32[4,64,128]{2,1,0:T(8,128)S(1)} %copy-done.4, f32[4,11,128,128]{3,2,1,0:T(8,128)S(1)} %copy-done.1, f32[4,128,128]{2,1,0:T(8,128)S(1)} %copy-done.13, ...), custom_call_target="tpu_custom_call" | custom-call | tf_op jit(solution)/shard_map/near_first/pallas_call | solution.py:228
  53.6 1.6 %gather_first.1 = (f32[4,64,128]{2,1,0:T(8,128)S(1)}, f32[352,128]{1,0:T(8,128)S(1)}, f32[2,64,128]{2,1,0:T(8,128)S(1)}) custom-call(f32[4,64,128]{2,1,0:T(8,128)S(1)} %copy-done.4, f32[4,64,128]{2,1,0:T(8,128)S(1)} %get-tuple-element.13.near, f32[16,64,128]{2,1,0:T(8,128)S(1)} %copy-done.10, f32[16,64,128]{2,1,0:T(8,128)S(1)} %copy-done.12, ...), custom_call_target="tpu_custom_call" | custom-call | tf_op jit(solution)/shard_map/gather_first/pallas_call | solution.py:281
  56.6 3.2 %returned_moved.1 = f32[32,64,128]{2,1,0:T(8,128)S(1)} custom-call(f32[4,64,128]{2,1,0:T(8,128)S(1)} %get-tuple-element.18.refs_8_.vectors, f32[4,11,128,128]{3,2,1,0:T(8,128)S(1)} %copy-done.1, s32[128,11]{1,0:T(8,128)S(1)} %copy-done.7, s32[128]{0:T(128)S(1)} %copy-done.43, s32[128]{0:T(128)S(1)} %copy-done.41), custom_call_target="tpu_custom_call" | custom-call | tf_op jit(solution)/shard_map/returned_moved/pallas_call | solution.py:121
  59.8 1.0 copy-done.2
  61.6 1.9 %collective-permute-start.10 = (f32[352,128]{1,0:T(8,128)}, f32[352,128]{1,0:T(8,128)S(1)}, u32[]{:S(2)}, u32[]{:S(2)}) collective-permute-start(f32[352,128]{1,0:T(8,128)} %copy-done.18), channel_id=1, source_target_pairs={{0,4},{1,5},{2,6},{3,7},{4,0},{5,1},{6,2},{7,3},{8,12},{9,13},{10,... | collective-permute-start | bytes 540680 | tf_op jit(solution)/shard_map/ppermute | solution.py:27
  63.5 2.4 %collective-permute-start.12 = (f32[352,128]{1,0:T(8,128)}, f32[352,128]{1,0:T(8,128)S(1)}, u32[]{:S(2)}, u32[]{:S(2)}) collective-permute-start(f32[352,128]{1,0:T(8,128)} %copy-done.18), channel_id=1, source_target_pairs={{0,6},{1,7},{2,4},{3,5},{4,2},{5,3},{6,0},{7,1},{8,14},{9,15},{10,... | collective-permute-start | bytes 540680 | tf_op jit(solution)/shard_map/ppermute | solution.py:27
  66.0 7.9 %collective-permute-done.8.refs_2_ = f32[352,128]{1,0:T(8,128)S(1)} collective-permute-done((f32[352,128]{1,0:T(8,128)}, f32[352,128]{1,0:T(8,128)S(1)}, u32[]{:S(2)}, u32[]{:S(2)}) %collective-permute-start.8) | collective-permute-done | bytes 180256 | tf_op jit(solution)/shard_map/ppermute | solution.py:27
  73.9 6.9 %collective-permute-done.10.refs_4_ = f32[352,128]{1,0:T(8,128)S(1)} collective-permute-done((f32[352,128]{1,0:T(8,128)}, f32[352,128]{1,0:T(8,128)S(1)}, u32[]{:S(2)}, u32[]{:S(2)}) %collective-permute-start.10) | collective-permute-done | bytes 180256 | tf_op jit(solution)/shard_map/ppermute | solution.py:27
  81.3 4.3 %collective-permute-done.15.refs_13_ = f32[2,64,128]{2,1,0:T(8,128)S(1)} collective-permute-done((f32[2,64,128]{2,1,0:T(8,128)S(1)}, f32[2,64,128]{2,1,0:T(8,128)S(1)}, u32[]{:S(2)}, u32[]{:S(2)}) %collective-permute-start.15) | collective-permute-done | bytes 65568 | tf_op jit(solution)/shard_map/ppermute | solution.py:27
  86.2 4.6 %collective-permute-done.16.refs_14_ = f32[2,64,128]{2,1,0:T(8,128)S(1)} collective-permute-done((f32[2,64,128]{2,1,0:T(8,128)S(1)}, f32[2,64,128]{2,1,0:T(8,128)S(1)}, u32[]{:S(2)}, u32[]{:S(2)}) %collective-permute-start.16) | collective-permute-done | bytes 65568 | tf_op jit(solution)/shard_map/ppermute | solution.py:27
  90.8 1.1 copy-done.14
  91.9 0.9 copy-done.17
  92.8 0.9 copy-done.19
  93.7 6.8 %near_second.1 = (f32[4,64,128]{2,1,0:T(8,128)S(1)}, f32[4,64,128]{2,1,0:T(8,128)S(1)}, f32[96,128]{1,0:T(8,128)S(1)}) custom-call(f32[352,128]{1,0:T(8,128)S(1)} %copy-done.19, f32[352,128]{1,0:T(8,128)S(1)} %collective-permute-done.7.refs_1_, f32[352,128]{1,0:T(8,128)S(1)} %collective-permute-done.8.refs_2_, ...), custom_call_target="tpu_custom_call" | custom-call | tf_op jit(solution)/shard_map/near_second/pallas_call | solution.py:228
  105.0 5.7 %collective-permute-start.18 = (f32[96,128]{1,0:T(8,128)S(1)}, f32[96,128]{1,0:T(8,128)S(1)}, u32[]{:S(2)}, u32[]{:S(2)}) collective-permute-start(f32[96,128]{1,0:T(8,128)S(1)} %select_select_fusion.2), channel_id=1, source_target_pairs={{0,2},{1,3},{2,0},{3,1},{4,6},{5,7},{6,4},{7,5},{8,10},{9,11},{10,... | collective-permute-start | bytes 147464 | tf_op jit(solution)/shard_map/ppermute | solution.py:27
  110.7 2.4 %collective-permute-done.18 = f32[96,128]{1,0:T(8,128)S(1)} collective-permute-done((f32[96,128]{1,0:T(8,128)S(1)}, f32[96,128]{1,0:T(8,128)S(1)}, u32[]{:S(2)}, u32[]{:S(2)}) %collective-permute-start.18) | collective-permute-done | bytes 49184 | tf_op jit(solution)/shard_map/ppermute | solution.py:27
  113.2 1.9 %collective-permute-start.19 = (f32[96,128]{1,0:T(8,128)S(1)}, f32[96,128]{1,0:T(8,128)S(1)}, u32[]{:S(2)}, u32[]{:S(2)}) collective-permute-start(f32[96,128]{1,0:T(8,128)S(1)} %select_select_fusion.1), channel_id=1, source_target_pairs={{0,4},{1,5},{2,6},{3,7},{4,0},{5,1},{6,2},{7,3},{8,12},{9,13},{10,... | collective-permute-start | bytes 147464 | tf_op jit(solution)/shard_map/ppermute | solution.py:27
  115.2 1.0 slice_add_fusion.3
  116.2 1.8 %collective-permute-start.22 = (f32[96,128]{1,0:T(8,128)S(1)}, f32[96,128]{1,0:T(8,128)S(1)}, u32[]{:S(2)}, u32[]{:S(2)}) collective-permute-start(f32[96,128]{1,0:T(8,128)S(1)} %slice_add_fusion.3), channel_id=1, source_target_pairs={{0,8},{8,0},{16,24},{24,16},{1,9},{9,1},{17,25},{25,17},{2,10},{10... | collective-permute-start | bytes 147464 | tf_op jit(solution)/shard_map/ppermute | solution.py:27
  119.2 1.3 collective-permute-done.22
  120.5 1.6 %collective-permute-start.23 = (f32[96,128]{1,0:T(8,128)S(1)}, f32[96,128]{1,0:T(8,128)S(1)}, u32[]{:S(2)}, u32[]{:S(2)}) collective-permute-start(f32[96,128]{1,0:T(8,128)S(1)} %add.90), channel_id=1, source_target_pairs={{0,16},{8,24},{16,0},{24,8},{1,17},{9,25},{17,1},{25,9},{2,18},{10... | collective-permute-start | bytes 147464 | tf_op jit(solution)/shard_map/ppermute | solution.py:27
  123.3 1.3 collective-permute-done.23
  124.6 7.7 %early_solves.1.small = f32[4,64,64]{2,1,0:T(8,128)S(1)} custom-call(f32[96,128]{1,0:T(8,128)S(1)} %add.91.packed), custom_call_target="tpu_custom_call" | custom-call | tf_op jit(solution)/shard_map/early_solves/pallas_call | solution.py:345
  132.4 0.9 copy-done.28
  133.3 0.9 copy-done.29
  134.2 0.9 copy-done.31
  135.2 0.9 copy-done.33
  136.1 8.4 %final.1 = (f32[4,64,128]{2,1,0:T(8,128)}, f32[4,64,128]{2,1,0:T(8,128)}) custom-call(f32[32,128]{1,0:T(8,128)S(1)} %add.82.packed, f32[4,64,64]{2,1,0:T(8,128)S(1)} %early_solves.1.small, f32[4,64,128]{2,1,0:T(8,128)S(1)} %copy-done.28, f32[4,64,128]{2,1,0:T(8,128)S(1)} %copy-done.33, f32[4,64,128]{2,1,0:T(8,128)S(1)} %copy-done.31, ...), custom_call_target="tpu_custom_call" | custom-call | tf_op jit(solution)/shard_map/final/pallas_call | solution.py:384
  (120 shorter events, 13.0 us)
Async XLA Ops:
  7.2 35.5 %copy-start.4 = (f32[4,64,128]{2,1,0:T(8,128)S(1)}, f32[4,64,128]{2,1,0:T(8,128)}, u32[]{:S(2)}) copy-start(f32[4,64,128]{2,1,0:T(8,128)} %vectors.3) | copy-start | bytes 393220
  7.2 35.5 %copy-start.43 = (s32[128]{0:T(128)S(1)}, s32[128]{0:T(128)}, u32[]{:S(2)}) copy-start(s32[128]{0:T(128)} %load.3) | copy-start | bytes 1540
  7.2 35.5 %copy-start.41 = (s32[128]{0:T(128)S(1)}, s32[128]{0:T(128)}, u32[]{:S(2)}) copy-start(s32[128]{0:T(128)} %new_slot.5) | copy-start | bytes 1540
  7.2 35.5 %all-gather.2.cloned.1.call-start = ((), (), s32[]{:S(2)}) async-start(), calls=%async_computation.1 | async-start | bytes 1179648 | tf_op jit(solution)/shard_map/all_gather | solution.py:407
  7.9 124.5 %reduce-scatter.2.cloned.1.call-start = ((), (), s32[]{:S(2)}) async-start(), calls=%async_computation.2 | async-start | bytes 1179648 | tf_op jit(solution)/shard_map/reduce_scatter | solution.py:423
  9.4 1.8 %copy-start = (f32[4,11,128,128]{3,2,1,0:T(8,128)S(1)}, f32[4,11,128,128]{3,2,1,0:T(8,128)}, u32[]{:S(2)}) copy-start(f32[4,11,128,128]{3,2,1,0:T(8,128)} %tiles.3) | copy-start | bytes 8650756
  14.3 28.4 %copy-start.1 = (f32[4,11,128,128]{3,2,1,0:T(8,128)S(1)}, f32[4,11,128,128]{3,2,1,0:T(8,128)}, u32[]{:S(2)}) copy-start(f32[4,11,128,128]{3,2,1,0:T(8,128)} %tiles.3) | copy-start | bytes 8650756
  14.3 28.4 %copy-start.5 = (f32[2,4,128,128]{3,2,1,0:T(8,128)S(1)}, f32[2,4,128,128]{3,2,1,0:T(8,128)}, u32[]{:S(2)}) copy-start(f32[2,4,128,128]{3,2,1,0:T(8,128)} %refs_11_.1) | copy-start | bytes 1572868
  17.6 3.1 %collective-permute-start.3 = (f32[16,64,128]{2,1,0:T(8,128)S(1)}, f32[16,64,128]{2,1,0:T(8,128)S(1)}, u32[]{:S(2)}, u32[]{:S(2)}) collective-permute-start(f32[16,64,128]{2,1,0:T(8,128)S(1)} %get-tuple-element.15), channel_id=1, source_target_pairs={{0,1},{1,0},{2,3},{3,2},{4,5},{5,4},{6,7},{7,6},{8,9},{9,8},{10,11... | collective-permute-start | bytes 1572872 | tf_op jit(solution)/shard_map/ppermute | solution.py:27
  18.1 10.6 %collective-permute-start = (f32[2,64,128]{2,1,0:T(8,128)S(1)}, f32[2,64,128]{2,1,0:T(8,128)S(1)}, u32[]{:S(2)}, u32[]{:S(2)}) collective-permute-start(f32[2,64,128]{2,1,0:T(8,128)S(1)} %slice.53), channel_id=1, source_target_pairs={{0,8},{8,0},{16,24},{24,16},{1,9},{9,1},{17,25},{25,17},{2,10},{10... | collective-permute-start | bytes 196616 | tf_op jit(solution)/shard_map/ppermute | solution.py:27
  20.7 1.0 copy-start.11
  22.4 31.1 %collective-permute-start.4 = (f32[4,64,128]{2,1,0:T(8,128)}, f32[4,64,128]{2,1,0:T(8,128)}, u32[]{:S(2)}, u32[]{:S(2)}) collective-permute-start(f32[4,64,128]{2,1,0:T(8,128)} %get-tuple-element.26), channel_id=1, source_target_pairs={{0,2},{1,3},{2,0},{3,1},{4,6},{5,7},{6,4},{7,5},{8,10},{9,11},{10,... | collective-permute-start | bytes 393224 | tf_op jit(solution)/shard_map/ppermute | solution.py:27
  24.3 29.2 %collective-permute-start.5 = (f32[4,64,128]{2,1,0:T(8,128)}, f32[4,64,128]{2,1,0:T(8,128)}, u32[]{:S(2)}, u32[]{:S(2)}) collective-permute-start(f32[4,64,128]{2,1,0:T(8,128)} %get-tuple-element.25), channel_id=1, source_target_pairs={{0,4},{1,5},{2,6},{3,7},{4,0},{5,1},{6,2},{7,3},{8,12},{9,13},{10,... | collective-permute-start | bytes 393224 | tf_op jit(solution)/shard_map/ppermute | solution.py:27
  26.9 26.7 %collective-permute-start.6 = (f32[4,64,128]{2,1,0:T(8,128)}, f32[4,64,128]{2,1,0:T(8,128)}, u32[]{:S(2)}, u32[]{:S(2)}) collective-permute-start(f32[4,64,128]{2,1,0:T(8,128)} %get-tuple-element.24), channel_id=1, source_target_pairs={{0,6},{1,7},{2,4},{3,5},{4,2},{5,3},{6,0},{7,1},{8,14},{9,15},{10,... | collective-permute-start | bytes 393224 | tf_op jit(solution)/shard_map/ppermute | solution.py:27
  26.9 4.3 %collective-permute-start.1 = (f32[2,64,128]{2,1,0:T(8,128)S(1)}, f32[2,64,128]{2,1,0:T(8,128)S(1)}, u32[]{:S(2)}, u32[]{:S(2)}) collective-permute-start(f32[2,64,128]{2,1,0:T(8,128)S(1)} %slice.53), channel_id=1, source_target_pairs={{0,16},{8,24},{16,0},{24,8},{1,17},{9,25},{17,1},{25,9},{2,18},{10... | collective-permute-start | bytes 196616 | tf_op jit(solution)/shard_map/ppermute | solution.py:27
  29.3 5.2 %collective-permute-start.2 = (f32[2,64,128]{2,1,0:T(8,128)S(1)}, f32[2,64,128]{2,1,0:T(8,128)S(1)}, u32[]{:S(2)}, u32[]{:S(2)}) collective-permute-start(f32[2,64,128]{2,1,0:T(8,128)S(1)} %slice.53), channel_id=1, source_target_pairs={{0,24},{8,16},{16,8},{24,0},{1,25},{9,17},{17,9},{25,1},{2,26},{10... | collective-permute-start | bytes 196616 | tf_op jit(solution)/shard_map/ppermute | solution.py:27
  44.5 1.2 copy-start.15
  48.3 5.4 %copy-start.10 = (f32[16,64,128]{2,1,0:T(8,128)S(1)}, f32[16,64,128]{2,1,0:T(8,128)}, u32[]{:S(2)}) copy-start(f32[16,64,128]{2,1,0:T(8,128)} %copy-done.9) | copy-start | bytes 1572868
  48.3 5.4 %copy-start.12 = (f32[16,64,128]{2,1,0:T(8,128)S(1)}, f32[16,64,128]{2,1,0:T(8,128)}, u32[]{:S(2)}) copy-start(f32[16,64,128]{2,1,0:T(8,128)} %copy-done.11) | copy-start | bytes 1572868
  53.6 1.7 %copy-start.27 = (f32[4,64,128]{2,1,0:T(8,128)}, f32[4,64,128]{2,1,0:T(8,128)S(1)}, u32[]{:S(2)}) copy-start(f32[4,64,128]{2,1,0:T(8,128)S(1)} %get-tuple-element.21.moving) | copy-start | bytes 393220
  56.6 34.2 %copy-start.8 = (s32[128,11]{1,0:T(8,128)S(1)}, s32[128,11]{1,0:T(8,128)}, u32[]{:S(2)}) copy-start(s32[128,11]{1,0:T(8,128)} %copy.13.refs_8_.col.refs_15_) | copy-start | bytes 16900
  56.6 9.4 %copy-start.45 = (f32[2,64,128]{2,1,0:T(8,128)S(1)}, f32[2,64,128]{2,1,0:T(8,128)}, u32[]{:S(2)}) copy-start(f32[2,64,128]{2,1,0:T(8,128)} %copy-done.44) | copy-start | bytes 196612
  59.8 1.0 copy-start.2
  61.5 12.4 %collective-permute-start.8 = (f32[352,128]{1,0:T(8,128)}, f32[352,128]{1,0:T(8,128)S(1)}, u32[]{:S(2)}, u32[]{:S(2)}) collective-permute-start(f32[352,128]{1,0:T(8,128)} %copy-done.18), channel_id=1, source_target_pairs={{0,2},{1,3},{2,0},{3,1},{4,6},{5,7},{6,4},{7,5},{8,10},{9,11},{10,... | collective-permute-start | bytes 540680 | tf_op jit(solution)/shard_map/ppermute | solution.py:27
  61.6 19.2 %collective-permute-start.10 = (f32[352,128]{1,0:T(8,128)}, f32[352,128]{1,0:T(8,128)S(1)}, u32[]{:S(2)}, u32[]{:S(2)}) collective-permute-start(f32[352,128]{1,0:T(8,128)} %copy-done.18), channel_id=1, source_target_pairs={{0,4},{1,5},{2,6},{3,7},{4,0},{5,1},{6,2},{7,3},{8,12},{9,13},{10,... | collective-permute-start | bytes 540680 | tf_op jit(solution)/shard_map/ppermute | solution.py:27
  63.5 17.3 %collective-permute-start.12 = (f32[352,128]{1,0:T(8,128)}, f32[352,128]{1,0:T(8,128)S(1)}, u32[]{:S(2)}, u32[]{:S(2)}) collective-permute-start(f32[352,128]{1,0:T(8,128)} %copy-done.18), channel_id=1, source_target_pairs={{0,6},{1,7},{2,4},{3,5},{4,2},{5,3},{6,0},{7,1},{8,14},{9,15},{10,... | collective-permute-start | bytes 540680 | tf_op jit(solution)/shard_map/ppermute | solution.py:27
  66.0 15.3 %collective-permute-start.14 = (f32[2,64,128]{2,1,0:T(8,128)S(1)}, f32[2,64,128]{2,1,0:T(8,128)S(1)}, u32[]{:S(2)}, u32[]{:S(2)}) collective-permute-start(f32[2,64,128]{2,1,0:T(8,128)S(1)} %copy-done.45), channel_id=1, source_target_pairs={{0,8},{8,0},{16,24},{24,16},{1,9},{9,1},{17,25},{25,17},{2,10},{10... | collective-permute-start | bytes 196616 | tf_op jit(solution)/shard_map/ppermute | solution.py:27
  66.0 24.8 %collective-permute-start.7 = (f32[352,128]{1,0:T(8,128)}, f32[352,128]{1,0:T(8,128)S(1)}, u32[]{:S(2)}, u32[]{:S(2)}) collective-permute-start(f32[352,128]{1,0:T(8,128)} %copy-done.18), channel_id=1, source_target_pairs={{0,1},{1,0},{2,3},{3,2},{4,5},{5,4},{6,7},{7,6},{8,9},{9,8},{10,11... | collective-permute-start | bytes 540680 | tf_op jit(solution)/shard_map/ppermute | solution.py:27
  73.9 26.7 %copy-start.20 = (f32[352,128]{1,0:T(8,128)}, f32[352,128]{1,0:T(8,128)S(1)}, u32[]{:S(2)}) copy-start(f32[352,128]{1,0:T(8,128)S(1)} %collective-permute-done.8.refs_2_) | copy-start | bytes 540676
  73.9 16.8 %collective-permute-start.9 = (f32[352,128]{1,0:T(8,128)S(1)}, f32[352,128]{1,0:T(8,128)S(1)}, u32[]{:S(2)}, u32[]{:S(2)}) collective-permute-start(f32[352,128]{1,0:T(8,128)S(1)} %collective-permute-done.8.refs_2_), channel_id=1, source_target_pairs={{0,1},{1,0},{2,3},{3,2},{4,5},{5,4},{6,7},{7,6},{8,9},{9,8},{10,11... | collective-permute-start | bytes 540680 | tf_op jit(solution)/shard_map/ppermute | solution.py:27
  80.8 21.1 %copy-start.21 = (f32[352,128]{1,0:T(8,128)}, f32[352,128]{1,0:T(8,128)S(1)}, u32[]{:S(2)}) copy-start(f32[352,128]{1,0:T(8,128)S(1)} %collective-permute-done.10.refs_4_) | copy-start | bytes 540676
  80.8 10.0 %collective-permute-start.11 = (f32[352,128]{1,0:T(8,128)S(1)}, f32[352,128]{1,0:T(8,128)S(1)}, u32[]{:S(2)}, u32[]{:S(2)}) collective-permute-start(f32[352,128]{1,0:T(8,128)S(1)} %collective-permute-done.10.refs_4_), channel_id=1, source_target_pairs={{0,1},{1,0},{2,3},{3,2},{4,5},{5,4},{6,7},{7,6},{8,9},{9,8},{10,11... | collective-permute-start | bytes 540680 | tf_op jit(solution)/shard_map/ppermute | solution.py:27
  80.8 21.1 %copy-start.22 = (f32[352,128]{1,0:T(8,128)}, f32[352,128]{1,0:T(8,128)S(1)}, u32[]{:S(2)}) copy-start(f32[352,128]{1,0:T(8,128)S(1)} %collective-permute-done.12.refs_6_) | copy-start | bytes 540676
  80.8 10.0 %collective-permute-start.13 = (f32[352,128]{1,0:T(8,128)S(1)}, f32[352,128]{1,0:T(8,128)S(1)}, u32[]{:S(2)}, u32[]{:S(2)}) collective-permute-start(f32[352,128]{1,0:T(8,128)S(1)} %collective-permute-done.12.refs_6_), channel_id=1, source_target_pairs={{0,1},{1,0},{2,3},{3,2},{4,5},{5,4},{6,7},{7,6},{8,9},{9,8},{10,11... | collective-permute-start | bytes 540680 | tf_op jit(solution)/shard_map/ppermute | solution.py:27
  81.3 4.3 %collective-permute-start.15 = (f32[2,64,128]{2,1,0:T(8,128)S(1)}, f32[2,64,128]{2,1,0:T(8,128)S(1)}, u32[]{:S(2)}, u32[]{:S(2)}) collective-permute-start(f32[2,64,128]{2,1,0:T(8,128)S(1)} %copy-done.45), channel_id=1, source_target_pairs={{0,16},{8,24},{16,0},{24,8},{1,17},{9,25},{17,1},{25,9},{2,18},{10... | collective-permute-start | bytes 196616 | tf_op jit(solution)/shard_map/ppermute | solution.py:27
  85.6 5.2 %collective-permute-start.16 = (f32[2,64,128]{2,1,0:T(8,128)S(1)}, f32[2,64,128]{2,1,0:T(8,128)S(1)}, u32[]{:S(2)}, u32[]{:S(2)}) collective-permute-start(f32[2,64,128]{2,1,0:T(8,128)S(1)} %copy-done.45), channel_id=1, source_target_pairs={{0,24},{8,16},{16,8},{24,0},{1,25},{9,17},{17,9},{25,1},{2,26},{10... | collective-permute-start | bytes 196616 | tf_op jit(solution)/shard_map/ppermute | solution.py:27
  90.7 11.2 %copy-start.23 = (f32[352,128]{1,0:T(8,128)}, f32[352,128]{1,0:T(8,128)S(1)}, u32[]{:S(2)}) copy-start(f32[352,128]{1,0:T(8,128)S(1)} %collective-permute-done.7.refs_1_) | copy-start | bytes 540676
  90.7 11.2 %copy-start.24 = (f32[352,128]{1,0:T(8,128)}, f32[352,128]{1,0:T(8,128)S(1)}, u32[]{:S(2)}) copy-start(f32[352,128]{1,0:T(8,128)S(1)} %collective-permute-done.9.refs_3_) | copy-start | bytes 540676
  90.8 11.2 %copy-start.25 = (f32[352,128]{1,0:T(8,128)}, f32[352,128]{1,0:T(8,128)S(1)}, u32[]{:S(2)}) copy-start(f32[352,128]{1,0:T(8,128)S(1)} %collective-permute-done.11.refs_5_) | copy-start | bytes 540676
  90.8 1.1 copy-start.14
  93.7 8.2 %copy-start.26 = (f32[352,128]{1,0:T(8,128)}, f32[352,128]{1,0:T(8,128)S(1)}, u32[]{:S(2)}) copy-start(f32[352,128]{1,0:T(8,128)S(1)} %collective-permute-done.13.refs_7_) | copy-start | bytes 540676
  101.9 3.0 %collective-permute-start.17 = (f32[96,128]{1,0:T(8,128)S(1)}, f32[96,128]{1,0:T(8,128)S(1)}, u32[]{:S(2)}, u32[]{:S(2)}) collective-permute-start(f32[96,128]{1,0:T(8,128)S(1)} %get-tuple-element.20), channel_id=1, source_target_pairs={{0,1},{1,0},{2,3},{3,2},{4,5},{5,4},{6,7},{7,6},{8,9},{9,8},{10,11... | collective-permute-start | bytes 147464 | tf_op jit(solution)/shard_map/ppermute | solution.py:27
  105.0 8.1 %collective-permute-start.18 = (f32[96,128]{1,0:T(8,128)S(1)}, f32[96,128]{1,0:T(8,128)S(1)}, u32[]{:S(2)}, u32[]{:S(2)}) collective-permute-start(f32[96,128]{1,0:T(8,128)S(1)} %select_select_fusion.2), channel_id=1, source_target_pairs={{0,2},{1,3},{2,0},{3,1},{4,6},{5,7},{6,4},{7,5},{8,10},{9,11},{10,... | collective-permute-start | bytes 147464 | tf_op jit(solution)/shard_map/ppermute | solution.py:27
  113.2 5.5 %collective-permute-start.19 = (f32[96,128]{1,0:T(8,128)S(1)}, f32[96,128]{1,0:T(8,128)S(1)}, u32[]{:S(2)}, u32[]{:S(2)}) collective-permute-start(f32[96,128]{1,0:T(8,128)S(1)} %select_select_fusion.1), channel_id=1, source_target_pairs={{0,4},{1,5},{2,6},{3,7},{4,0},{5,1},{6,2},{7,3},{8,12},{9,13},{10,... | collective-permute-start | bytes 147464 | tf_op jit(solution)/shard_map/ppermute | solution.py:27
  116.2 4.3 %collective-permute-start.22 = (f32[96,128]{1,0:T(8,128)S(1)}, f32[96,128]{1,0:T(8,128)S(1)}, u32[]{:S(2)}, u32[]{:S(2)}) collective-permute-start(f32[96,128]{1,0:T(8,128)S(1)} %slice_add_fusion.3), channel_id=1, source_target_pairs={{0,8},{8,0},{16,24},{24,16},{1,9},{9,1},{17,25},{25,17},{2,10},{10... | collective-permute-start | bytes 147464 | tf_op jit(solution)/shard_map/ppermute | solution.py:27
  118.8 3.8 %collective-permute-start.20 = (f32[32,128]{1,0:T(8,128)S(1)}, f32[32,128]{1,0:T(8,128)S(1)}, u32[]{:S(2)}, u32[]{:S(2)}) collective-permute-start(f32[32,128]{1,0:T(8,128)S(1)} %slice.73), channel_id=1, source_target_pairs={{0,8},{8,0},{16,24},{24,16},{1,9},{9,1},{17,25},{25,17},{2,10},{10... | collective-permute-start | bytes 49160 | tf_op jit(solution)/shard_map/ppermute | solution.py:27
  120.5 4.2 %collective-permute-start.23 = (f32[96,128]{1,0:T(8,128)S(1)}, f32[96,128]{1,0:T(8,128)S(1)}, u32[]{:S(2)}, u32[]{:S(2)}) collective-permute-start(f32[96,128]{1,0:T(8,128)S(1)} %add.90), channel_id=1, source_target_pairs={{0,16},{8,24},{16,0},{24,8},{1,17},{9,25},{17,1},{25,9},{2,18},{10... | collective-permute-start | bytes 147464 | tf_op jit(solution)/shard_map/ppermute | solution.py:27
  122.6 9.8 %collective-permute-start.21 = (f32[32,128]{1,0:T(8,128)S(1)}, f32[32,128]{1,0:T(8,128)S(1)}, u32[]{:S(2)}, u32[]{:S(2)}) collective-permute-start(f32[32,128]{1,0:T(8,128)S(1)} %slice_add_fusion.10), channel_id=1, source_target_pairs={{0,16},{8,24},{16,0},{24,8},{1,17},{9,25},{17,1},{25,9},{2,18},{10... | collective-permute-start | bytes 49160 | tf_op jit(solution)/shard_map/ppermute | solution.py:27
  (24 other events, 18.7 us)
Sparse Core Ops, SparseCore 0:
  9.6 33.0 all-gather.1
  61.6 34.4 reduce-scatter.1

commit v3 on v2

v3 whole, which is shorter than its diff:
```python
import functools

import jax
import jax.numpy as jnp
from jax import lax
from jax.experimental import pallas as pl
from jax.experimental.pallas import tpu as pltpu
from jax.sharding import PartitionSpec as P

shift = 4.0
f32 = jnp.float32
bf16 = jnp.bfloat16
normal = (((1,), (0,)), ((), ()))
right_t = (((1,), (1,)), ((), ()))
left_t = (((0,), (0,)), ((), ()))
vmem = pl.BlockSpec(memory_space=pltpu.VMEM)
smem = pl.BlockSpec(memory_space=pltpu.SMEM)
vmem_bytes = 60 * 2**20


def params():
    return pltpu.CompilerParams(vmem_limit_bytes=vmem_bytes)


def swap(value, axis, mask):
    pairs = [(source, source ^ mask) for source in range(lax.axis_size(axis))]
    return lax.ppermute(value, axis, pairs)


def split(value):
    high = value.astype(bf16)
    return high, (value - high.astype(f32)).astype(bf16)


def dot16(left, right, dims):
    return lax.dot_general(left, right, dims, preferred_element_type=f32)


def dot32(left, right, dims=normal):
    return lax.dot_general(
        left, right, dims, preferred_element_type=f32, precision=lax.Precision.HIGHEST
    )


def split_rows(vectors):
    high, low = split(vectors)
    return jnp.concatenate([high, low], axis=0)


def times_tile(rows, tile, dims):
    count = rows.shape[0] // 2
    high, low = split(tile)
    both = dot16(rows, high, dims)
    return both[:count] + both[count:] + dot16(rows[:count], low, dims)


def pack(gram):
    half = gram.shape[0] // 2
    return jnp.concatenate([gram[:half], gram[half:]], axis=1)


def unpack(packed):
    half = packed.shape[1] // 2
    return jnp.concatenate([packed[:, :half], packed[:, half:]], axis=0)


def sym(gram):
    return 0.5 * (gram + gram.T)


def first_slot(row_count):
    device = lax.axis_index("group") * lax.axis_size("bulk") + lax.axis_index("bulk")
    return device * row_count


def live(load_ref, slot, tile):
    return jnp.where(tile < load_ref[slot], 1.0, 0.0)


def returned_kernel(bulk_count, moved, vectors, tiles, col, load, new_slot, keep, send, total):
    row_count = vectors.shape[0]
    me = lax.axis_index("bulk")
    base = lax.axis_index("group") * bulk_count * row_count
    s = pl.program_id(0)
    slot = first_slot(row_count) + s

    @pl.when(s == 0)
    def _():
        total[...] = jnp.zeros_like(total)

    rows = split_rows(vectors[s])
    for t in range(tiles.shape[1]):
        product = times_tile(rows, tiles[0, t], normal)
        target = col[t, slot]
        if moved:
            target = new_slot[target]
        target = target - base
        owner = target // row_count
        rel = owner ^ me
        order = (rel & 1) * (bulk_count // 2) + (rel >> 1)
        place = order * row_count + target - owner * row_count
        total[place] += live(load, slot, t) * product

    @pl.when(s == row_count - 1)
    def _():
        half = total.shape[0] // 2
        keep[...] = total[:half]
        send[...] = total[half:]


def returned(vectors, tiles, col, load, new_slot, bulk_count, moved):
    row_count, count, order = vectors.shape
    tile_count = tiles.shape[1]
    half = (bulk_count * row_count // 2, count, order)
    return pl.pallas_call(
        functools.partial(returned_kernel, bulk_count, moved),
        grid=(row_count,),
        out_shape=[jax.ShapeDtypeStruct(half, f32)] * 2,
        in_specs=[
            vmem,
            pl.BlockSpec((1, tile_count, order, order), lambda s: (s, 0, 0, 0)),
            smem,
            smem,
            smem,
        ],
        out_specs=[vmem] * 2,
        scratch_shapes=[pltpu.VMEM((2 * half[0], count, order), f32)],
        compiler_params=params(),
        name="returned_moved" if moved else "returned",
    )(vectors, tiles, col, load, new_slot)


def near_kernel(bulk_count, second, *refs):
    panel, refs = refs[:bulk_count], refs[bulk_count:]
    vectors, tiles, diag, coupling = refs[:4]
    edge_rows, part_count = coupling.shape[:2]
    border, refs = refs[4 : 3 + part_count], refs[3 + part_count :]
    col, load, new_slot, near, moving, gram_out, *more, rows_of, gram = refs
    row_count, count = vectors.shape[:2]
    me = lax.axis_index("bulk")
    mine = lax.axis_index("group")
    base = mine * bulk_count * row_count
    s = pl.program_id(0)
    slot = first_slot(row_count) + s

    def place_of(target):
        target = target - base
        owner = target // row_count
        return (owner ^ me) * row_count + target - owner * row_count

    @pl.when(s == 0)
    def _():
        for index, piece in enumerate(panel):
            for k in range(row_count):
                rows_of[index * row_count + k] = split_rows(piece[k * count : (k + 1) * count])
        gram[...] = jnp.zeros_like(gram)
        if second:
            tail = panel[0][row_count * count :]
            for piece in panel[1:]:
                tail = tail + piece[row_count * count :]
            gram_out[count // 2 :] = tail

    direct = None
    for t in range(tiles.shape[1]):
        rows = rows_of[place_of(col[t, slot])]
        high, low = split(tiles[0, t])
        alive = live(load, slot, t)
        both = alive * dot16(rows, high, right_t)
        rest = alive * dot16(rows[:count], low, right_t)
        direct = (both, rest) if direct is None else (direct[0] + both, direct[1] + rest)
    direct = direct[0][:count] + direct[0][count:] + direct[1]
    value = vectors[s]
    near_value = times_tile(split_rows(value), diag[0], right_t)
    near[s] = near_value + direct
    if second:
        gram[...] += dot32(value, near_value + 2.0 * direct, right_t)
    else:
        gram[...] += dot32(value, value, right_t)

    @pl.when(s < edge_rows)
    def _():
        k = jnp.minimum(s, edge_rows - 1)
        crossed = times_tile(split_rows(value), coupling[k, mine], right_t)
        for index, ref in enumerate(border):
            tile = coupling[k, mine ^ (index + 1)]
            crossed = crossed + times_tile(split_rows(ref[k]), tile, right_t)
        near[s] += crossed
        if second:
            gram[...] += dot32(value, crossed, right_t)

    arriving = new_slot[slot]
    incoming = place_of(arriving)
    for index, piece in enumerate(panel):

        @pl.when(incoming // row_count == index)
        def _(piece=piece):
            start = pl.multiple_of(incoming % row_count * count, count)
            moving[s] = piece[pl.ds(start, count)]

    if second:
        (leaving,) = more

        @pl.when(arriving != slot)
        def _():
            leaving[count // 2 :] = near[s]

    @pl.when(s == row_count - 1)
    def _():
        if second:
            leaving[: count // 2] = pack(gram[...])
        else:
            gram_out[...] = pack(gram[...])


def near_part(panel, vectors, tiles, diag, coupling, border, col, load, new_slot, second):
    row_count, count, order = vectors.shape
    bulk_count = len(panel)
    tile_count = tiles.shape[1]
    half = count // 2
    shapes = [vectors.shape, vectors.shape, (half, order)]
    if second:
        shapes = [vectors.shape, vectors.shape, (4 * half, order), (half + count, order)]
    return pl.pallas_call(
        functools.partial(near_kernel, bulk_count, second),
        grid=(row_count,),
        out_shape=[jax.ShapeDtypeStruct(shape, f32) for shape in shapes],
        in_specs=[vmem] * bulk_count
        + [
            vmem,
            pl.BlockSpec((1, tile_count, order, order), lambda s: (s, 0, 0, 0)),
            pl.BlockSpec((1, order, order), lambda s: (s, 0, 0)),
            vmem,
        ]
        + [vmem] * len(border)
        + [smem] * 3,
        out_specs=[vmem] * len(shapes),
        scratch_shapes=[
            pltpu.VMEM((bulk_count * row_count, 2 * count, order), bf16),
            pltpu.VMEM((count, count), f32),
        ],
        compiler_params=params(),
        name="near_second" if second else "near_first",
    )(*panel, vectors, tiles, diag, coupling, *border, col, load, new_slot)


def gather_first_kernel(vectors, near, keep, *refs):
    received = refs[:-4]
    packed, first, flat, edge = refs[-4:]
    row_count, count = vectors.shape[:2]
    grams = [None, None]
    for k in range(row_count):
        value = near[k] + keep[k]
        for ref in received:
            value = value + ref[k]
        first[k] = value
        flat[k * count : (k + 1) * count] = value
        if k < edge.shape[0]:
            edge[k] = value
        terms = (dot32(vectors[k], value, right_t), dot32(value, value, right_t))
        grams = [term if old is None else old + term for old, term in zip(grams, terms)]
    start = row_count * count
    half = count // 2
    flat[start : start + half] = packed[...]
    flat[start + half : start + 2 * half] = pack(grams[0])
    flat[start + 2 * half :] = pack(grams[1])


def gather_first(vectors, near, keep, received, packed, edge_rows):
    row_count, count, order = vectors.shape
    shapes = [
        vectors.shape,
        (row_count * count + 3 * (count // 2), order),
        (edge_rows, count, order),
    ]
    specs = [pl.BlockSpec((row_count, count, order), lambda s: (0, 0, 0))] * (3 + len(received))
    return pl.pallas_call(
        gather_first_kernel,
        grid=(1,),
        out_shape=[jax.ShapeDtypeStruct(shape, f32) for shape in shapes],
        in_specs=specs + [vmem],
        out_specs=[vmem] * 3,
        compiler_params=params(),
        name="gather_first",
    )(vectors, near, keep, *received, packed)


def inverse_factors(matrices):
    count = matrices[0].shape[0]
    blocks = count // 8
    row_ids = lax.broadcasted_iota(jnp.int32, (count, count), 0)
    col_ids = lax.broadcasted_iota(jnp.int32, (count, count), 1)
    eye = (row_ids == col_ids).astype(f32)
    sub = lax.broadcasted_iota(jnp.int32, (8, 2 * count), 0)
    work = []
    for matrix in matrices:
        both = jnp.concatenate([matrix, eye], axis=1)
        work.append([both[8 * i : 8 * i + 8] for i in range(blocks)])
    for j in range(count):
        block, k = divmod(j, 8)
        for w in work:
            row = w[block][k : k + 1]
            scale = lax.rsqrt(row[:, j : j + 1])
            pivot = row * scale
            for i in range(block, blocks):
                changed = w[i] - w[i][:, j : j + 1] * scale * pivot
                if i == block:
                    changed = jnp.where(sub > k, changed, jnp.where(sub == k, pivot, w[i]))
                w[i] = changed
    return [jnp.concatenate(w, axis=0)[:, count:] for w in work]


def solve(inverse_factor, right):
    return dot32(inverse_factor, dot32(inverse_factor, right), left_t)


def final_kernel(packed, moving, first, near, row, new_slot, keep, *refs):
    received, (solution, resid) = refs[:-2], refs[-2:]
    row_count, count = moving.shape[:2]
    half = count // 2
    grams = [unpack(packed[i * half : (i + 1) * half]) for i in range(4)]
    g3, g0, g1, g2 = (sym(gram) for gram in grams)
    eye = (
        lax.broadcasted_iota(jnp.int32, (count, count), 0)
        == lax.broadcasted_iota(jnp.int32, (count, count), 1)
    ).astype(f32)
    factor_pq, factor_rr = inverse_factors([shift * g0 + g1, g0])
    a = solve(factor_pq, g0)
    m = eye - shift * a
    g2a = dot32(g2, a)
    cross = dot32(m, dot32(g1, a), left_t)
    g_new = dot32(m, dot32(g0, m), left_t) - cross - cross.T + dot32(a, g2a, left_t)
    g_new = sym(g_new)
    c = m + solve(factor_rr, g_new)
    cross = dot32(c, shift * dot32(g1, a) + g2a, left_t)
    g_pq = dot32(c, dot32(shift * g0 + g1, c), left_t) - cross - cross.T
    g_pq = sym(g_pq + dot32(a, shift * g2a + dot32(g3, a), left_t))
    (factor,) = inverse_factors([g_pq])
    a1 = solve(factor, g_new)
    aa1 = dot32(a, a1)
    ca1 = dot32(c, a1)
    zero = jnp.zeros_like(a)
    top = jnp.concatenate([a + ca1, -aa1, zero], axis=0)
    low = jnp.concatenate([m - shift * ca1, shift * aa1 - a - ca1, aa1], axis=0)
    coef = jnp.concatenate([top, low], axis=1)
    slot = first_slot(row_count)
    for k in range(row_count):
        stays = new_slot[slot + k] == slot + k
        second = jnp.where(stays, near[k], row[half:]) + keep[k]
        for ref in received:
            second = second + ref[k]
        basis = jnp.concatenate([moving[k], first[k], second], axis=0)
        both = dot32(coef, basis, left_t)
        solution[k] = both[:count]
        resid[k] = both[count:]


def final(packed, moving, first, near, row, new_slot, keep, received):
    block = pl.BlockSpec(near.shape, lambda s: (0, 0, 0))
    return pl.pallas_call(
        final_kernel,
        grid=(1,),
        out_shape=[jax.ShapeDtypeStruct(near.shape, f32)] * 2,
        in_specs=[vmem] * 5 + [smem] + [block] * (1 + len(received)),
        out_specs=[vmem] * 2,
        compiler_params=params(),
        name="final",
    )(packed, moving, first, near, row, new_slot, keep, *received)


def spread(piece, bulk_count):
    pieces = [piece] + [swap(piece, "bulk", 2 * z) for z in range(1, bulk_count // 2)]
    return [own for piece in pieces for own in (piece, swap(piece, "bulk", 1))]


def give_back(keep, send, row_count, bulk_count):
    from_core = swap(send, "bulk", 1)
    received = [from_core]
    for z in range(1, bulk_count // 2):
        rows = slice(z * row_count, (z + 1) * row_count)
        received.append(swap(keep[rows] + from_core[rows], "bulk", 2 * z))
    return received


def local(rhs, diag_tiles, offdiag_blocks, coupling, col_index, load, new_slot):
    row_count, count, order = rhs.shape
    edge_rows, part_count = coupling.shape[:2]
    bulk_count = lax.axis_size("bulk")
    half = count // 2
    my_bulk = lax.axis_index("bulk")
    slot = first_slot(row_count)
    col = col_index.T
    own_new = lax.dynamic_slice(new_slot, (slot,), (row_count,))
    own_slots = slot + jnp.arange(row_count, dtype=jnp.int32)
    target = jnp.max(jnp.where(own_new != own_slots, own_new, -1))
    xor_mask = (target // row_count % bulk_count) ^ my_bulk

    panel = spread(rhs.reshape(row_count * count, order), bulk_count)
    border = [swap(rhs[:edge_rows], "group", mask) for mask in range(1, part_count)]
    keep, send = returned(rhs, offdiag_blocks, col, load, new_slot, bulk_count, False)
    received = give_back(keep, send, row_count, bulk_count)
    near, moving, packed = near_part(
        panel, rhs, offdiag_blocks, diag_tiles, coupling, border, col, load, new_slot, False
    )
    first, flat, edge = gather_first(rhs, near, keep, received, packed, edge_rows)

    panel = spread(flat, bulk_count)
    border = [swap(edge, "group", mask) for mask in range(1, part_count)]
    keep, send = returned(first, offdiag_blocks, col, load, new_slot, bulk_count, True)
    received = give_back(keep, send, row_count, bulk_count)
    near, first, grams, leaving = near_part(
        panel, first, offdiag_blocks, diag_tiles, coupling, border, col, load, new_slot, True
    )

    is_gram = lax.broadcasted_iota(jnp.int32, leaving.shape, 0) < half
    mask = 1
    while mask < bulk_count:
        partner = swap(leaving, "bulk", mask)
        chosen = jnp.bitwise_and(xor_mask, mask) != 0
        leaving = jnp.where(is_gram, leaving + partner, jnp.where(chosen, partner, leaving))
        mask *= 2
    grams = jnp.concatenate([leaving[:half], grams[half:]], axis=0)
    mask = 1
    while mask < part_count:
        grams = grams + swap(grams, "group", mask)
        mask *= 2
    return tuple(final(grams, moving, first, near, leaving, new_slot, keep, received))


def solution(mesh):
    rows = P(("group", "bulk"))
    return jax.shard_map(
        local,
        mesh=mesh,
        in_specs=(rows, rows, rows, rows, P(), P(), P()),
        out_specs=(rows, rows),
        check_vma=False,
    )
```

time: 152 us -> 132 us (0.87)
  local copies, waits for them, and re-layouts: 25.5 us -> 3.44 us
  between operations: 16.7 us -> 3.64 us
  starting transfers between devices: 28.5 us -> 39.6 us
  Pallas kernels: 36.3 us -> 42.9 us
  waiting for transfers between devices: 41.4 us -> 37.3 us
  other arithmetic: 2.8 us -> 4.92 us
    unnamed x93 -> x64, local copies, waits for them, and re-layouts: 25.5 us -> 3.43 us
    ppermute x24 -> x33, starting transfers between devices: 28.5 us -> 39.6 us  [swap(): return lax.ppermute(value, axis, pairs)]
    all_gather x1 -> x0, waiting for transfers between devices: 7.62 us -> none  [local(): panel = lax.all_gather(rhs, 'bulk', axis=0, tiled=True)]
    ppermute x24 -> x33, waiting for transfers between devices: 33 us -> 37.3 us  [swap(): return lax.ppermute(value, axis, pairs)]
    pallas_call x4 -> x3, Pallas kernels: 28.2 us -> 31.1 us  [the longest x1 16.3 us: final(): pl.pallas_call(final_kernel, grid=(1,), out_shape=[jax.ShapeDtypeStruct(n...]
    pallas_call x2, Pallas kernels: 6.52 us -> 9.23 us  [returned(): pl.pallas_call(functools.partial(returned_kernel, bulk_count, moved), gri...]
  transfers between devices with their start and end apart: 26 -> 33, of which waited for: 12 -> 10; matrix products, arithmetic and copies ran while one was open for 3% -> 3% of each run, Pallas kernels for 15% -> 9%
where the time goes in v3:
time: 132 us
  Pallas kernels  42.9 us (32%)
  starting transfers between devices  39.6 us (30%)
  waiting for transfers between devices  37.3 us (28%)
  other arithmetic  4.92 us (4%)
  between operations  3.64 us (3%)
  local copies, waits for them, and re-layouts  3.44 us (3%)
    ppermute x33, starting transfers between devices, swap(): return lax.ppermute(value, axis, pairs)  39.6 us
    ppermute x33, waiting for transfers between devices, swap(): return lax.ppermute(value, axis, pairs)  37.3 us
    pallas_call x1, Pallas kernels, final(): pl.pallas_call(final_kernel, grid=(1,), out_shape=[jax.ShapeDtypeStruct(n...  16.3 us
    pallas_call x2, Pallas kernels, near_part(): pl.pallas_call(functools.partial(near_kernel, bulk_count, second), grid=(...  14.8 us
    pallas_call x2, Pallas kernels, returned(): pl.pallas_call(functools.partial(returned_kernel, bulk_count, moved), gri...  9.23 us
    unnamed x64, local copies, waits for them, and re-layouts  3.43 us
  transfers between devices with their start and end apart: 33, of which 10 were waited for; matrix products, arithmetic and copies ran while one was open for 3% of the time, Pallas kernels for 9%

profile of v3, /device:TPU:0, one launch (start us, length us, event | category | flops | bytes accessed | tf_op | source)
XLA Modules:
  0.0 131.9 jit_solution(6740074895922729146)
XLA Ops:
  0.6 4.7 %returned.1 = (f32[16,64,128]{2,1,0:T(8,128)}, f32[16,64,128]{2,1,0:T(8,128)}) custom-call(f32[4,64,128]{2,1,0:T(8,128)} %vectors.3, f32[4,11,128,128]{3,2,1,0:T(8,128)} %tiles.3, s32[11,128]{1,0:T(8,128)} %bitcast.7, s32[128]{0:T(128)} %load.3, s32[128]{0:T(128)} %new_slot.5), custom_call_target="tpu_custom_call" | custom-call | tf_op jit(solution)/shard_map/returned/pallas_call | solution.py:115
  5.8 2.6 %collective-permute-start.1 = (f32[256,128]{1,0:T(8,128)S(1)}, f32[256,128]{1,0:T(8,128)S(1)}, u32[]{:S(2)}, u32[]{:S(2)}) collective-permute-start(f32[256,128]{1,0:T(8,128)S(1)} %bitcast.3), channel_id=1, source_target_pairs={{0,2},{1,3},{2,0},{3,1},{4,6},{5,7},{6,4},{7,5},{8,10},{9,11},{10,... | collective-permute-start | bytes 393224 | tf_op jit(solution)/shard_map/ppermute | solution.py:27
  8.4 1.5 %collective-permute-start.7 = (f32[2,64,128]{2,1,0:T(8,128)S(1)}, f32[2,64,128]{2,1,0:T(8,128)S(1)}, u32[]{:S(2)}, u32[]{:S(2)}) collective-permute-start(f32[2,64,128]{2,1,0:T(8,128)S(1)} %slice.47), channel_id=1, source_target_pairs={{0,8},{8,0},{16,24},{24,16},{1,9},{9,1},{17,25},{25,17},{2,10},{10... | collective-permute-start | bytes 196616 | tf_op jit(solution)/shard_map/ppermute | solution.py:27
  9.9 1.5 %collective-permute-start.8 = (f32[2,64,128]{2,1,0:T(8,128)S(1)}, f32[2,64,128]{2,1,0:T(8,128)S(1)}, u32[]{:S(2)}, u32[]{:S(2)}) collective-permute-start(f32[2,64,128]{2,1,0:T(8,128)S(1)} %slice.47), channel_id=1, source_target_pairs={{0,16},{8,24},{16,0},{24,8},{1,17},{9,25},{17,1},{25,9},{2,18},{10... | collective-permute-start | bytes 196616 | tf_op jit(solution)/shard_map/ppermute | solution.py:27
  11.4 1.3 collective-permute-done.7.refs_12_
  12.7 2.6 %collective-permute-start.3 = (f32[256,128]{1,0:T(8,128)S(1)}, f32[256,128]{1,0:T(8,128)S(1)}, u32[]{:S(2)}, u32[]{:S(2)}) collective-permute-start(f32[256,128]{1,0:T(8,128)S(1)} %bitcast.5), channel_id=1, source_target_pairs={{0,4},{1,5},{2,6},{3,7},{4,0},{5,1},{6,2},{7,3},{8,12},{9,13},{10,... | collective-permute-start | bytes 393224 | tf_op jit(solution)/shard_map/ppermute | solution.py:27
  15.3 1.4 %collective-permute-start.5 = (f32[256,128]{1,0:T(8,128)S(1)}, f32[256,128]{1,0:T(8,128)S(1)}, u32[]{:S(2)}, u32[]{:S(2)}) collective-permute-start(f32[256,128]{1,0:T(8,128)S(1)} %bitcast.6), channel_id=1, source_target_pairs={{0,6},{1,7},{2,4},{3,5},{4,2},{5,3},{6,0},{7,1},{8,14},{9,15},{10,... | collective-permute-start | bytes 393224 | tf_op jit(solution)/shard_map/ppermute | solution.py:27
  16.6 1.5 %collective-permute-start.9 = (f32[2,64,128]{2,1,0:T(8,128)S(1)}, f32[2,64,128]{2,1,0:T(8,128)S(1)}, u32[]{:S(2)}, u32[]{:S(2)}) collective-permute-start(f32[2,64,128]{2,1,0:T(8,128)S(1)} %slice.47), channel_id=1, source_target_pairs={{0,24},{8,16},{16,8},{24,0},{1,25},{9,17},{17,9},{25,1},{2,26},{10... | collective-permute-start | bytes 196616 | tf_op jit(solution)/shard_map/ppermute | solution.py:27
  18.2 1.3 slice_add_fusion.3
  19.4 4.6 %collective-permute-done.3.refs_4_ = f32[256,128]{1,0:T(8,128)S(1)} collective-permute-done((f32[256,128]{1,0:T(8,128)S(1)}, f32[256,128]{1,0:T(8,128)S(1)}, u32[]{:S(2)}, u32[]{:S(2)}) %collective-permute-start.3) | collective-permute-done | bytes 131104 | tf_op jit(solution)/shard_map/ppermute | solution.py:27
  24.1 0.5 collective-permute-start.6
  24.6 2.8 %collective-permute-start.11 = (f32[4,64,128]{2,1,0:T(8,128)S(1)}, f32[4,64,128]{2,1,0:T(8,128)S(1)}, u32[]{:S(2)}, u32[]{:S(2)}) collective-permute-start(f32[4,64,128]{2,1,0:T(8,128)S(1)} %get-tuple-element.35), channel_id=1, source_target_pairs={{0,2},{1,3},{2,0},{3,1},{4,6},{5,7},{6,4},{7,5},{8,10},{9,11},{10,... | collective-permute-start | bytes 393224 | tf_op jit(solution)/shard_map/ppermute | solution.py:27
  27.4 1.3 collective-permute-start.12
  28.7 1.3 collective-permute-start.13
  30.0 0.6 copy-done.17
  30.6 0.6 copy-done.20
  31.2 6.9 %near_first.1 = (f32[4,64,128]{2,1,0:T(8,128)}, f32[4,64,128]{2,1,0:T(8,128)}, f32[32,128]{1,0:T(8,128)}) custom-call(f32[256,128]{1,0:T(8,128)} %bitcast.2, f32[256,128]{1,0:T(8,128)} %copy-done.12, f32[256,128]{1,0:T(8,128)} %copy-done.11, f32[256,128]{1,0:T(8,128)} %copy-done.15, f32[256,128]{1,0:T(8,128)} %copy-done.13, f32[256,128]{1,0:T(8,128)} %copy-done.17, ...), custom_call_target="tpu_custom_call" | custom-call | tf_op jit(solution)/shard_map/near_first/pallas_call | solution.py:223
  38.1 2.1 %collective-permute-done.12.refs_2_ = f32[4,64,128]{2,1,0:T(8,128)S(1)} collective-permute-done((f32[4,64,128]{2,1,0:T(8,128)S(1)}, f32[4,64,128]{2,1,0:T(8,128)S(1)}, u32[]{:S(2)}, u32[]{:S(2)}) %collective-permute-start.12) | collective-permute-done | bytes 131104 | tf_op jit(solution)/shard_map/ppermute | solution.py:27
  40.3 0.6 copy-done.22
  41.0 2.6 %gather_first.1 = (f32[4,64,128]{2,1,0:T(8,128)}, f32[352,128]{1,0:T(8,128)}, f32[2,64,128]{2,1,0:T(8,128)}) custom-call(f32[4,64,128]{2,1,0:T(8,128)} %vectors.3, f32[4,64,128]{2,1,0:T(8,128)} %get-tuple-element.16.near, f32[16,64,128]{2,1,0:T(8,128)} %get-tuple-element.17.keep, f32[16,64,128]{2,1,0:T(8,128)} %copy-done.2, f32[4,64,128]{2,1,0:T(8,128)} %copy-done.21, ...), custom_call_target="tpu_custom_call" | custom-call | tf_op jit(solution)/shard_map/gather_first/pallas_call | solution.py:276
  43.5 2.6 %collective-permute-start.15 = (f32[352,128]{1,0:T(8,128)}, f32[352,128]{1,0:T(8,128)S(1)}, u32[]{:S(2)}, u32[]{:S(2)}) collective-permute-start(f32[352,128]{1,0:T(8,128)} %get-tuple-element.20.refs_0_), channel_id=1, source_target_pairs={{0,2},{1,3},{2,0},{3,1},{4,6},{5,7},{6,4},{7,5},{8,10},{9,11},{10,... | collective-permute-start | bytes 540680 | tf_op jit(solution)/shard_map/ppermute | solution.py:27
  46.1 1.1 collective-permute-start.17
  47.2 1.4 %collective-permute-start.19 = (f32[352,128]{1,0:T(8,128)}, f32[352,128]{1,0:T(8,128)S(1)}, u32[]{:S(2)}, u32[]{:S(2)}) collective-permute-start(f32[352,128]{1,0:T(8,128)} %get-tuple-element.20.refs_0_), channel_id=1, source_target_pairs={{0,6},{1,7},{2,4},{3,5},{4,2},{5,3},{6,0},{7,1},{8,14},{9,15},{10,... | collective-permute-start | bytes 540680 | tf_op jit(solution)/shard_map/ppermute | solution.py:27
  48.5 1.5 %collective-permute-start.21 = (f32[2,64,128]{2,1,0:T(8,128)}, f32[2,64,128]{2,1,0:T(8,128)S(1)}, u32[]{:S(2)}, u32[]{:S(2)}) collective-permute-start(f32[2,64,128]{2,1,0:T(8,128)} %get-tuple-element.22), channel_id=1, source_target_pairs={{0,8},{8,0},{16,24},{24,16},{1,9},{9,1},{17,25},{25,17},{2,10},{10... | collective-permute-start | bytes 196616 | tf_op jit(solution)/shard_map/ppermute | solution.py:27
  50.0 2.7 %collective-permute-done.15.refs_2_ = f32[352,128]{1,0:T(8,128)S(1)} collective-permute-done((f32[352,128]{1,0:T(8,128)}, f32[352,128]{1,0:T(8,128)S(1)}, u32[]{:S(2)}, u32[]{:S(2)}) %collective-permute-start.15) | collective-permute-done | bytes 180256 | tf_op jit(solution)/shard_map/ppermute | solution.py:27
  52.8 9.6 %collective-permute-done.17.refs_4_ = f32[352,128]{1,0:T(8,128)S(1)} collective-permute-done((f32[352,128]{1,0:T(8,128)}, f32[352,128]{1,0:T(8,128)S(1)}, u32[]{:S(2)}, u32[]{:S(2)}) %collective-permute-start.17) | collective-permute-done | bytes 180256 | tf_op jit(solution)/shard_map/ppermute | solution.py:27
  62.9 1.4 %collective-permute-start.22 = (f32[2,64,128]{2,1,0:T(8,128)}, f32[2,64,128]{2,1,0:T(8,128)S(1)}, u32[]{:S(2)}, u32[]{:S(2)}) collective-permute-start(f32[2,64,128]{2,1,0:T(8,128)} %get-tuple-element.22), channel_id=1, source_target_pairs={{0,16},{8,24},{16,0},{24,8},{1,17},{9,25},{17,1},{25,9},{2,18},{10... | collective-permute-start | bytes 196616 | tf_op jit(solution)/shard_map/ppermute | solution.py:27
  64.3 3.1 %collective-permute-done.22.refs_13_ = f32[2,64,128]{2,1,0:T(8,128)S(1)} collective-permute-done((f32[2,64,128]{2,1,0:T(8,128)}, f32[2,64,128]{2,1,0:T(8,128)S(1)}, u32[]{:S(2)}, u32[]{:S(2)}) %collective-permute-start.22) | collective-permute-done | bytes 65568 | tf_op jit(solution)/shard_map/ppermute | solution.py:27
  67.4 2.3 %collective-permute-start.23 = (f32[2,64,128]{2,1,0:T(8,128)}, f32[2,64,128]{2,1,0:T(8,128)S(1)}, u32[]{:S(2)}, u32[]{:S(2)}) collective-permute-start(f32[2,64,128]{2,1,0:T(8,128)} %get-tuple-element.22), channel_id=1, source_target_pairs={{0,24},{8,16},{16,8},{24,0},{1,25},{9,17},{17,9},{25,1},{2,26},{10... | collective-permute-start | bytes 196616 | tf_op jit(solution)/shard_map/ppermute | solution.py:27
  69.7 3.0 %collective-permute-done.23.refs_14_ = f32[2,64,128]{2,1,0:T(8,128)S(1)} collective-permute-done((f32[2,64,128]{2,1,0:T(8,128)}, f32[2,64,128]{2,1,0:T(8,128)S(1)}, u32[]{:S(2)}, u32[]{:S(2)}) %collective-permute-start.23) | collective-permute-done | bytes 65568 | tf_op jit(solution)/shard_map/ppermute | solution.py:27
  72.9 0.5 copy-done.29
  73.7 8.0 %near_second.1 = (f32[4,64,128]{2,1,0:T(8,128)}, f32[4,64,128]{2,1,0:T(8,128)}, f32[128,128]{1,0:T(8,128)}, f32[96,128]{1,0:T(8,128)}) custom-call(f32[352,128]{1,0:T(8,128)} %get-tuple-element.20.refs_0_, f32[352,128]{1,0:T(8,128)} %copy-done.7, f32[352,128]{1,0:T(8,128)} %copy-done.4, f32[352,128]{1,0:T(8,128)} %copy-done.8, f32[352,128]{1,0:T(8,128)} %copy-done.5, ...), custom_call_target="tpu_custom_call" | custom-call | tf_op jit(solution)/shard_map/near_second/pallas_call | solution.py:223
  81.8 0.7 fusion
  85.1 0.9 select_select_fusion.2
  86.0 2.3 %collective-permute-start.25 = (f32[96,128]{1,0:T(8,128)S(1)}, f32[96,128]{1,0:T(8,128)S(1)}, u32[]{:S(2)}, u32[]{:S(2)}) collective-permute-start(f32[96,128]{1,0:T(8,128)S(1)} %select_select_fusion.2), channel_id=1, source_target_pairs={{0,2},{1,3},{2,0},{3,1},{4,6},{5,7},{6,4},{7,5},{8,10},{9,11},{10,... | collective-permute-start | bytes 147464 | tf_op jit(solution)/shard_map/ppermute | solution.py:27
  88.3 4.6 %returned_moved.1 = (f32[16,64,128]{2,1,0:T(8,128)}, f32[16,64,128]{2,1,0:T(8,128)}) custom-call(f32[4,64,128]{2,1,0:T(8,128)} %get-tuple-element.21.refs_8_.vectors, f32[4,11,128,128]{3,2,1,0:T(8,128)} %tiles.3, s32[11,128]{1,0:T(8,128)} %bitcast.10, s32[128]{0:T(128)} %load.3, s32[128]{0:T(128)} %new_slot.5), custom_call_target="tpu_custom_call" | custom-call | tf_op jit(solution)/shard_map/returned_moved/pallas_call | solution.py:115
  93.1 1.4 %collective-permute-start.26 = (f32[96,128]{1,0:T(8,128)S(1)}, f32[96,128]{1,0:T(8,128)S(1)}, u32[]{:S(2)}, u32[]{:S(2)}) collective-permute-start(f32[96,128]{1,0:T(8,128)S(1)} %select_select_fusion.1), channel_id=1, source_target_pairs={{0,4},{1,5},{2,6},{3,7},{4,0},{5,1},{6,2},{7,3},{8,12},{9,13},{10,... | collective-permute-start | bytes 147464 | tf_op jit(solution)/shard_map/ppermute | solution.py:27
  94.5 4.4 %collective-permute-done.26 = f32[96,128]{1,0:T(8,128)S(1)} collective-permute-done((f32[96,128]{1,0:T(8,128)S(1)}, f32[96,128]{1,0:T(8,128)S(1)}, u32[]{:S(2)}, u32[]{:S(2)}) %collective-permute-start.26) | collective-permute-done | bytes 49184 | tf_op jit(solution)/shard_map/ppermute | solution.py:27
  99.0 1.5 %collective-permute-start.27 = (f32[128,128]{1,0:T(8,128)S(1)}, f32[128,128]{1,0:T(8,128)S(1)}, u32[]{:S(2)}, u32[]{:S(2)}) collective-permute-start(f32[128,128]{1,0:T(8,128)S(1)} %pad_maximum_fusion), channel_id=1, source_target_pairs={{0,8},{8,0},{16,24},{24,16},{1,9},{9,1},{17,25},{25,17},{2,10},{10... | collective-permute-start | bytes 196616 | tf_op jit(solution)/shard_map/ppermute | solution.py:27
  100.5 1.3 slice_add_fusion
  101.9 2.7 %collective-permute-start.31 = (f32[4,64,128]{2,1,0:T(8,128)S(1)}, f32[4,64,128]{2,1,0:T(8,128)S(1)}, u32[]{:S(2)}, u32[]{:S(2)}) collective-permute-start(f32[4,64,128]{2,1,0:T(8,128)S(1)} %get-tuple-element.31), channel_id=1, source_target_pairs={{0,4},{1,5},{2,6},{3,7},{4,0},{5,1},{6,2},{7,3},{8,12},{9,13},{10,... | collective-permute-start | bytes 393224 | tf_op jit(solution)/shard_map/ppermute | solution.py:27
  104.6 1.7 %collective-permute-start.32 = (f32[4,64,128]{2,1,0:T(8,128)S(1)}, f32[4,64,128]{2,1,0:T(8,128)S(1)}, u32[]{:S(2)}, u32[]{:S(2)}) collective-permute-start(f32[4,64,128]{2,1,0:T(8,128)S(1)} %get-tuple-element.30), channel_id=1, source_target_pairs={{0,6},{1,7},{2,4},{3,5},{4,2},{5,3},{6,0},{7,1},{8,14},{9,15},{10,... | collective-permute-start | bytes 393224 | tf_op jit(solution)/shard_map/ppermute | solution.py:27
  106.3 1.6 %collective-permute-start.28 = (f32[128,128]{1,0:T(8,128)S(1)}, f32[128,128]{1,0:T(8,128)S(1)}, u32[]{:S(2)}, u32[]{:S(2)}) collective-permute-start(f32[128,128]{1,0:T(8,128)S(1)} %fusion.1), channel_id=1, source_target_pairs={{0,16},{8,24},{16,0},{24,8},{1,17},{9,25},{17,1},{25,9},{2,18},{10... | collective-permute-start | bytes 196616 | tf_op jit(solution)/shard_map/ppermute | solution.py:27
  107.9 2.7 %collective-permute-done.28 = f32[128,128]{1,0:T(8,128)S(1)} collective-permute-done((f32[128,128]{1,0:T(8,128)S(1)}, f32[128,128]{1,0:T(8,128)S(1)}, u32[]{:S(2)}, u32[]{:S(2)}) %collective-permute-start.28) | collective-permute-done | bytes 65568 | tf_op jit(solution)/shard_map/ppermute | solution.py:27
  110.6 0.6 add.62.packed
  111.3 3.6 %collective-permute-done.31.refs_2_ = f32[4,64,128]{2,1,0:T(8,128)S(1)} collective-permute-done((f32[4,64,128]{2,1,0:T(8,128)S(1)}, f32[4,64,128]{2,1,0:T(8,128)S(1)}, u32[]{:S(2)}, u32[]{:S(2)}) %collective-permute-start.31) | collective-permute-done | bytes 131104 | tf_op jit(solution)/shard_map/ppermute | solution.py:27
  114.9 0.6 copy-done.18
  115.6 16.3 %final.1 = (f32[4,64,128]{2,1,0:T(8,128)}, f32[4,64,128]{2,1,0:T(8,128)}) custom-call(f32[128,128]{1,0:T(8,128)} %add.62.packed, f32[4,64,128]{2,1,0:T(8,128)} %get-tuple-element.25.moving, f32[4,64,128]{2,1,0:T(8,128)} %get-tuple-element.26.first, f32[4,64,128]{2,1,0:T(8,128)} %get-tuple-element.27.near, f32[96,128]{1,0:T(8,128)} %copy-done.3, ...), custom_call_target="tpu_custom_call" | custom-call | tf_op jit(solution)/shard_map/final/pallas_call | solution.py:359
  (101 shorter events, 2.0 us)
Async XLA Ops:
  5.3 12.8 %collective-permute-start.10 = (f32[16,64,128]{2,1,0:T(8,128)}, f32[16,64,128]{2,1,0:T(8,128)S(1)}, u32[]{:S(2)}, u32[]{:S(2)}) collective-permute-start(f32[16,64,128]{2,1,0:T(8,128)} %get-tuple-element.18), channel_id=1, source_target_pairs={{0,1},{1,0},{2,3},{3,2},{4,5},{5,4},{6,7},{7,6},{8,9},{9,8},{10,11... | collective-permute-start | bytes 1572872 | tf_op jit(solution)/shard_map/ppermute | solution.py:27
  5.8 10.9 %collective-permute-start.1 = (f32[256,128]{1,0:T(8,128)S(1)}, f32[256,128]{1,0:T(8,128)S(1)}, u32[]{:S(2)}, u32[]{:S(2)}) collective-permute-start(f32[256,128]{1,0:T(8,128)S(1)} %bitcast.3), channel_id=1, source_target_pairs={{0,2},{1,3},{2,0},{3,1},{4,6},{5,7},{6,4},{7,5},{8,10},{9,11},{10,... | collective-permute-start | bytes 393224 | tf_op jit(solution)/shard_map/ppermute | solution.py:27
  8.4 4.3 %collective-permute-start.7 = (f32[2,64,128]{2,1,0:T(8,128)S(1)}, f32[2,64,128]{2,1,0:T(8,128)S(1)}, u32[]{:S(2)}, u32[]{:S(2)}) collective-permute-start(f32[2,64,128]{2,1,0:T(8,128)S(1)} %slice.47), channel_id=1, source_target_pairs={{0,8},{8,0},{16,24},{24,16},{1,9},{9,1},{17,25},{25,17},{2,10},{10... | collective-permute-start | bytes 196616 | tf_op jit(solution)/shard_map/ppermute | solution.py:27
  9.9 5.4 %collective-permute-start.8 = (f32[2,64,128]{2,1,0:T(8,128)S(1)}, f32[2,64,128]{2,1,0:T(8,128)S(1)}, u32[]{:S(2)}, u32[]{:S(2)}) collective-permute-start(f32[2,64,128]{2,1,0:T(8,128)S(1)} %slice.47), channel_id=1, source_target_pairs={{0,16},{8,24},{16,0},{24,8},{1,17},{9,25},{17,1},{25,9},{2,18},{10... | collective-permute-start | bytes 196616 | tf_op jit(solution)/shard_map/ppermute | solution.py:27
  11.4 15.9 %collective-permute-start = (f32[256,128]{1,0:T(8,128)S(1)}, f32[256,128]{1,0:T(8,128)S(1)}, u32[]{:S(2)}, u32[]{:S(2)}) collective-permute-start(f32[256,128]{1,0:T(8,128)S(1)} %bitcast.4), channel_id=1, source_target_pairs={{0,1},{1,0},{2,3},{3,2},{4,5},{5,4},{6,7},{7,6},{8,9},{9,8},{10,11... | collective-permute-start | bytes 393224 | tf_op jit(solution)/shard_map/ppermute | solution.py:27
  12.7 17.3 %copy-start.24 = (f32[2,64,128]{2,1,0:T(8,128)}, f32[2,64,128]{2,1,0:T(8,128)S(1)}, u32[]{:S(2)}) copy-start(f32[2,64,128]{2,1,0:T(8,128)S(1)} %collective-permute-done.7.refs_12_) | copy-start | bytes 196612
  12.7 11.4 %collective-permute-start.3 = (f32[256,128]{1,0:T(8,128)S(1)}, f32[256,128]{1,0:T(8,128)S(1)}, u32[]{:S(2)}, u32[]{:S(2)}) collective-permute-start(f32[256,128]{1,0:T(8,128)S(1)} %bitcast.5), channel_id=1, source_target_pairs={{0,4},{1,5},{2,6},{3,7},{4,0},{5,1},{6,2},{7,3},{8,12},{9,13},{10,... | collective-permute-start | bytes 393224 | tf_op jit(solution)/shard_map/ppermute | solution.py:27
  15.3 14.7 %copy-start.25 = (f32[2,64,128]{2,1,0:T(8,128)}, f32[2,64,128]{2,1,0:T(8,128)S(1)}, u32[]{:S(2)}) copy-start(f32[2,64,128]{2,1,0:T(8,128)S(1)} %collective-permute-done.8.refs_13_) | copy-start | bytes 196612
  15.3 8.8 %collective-permute-start.5 = (f32[256,128]{1,0:T(8,128)S(1)}, f32[256,128]{1,0:T(8,128)S(1)}, u32[]{:S(2)}, u32[]{:S(2)}) collective-permute-start(f32[256,128]{1,0:T(8,128)S(1)} %bitcast.6), channel_id=1, source_target_pairs={{0,6},{1,7},{2,4},{3,5},{4,2},{5,3},{6,0},{7,1},{8,14},{9,15},{10,... | collective-permute-start | bytes 393224 | tf_op jit(solution)/shard_map/ppermute | solution.py:27
  16.6 13.3 %copy-start.11 = (f32[256,128]{1,0:T(8,128)}, f32[256,128]{1,0:T(8,128)S(1)}, u32[]{:S(2)}) copy-start(f32[256,128]{1,0:T(8,128)S(1)} %collective-permute-done.1.refs_2_) | copy-start | bytes 393220
  16.6 7.9 %collective-permute-start.9 = (f32[2,64,128]{2,1,0:T(8,128)S(1)}, f32[2,64,128]{2,1,0:T(8,128)S(1)}, u32[]{:S(2)}, u32[]{:S(2)}) collective-permute-start(f32[2,64,128]{2,1,0:T(8,128)S(1)} %slice.47), channel_id=1, source_target_pairs={{0,24},{8,16},{16,8},{24,0},{1,25},{9,17},{17,9},{25,1},{2,26},{10... | collective-permute-start | bytes 196616 | tf_op jit(solution)/shard_map/ppermute | solution.py:27
  18.1 20.0 %copy-start.2 = (f32[16,64,128]{2,1,0:T(8,128)}, f32[16,64,128]{2,1,0:T(8,128)S(1)}, u32[]{:S(2)}) copy-start(f32[16,64,128]{2,1,0:T(8,128)S(1)} %collective-permute-done.10.refs_0_) | copy-start | bytes 1572868
  18.1 10.5 %collective-permute-start.2 = (f32[256,128]{1,0:T(8,128)S(1)}, f32[256,128]{1,0:T(8,128)S(1)}, u32[]{:S(2)}, u32[]{:S(2)}) collective-permute-start(f32[256,128]{1,0:T(8,128)S(1)} %collective-permute-done.1.refs_2_), channel_id=1, source_target_pairs={{0,1},{1,0},{2,3},{3,2},{4,5},{5,4},{6,7},{7,6},{8,9},{9,8},{10,11... | collective-permute-start | bytes 393224 | tf_op jit(solution)/shard_map/ppermute | solution.py:27
  24.0 5.9 %copy-start.13 = (f32[256,128]{1,0:T(8,128)}, f32[256,128]{1,0:T(8,128)S(1)}, u32[]{:S(2)}) copy-start(f32[256,128]{1,0:T(8,128)S(1)} %collective-permute-done.3.refs_4_) | copy-start | bytes 393220
  24.0 5.9 %collective-permute-start.4 = (f32[256,128]{1,0:T(8,128)S(1)}, f32[256,128]{1,0:T(8,128)S(1)}, u32[]{:S(2)}, u32[]{:S(2)}) collective-permute-start(f32[256,128]{1,0:T(8,128)S(1)} %collective-permute-done.3.refs_4_), channel_id=1, source_target_pairs={{0,1},{1,0},{2,3},{3,2},{4,5},{5,4},{6,7},{7,6},{8,9},{9,8},{10,11... | collective-permute-start | bytes 393224 | tf_op jit(solution)/shard_map/ppermute | solution.py:27
  24.0 5.9 %copy-start.14 = (f32[256,128]{1,0:T(8,128)}, f32[256,128]{1,0:T(8,128)S(1)}, u32[]{:S(2)}) copy-start(f32[256,128]{1,0:T(8,128)S(1)} %collective-permute-done.5.refs_6_) | copy-start | bytes 393220
  24.1 5.9 %collective-permute-start.6 = (f32[256,128]{1,0:T(8,128)S(1)}, f32[256,128]{1,0:T(8,128)S(1)}, u32[]{:S(2)}, u32[]{:S(2)}) collective-permute-start(f32[256,128]{1,0:T(8,128)S(1)} %collective-permute-done.5.refs_6_), channel_id=1, source_target_pairs={{0,1},{1,0},{2,3},{3,2},{4,5},{5,4},{6,7},{7,6},{8,9},{9,8},{10,11... | collective-permute-start | bytes 393224 | tf_op jit(solution)/shard_map/ppermute | solution.py:27
  24.6 13.5 %collective-permute-start.11 = (f32[4,64,128]{2,1,0:T(8,128)S(1)}, f32[4,64,128]{2,1,0:T(8,128)S(1)}, u32[]{:S(2)}, u32[]{:S(2)}) collective-permute-start(f32[4,64,128]{2,1,0:T(8,128)S(1)} %get-tuple-element.35), channel_id=1, source_target_pairs={{0,2},{1,3},{2,0},{3,1},{4,6},{5,7},{6,4},{7,5},{8,10},{9,11},{10,... | collective-permute-start | bytes 393224 | tf_op jit(solution)/shard_map/ppermute | solution.py:27
  27.4 12.9 %collective-permute-start.12 = (f32[4,64,128]{2,1,0:T(8,128)S(1)}, f32[4,64,128]{2,1,0:T(8,128)S(1)}, u32[]{:S(2)}, u32[]{:S(2)}) collective-permute-start(f32[4,64,128]{2,1,0:T(8,128)S(1)} %get-tuple-element.34), channel_id=1, source_target_pairs={{0,4},{1,5},{2,6},{3,7},{4,0},{5,1},{6,2},{7,3},{8,12},{9,13},{10,... | collective-permute-start | bytes 393224 | tf_op jit(solution)/shard_map/ppermute | solution.py:27
  28.7 11.6 %collective-permute-start.13 = (f32[4,64,128]{2,1,0:T(8,128)S(1)}, f32[4,64,128]{2,1,0:T(8,128)S(1)}, u32[]{:S(2)}, u32[]{:S(2)}) collective-permute-start(f32[4,64,128]{2,1,0:T(8,128)S(1)} %get-tuple-element.33), channel_id=1, source_target_pairs={{0,6},{1,7},{2,4},{3,5},{4,2},{5,3},{6,0},{7,1},{8,14},{9,15},{10,... | collective-permute-start | bytes 393224 | tf_op jit(solution)/shard_map/ppermute | solution.py:27
  43.5 38.2 %copy-start.31 = (s32[128]{0:T(128)S(1)}, s32[128]{0:T(128)}, u32[]{:S(2)}) copy-start(s32[128]{0:T(128)} %new_slot.5) | copy-start | bytes 1540
  43.5 9.2 %collective-permute-start.15 = (f32[352,128]{1,0:T(8,128)}, f32[352,128]{1,0:T(8,128)S(1)}, u32[]{:S(2)}, u32[]{:S(2)}) collective-permute-start(f32[352,128]{1,0:T(8,128)} %get-tuple-element.20.refs_0_), channel_id=1, source_target_pairs={{0,2},{1,3},{2,0},{3,1},{4,6},{5,7},{6,4},{7,5},{8,10},{9,11},{10,... | collective-permute-start | bytes 540680 | tf_op jit(solution)/shard_map/ppermute | solution.py:27
  46.1 16.3 %collective-permute-start.17 = (f32[352,128]{1,0:T(8,128)}, f32[352,128]{1,0:T(8,128)S(1)}, u32[]{:S(2)}, u32[]{:S(2)}) collective-permute-start(f32[352,128]{1,0:T(8,128)} %get-tuple-element.20.refs_0_), channel_id=1, source_target_pairs={{0,4},{1,5},{2,6},{3,7},{4,0},{5,1},{6,2},{7,3},{8,12},{9,13},{10,... | collective-permute-start | bytes 540680 | tf_op jit(solution)/shard_map/ppermute | solution.py:27
  47.2 15.2 %collective-permute-start.19 = (f32[352,128]{1,0:T(8,128)}, f32[352,128]{1,0:T(8,128)S(1)}, u32[]{:S(2)}, u32[]{:S(2)}) collective-permute-start(f32[352,128]{1,0:T(8,128)} %get-tuple-element.20.refs_0_), channel_id=1, source_target_pairs={{0,6},{1,7},{2,4},{3,5},{4,2},{5,3},{6,0},{7,1},{8,14},{9,15},{10,... | collective-permute-start | bytes 540680 | tf_op jit(solution)/shard_map/ppermute | solution.py:27
  48.5 14.4 %collective-permute-start.21 = (f32[2,64,128]{2,1,0:T(8,128)}, f32[2,64,128]{2,1,0:T(8,128)S(1)}, u32[]{:S(2)}, u32[]{:S(2)}) collective-permute-start(f32[2,64,128]{2,1,0:T(8,128)} %get-tuple-element.22), channel_id=1, source_target_pairs={{0,8},{8,0},{16,24},{24,16},{1,9},{9,1},{17,25},{25,17},{2,10},{10... | collective-permute-start | bytes 196616 | tf_op jit(solution)/shard_map/ppermute | solution.py:27
  50.0 22.8 %collective-permute-start.14 = (f32[352,128]{1,0:T(8,128)}, f32[352,128]{1,0:T(8,128)S(1)}, u32[]{:S(2)}, u32[]{:S(2)}) collective-permute-start(f32[352,128]{1,0:T(8,128)} %get-tuple-element.20.refs_0_), channel_id=1, source_target_pairs={{0,1},{1,0},{2,3},{3,2},{4,5},{5,4},{6,7},{7,6},{8,9},{9,8},{10,11... | collective-permute-start | bytes 540680 | tf_op jit(solution)/shard_map/ppermute | solution.py:27
  52.7 20.1 %copy-start.4 = (f32[352,128]{1,0:T(8,128)}, f32[352,128]{1,0:T(8,128)S(1)}, u32[]{:S(2)}) copy-start(f32[352,128]{1,0:T(8,128)S(1)} %collective-permute-done.15.refs_2_) | copy-start | bytes 540676
  52.8 20.0 %collective-permute-start.16 = (f32[352,128]{1,0:T(8,128)S(1)}, f32[352,128]{1,0:T(8,128)S(1)}, u32[]{:S(2)}, u32[]{:S(2)}) collective-permute-start(f32[352,128]{1,0:T(8,128)S(1)} %collective-permute-done.15.refs_2_), channel_id=1, source_target_pairs={{0,1},{1,0},{2,3},{3,2},{4,5},{5,4},{6,7},{7,6},{8,9},{9,8},{10,11... | collective-permute-start | bytes 540680 | tf_op jit(solution)/shard_map/ppermute | solution.py:27
  62.4 10.5 %copy-start.5 = (f32[352,128]{1,0:T(8,128)}, f32[352,128]{1,0:T(8,128)S(1)}, u32[]{:S(2)}) copy-start(f32[352,128]{1,0:T(8,128)S(1)} %collective-permute-done.17.refs_4_) | copy-start | bytes 540676
  62.4 10.4 %collective-permute-start.18 = (f32[352,128]{1,0:T(8,128)S(1)}, f32[352,128]{1,0:T(8,128)S(1)}, u32[]{:S(2)}, u32[]{:S(2)}) collective-permute-start(f32[352,128]{1,0:T(8,128)S(1)} %collective-permute-done.17.refs_4_), channel_id=1, source_target_pairs={{0,1},{1,0},{2,3},{3,2},{4,5},{5,4},{6,7},{7,6},{8,9},{9,8},{10,11... | collective-permute-start | bytes 540680 | tf_op jit(solution)/shard_map/ppermute | solution.py:27
  62.4 10.5 %copy-start.6 = (f32[352,128]{1,0:T(8,128)}, f32[352,128]{1,0:T(8,128)S(1)}, u32[]{:S(2)}) copy-start(f32[352,128]{1,0:T(8,128)S(1)} %collective-permute-done.19.refs_6_) | copy-start | bytes 540676
  62.4 10.4 %collective-permute-start.20 = (f32[352,128]{1,0:T(8,128)S(1)}, f32[352,128]{1,0:T(8,128)S(1)}, u32[]{:S(2)}, u32[]{:S(2)}) collective-permute-start(f32[352,128]{1,0:T(8,128)S(1)} %collective-permute-done.19.refs_6_), channel_id=1, source_target_pairs={{0,1},{1,0},{2,3},{3,2},{4,5},{5,4},{6,7},{7,6},{8,9},{9,8},{10,11... | collective-permute-start | bytes 540680 | tf_op jit(solution)/shard_map/ppermute | solution.py:27
  62.9 10.0 %copy-start.27 = (f32[2,64,128]{2,1,0:T(8,128)}, f32[2,64,128]{2,1,0:T(8,128)S(1)}, u32[]{:S(2)}) copy-start(f32[2,64,128]{2,1,0:T(8,128)S(1)} %collective-permute-done.21.refs_12_) | copy-start | bytes 196612
  62.9 4.5 %collective-permute-start.22 = (f32[2,64,128]{2,1,0:T(8,128)}, f32[2,64,128]{2,1,0:T(8,128)S(1)}, u32[]{:S(2)}, u32[]{:S(2)}) collective-permute-start(f32[2,64,128]{2,1,0:T(8,128)} %get-tuple-element.22), channel_id=1, source_target_pairs={{0,16},{8,24},{16,0},{24,8},{1,17},{9,25},{17,1},{25,9},{2,18},{10... | collective-permute-start | bytes 196616 | tf_op jit(solution)/shard_map/ppermute | solution.py:27
  67.4 5.5 %copy-start.28 = (f32[2,64,128]{2,1,0:T(8,128)}, f32[2,64,128]{2,1,0:T(8,128)S(1)}, u32[]{:S(2)}) copy-start(f32[2,64,128]{2,1,0:T(8,128)S(1)} %collective-permute-done.22.refs_13_) | copy-start | bytes 196612
  67.4 5.4 %collective-permute-start.23 = (f32[2,64,128]{2,1,0:T(8,128)}, f32[2,64,128]{2,1,0:T(8,128)S(1)}, u32[]{:S(2)}, u32[]{:S(2)}) collective-permute-start(f32[2,64,128]{2,1,0:T(8,128)} %get-tuple-element.22), channel_id=1, source_target_pairs={{0,24},{8,16},{16,8},{24,0},{1,25},{9,17},{17,9},{25,1},{2,26},{10... | collective-permute-start | bytes 196616 | tf_op jit(solution)/shard_map/ppermute | solution.py:27
  81.6 12.9 %copy-start.30 = (f32[128,128]{1,0:T(8,128)S(1)}, f32[128,128]{1,0:T(8,128)}, u32[]{:S(2)}) copy-start(f32[128,128]{1,0:T(8,128)} %get-tuple-element.24) | copy-start | bytes 196612
  81.6 3.4 %collective-permute-start.24 = (f32[96,128]{1,0:T(8,128)}, f32[96,128]{1,0:T(8,128)S(1)}, u32[]{:S(2)}, u32[]{:S(2)}) collective-permute-start(f32[96,128]{1,0:T(8,128)} %get-tuple-element.23), channel_id=1, source_target_pairs={{0,1},{1,0},{2,3},{3,2},{4,5},{5,4},{6,7},{7,6},{8,9},{9,8},{10,11... | collective-permute-start | bytes 147464 | tf_op jit(solution)/shard_map/ppermute | solution.py:27
  86.0 7.1 %collective-permute-start.25 = (f32[96,128]{1,0:T(8,128)S(1)}, f32[96,128]{1,0:T(8,128)S(1)}, u32[]{:S(2)}, u32[]{:S(2)}) collective-permute-start(f32[96,128]{1,0:T(8,128)S(1)} %select_select_fusion.2), channel_id=1, source_target_pairs={{0,2},{1,3},{2,0},{3,1},{4,6},{5,7},{6,4},{7,5},{8,10},{9,11},{10,... | collective-permute-start | bytes 147464 | tf_op jit(solution)/shard_map/ppermute | solution.py:27
  92.9 7.7 %collective-permute-start.29 = (f32[16,64,128]{2,1,0:T(8,128)}, f32[16,64,128]{2,1,0:T(8,128)S(1)}, u32[]{:S(2)}, u32[]{:S(2)}) collective-permute-start(f32[16,64,128]{2,1,0:T(8,128)} %get-tuple-element.29), channel_id=1, source_target_pairs={{0,1},{1,0},{2,3},{3,2},{4,5},{5,4},{6,7},{7,6},{8,9},{9,8},{10,11... | collective-permute-start | bytes 1572872 | tf_op jit(solution)/shard_map/ppermute | solution.py:27
  93.1 5.8 %collective-permute-start.26 = (f32[96,128]{1,0:T(8,128)S(1)}, f32[96,128]{1,0:T(8,128)S(1)}, u32[]{:S(2)}, u32[]{:S(2)}) collective-permute-start(f32[96,128]{1,0:T(8,128)S(1)} %select_select_fusion.1), channel_id=1, source_target_pairs={{0,4},{1,5},{2,6},{3,7},{4,0},{5,1},{6,2},{7,3},{8,12},{9,13},{10,... | collective-permute-start | bytes 147464 | tf_op jit(solution)/shard_map/ppermute | solution.py:27
  99.0 15.9 %copy-start.3 = (f32[96,128]{1,0:T(8,128)}, f32[96,128]{1,0:T(8,128)S(1)}, u32[]{:S(2)}) copy-start(f32[96,128]{1,0:T(8,128)S(1)} %select_select_fusion.row) | copy-start | bytes 147460
  99.0 7.2 %collective-permute-start.27 = (f32[128,128]{1,0:T(8,128)S(1)}, f32[128,128]{1,0:T(8,128)S(1)}, u32[]{:S(2)}, u32[]{:S(2)}) collective-permute-start(f32[128,128]{1,0:T(8,128)S(1)} %pad_maximum_fusion), channel_id=1, source_target_pairs={{0,8},{8,0},{16,24},{24,16},{1,9},{9,1},{17,25},{25,17},{2,10},{10... | collective-permute-start | bytes 196616 | tf_op jit(solution)/shard_map/ppermute | solution.py:27
  100.5 14.3 %copy-start.1 = (f32[16,64,128]{2,1,0:T(8,128)}, f32[16,64,128]{2,1,0:T(8,128)S(1)}, u32[]{:S(2)}) copy-start(f32[16,64,128]{2,1,0:T(8,128)S(1)} %collective-permute-done.29.refs_0_) | copy-start | bytes 1572868
  101.8 9.4 %collective-permute-start.30 = (f32[4,64,128]{2,1,0:T(8,128)S(1)}, f32[4,64,128]{2,1,0:T(8,128)S(1)}, u32[]{:S(2)}, u32[]{:S(2)}) collective-permute-start(f32[4,64,128]{2,1,0:T(8,128)S(1)} %get-tuple-element.32), channel_id=1, source_target_pairs={{0,2},{1,3},{2,0},{3,1},{4,6},{5,7},{6,4},{7,5},{8,10},{9,11},{10,... | collective-permute-start | bytes 393224 | tf_op jit(solution)/shard_map/ppermute | solution.py:27
  101.9 13.0 %collective-permute-start.31 = (f32[4,64,128]{2,1,0:T(8,128)S(1)}, f32[4,64,128]{2,1,0:T(8,128)S(1)}, u32[]{:S(2)}, u32[]{:S(2)}) collective-permute-start(f32[4,64,128]{2,1,0:T(8,128)S(1)} %get-tuple-element.31), channel_id=1, source_target_pairs={{0,4},{1,5},{2,6},{3,7},{4,0},{5,1},{6,2},{7,3},{8,12},{9,13},{10,... | collective-permute-start | bytes 393224 | tf_op jit(solution)/shard_map/ppermute | solution.py:27
  104.6 10.3 %collective-permute-start.32 = (f32[4,64,128]{2,1,0:T(8,128)S(1)}, f32[4,64,128]{2,1,0:T(8,128)S(1)}, u32[]{:S(2)}, u32[]{:S(2)}) collective-permute-start(f32[4,64,128]{2,1,0:T(8,128)S(1)} %get-tuple-element.30), channel_id=1, source_target_pairs={{0,6},{1,7},{2,4},{3,5},{4,2},{5,3},{6,0},{7,1},{8,14},{9,15},{10,... | collective-permute-start | bytes 393224 | tf_op jit(solution)/shard_map/ppermute | solution.py:27
  106.3 4.3 %collective-permute-start.28 = (f32[128,128]{1,0:T(8,128)S(1)}, f32[128,128]{1,0:T(8,128)S(1)}, u32[]{:S(2)}, u32[]{:S(2)}) collective-permute-start(f32[128,128]{1,0:T(8,128)S(1)} %fusion.1), channel_id=1, source_target_pairs={{0,16},{8,24},{16,0},{24,8},{1,17},{9,25},{17,1},{25,9},{2,18},{10... | collective-permute-start | bytes 196616 | tf_op jit(solution)/shard_map/ppermute | solution.py:27
  (17 other events, 28.1 us)

commit v4 on v3

--- a/solution.py
+++ b/solution.py
@@ -15,11 +15,12 @@
 left_t = (((0,), (0,)), ((), ()))
 vmem = pl.BlockSpec(memory_space=pltpu.VMEM)
 smem = pl.BlockSpec(memory_space=pltpu.SMEM)
-vmem_bytes = 60 * 2**20
-
-
-def params():
-    return pltpu.CompilerParams(vmem_limit_bytes=vmem_bytes)
+vmem_bytes = 40 * 2**20
+all_vmem = 60 * 2**20
+
+
+def params(limit=vmem_bytes):
+    return pltpu.CompilerParams(vmem_limit_bytes=limit)
 
 
 def swap(value, axis, mask):
@@ -125,18 +126,18 @@
         ],
         out_specs=[vmem] * 2,
         scratch_shapes=[pltpu.VMEM((2 * half[0], count, order), f32)],
-        compiler_params=params(),
+        compiler_params=params(vmem_bytes if moved else all_vmem),
         name="returned_moved" if moved else "returned",
     )(vectors, tiles, col, load, new_slot)
 
 
 def near_kernel(bulk_count, second, *refs):
     panel, refs = refs[:bulk_count], refs[bulk_count:]
-    vectors, tiles, diag, coupling = refs[:4]
+    vectors, tiles, diag, coupling, sides, other_sides, col, load, new_slot, near, moving = refs[:11]
+    extra, *more, rows_of, gram = refs[11:]
     edge_rows, part_count = coupling.shape[:2]
-    border, refs = refs[4 : 3 + part_count], refs[3 + part_count :]
-    col, load, new_slot, near, moving, gram_out, *more, rows_of, gram = refs
     row_count, count = vectors.shape[:2]
+    half = count // 2
     me = lax.axis_index("bulk")
     mine = lax.axis_index("group")
     base = mine * bulk_count * row_count
@@ -152,13 +153,8 @@
     def _():
         for index, piece in enumerate(panel):
             for k in range(row_count):
-                rows_of[index * row_count + k] = split_rows(piece[k * count : (k + 1) * count])
+                rows_of[index * row_count + k] = split_rows(piece[k])
         gram[...] = jnp.zeros_like(gram)
-        if second:
-            tail = panel[0][row_count * count :]
-            for piece in panel[1:]:
-                tail = tail + piece[row_count * count :]
-            gram_out[count // 2 :] = tail
 
     direct = None
     for t in range(tiles.shape[1]):
@@ -180,10 +176,13 @@
     @pl.when(s < edge_rows)
     def _():
         k = jnp.minimum(s, edge_rows - 1)
-        crossed = times_tile(split_rows(value), coupling[k, mine], right_t)
-        for index, ref in enumerate(border):
-            tile = coupling[k, mine ^ (index + 1)]
-            crossed = crossed + times_tile(split_rows(ref[k]), tile, right_t)
+        crossed = None
+        for h in range(part_count):
+            ref = sides if h < part_count // 2 else other_sides
+            start = (h % (part_count // 2) * edge_rows + k) * count
+            rows = split_rows(ref[pl.ds(pl.multiple_of(start, count), count)])
+            term = times_tile(rows, coupling[k, mine ^ h], right_t)
+            crossed = term if crossed is None else crossed + term
         near[s] += crossed
         if second:
             gram[...] += dot32(value, crossed, right_t)
@@ -194,22 +193,30 @@
 
         @pl.when(incoming // row_count == index)
         def _(piece=piece):
-            start = pl.multiple_of(incoming % row_count * count, count)
-            moving[s] = piece[pl.ds(start, count)]
+            moving[s] = piece[incoming % row_count]
 
     if second:
-        (leaving,) = more
 
         @pl.when(arriving != slot)
         def _():
-            leaving[count // 2 :] = near[s]
+            extra[4 * half :] = near[s]
+
+    else:
+        (flags,) = more
+
+        @pl.when(arriving != slot)
+        def _():
+            distance = ((arriving - base) // row_count) ^ me
+            for index in range(flags.shape[0] // 8):
+                bit = ((distance >> index) & 1).astype(f32)
+                flags[8 * index : 8 * index + 8] = jnp.full((8, flags.shape[1]), bit, f32)
 
     @pl.when(s == row_count - 1)
     def _():
+        extra[:half] = pack(gram[...])
         if second:
-            leaving[: count // 2] = pack(gram[...])
-        else:
-            gram_out[...] = pack(gram[...])
+            start = part_count // 2 * edge_rows * count
+            extra[half : 4 * half] = sides[start:] + other_sides[start:]
 
 
 def near_part(panel, vectors, tiles, diag, coupling, border, col, load, new_slot, second):
@@ -217,9 +224,11 @@
     bulk_count = len(panel)
     tile_count = tiles.shape[1]
     half = count // 2
-    shapes = [vectors.shape, vectors.shape, (half, order)]
+    shapes = [vectors.shape, vectors.shape]
     if second:
-        shapes = [vectors.shape, vectors.shape, (4 * half, order), (half + count, order)]
+        shapes += [(4 * half + count, order)]
+    else:
+        shapes += [(half, order), (8 * (bulk_count.bit_length() - 1), order)]
     return pl.pallas_call(
         functools.partial(near_kernel, bulk_count, second),
         grid=(row_count,),
@@ -230,9 +239,12 @@
             pl.BlockSpec((1, tile_count, order, order), lambda s: (s, 0, 0, 0)),
             pl.BlockSpec((1, order, order), lambda s: (s, 0, 0)),
             vmem,
-        ]
-        + [vmem] * len(border)
-        + [smem] * 3,
+            vmem,
+            vmem,
+            smem,
+            smem,
+            smem,
+        ],
         out_specs=[vmem] * len(shapes),
         scratch_shapes=[
             pltpu.VMEM((bulk_count * row_count, 2 * count, order), bf16),
@@ -244,68 +256,95 @@
 
 
 def gather_first_kernel(vectors, near, keep, *refs):
-    received = refs[:-4]
-    packed, first, flat, edge = refs[-4:]
+    received = refs[:-3]
+    packed, first, side = refs[-3:]
     row_count, count = vectors.shape[:2]
+    half = count // 2
+    edge_rows = (side.shape[0] - 3 * half) // count
     grams = [None, None]
     for k in range(row_count):
         value = near[k] + keep[k]
         for ref in received:
             value = value + ref[k]
         first[k] = value
-        flat[k * count : (k + 1) * count] = value
-        if k < edge.shape[0]:
-            edge[k] = value
+        if k < edge_rows:
+            side[k * count : (k + 1) * count] = value
         terms = (dot32(vectors[k], value, right_t), dot32(value, value, right_t))
         grams = [term if old is None else old + term for old, term in zip(grams, terms)]
-    start = row_count * count
-    half = count // 2
-    flat[start : start + half] = packed[...]
-    flat[start + half : start + 2 * half] = pack(grams[0])
-    flat[start + 2 * half :] = pack(grams[1])
+    start = edge_rows * count
+    side[start : start + half] = packed[...]
+    side[start + half : start + 2 * half] = pack(grams[0])
+    side[start + 2 * half :] = pack(grams[1])
 
 
 def gather_first(vectors, near, keep, received, packed, edge_rows):
     row_count, count, order = vectors.shape
-    shapes = [
-        vectors.shape,
-        (row_count * count + 3 * (count // 2), order),
-        (edge_rows, count, order),
-    ]
+    shapes = [vectors.shape, (edge_rows * count + 3 * (count // 2), order)]
     specs = [pl.BlockSpec((row_count, count, order), lambda s: (0, 0, 0))] * (3 + len(received))
     return pl.pallas_call(
         gather_first_kernel,
         grid=(1,),
         out_shape=[jax.ShapeDtypeStruct(shape, f32) for shape in shapes],
         in_specs=specs + [vmem],
-        out_specs=[vmem] * 3,
+        out_specs=[vmem] * 2,
         compiler_params=params(),
         name="gather_first",
     )(vectors, near, keep, *received, packed)
 
 
+def spread_row(rows, index):
+    return jnp.broadcast_to(rows[index : index + 1], rows.shape)
+
+
 def inverse_factors(matrices):
     count = matrices[0].shape[0]
-    blocks = count // 8
+    step = 8
+    shape = (step, 2 * count)
     row_ids = lax.broadcasted_iota(jnp.int32, (count, count), 0)
     col_ids = lax.broadcasted_iota(jnp.int32, (count, count), 1)
     eye = (row_ids == col_ids).astype(f32)
-    sub = lax.broadcasted_iota(jnp.int32, (8, 2 * count), 0)
+    sub = lax.broadcasted_iota(jnp.int32, shape, 0)
     work = []
     for matrix in matrices:
         both = jnp.concatenate([matrix, eye], axis=1)
-        work.append([both[8 * i : 8 * i + 8] for i in range(blocks)])
-    for j in range(count):
-        block, k = divmod(j, 8)
+        work.append([both[i : i + step] for i in range(0, count, step)])
+    for block in range(count // step):
+        start = block * step
         for w in work:
-            row = w[block][k : k + 1]
-            scale = lax.rsqrt(row[:, j : j + 1])
-            pivot = row * scale
-            for i in range(block, blocks):
-                changed = w[i] - w[i][:, j : j + 1] * scale * pivot
-                if i == block:
-                    changed = jnp.where(sub > k, changed, jnp.where(sub == k, pivot, w[i]))
-                w[i] = changed
+            cols = [
+                [jnp.broadcast_to(rows[:, start + m : start + m + 1], shape) for m in range(step)]
+                for rows in w[block:]
+            ]
+            factor = [[None] * step for _ in range(step)]
+            scales, pivots = [], []
+            for m in range(step):
+                value = spread_row(cols[0][m], m)
+                row = spread_row(w[block], m)
+                for u in range(m):
+                    value = value - factor[m][u] * factor[m][u]
+                    row = row - factor[m][u] * pivots[u]
+                scales.append(lax.rsqrt(value))
+                pivots.append(row * scales[m])
+                for v in range(m + 1, step):
+                    value = spread_row(cols[0][m], v)
+                    for u in range(m):
+                        value = value - factor[v][u] * factor[m][u]
+                    factor[v][m] = value * scales[m]
+            for i in range(block + 1, count // step):
+                left = []
+                for m in range(step):
+                    value = cols[i - block][m]
+                    for u in range(m):
+                        value = value - left[u] * factor[m][u]
+                    left.append(value * scales[m])
+                terms = [one * pivot for one, pivot in zip(left, pivots)]
+                while len(terms) > 1:
+                    terms = [x + y for x, y in zip(terms[::2], terms[1::2])]
+                w[i] = w[i] - terms[0]
+            rows = pivots[0]
+            for m in range(1, step):
+                rows = jnp.where(sub == m, pivots[m], rows)
+            w[block] = rows
     return [jnp.concatenate(w, axis=0)[:, count:] for w in work]
 
 
@@ -313,12 +352,11 @@
     return dot32(inverse_factor, dot32(inverse_factor, right), left_t)
 
 
-def final_kernel(packed, moving, first, near, row, new_slot, keep, *refs):
-    received, (solution, resid) = refs[:-2], refs[-2:]
+def final_kernel(gram, extra, moving, first, other, new_slot, solution, resid):
     row_count, count = moving.shape[:2]
     half = count // 2
-    grams = [unpack(packed[i * half : (i + 1) * half]) for i in range(4)]
-    g3, g0, g1, g2 = (sym(gram) for gram in grams)
+    g3 = sym(unpack(gram[...]))
+    g0, g1, g2 = (sym(unpack(extra[i * half : (i + 1) * half])) for i in (1, 2, 3))
     eye = (
         lax.broadcasted_iota(jnp.int32, (count, count), 0)
         == lax.broadcasted_iota(jnp.int32, (count, count), 1)
@@ -344,32 +382,66 @@
     coef = jnp.concatenate([top, low], axis=1)
     slot = first_slot(row_count)
     for k in range(row_count):
-        stays = new_slot[slot + k] == slot + k
-        second = jnp.where(stays, near[k], row[half:]) + keep[k]
-        for ref in received:
-            second = second + ref[k]
+        moved = new_slot[slot + k] != slot + k
+        second = other[k] + jnp.where(moved, extra[4 * half :], 0.0)
         basis = jnp.concatenate([moving[k], first[k], second], axis=0)
         both = dot32(coef, basis, left_t)
         solution[k] = both[:count]
         resid[k] = both[count:]
 
 
-def final(packed, moving, first, near, row, new_slot, keep, received):
-    block = pl.BlockSpec(near.shape, lambda s: (0, 0, 0))
+def final(gram, extra, moving, first, other, new_slot):
     return pl.pallas_call(
         final_kernel,
-        grid=(1,),
-        out_shape=[jax.ShapeDtypeStruct(near.shape, f32)] * 2,
-        in_specs=[vmem] * 5 + [smem] + [block] * (1 + len(received)),
+        out_shape=[jax.ShapeDtypeStruct(other.shape, f32)] * 2,
+        in_specs=[vmem] * 5 + [smem],
         out_specs=[vmem] * 2,
         compiler_params=params(),
         name="final",
-    )(packed, moving, first, near, row, new_slot, keep, *received)
+    )(gram, extra, moving, first, other, new_slot)
+
+
+def settle_kernel(extra, partner, flags, new_slot, near, keep, *refs):
+    received, (new_extra, other) = refs[:-2], refs[-2:]
+    row_count, count = near.shape[:2]
+    start = extra.shape[0] - count
+    new_extra[:start] = extra[:start] + partner[:start]
+    new_extra[start:] = jnp.where(flags[:1] > 0.5, partner[start:], extra[start:])
+    slot = first_slot(row_count)
+    for k in range(row_count):
+        stays = new_slot[slot + k] == slot + k
+        value = jnp.where(stays, near[k], 0.0) + keep[k]
+        for ref in received:
+            value = value + ref[k]
+        other[k] = value
+
+
+def settle(extra, partner, flags, new_slot, near, keep, received):
+    block = pl.BlockSpec(near.shape, lambda s: (0, 0, 0))
+    return pl.pallas_call(
+        settle_kernel,
+        grid=(1,),
+        out_shape=[jax.ShapeDtypeStruct(extra.shape, f32), jax.ShapeDtypeStruct(near.shape, f32)],
+        in_specs=[vmem] * 3 + [smem, vmem] + [block] * (1 + len(received)),
+        out_specs=[vmem] * 2,
+        compiler_params=params(),
+        name="settle",
+    )(extra, partner, flags, new_slot, near, keep, *received)
 
 
 def spread(piece, bulk_count):
-    pieces = [piece] + [swap(piece, "bulk", 2 * z) for z in range(1, bulk_count // 2)]
+    pieces = [piece] + [swap(piece, "bulk", rel) for rel in range(2, bulk_count, 2)]
     return [own for piece in pieces for own in (piece, swap(piece, "bulk", 1))]
+
+
+def share_side(side, edge, part_count):
+    mask = 1
+    while 2 * mask < part_count:
+        other = swap(side, "group", mask)
+        side = jnp.concatenate([side[:edge], other[:edge], side[edge:] + other[edge:]], axis=0)
+        edge *= 2
+        mask *= 2
+    return side, swap(side, "group", mask)
 
 
 def give_back(keep, send, row_count, bulk_count):
@@ -386,44 +458,39 @@
     edge_rows, part_count = coupling.shape[:2]
     bulk_count = lax.axis_size("bulk")
     half = count // 2
-    my_bulk = lax.axis_index("bulk")
-    slot = first_slot(row_count)
-    col = col_index.T
-    own_new = lax.dynamic_slice(new_slot, (slot,), (row_count,))
-    own_slots = slot + jnp.arange(row_count, dtype=jnp.int32)
-    target = jnp.max(jnp.where(own_new != own_slots, own_new, -1))
-    xor_mask = (target // row_count % bulk_count) ^ my_bulk
-
-    panel = spread(rhs.reshape(row_count * count, order), bulk_count)
-    border = [swap(rhs[:edge_rows], "group", mask) for mask in range(1, part_count)]
-    keep, send = returned(rhs, offdiag_blocks, col, load, new_slot, bulk_count, False)
+    edge = edge_rows * count
+    indices = (col_index.T, load, new_slot)
+
+    panel = spread(rhs, bulk_count)
+    border = share_side(rhs.reshape(row_count * count, order)[:edge], edge, part_count)
+    keep, send = returned(rhs, offdiag_blocks, *indices, bulk_count, False)
     received = give_back(keep, send, row_count, bulk_count)
-    near, moving, packed = near_part(
-        panel, rhs, offdiag_blocks, diag_tiles, coupling, border, col, load, new_slot, False
+    near, moving, packed, flags = near_part(
+        panel, rhs, offdiag_blocks, diag_tiles, coupling, border, *indices, False
     )
-    first, flat, edge = gather_first(rhs, near, keep, received, packed, edge_rows)
-
-    panel = spread(flat, bulk_count)
-    border = [swap(edge, "group", mask) for mask in range(1, part_count)]
-    keep, send = returned(first, offdiag_blocks, col, load, new_slot, bulk_count, True)
+    first, side = gather_first(rhs, near, keep, received, packed, edge_rows)
+
+    panel = spread(first, bulk_count)
+    border = share_side(side, edge, part_count)
+    keep, send = returned(first, offdiag_blocks, *indices, bulk_count, True)
     received = give_back(keep, send, row_count, bulk_count)
-    near, first, grams, leaving = near_part(
-        panel, first, offdiag_blocks, diag_tiles, coupling, border, col, load, new_slot, True
+    near, first, extra = near_part(
+        panel, first, offdiag_blocks, diag_tiles, coupling, border, *indices, True
     )
 
-    is_gram = lax.broadcasted_iota(jnp.int32, leaving.shape, 0) < half
-    mask = 1
-    while mask < bulk_count:
-        partner = swap(leaving, "bulk", mask)
-        chosen = jnp.bitwise_and(xor_mask, mask) != 0
-        leaving = jnp.where(is_gram, leaving + partner, jnp.where(chosen, partner, leaving))
-        mask *= 2
-    grams = jnp.concatenate([leaving[:half], grams[half:]], axis=0)
+    partner = swap(extra, "bulk", 1)
+    extra, other = settle(extra, partner, flags, new_slot, near, keep, received)
+    is_gram = lax.broadcasted_iota(jnp.int32, extra.shape, 0) < 4 * half
+    for index in range(1, bulk_count.bit_length() - 1):
+        partner = swap(extra, "bulk", 2**index)
+        chosen = flags[8 * index : 8 * index + 1] > 0.5
+        extra = jnp.where(is_gram, extra + partner, jnp.where(chosen, partner, extra))
+    gram = extra[:half]
     mask = 1
     while mask < part_count:
-        grams = grams + swap(grams, "group", mask)
+        gram = gram + swap(gram, "group", mask)
         mask *= 2
-    return tuple(final(grams, moving, first, near, leaving, new_slot, keep, received))
+    return tuple(final(gram, extra, moving, first, other, new_slot))
 
 
 def solution(mesh):

time: 132 us -> 103 us (0.78)
  Pallas kernels: 42.9 us -> 27.6 us
  other arithmetic: 4.92 us -> 1.42 us
  local copies, waits for them, and re-layouts: 3.44 us -> 0.05 us
  starting transfers between devices: 39.6 us -> 36.5 us
  between operations: 3.64 us -> 0.88 us
    pallas_call x1 -> x2, Pallas kernels: 16.3 us -> 9.25 us  [the longest x1 8.66 us: final(): pl.pallas_call(final_kernel, out_shape=[jax.ShapeDtypeStruct(other.shape,...]
    pallas_call x2, Pallas kernels: 14.8 us -> 10.6 us  [near_part(): pl.pallas_call(functools.partial(near_kernel, bulk_count, second), grid=(...]
    unnamed x64 -> x16, local copies, waits for them, and re-layouts: 3.43 us -> 0.03 us
    ppermute x33 -> x31, starting transfers between devices: 39.6 us -> 36.5 us  [swap(): return lax.ppermute(value, axis, pairs)]
    pallas_call x2, Pallas kernels: 9.23 us -> 7.21 us  [returned(): pl.pallas_call(functools.partial(returned_kernel, bulk_count, moved), gri...]
    pallas_call x1, Pallas kernels: 2.56 us -> 0.55 us  [gather_first(): pl.pallas_call(gather_first_kernel, grid=(1,), out_shape=[jax.ShapeDtypeS...]
    add x2, other arithmetic: 2.53 us -> 1.18 us  [give_back(): received.append(swap(keep[rows] + from_core[rows], 'bulk', 2 * z))]
    ppermute x33 -> x31, waiting for transfers between devices: 37.3 us -> 36 us  [swap(): return lax.ppermute(value, axis, pairs)]
  transfers between devices with their start and end apart: 33 -> 31, of which waited for: 10 -> 12; matrix products, arithmetic and copies ran while one was open for 3% -> 1% of each run, Pallas kernels for 9% -> 10%
where the time goes in v4:
time: 103 us; the launch traced here: 102 us
  starting transfers between devices  36.5 us (35%)
  waiting for transfers between devices  36 us (35%)
  Pallas kernels  27.6 us (27%)
  other arithmetic  1.42 us (1%)
    ppermute x31, starting transfers between devices, swap(): return lax.ppermute(value, axis, pairs)  36.5 us
    ppermute x31, waiting for transfers between devices, swap(): return lax.ppermute(value, axis, pairs)  36 us
    pallas_call x2, Pallas kernels, near_part(): pl.pallas_call(functools.partial(near_kernel, bulk_count, second), grid=(...  10.6 us
    pallas_call x1, Pallas kernels, final(): pl.pallas_call(final_kernel, out_shape=[jax.ShapeDtypeStruct(other.shape,...  8.66 us
    pallas_call x2, Pallas kernels, returned(): pl.pallas_call(functools.partial(returned_kernel, bulk_count, moved), gri...  7.21 us
  transfers between devices with their start and end apart: 31, of which 12 were waited for; matrix products, arithmetic and copies ran while one was open for 1% of the time, Pallas kernels for 10%

profile of v4, /device:TPU:0, one launch (start us, length us, event | category | flops | bytes accessed | tf_op | source)
XLA Modules:
  0.0 102.4 jit_solution(16020332768128361645)
XLA Ops:
  0.7 4.8 %returned.1 = (f32[16,64,128]{2,1,0:T(8,128)}, f32[16,64,128]{2,1,0:T(8,128)}) custom-call(f32[4,64,128]{2,1,0:T(8,128)} %vectors.3, f32[4,11,128,128]{3,2,1,0:T(8,128)} %tiles.3, s32[11,128]{1,0:T(8,128)} %bitcast.6, s32[128]{0:T(128)} %load.3, s32[128]{0:T(128)} %new_slot.7), custom_call_target="tpu_custom_call" | custom-call | tf_op jit(solution)/shard_map/returned/pallas_call | solution.py:116
  5.5 0.5 collective-permute-start.9
  5.9 2.6 %collective-permute-start.7 = (f32[128,128]{1,0:T(8,128)S(1)}, f32[128,128]{1,0:T(8,128)S(1)}, u32[]{:S(2)}, u32[]{:S(2)}) collective-permute-start(f32[128,128]{1,0:T(8,128)S(1)} %bitcast.10), channel_id=1, source_target_pairs={{0,8},{8,0},{16,24},{24,16},{1,9},{9,1},{17,25},{25,17},{2,10},{10... | collective-permute-start | bytes 196616 | tf_op jit(solution)/shard_map/ppermute | solution.py:28
  8.5 1.6 %collective-permute-start.1 = (f32[4,64,128]{2,1,0:T(8,128)S(1)}, f32[4,64,128]{2,1,0:T(8,128)S(1)}, u32[]{:S(2)}, u32[]{:S(2)}) collective-permute-start(f32[4,64,128]{2,1,0:T(8,128)S(1)} %copy-done.1), channel_id=1, source_target_pairs={{0,2},{1,3},{2,0},{3,1},{4,6},{5,7},{6,4},{7,5},{8,10},{9,11},{10,... | collective-permute-start | bytes 393224 | tf_op jit(solution)/shard_map/ppermute | solution.py:28
  10.1 2.6 %collective-permute-start.3 = (f32[4,64,128]{2,1,0:T(8,128)S(1)}, f32[4,64,128]{2,1,0:T(8,128)S(1)}, u32[]{:S(2)}, u32[]{:S(2)}) collective-permute-start(f32[4,64,128]{2,1,0:T(8,128)S(1)} %copy-done.1), channel_id=1, source_target_pairs={{0,4},{1,5},{2,6},{3,7},{4,0},{5,1},{6,2},{7,3},{8,12},{9,13},{10,... | collective-permute-start | bytes 393224 | tf_op jit(solution)/shard_map/ppermute | solution.py:28
  12.7 0.2 collective-permute-start.5
  12.9 3.2 %collective-permute-done.1.refs_2_ = f32[4,64,128]{2,1,0:T(8,128)S(1)} collective-permute-done((f32[4,64,128]{2,1,0:T(8,128)S(1)}, f32[4,64,128]{2,1,0:T(8,128)S(1)}, u32[]{:S(2)}, u32[]{:S(2)}) %collective-permute-start.1) | collective-permute-done | bytes 131104 | tf_op jit(solution)/shard_map/ppermute | solution.py:28
  16.2 1.5 %collective-permute-start.8 = (f32[256,128]{1,0:T(8,128)S(1)}, f32[256,128]{1,0:T(8,128)S(1)}, u32[]{:S(2)}, u32[]{:S(2)}) collective-permute-start(f32[256,128]{1,0:T(8,128)S(1)} %pad_maximum_fusion.1.refs_12_), channel_id=1, source_target_pairs={{0,16},{8,24},{16,0},{24,8},{1,17},{9,25},{17,1},{25,9},{2,18},{10... | collective-permute-start | bytes 393224 | tf_op jit(solution)/shard_map/ppermute | solution.py:28
  17.7 5.3 %collective-permute-done.3.refs_4_ = f32[4,64,128]{2,1,0:T(8,128)S(1)} collective-permute-done((f32[4,64,128]{2,1,0:T(8,128)S(1)}, f32[4,64,128]{2,1,0:T(8,128)S(1)}, u32[]{:S(2)}, u32[]{:S(2)}) %collective-permute-start.3) | collective-permute-done | bytes 131104 | tf_op jit(solution)/shard_map/ppermute | solution.py:28
  23.0 0.5 collective-permute-start.4
  23.5 0.1 collective-permute-start.6
  23.6 1.1 %slice_add_fusion.3 = (f32[4,64,128]{2,1,0:T(8,128)S(1)}, f32[4,64,128]{2,1,0:T(8,128)S(1)}, f32[4,64,128]{2,1,0:T(8,128)S(1)}) fusion(f32[16,64,128]{2,1,0:T(8,128)S(1)} %collective-permute-done.9.refs_0_, f32[16,64,128]{2,1,0:T(8,128)} %get-tuple-element.18.keep), kind=kLoop, calls=%fused_computation.4 | loop fusion | flops 98304 | bytes 1179648 | tf_op jit(solution)/shard_map/add | solution.py:452
  24.7 2.4 %collective-permute-start.10 = (f32[4,64,128]{2,1,0:T(8,128)S(1)}, f32[4,64,128]{2,1,0:T(8,128)S(1)}, u32[]{:S(2)}, u32[]{:S(2)}) collective-permute-start(f32[4,64,128]{2,1,0:T(8,128)S(1)} %get-tuple-element.37), channel_id=1, source_target_pairs={{0,2},{1,3},{2,0},{3,1},{4,6},{5,7},{6,4},{7,5},{8,10},{9,11},{10,... | collective-permute-start | bytes 393224 | tf_op jit(solution)/shard_map/ppermute | solution.py:28
  27.1 1.1 %collective-permute-start.11 = (f32[4,64,128]{2,1,0:T(8,128)S(1)}, f32[4,64,128]{2,1,0:T(8,128)S(1)}, u32[]{:S(2)}, u32[]{:S(2)}) collective-permute-start(f32[4,64,128]{2,1,0:T(8,128)S(1)} %get-tuple-element.36), channel_id=1, source_target_pairs={{0,4},{1,5},{2,6},{3,7},{4,0},{5,1},{6,2},{7,3},{8,12},{9,13},{10,... | collective-permute-start | bytes 393224 | tf_op jit(solution)/shard_map/ppermute | solution.py:28
  28.2 1.4 %collective-permute-start.12 = (f32[4,64,128]{2,1,0:T(8,128)S(1)}, f32[4,64,128]{2,1,0:T(8,128)S(1)}, u32[]{:S(2)}, u32[]{:S(2)}) collective-permute-start(f32[4,64,128]{2,1,0:T(8,128)S(1)} %get-tuple-element.35), channel_id=1, source_target_pairs={{0,6},{1,7},{2,4},{3,5},{4,2},{5,3},{6,0},{7,1},{8,14},{9,15},{10,... | collective-permute-start | bytes 393224 | tf_op jit(solution)/shard_map/ppermute | solution.py:28
  29.7 4.7 %near_first.1 = (f32[4,64,128]{2,1,0:T(8,128)S(1)}, f32[4,64,128]{2,1,0:T(8,128)S(1)}, f32[32,128]{1,0:T(8,128)S(1)}, f32[24,128]{1,0:T(8,128)S(1)}) custom-call(f32[4,64,128]{2,1,0:T(8,128)S(1)} %copy-done.1, f32[4,64,128]{2,1,0:T(8,128)S(1)} %collective-permute-done.refs_1_, f32[4,64,128]{2,1,0:T(8,128)S(1)} %collective-permute-done.1.refs_2_, ...), custom_call_target="tpu_custom_call" | custom-call | tf_op jit(solution)/shard_map/near_first/pallas_call | solution.py:232
  34.4 5.6 %collective-permute-done.11.refs_2_ = f32[4,64,128]{2,1,0:T(8,128)S(1)} collective-permute-done((f32[4,64,128]{2,1,0:T(8,128)S(1)}, f32[4,64,128]{2,1,0:T(8,128)S(1)}, u32[]{:S(2)}, u32[]{:S(2)}) %collective-permute-start.11) | collective-permute-done | bytes 131104 | tf_op jit(solution)/shard_map/ppermute | solution.py:28
  40.0 0.5 gather_first.1
  40.6 2.4 %returned_moved.1 = (f32[16,64,128]{2,1,0:T(8,128)S(1)}, f32[16,64,128]{2,1,0:T(8,128)S(1)}) custom-call(f32[4,64,128]{2,1,0:T(8,128)S(1)} %get-tuple-element.21.refs_0_.refs_8_.vectors, f32[4,11,128,128]{3,2,1,0:T(8,128)S(1)} %copy-done, s32[11,128]{1,0:T(8,128)S(1)} %bitcast.8, s32[128]{0:T(128)S(1)} %copy-done.7, s32[128]{0:T(128)S(1)} %copy-done.6), custom_call_target="tpu_custom_call" | custom-call | tf_op jit(solution)/shard_map/returned_moved/pallas_call | solution.py:116
  43.0 0.1 collective-permute-start.23
  43.1 0.6 collective-permute-start.20
  43.7 0.2 collective-permute-start.13
  43.9 2.1 %collective-permute-start.14 = (f32[4,64,128]{2,1,0:T(8,128)S(1)}, f32[4,64,128]{2,1,0:T(8,128)S(1)}, u32[]{:S(2)}, u32[]{:S(2)}) collective-permute-start(f32[4,64,128]{2,1,0:T(8,128)S(1)} %get-tuple-element.21.refs_0_.refs_8_.vectors), channel_id=1, source_target_pairs={{0,2},{1,3},{2,0},{3,1},{4,6},{5,7},{6,4},{7,5},{8,10},{9,11},{10,... | collective-permute-start | bytes 393224 | tf_op jit(solution)/shard_map/ppermute | solution.py:28
  46.0 1.0 collective-permute-start.16
  47.0 1.7 %collective-permute-done.20 = f32[224,128]{1,0:T(8,128)S(1)} collective-permute-done((f32[224,128]{1,0:T(8,128)S(1)}, f32[224,128]{1,0:T(8,128)S(1)}, u32[]{:S(2)}, u32[]{:S(2)}) %collective-permute-start.20) | collective-permute-done | bytes 114720 | tf_op jit(solution)/shard_map/ppermute | solution.py:28
  48.7 2.1 %collective-permute-start.18 = (f32[4,64,128]{2,1,0:T(8,128)S(1)}, f32[4,64,128]{2,1,0:T(8,128)S(1)}, u32[]{:S(2)}, u32[]{:S(2)}) collective-permute-start(f32[4,64,128]{2,1,0:T(8,128)S(1)} %get-tuple-element.21.refs_0_.refs_8_.vectors), channel_id=1, source_target_pairs={{0,6},{1,7},{2,4},{3,5},{4,2},{5,3},{6,0},{7,1},{8,14},{9,15},{10,... | collective-permute-start | bytes 393224 | tf_op jit(solution)/shard_map/ppermute | solution.py:28
  50.8 1.6 %collective-permute-done.14.refs_2_ = f32[4,64,128]{2,1,0:T(8,128)S(1)} collective-permute-done((f32[4,64,128]{2,1,0:T(8,128)S(1)}, f32[4,64,128]{2,1,0:T(8,128)S(1)}, u32[]{:S(2)}, u32[]{:S(2)}) %collective-permute-start.14) | collective-permute-done | bytes 131104 | tf_op jit(solution)/shard_map/ppermute | solution.py:28
  52.4 1.5 %collective-permute-start.21 = (f32[352,128]{1,0:T(8,128)S(1)}, f32[352,128]{1,0:T(8,128)S(1)}, u32[]{:S(2)}, u32[]{:S(2)}) collective-permute-start(f32[352,128]{1,0:T(8,128)S(1)} %pad_maximum_fusion.refs_12_), channel_id=1, source_target_pairs={{0,16},{8,24},{16,0},{24,8},{1,17},{9,25},{17,1},{25,9},{2,18},{10... | collective-permute-start | bytes 540680 | tf_op jit(solution)/shard_map/ppermute | solution.py:28
  53.9 4.4 %collective-permute-done.16.refs_4_ = f32[4,64,128]{2,1,0:T(8,128)S(1)} collective-permute-done((f32[4,64,128]{2,1,0:T(8,128)S(1)}, f32[4,64,128]{2,1,0:T(8,128)S(1)}, u32[]{:S(2)}, u32[]{:S(2)}) %collective-permute-start.16) | collective-permute-done | bytes 131104 | tf_op jit(solution)/shard_map/ppermute | solution.py:28
  58.3 0.5 collective-permute-start.17
  59.0 3.1 %collective-permute-start.24 = (f32[4,64,128]{2,1,0:T(8,128)S(1)}, f32[4,64,128]{2,1,0:T(8,128)S(1)}, u32[]{:S(2)}, u32[]{:S(2)}) collective-permute-start(f32[4,64,128]{2,1,0:T(8,128)S(1)} %get-tuple-element.34), channel_id=1, source_target_pairs={{0,2},{1,3},{2,0},{3,1},{4,6},{5,7},{6,4},{7,5},{8,10},{9,11},{10,... | collective-permute-start | bytes 393224 | tf_op jit(solution)/shard_map/ppermute | solution.py:28
  62.0 1.0 %collective-permute-start.25 = (f32[4,64,128]{2,1,0:T(8,128)S(1)}, f32[4,64,128]{2,1,0:T(8,128)S(1)}, u32[]{:S(2)}, u32[]{:S(2)}) collective-permute-start(f32[4,64,128]{2,1,0:T(8,128)S(1)} %get-tuple-element.33), channel_id=1, source_target_pairs={{0,4},{1,5},{2,6},{3,7},{4,0},{5,1},{6,2},{7,3},{8,12},{9,13},{10,... | collective-permute-start | bytes 393224 | tf_op jit(solution)/shard_map/ppermute | solution.py:28
  63.1 1.4 %collective-permute-start.26 = (f32[4,64,128]{2,1,0:T(8,128)S(1)}, f32[4,64,128]{2,1,0:T(8,128)S(1)}, u32[]{:S(2)}, u32[]{:S(2)}) collective-permute-start(f32[4,64,128]{2,1,0:T(8,128)S(1)} %get-tuple-element.32), channel_id=1, source_target_pairs={{0,6},{1,7},{2,4},{3,5},{4,2},{5,3},{6,0},{7,1},{8,14},{9,15},{10,... | collective-permute-start | bytes 393224 | tf_op jit(solution)/shard_map/ppermute | solution.py:28
  64.5 5.9 %near_second.1 = (f32[4,64,128]{2,1,0:T(8,128)S(1)}, f32[4,64,128]{2,1,0:T(8,128)S(1)}, f32[192,128]{1,0:T(8,128)S(1)}) custom-call(f32[4,64,128]{2,1,0:T(8,128)S(1)} %get-tuple-element.21.refs_0_.refs_8_.vectors, f32[4,64,128]{2,1,0:T(8,128)S(1)} %collective-permute-done.13.refs_1_, f32[4,64,128]{2,1,0:T(8,128)S(1)} %collective-permute-done.14.refs_2_, ...), custom_call_target="tpu_custom_call" | custom-call | tf_op jit(solution)/shard_map/near_second/pallas_call | solution.py:232
  70.5 1.3 %collective-permute-done.22.partner = f32[192,128]{1,0:T(8,128)S(1)} collective-permute-done((f32[192,128]{1,0:T(8,128)S(1)}, f32[192,128]{1,0:T(8,128)S(1)}, u32[]{:S(2)}, u32[]{:S(2)}) %collective-permute-start.22) | collective-permute-done | bytes 98336 | tf_op jit(solution)/shard_map/ppermute | solution.py:28
  71.8 3.2 %collective-permute-done.25.refs_2_ = f32[4,64,128]{2,1,0:T(8,128)S(1)} collective-permute-done((f32[4,64,128]{2,1,0:T(8,128)S(1)}, f32[4,64,128]{2,1,0:T(8,128)S(1)}, u32[]{:S(2)}, u32[]{:S(2)}) %collective-permute-start.25) | collective-permute-done | bytes 131104 | tf_op jit(solution)/shard_map/ppermute | solution.py:28
  75.0 0.6 settle.1
  75.6 2.2 %collective-permute-start.27 = (f32[192,128]{1,0:T(8,128)S(1)}, f32[192,128]{1,0:T(8,128)S(1)}, u32[]{:S(2)}, u32[]{:S(2)}) collective-permute-start(f32[192,128]{1,0:T(8,128)S(1)} %get-tuple-element.28), channel_id=1, source_target_pairs={{0,2},{1,3},{2,0},{3,1},{4,6},{5,7},{6,4},{7,5},{8,10},{9,11},{10,... | collective-permute-start | bytes 294920 | tf_op jit(solution)/shard_map/ppermute | solution.py:28
  77.8 2.6 %collective-permute-done.27 = f32[192,128]{1,0:T(8,128)S(1)} collective-permute-done((f32[192,128]{1,0:T(8,128)S(1)}, f32[192,128]{1,0:T(8,128)S(1)}, u32[]{:S(2)}, u32[]{:S(2)}) %collective-permute-start.27) | collective-permute-done | bytes 98336 | tf_op jit(solution)/shard_map/ppermute | solution.py:28
  80.4 0.1 select_select_fusion.1
  80.5 3.0 %collective-permute-start.28 = (f32[192,128]{1,0:T(8,128)S(1)}, f32[192,128]{1,0:T(8,128)S(1)}, u32[]{:S(2)}, u32[]{:S(2)}) collective-permute-start(f32[192,128]{1,0:T(8,128)S(1)} %select_select_fusion.1), channel_id=1, source_target_pairs={{0,4},{1,5},{2,6},{3,7},{4,0},{5,1},{6,2},{7,3},{8,12},{9,13},{10,... | collective-permute-start | bytes 294920 | tf_op jit(solution)/shard_map/ppermute | solution.py:28
  83.5 2.6 %collective-permute-done.28 = f32[192,128]{1,0:T(8,128)S(1)} collective-permute-done((f32[192,128]{1,0:T(8,128)S(1)}, f32[192,128]{1,0:T(8,128)S(1)}, u32[]{:S(2)}, u32[]{:S(2)}) %collective-permute-start.28) | collective-permute-done | bytes 98336 | tf_op jit(solution)/shard_map/ppermute | solution.py:28
  86.1 0.1 select_select_fusion.extra
  86.2 1.6 %collective-permute-start.29 = (f32[32,128]{1,0:T(8,128)S(1)}, f32[32,128]{1,0:T(8,128)S(1)}, u32[]{:S(2)}, u32[]{:S(2)}) collective-permute-start(f32[32,128]{1,0:T(8,128)S(1)} %slice.92), channel_id=1, source_target_pairs={{0,8},{8,0},{16,24},{24,16},{1,9},{9,1},{17,25},{25,17},{2,10},{10... | collective-permute-start | bytes 49160 | tf_op jit(solution)/shard_map/ppermute | solution.py:28
  87.7 2.2 %collective-permute-done.29 = f32[32,128]{1,0:T(8,128)S(1)} collective-permute-done((f32[32,128]{1,0:T(8,128)S(1)}, f32[32,128]{1,0:T(8,128)S(1)}, u32[]{:S(2)}, u32[]{:S(2)}) %collective-permute-start.29) | collective-permute-done | bytes 16416 | tf_op jit(solution)/shard_map/ppermute | solution.py:28
  90.0 1.5 %collective-permute-start.30 = (f32[32,128]{1,0:T(8,128)S(1)}, f32[32,128]{1,0:T(8,128)S(1)}, u32[]{:S(2)}, u32[]{:S(2)}) collective-permute-start(f32[32,128]{1,0:T(8,128)S(1)} %slice_add_fusion.7), channel_id=1, source_target_pairs={{0,16},{8,24},{16,0},{24,8},{1,17},{9,25},{17,1},{25,9},{2,18},{10... | collective-permute-start | bytes 49160 | tf_op jit(solution)/shard_map/ppermute | solution.py:28
  91.5 2.2 %collective-permute-done.30 = f32[32,128]{1,0:T(8,128)S(1)} collective-permute-done((f32[32,128]{1,0:T(8,128)S(1)}, f32[32,128]{1,0:T(8,128)S(1)}, u32[]{:S(2)}, u32[]{:S(2)}) %collective-permute-start.30) | collective-permute-done | bytes 16416 | tf_op jit(solution)/shard_map/ppermute | solution.py:28
  93.7 8.7 %final.1 = (f32[4,64,128]{2,1,0:T(8,128)}, f32[4,64,128]{2,1,0:T(8,128)}) custom-call(f32[32,128]{1,0:T(8,128)S(1)} %add.43.gram, f32[192,128]{1,0:T(8,128)S(1)} %select_select_fusion.extra, f32[4,64,128]{2,1,0:T(8,128)S(1)} %get-tuple-element.29.moving, f32[4,64,128]{2,1,0:T(8,128)S(1)} %get-tuple-element.30.first, ...), custom_call_target="tpu_custom_call" | custom-call | tf_op jit(solution)/shard_map/final/pallas_call | solution.py:394
  (52 shorter events, 0.3 us)
Async XLA Ops:
  0.6 5.3 %copy-start.1 = (f32[4,64,128]{2,1,0:T(8,128)S(1)}, f32[4,64,128]{2,1,0:T(8,128)}, u32[]{:S(2)}) copy-start(f32[4,64,128]{2,1,0:T(8,128)} %vectors.3) | copy-start | bytes 393220
  0.6 29.0 %copy-start = (f32[4,11,128,128]{3,2,1,0:T(8,128)S(1)}, f32[4,11,128,128]{3,2,1,0:T(8,128)}, u32[]{:S(2)}) copy-start(f32[4,11,128,128]{3,2,1,0:T(8,128)} %tiles.3) | copy-start | bytes 8650756
  0.7 29.0 %copy-start.5 = (s32[128,11]{0,1:T(8,128)S(1)}, s32[128,11]{0,1:T(8,128)}, u32[]{:S(2)}) copy-start(s32[128,11]{0,1:T(8,128)} %param.11) | copy-start | bytes 16900
  0.7 29.0 %copy-start.7 = (s32[128]{0:T(128)S(1)}, s32[128]{0:T(128)}, u32[]{:S(2)}) copy-start(s32[128]{0:T(128)} %load.3) | copy-start | bytes 1540
  0.7 29.0 %copy-start.6 = (s32[128]{0:T(128)S(1)}, s32[128]{0:T(128)}, u32[]{:S(2)}) copy-start(s32[128]{0:T(128)} %new_slot.7) | copy-start | bytes 1540
  0.7 29.0 %copy-start.4 = (f32[4,128,128]{2,1,0:T(8,128)S(1)}, f32[4,128,128]{2,1,0:T(8,128)}, u32[]{:S(2)}) copy-start(f32[4,128,128]{2,1,0:T(8,128)} %refs_10_.3) | copy-start | bytes 786436
  0.7 29.0 %copy-start.2 = (f32[2,4,128,128]{3,2,1,0:T(8,128)S(1)}, f32[2,4,128,128]{3,2,1,0:T(8,128)}, u32[]{:S(2)}) copy-start(f32[2,4,128,128]{3,2,1,0:T(8,128)} %refs_11_.3) | copy-start | bytes 1572868
  5.5 18.0 %collective-permute-start.9 = (f32[16,64,128]{2,1,0:T(8,128)}, f32[16,64,128]{2,1,0:T(8,128)S(1)}, u32[]{:S(2)}, u32[]{:S(2)}) collective-permute-start(f32[16,64,128]{2,1,0:T(8,128)} %get-tuple-element.19), channel_id=1, source_target_pairs={{0,1},{1,0},{2,3},{3,2},{4,5},{5,4},{6,7},{7,6},{8,9},{9,8},{10,11... | collective-permute-start | bytes 1572872 | tf_op jit(solution)/shard_map/ppermute | solution.py:28
  5.9 7.0 %collective-permute-start.7 = (f32[128,128]{1,0:T(8,128)S(1)}, f32[128,128]{1,0:T(8,128)S(1)}, u32[]{:S(2)}, u32[]{:S(2)}) collective-permute-start(f32[128,128]{1,0:T(8,128)S(1)} %bitcast.10), channel_id=1, source_target_pairs={{0,8},{8,0},{16,24},{24,16},{1,9},{9,1},{17,25},{25,17},{2,10},{10... | collective-permute-start | bytes 196616 | tf_op jit(solution)/shard_map/ppermute | solution.py:28
  8.5 7.7 %collective-permute-start.1 = (f32[4,64,128]{2,1,0:T(8,128)S(1)}, f32[4,64,128]{2,1,0:T(8,128)S(1)}, u32[]{:S(2)}, u32[]{:S(2)}) collective-permute-start(f32[4,64,128]{2,1,0:T(8,128)S(1)} %copy-done.1), channel_id=1, source_target_pairs={{0,2},{1,3},{2,0},{3,1},{4,6},{5,7},{6,4},{7,5},{8,10},{9,11},{10,... | collective-permute-start | bytes 393224 | tf_op jit(solution)/shard_map/ppermute | solution.py:28
  10.1 12.9 %collective-permute-start.3 = (f32[4,64,128]{2,1,0:T(8,128)S(1)}, f32[4,64,128]{2,1,0:T(8,128)S(1)}, u32[]{:S(2)}, u32[]{:S(2)}) collective-permute-start(f32[4,64,128]{2,1,0:T(8,128)S(1)} %copy-done.1), channel_id=1, source_target_pairs={{0,4},{1,5},{2,6},{3,7},{4,0},{5,1},{6,2},{7,3},{8,12},{9,13},{10,... | collective-permute-start | bytes 393224 | tf_op jit(solution)/shard_map/ppermute | solution.py:28
  12.7 10.3 %collective-permute-start.5 = (f32[4,64,128]{2,1,0:T(8,128)S(1)}, f32[4,64,128]{2,1,0:T(8,128)S(1)}, u32[]{:S(2)}, u32[]{:S(2)}) collective-permute-start(f32[4,64,128]{2,1,0:T(8,128)S(1)} %copy-done.1), channel_id=1, source_target_pairs={{0,6},{1,7},{2,4},{3,5},{4,2},{5,3},{6,0},{7,1},{8,14},{9,15},{10,... | collective-permute-start | bytes 393224 | tf_op jit(solution)/shard_map/ppermute | solution.py:28
  12.9 11.8 %collective-permute-start = (f32[4,64,128]{2,1,0:T(8,128)S(1)}, f32[4,64,128]{2,1,0:T(8,128)S(1)}, u32[]{:S(2)}, u32[]{:S(2)}) collective-permute-start(f32[4,64,128]{2,1,0:T(8,128)S(1)} %copy-done.1), channel_id=1, source_target_pairs={{0,1},{1,0},{2,3},{3,2},{4,5},{5,4},{6,7},{7,6},{8,9},{9,8},{10,11... | collective-permute-start | bytes 393224 | tf_op jit(solution)/shard_map/ppermute | solution.py:28
  16.2 10.9 %collective-permute-start.8 = (f32[256,128]{1,0:T(8,128)S(1)}, f32[256,128]{1,0:T(8,128)S(1)}, u32[]{:S(2)}, u32[]{:S(2)}) collective-permute-start(f32[256,128]{1,0:T(8,128)S(1)} %pad_maximum_fusion.1.refs_12_), channel_id=1, source_target_pairs={{0,16},{8,24},{16,0},{24,8},{1,17},{9,25},{17,1},{25,9},{2,18},{10... | collective-permute-start | bytes 393224 | tf_op jit(solution)/shard_map/ppermute | solution.py:28
  23.0 5.2 %collective-permute-start.2 = (f32[4,64,128]{2,1,0:T(8,128)S(1)}, f32[4,64,128]{2,1,0:T(8,128)S(1)}, u32[]{:S(2)}, u32[]{:S(2)}) collective-permute-start(f32[4,64,128]{2,1,0:T(8,128)S(1)} %collective-permute-done.1.refs_2_), channel_id=1, source_target_pairs={{0,1},{1,0},{2,3},{3,2},{4,5},{5,4},{6,7},{7,6},{8,9},{9,8},{10,11... | collective-permute-start | bytes 393224 | tf_op jit(solution)/shard_map/ppermute | solution.py:28
  23.0 6.7 %collective-permute-start.4 = (f32[4,64,128]{2,1,0:T(8,128)S(1)}, f32[4,64,128]{2,1,0:T(8,128)S(1)}, u32[]{:S(2)}, u32[]{:S(2)}) collective-permute-start(f32[4,64,128]{2,1,0:T(8,128)S(1)} %collective-permute-done.3.refs_4_), channel_id=1, source_target_pairs={{0,1},{1,0},{2,3},{3,2},{4,5},{5,4},{6,7},{7,6},{8,9},{9,8},{10,11... | collective-permute-start | bytes 393224 | tf_op jit(solution)/shard_map/ppermute | solution.py:28
  23.5 6.2 %collective-permute-start.6 = (f32[4,64,128]{2,1,0:T(8,128)S(1)}, f32[4,64,128]{2,1,0:T(8,128)S(1)}, u32[]{:S(2)}, u32[]{:S(2)}) collective-permute-start(f32[4,64,128]{2,1,0:T(8,128)S(1)} %collective-permute-done.5.refs_6_), channel_id=1, source_target_pairs={{0,1},{1,0},{2,3},{3,2},{4,5},{5,4},{6,7},{7,6},{8,9},{9,8},{10,11... | collective-permute-start | bytes 393224 | tf_op jit(solution)/shard_map/ppermute | solution.py:28
  23.6 16.5 %copy-start.3 = (f32[16,64,128]{2,1,0:T(8,128)S(1)}, f32[16,64,128]{2,1,0:T(8,128)}, u32[]{:S(2)}) copy-start(f32[16,64,128]{2,1,0:T(8,128)} %get-tuple-element.18.keep) | copy-start | bytes 1572868
  24.7 9.7 %collective-permute-start.10 = (f32[4,64,128]{2,1,0:T(8,128)S(1)}, f32[4,64,128]{2,1,0:T(8,128)S(1)}, u32[]{:S(2)}, u32[]{:S(2)}) collective-permute-start(f32[4,64,128]{2,1,0:T(8,128)S(1)} %get-tuple-element.37), channel_id=1, source_target_pairs={{0,2},{1,3},{2,0},{3,1},{4,6},{5,7},{6,4},{7,5},{8,10},{9,11},{10,... | collective-permute-start | bytes 393224 | tf_op jit(solution)/shard_map/ppermute | solution.py:28
  27.1 12.9 %collective-permute-start.11 = (f32[4,64,128]{2,1,0:T(8,128)S(1)}, f32[4,64,128]{2,1,0:T(8,128)S(1)}, u32[]{:S(2)}, u32[]{:S(2)}) collective-permute-start(f32[4,64,128]{2,1,0:T(8,128)S(1)} %get-tuple-element.36), channel_id=1, source_target_pairs={{0,4},{1,5},{2,6},{3,7},{4,0},{5,1},{6,2},{7,3},{8,12},{9,13},{10,... | collective-permute-start | bytes 393224 | tf_op jit(solution)/shard_map/ppermute | solution.py:28
  28.2 11.8 %collective-permute-start.12 = (f32[4,64,128]{2,1,0:T(8,128)S(1)}, f32[4,64,128]{2,1,0:T(8,128)S(1)}, u32[]{:S(2)}, u32[]{:S(2)}) collective-permute-start(f32[4,64,128]{2,1,0:T(8,128)S(1)} %get-tuple-element.35), channel_id=1, source_target_pairs={{0,6},{1,7},{2,4},{3,5},{4,2},{5,3},{6,0},{7,1},{8,14},{9,15},{10,... | collective-permute-start | bytes 393224 | tf_op jit(solution)/shard_map/ppermute | solution.py:28
  43.0 15.8 %collective-permute-start.23 = (f32[16,64,128]{2,1,0:T(8,128)S(1)}, f32[16,64,128]{2,1,0:T(8,128)S(1)}, u32[]{:S(2)}, u32[]{:S(2)}) collective-permute-start(f32[16,64,128]{2,1,0:T(8,128)S(1)} %get-tuple-element.27), channel_id=1, source_target_pairs={{0,1},{1,0},{2,3},{3,2},{4,5},{5,4},{6,7},{7,6},{8,9},{9,8},{10,11... | collective-permute-start | bytes 1572872 | tf_op jit(solution)/shard_map/ppermute | solution.py:28
  43.1 5.6 %collective-permute-start.20 = (f32[224,128]{1,0:T(8,128)S(1)}, f32[224,128]{1,0:T(8,128)S(1)}, u32[]{:S(2)}, u32[]{:S(2)}) collective-permute-start(f32[224,128]{1,0:T(8,128)S(1)} %get-tuple-element.22), channel_id=1, source_target_pairs={{0,8},{8,0},{16,24},{24,16},{1,9},{9,1},{17,25},{25,17},{2,10},{10... | collective-permute-start | bytes 344072 | tf_op jit(solution)/shard_map/ppermute | solution.py:28
  43.7 15.3 %collective-permute-start.13 = (f32[4,64,128]{2,1,0:T(8,128)S(1)}, f32[4,64,128]{2,1,0:T(8,128)S(1)}, u32[]{:S(2)}, u32[]{:S(2)}) collective-permute-start(f32[4,64,128]{2,1,0:T(8,128)S(1)} %get-tuple-element.21.refs_0_.refs_8_.vectors), channel_id=1, source_target_pairs={{0,1},{1,0},{2,3},{3,2},{4,5},{5,4},{6,7},{7,6},{8,9},{9,8},{10,11... | collective-permute-start | bytes 393224 | tf_op jit(solution)/shard_map/ppermute | solution.py:28
  43.9 8.5 %collective-permute-start.14 = (f32[4,64,128]{2,1,0:T(8,128)S(1)}, f32[4,64,128]{2,1,0:T(8,128)S(1)}, u32[]{:S(2)}, u32[]{:S(2)}) collective-permute-start(f32[4,64,128]{2,1,0:T(8,128)S(1)} %get-tuple-element.21.refs_0_.refs_8_.vectors), channel_id=1, source_target_pairs={{0,2},{1,3},{2,0},{3,1},{4,6},{5,7},{6,4},{7,5},{8,10},{9,11},{10,... | collective-permute-start | bytes 393224 | tf_op jit(solution)/shard_map/ppermute | solution.py:28
  46.0 12.3 %collective-permute-start.16 = (f32[4,64,128]{2,1,0:T(8,128)S(1)}, f32[4,64,128]{2,1,0:T(8,128)S(1)}, u32[]{:S(2)}, u32[]{:S(2)}) collective-permute-start(f32[4,64,128]{2,1,0:T(8,128)S(1)} %get-tuple-element.21.refs_0_.refs_8_.vectors), channel_id=1, source_target_pairs={{0,4},{1,5},{2,6},{3,7},{4,0},{5,1},{6,2},{7,3},{8,12},{9,13},{10,... | collective-permute-start | bytes 393224 | tf_op jit(solution)/shard_map/ppermute | solution.py:28
  48.7 9.7 %collective-permute-start.18 = (f32[4,64,128]{2,1,0:T(8,128)S(1)}, f32[4,64,128]{2,1,0:T(8,128)S(1)}, u32[]{:S(2)}, u32[]{:S(2)}) collective-permute-start(f32[4,64,128]{2,1,0:T(8,128)S(1)} %get-tuple-element.21.refs_0_.refs_8_.vectors), channel_id=1, source_target_pairs={{0,6},{1,7},{2,4},{3,5},{4,2},{5,3},{6,0},{7,1},{8,14},{9,15},{10,... | collective-permute-start | bytes 393224 | tf_op jit(solution)/shard_map/ppermute | solution.py:28
  52.4 12.2 %collective-permute-start.21 = (f32[352,128]{1,0:T(8,128)S(1)}, f32[352,128]{1,0:T(8,128)S(1)}, u32[]{:S(2)}, u32[]{:S(2)}) collective-permute-start(f32[352,128]{1,0:T(8,128)S(1)} %pad_maximum_fusion.refs_12_), channel_id=1, source_target_pairs={{0,16},{8,24},{16,0},{24,8},{1,17},{9,25},{17,1},{25,9},{2,18},{10... | collective-permute-start | bytes 540680 | tf_op jit(solution)/shard_map/ppermute | solution.py:28
  58.3 3.7 %collective-permute-start.15 = (f32[4,64,128]{2,1,0:T(8,128)S(1)}, f32[4,64,128]{2,1,0:T(8,128)S(1)}, u32[]{:S(2)}, u32[]{:S(2)}) collective-permute-start(f32[4,64,128]{2,1,0:T(8,128)S(1)} %collective-permute-done.14.refs_2_), channel_id=1, source_target_pairs={{0,1},{1,0},{2,3},{3,2},{4,5},{5,4},{6,7},{7,6},{8,9},{9,8},{10,11... | collective-permute-start | bytes 393224 | tf_op jit(solution)/shard_map/ppermute | solution.py:28
  58.3 4.7 %collective-permute-start.17 = (f32[4,64,128]{2,1,0:T(8,128)S(1)}, f32[4,64,128]{2,1,0:T(8,128)S(1)}, u32[]{:S(2)}, u32[]{:S(2)}) collective-permute-start(f32[4,64,128]{2,1,0:T(8,128)S(1)} %collective-permute-done.16.refs_4_), channel_id=1, source_target_pairs={{0,1},{1,0},{2,3},{3,2},{4,5},{5,4},{6,7},{7,6},{8,9},{9,8},{10,11... | collective-permute-start | bytes 393224 | tf_op jit(solution)/shard_map/ppermute | solution.py:28
  58.9 5.7 %collective-permute-start.19 = (f32[4,64,128]{2,1,0:T(8,128)S(1)}, f32[4,64,128]{2,1,0:T(8,128)S(1)}, u32[]{:S(2)}, u32[]{:S(2)}) collective-permute-start(f32[4,64,128]{2,1,0:T(8,128)S(1)} %collective-permute-done.18.refs_6_), channel_id=1, source_target_pairs={{0,1},{1,0},{2,3},{3,2},{4,5},{5,4},{6,7},{7,6},{8,9},{9,8},{10,11... | collective-permute-start | bytes 393224 | tf_op jit(solution)/shard_map/ppermute | solution.py:28
  59.0 12.8 %collective-permute-start.24 = (f32[4,64,128]{2,1,0:T(8,128)S(1)}, f32[4,64,128]{2,1,0:T(8,128)S(1)}, u32[]{:S(2)}, u32[]{:S(2)}) collective-permute-start(f32[4,64,128]{2,1,0:T(8,128)S(1)} %get-tuple-element.34), channel_id=1, source_target_pairs={{0,2},{1,3},{2,0},{3,1},{4,6},{5,7},{6,4},{7,5},{8,10},{9,11},{10,... | collective-permute-start | bytes 393224 | tf_op jit(solution)/shard_map/ppermute | solution.py:28
  62.0 12.9 %collective-permute-start.25 = (f32[4,64,128]{2,1,0:T(8,128)S(1)}, f32[4,64,128]{2,1,0:T(8,128)S(1)}, u32[]{:S(2)}, u32[]{:S(2)}) collective-permute-start(f32[4,64,128]{2,1,0:T(8,128)S(1)} %get-tuple-element.33), channel_id=1, source_target_pairs={{0,4},{1,5},{2,6},{3,7},{4,0},{5,1},{6,2},{7,3},{8,12},{9,13},{10,... | collective-permute-start | bytes 393224 | tf_op jit(solution)/shard_map/ppermute | solution.py:28
  63.1 11.9 %collective-permute-start.26 = (f32[4,64,128]{2,1,0:T(8,128)S(1)}, f32[4,64,128]{2,1,0:T(8,128)S(1)}, u32[]{:S(2)}, u32[]{:S(2)}) collective-permute-start(f32[4,64,128]{2,1,0:T(8,128)S(1)} %get-tuple-element.32), channel_id=1, source_target_pairs={{0,6},{1,7},{2,4},{3,5},{4,2},{5,3},{6,0},{7,1},{8,14},{9,15},{10,... | collective-permute-start | bytes 393224 | tf_op jit(solution)/shard_map/ppermute | solution.py:28
  70.4 1.3 %collective-permute-start.22 = (f32[192,128]{1,0:T(8,128)S(1)}, f32[192,128]{1,0:T(8,128)S(1)}, u32[]{:S(2)}, u32[]{:S(2)}) collective-permute-start(f32[192,128]{1,0:T(8,128)S(1)} %get-tuple-element.23.extra), channel_id=1, source_target_pairs={{0,1},{1,0},{2,3},{3,2},{4,5},{5,4},{6,7},{7,6},{8,9},{9,8},{10,11... | collective-permute-start | bytes 294920 | tf_op jit(solution)/shard_map/ppermute | solution.py:28
  75.6 4.8 %collective-permute-start.27 = (f32[192,128]{1,0:T(8,128)S(1)}, f32[192,128]{1,0:T(8,128)S(1)}, u32[]{:S(2)}, u32[]{:S(2)}) collective-permute-start(f32[192,128]{1,0:T(8,128)S(1)} %get-tuple-element.28), channel_id=1, source_target_pairs={{0,2},{1,3},{2,0},{3,1},{4,6},{5,7},{6,4},{7,5},{8,10},{9,11},{10,... | collective-permute-start | bytes 294920 | tf_op jit(solution)/shard_map/ppermute | solution.py:28
  80.5 5.6 %collective-permute-start.28 = (f32[192,128]{1,0:T(8,128)S(1)}, f32[192,128]{1,0:T(8,128)S(1)}, u32[]{:S(2)}, u32[]{:S(2)}) collective-permute-start(f32[192,128]{1,0:T(8,128)S(1)} %select_select_fusion.1), channel_id=1, source_target_pairs={{0,4},{1,5},{2,6},{3,7},{4,0},{5,1},{6,2},{7,3},{8,12},{9,13},{10,... | collective-permute-start | bytes 294920 | tf_op jit(solution)/shard_map/ppermute | solution.py:28
  86.2 3.8 %collective-permute-start.29 = (f32[32,128]{1,0:T(8,128)S(1)}, f32[32,128]{1,0:T(8,128)S(1)}, u32[]{:S(2)}, u32[]{:S(2)}) collective-permute-start(f32[32,128]{1,0:T(8,128)S(1)} %slice.92), channel_id=1, source_target_pairs={{0,8},{8,0},{16,24},{24,16},{1,9},{9,1},{17,25},{25,17},{2,10},{10... | collective-permute-start | bytes 49160 | tf_op jit(solution)/shard_map/ppermute | solution.py:28
  90.0 3.7 %collective-permute-start.30 = (f32[32,128]{1,0:T(8,128)S(1)}, f32[32,128]{1,0:T(8,128)S(1)}, u32[]{:S(2)}, u32[]{:S(2)}) collective-permute-start(f32[32,128]{1,0:T(8,128)S(1)} %slice_add_fusion.7), channel_id=1, source_target_pairs={{0,16},{8,24},{16,0},{24,8},{1,17},{9,25},{17,1},{25,9},{2,18},{10... | collective-permute-start | bytes 49160 | tf_op jit(solution)/shard_map/ppermute | solution.py:28

commit v5 on v4

v5 whole, which is shorter than its diff:
```python
import functools

import jax
import jax.numpy as jnp
from jax import lax
from jax.experimental import pallas as pl
from jax.experimental.pallas import tpu as pltpu
from jax.sharding import PartitionSpec as P

shift = 4.0
f32 = jnp.float32
bf16 = jnp.bfloat16
normal = (((1,), (0,)), ((), ()))
right_t = (((1,), (1,)), ((), ()))
left_t = (((0,), (0,)), ((), ()))
vmem = pl.BlockSpec(memory_space=pltpu.VMEM)
smem = pl.BlockSpec(memory_space=pltpu.SMEM)
anywhere = pl.BlockSpec(memory_space=pl.ANY)
vmem_bytes = 40 * 2**20
all_vmem = 60 * 2**20


def params(limit=vmem_bytes):
    return pltpu.CompilerParams(vmem_limit_bytes=limit)


def swap(value, axis, mask):
    pairs = [(source, source ^ mask) for source in range(lax.axis_size(axis))]
    return lax.ppermute(value, axis, pairs)


def split(value):
    high = value.astype(bf16)
    return high, (value - high.astype(f32)).astype(bf16)


def dot16(left, right, dims):
    return lax.dot_general(left, right, dims, preferred_element_type=f32)


def dot32(left, right, dims=normal):
    return lax.dot_general(
        left, right, dims, preferred_element_type=f32, precision=lax.Precision.HIGHEST
    )


def split_rows(vectors):
    high, low = split(vectors)
    return jnp.concatenate([high, low], axis=0)


def times_tile(rows, tile, dims):
    count = rows.shape[0] // 2
    high, low = split(tile)
    both = dot16(rows, high, dims)
    return both[:count] + both[count:] + dot16(rows[:count], low, dims)


def pack(gram):
    half = gram.shape[0] // 2
    return jnp.concatenate([gram[:half], gram[half:]], axis=1)


def unpack(packed):
    half = packed.shape[1] // 2
    return jnp.concatenate([packed[:, :half], packed[:, half:]], axis=0)


def above(count):
    rows = lax.broadcasted_iota(jnp.int32, (count, count), 0)
    cols = lax.broadcasted_iota(jnp.int32, (count, count), 1)
    return cols > rows, cols == rows


def identity(count):
    return above(count)[1].astype(f32)


def join_symmetric(upper, lower):
    over, diagonal = above(upper.shape[0])
    row = jnp.sum(jnp.where(diagonal, upper, 0.0), axis=0, keepdims=True)
    return jnp.where(over, upper, lower), row


def part_symmetric(joined, row):
    over, diagonal = above(joined.shape[0])
    turned = joined.T
    upper = jnp.where(diagonal, row, jnp.where(over, joined, turned))
    return upper, jnp.where(over, turned, joined)


def sym(gram):
    return 0.5 * (gram + gram.T)


def first_slot(row_count):
    device = lax.axis_index("group") * lax.axis_size("bulk") + lax.axis_index("bulk")
    return device * row_count


def live(load_ref, slot, tile):
    return jnp.where(tile < load_ref[slot], 1.0, 0.0)


def far_masks(bulk_count):
    masks = []
    bit = bulk_count // 2
    while bit >= 4:
        masks += [bit | bit // 2, bit // 2]
        bit //= 4
    return masks + ([bit] if bit == 2 else [])


def owed_place(rel, bulk_count):
    place = 0
    index = 0
    bit = bulk_count.bit_length() - 2
    while bit >= 2:
        high = (rel >> bit) & 1
        low = (rel >> (bit - 1)) & 1
        place = place | (high << index) | ((high ^ low) << (index + 1))
        index += 2
        bit -= 2
    if bit == 1:
        place = place | (((rel >> 1) & 1) << index)
        index += 1
    return place | ((rel & 1) << index)


def returned_kernel(bulk_count, moved, vectors, tiles, col, load, new_slot, *refs):
    keep, send, total = refs[-3:]
    row_count = vectors.shape[0]
    me = lax.axis_index("bulk")
    base = lax.axis_index("group") * bulk_count * row_count
    s = pl.program_id(0)
    slot = first_slot(row_count) + s

    @pl.when(s == 0)
    def _():
        total[...] = jnp.zeros_like(total)

    rows = split_rows(vectors[s])
    for t in range(tiles.shape[1]):
        product = times_tile(rows, tiles[0, t], normal)
        target = col[t, slot]
        if moved:
            target = new_slot[target]
        target = target - base
        owner = target // row_count
        place = owed_place(owner ^ me, bulk_count) * row_count + target - owner * row_count
        total[place] += live(load, slot, t) * product

    @pl.when(s == row_count - 1)
    def _():
        half = total.shape[0] // 2
        keep[...] = total[:half]
        send[...] = total[half:]


def returned(vectors, tiles, col, load, new_slot, bulk_count, moved, *earlier):
    row_count, count, order = vectors.shape
    tile_count = tiles.shape[1]
    half = (bulk_count * row_count // 2, count, order)
    return pl.pallas_call(
        functools.partial(returned_kernel, bulk_count, moved),
        grid=(row_count,),
        out_shape=[jax.ShapeDtypeStruct(half, f32)] * 2,
        in_specs=[
            vmem,
            pl.BlockSpec((1, tile_count, order, order), lambda s: (s, 0, 0, 0)),
            smem,
            smem,
            smem,
        ]
        + [anywhere] * len(earlier),
        out_specs=[vmem] * 2,
        scratch_shapes=[pltpu.VMEM((2 * half[0], count, order), f32)],
        compiler_params=params(vmem_bytes if moved else all_vmem),
        name="returned_moved" if moved else "returned",
    )(vectors, tiles, col, load, new_slot, *earlier)


def near_kernel(bulk_count, pieces, second, *refs):
    panel, refs = refs[:pieces], refs[pieces:]
    vectors, tiles, diag, col, load, new_slot, near, moving, packed, *more, rows_of, gram = refs
    row_count, count = vectors.shape[:2]
    me = lax.axis_index("bulk")
    mine = lax.axis_index("group")
    base = mine * bulk_count * row_count
    s = pl.program_id(0)
    slot = first_slot(row_count) + s
    half_rows = bulk_count * row_count // 2
    held = [piece.shape[0] // count for piece in panel]
    starts = [sum(held[:index]) for index in range(pieces)]

    def place_of(target):
        target = target - base
        owner = target // row_count
        rel = owner ^ me
        return (rel & 1) * half_rows + (rel >> 1) * row_count + target - owner * row_count

    @pl.when(s == 0)
    def _():
        for piece, first, rows in zip(panel, starts, held):
            for k in range(rows):
                rows_of[first + k] = split_rows(piece[k * count : (k + 1) * count])
        gram[...] = jnp.zeros_like(gram)

    direct = None
    for t in range(tiles.shape[1]):
        rows = rows_of[place_of(col[t, slot])]
        high, low = split(tiles[0, t])
        alive = live(load, slot, t)
        both = alive * dot16(rows, high, right_t)
        rest = alive * dot16(rows[:count], low, right_t)
        direct = (both, rest) if direct is None else (direct[0] + both, direct[1] + rest)
    direct = direct[0][:count] + direct[0][count:] + direct[1]
    value = vectors[s]
    near_value = times_tile(split_rows(value), diag[0], right_t)
    near[s] = near_value + direct
    if second:
        gram[...] += dot32(value, near_value + 2.0 * direct, right_t)
    else:
        gram[...] += dot32(value, value, right_t)

    arriving = new_slot[slot]
    incoming = place_of(arriving)
    for piece, first, rows in zip(panel, starts, held):

        @pl.when((incoming >= first) & (incoming < first + rows))
        def _(piece=piece, first=first):
            start = pl.multiple_of((incoming - first) * count, count)
            moving[s] = piece[pl.ds(start, count)]

    if not second:
        (flags,) = more

        @pl.when(arriving != slot)
        def _():
            route = owed_place(((arriving - base) // row_count) ^ me, bulk_count)
            steps = flags.shape[0] // 8
            for index in range(steps):
                bit = ((route >> (steps - 1 - index)) & 1).astype(f32)
                flags[8 * index : 8 * index + 8] = jnp.full((8, flags.shape[1]), bit, f32)

    @pl.when(s == row_count - 1)
    def _():
        packed[...] = pack(gram[...])


def near_part(panel, vectors, tiles, diag, col, load, new_slot, second):
    row_count, count, order = vectors.shape
    bulk_count = sum(piece.shape[0] for piece in panel) // (row_count * count)
    tile_count = tiles.shape[1]
    shapes = [vectors.shape, vectors.shape, (count // 2, order)]
    if not second:
        shapes += [(8 * (bulk_count.bit_length() - 1), order)]
    return pl.pallas_call(
        functools.partial(near_kernel, bulk_count, len(panel), second),
        grid=(row_count,),
        out_shape=[jax.ShapeDtypeStruct(shape, f32) for shape in shapes],
        in_specs=[vmem] * len(panel)
        + [
            vmem,
            pl.BlockSpec((1, tile_count, order, order), lambda s: (s, 0, 0, 0)),
            pl.BlockSpec((1, order, order), lambda s: (s, 0, 0)),
            smem,
            smem,
            smem,
        ],
        out_specs=[vmem] * len(shapes),
        scratch_shapes=[
            pltpu.VMEM((bulk_count * row_count, 2 * count, order), bf16),
            pltpu.VMEM((count, count), f32),
        ],
        compiler_params=params(),
        name="near_second" if second else "near_first",
    )(*panel, vectors, tiles, diag, col, load, new_slot)


def crossed(side, coupling, k):
    edge_rows, part_count = coupling.shape[:2]
    count = side.shape[1] // 2
    mine = lax.axis_index("group")
    total = None
    for h in range(part_count):
        start = (h * edge_rows + k) * count
        rows = split_rows(side[start : start + count])
        term = times_tile(rows, coupling[k, mine ^ h], right_t)
        total = term if total is None else total + term
    return total


def gather_first_kernel(vectors, near, keep, *refs):
    received = refs[:-5]
    coupling, old_side, packed, first, side = refs[-5:]
    row_count, count = vectors.shape[:2]
    half = count // 2
    edge_rows = (side.shape[0] - 2 * half - 8) // count
    grams = [None, None]
    for k in range(row_count):
        value = near[k] + keep[k]
        for ref in received:
            value = value + ref[k]
        if k < edge_rows:
            value = value + crossed(old_side, coupling, k)
        first[k] = value
        if k < edge_rows:
            side[k * count : (k + 1) * count] = value
        terms = (dot32(vectors[k], value, right_t), dot32(value, value, right_t))
        grams = [term if old is None else old + term for old, term in zip(grams, terms)]
    start = edge_rows * count
    joined, row = join_symmetric(unpack(packed[...]), grams[1])
    side[start : start + half] = pack(joined)
    side[start + half : start + 2 * half] = pack(sym(grams[0]))
    rows = jnp.concatenate([row, jnp.zeros_like(row)], axis=1)
    side[start + 2 * half :] = jnp.broadcast_to(rows, (8, 2 * count))


def gather_first(vectors, near, terms, coupling, old_side, packed):
    row_count, count, order = vectors.shape
    edge_rows = coupling.shape[0]
    shapes = [vectors.shape, (edge_rows * count + count + 8, order)]
    specs = [pl.BlockSpec((row_count, count, order), lambda s: (0, 0, 0))] * (2 + len(terms))
    return pl.pallas_call(
        gather_first_kernel,
        grid=(1,),
        out_shape=[jax.ShapeDtypeStruct(shape, f32) for shape in shapes],
        in_specs=specs + [vmem] * 3,
        out_specs=[vmem] * 2,
        compiler_params=params(),
        name="gather_first",
    )(vectors, near, *terms, coupling, old_side, packed)


def edge_second_kernel(first, near, packed, coupling, side, new_slot, out, extra):
    row_count, count = first.shape[:2]
    edge_rows, part_count = coupling.shape[:2]
    half = count // 2
    gram = unpack(packed[...])
    for k in range(row_count):
        value = near[k]
        if k < edge_rows:
            more = crossed(side, coupling, k)
            gram = gram + dot32(first[k], more, right_t)
            value = value + more
        out[k] = value
    start = part_count * edge_rows * count
    joined, row = join_symmetric(unpack(side[start + half : start + 2 * half]), sym(gram))
    extra[:count] = jnp.concatenate([unpack(side[start : start + half]), joined], axis=1)
    row = jnp.concatenate([jnp.zeros_like(row), row], axis=1)
    extra[count : count + 8] = side[start + 2 * half :] + jnp.broadcast_to(row, (8, 2 * count))
    slot = first_slot(row_count)
    for k in range(row_count):

        @pl.when(new_slot[slot + k] != slot + k)
        def _(k=k):
            extra[count + 8 :] = out[k]


def edge_second(first, near, packed, coupling, side, new_slot):
    count, order = first.shape[1:]
    shapes = [near.shape, (2 * count + 8, order)]
    return pl.pallas_call(
        edge_second_kernel,
        out_shape=[jax.ShapeDtypeStruct(shape, f32) for shape in shapes],
        in_specs=[vmem] * 5 + [smem],
        out_specs=[vmem] * 2,
        compiler_params=params(),
        name="edge_second",
    )(first, near, packed, coupling, side, new_slot)


def spread_row(rows, index):
    return jnp.broadcast_to(rows[index : index + 1], rows.shape)


def inverse_factors(matrices):
    count = matrices[0].shape[0]
    step = 8
    shape = (step, 2 * count)
    eye = identity(count)
    sub = lax.broadcasted_iota(jnp.int32, shape, 0)
    work = []
    for matrix in matrices:
        both = jnp.concatenate([matrix, eye], axis=1)
        work.append([both[i : i + step] for i in range(0, count, step)])
    for block in range(count // step):
        start = block * step
        for w in work:
            cols = [
                [jnp.broadcast_to(rows[:, start + m : start + m + 1], shape) for m in range(step)]
                for rows in w[block:]
            ]
            factor = [[None] * step for _ in range(step)]
            scales, pivots = [], []
            for m in range(step):
                value = spread_row(cols[0][m], m)
                row = spread_row(w[block], m)
                for u in range(m):
                    value = value - factor[m][u] * factor[m][u]
                    row = row - factor[m][u] * pivots[u]
                scales.append(lax.rsqrt(value))
                pivots.append(row * scales[m])
                for v in range(m + 1, step):
                    value = spread_row(cols[0][m], v)
                    for u in range(m):
                        value = value - factor[v][u] * factor[m][u]
                    factor[v][m] = value * scales[m]
            for i in range(block + 1, count // step):
                left = []
                for m in range(step):
                    value = cols[i - block][m]
                    for u in range(m):
                        value = value - left[u] * factor[m][u]
                    left.append(value * scales[m])
                terms = [one * pivot for one, pivot in zip(left, pivots)]
                while len(terms) > 1:
                    terms = [x + y for x, y in zip(terms[::2], terms[1::2])]
                w[i] = w[i] - terms[0]
            rows = pivots[0]
            for m in range(1, step):
                rows = jnp.where(sub == m, pivots[m], rows)
            w[block] = rows
    return [jnp.concatenate(w, axis=0)[:, count:] for w in work]


def solve(inverse_factor, right):
    return dot32(inverse_factor, dot32(inverse_factor, right), left_t)


def grams_of(sums):
    count = sums.shape[1] // 2
    row = sums[count : count + 1]
    g0, g2 = part_symmetric(sums[:count, :count], row[:, :count])
    g1, g3 = part_symmetric(sums[:count, count:], row[:, count:])
    return g0, g1, g2, g3


def first_solves_kernel(extra, out):
    g0, g1, _, _ = grams_of(extra[...])
    factor_pq, factor_rr = inverse_factors([shift * g0 + g1, g0])
    out[0] = solve(factor_pq, g0)
    out[1] = dot32(factor_rr, factor_rr, left_t)


def next_gram_kernel(extra, solved, out):
    g0, g1, g2, _ = grams_of(extra[...])
    a, inverse_rr = solved[0], solved[1]
    count = a.shape[0]
    m = identity(count) - shift * a
    by_a = dot32(jnp.concatenate([g0, g1, g2], axis=0), a)
    g0a, g1a, g2a = (by_a[i * count : (i + 1) * count] for i in range(3))
    g0m, g1m = g0 - shift * g0a, g1 - shift * g1a
    left = jnp.concatenate([m, a], axis=0)
    g_new = sym(dot32(left, jnp.concatenate([g0m - g1a, g2a - g1m], axis=0), left_t))
    c = m + dot32(inverse_rr, g_new)
    by_c = dot32(jnp.concatenate([shift * g0 + g1, shift * g1 + g2], axis=0), c)
    left = jnp.concatenate([c, a], axis=0)
    upper = by_c[:count] - (shift * g1a + g2a)
    lower = shift * g2a - by_c[count:]
    out[0] = c
    out[1] = g_new
    out[2] = dot32(left, jnp.concatenate([upper, lower], axis=0), left_t)


def small_call(kernel, count, matrices, name, *operands):
    return pl.pallas_call(
        kernel,
        out_shape=jax.ShapeDtypeStruct((matrices, count, count), f32),
        in_specs=[vmem] * len(operands),
        out_specs=vmem,
        compiler_params=params(),
        name=name,
    )(*operands)


def final_kernel(gram, solved, following, moving, first, near, new_slot, row, *refs):
    last_row, flags, *terms, solution, resid = refs
    row_count, count = moving.shape[:2]
    arrived = jnp.where(flags[flags.shape[0] - 8 :][:1] > 0.5, last_row[0], row[...])
    a, c, g_new = solved[0], following[0], following[1]
    g3 = sym(unpack(gram[...]))
    g_pq = sym(following[2] + dot32(a, dot32(g3, a), left_t))
    (factor,) = inverse_factors([g_pq])
    a1 = solve(factor, g_new)
    by_a1 = dot32(jnp.concatenate([a, c], axis=0), a1)
    aa1, ca1 = by_a1[:count], by_a1[count:]
    m = identity(count) - shift * a
    top = jnp.concatenate([a + ca1, -aa1, jnp.zeros_like(a)], axis=0)
    low = jnp.concatenate([m - shift * ca1, shift * aa1 - a - ca1, aa1], axis=0)
    coef = jnp.concatenate([top, low], axis=1)
    slot = first_slot(row_count)
    basis = []
    for k in range(row_count):
        stays = new_slot[slot + k] == slot + k
        second = jnp.where(stays, near[k], arrived)
        for ref in terms:
            second = second + ref[k]
        basis.append(jnp.concatenate([moving[k], first[k], second], axis=0))
    order = moving.shape[2]
    both = dot32(coef, jnp.concatenate(basis, axis=1), left_t)
    for k in range(row_count):
        solution[k] = both[:count, k * order : (k + 1) * order]
        resid[k] = both[count:, k * order : (k + 1) * order]


def final(gram, solved, following, moving, first, near, new_slot, row, flags, terms):
    block = pl.BlockSpec(near.shape, lambda s: (0, 0, 0))
    last = pl.BlockSpec((1,) + near.shape[1:], lambda s: (terms[-1].shape[0] - 1, 0, 0))
    return pl.pallas_call(
        final_kernel,
        grid=(1,),
        out_shape=[jax.ShapeDtypeStruct(near.shape, f32)] * 2,
        in_specs=[vmem] * 6 + [smem, vmem, last, vmem] + [block] * len(terms),
        out_specs=[vmem] * 2,
        compiler_params=params(),
        name="final",
    )(gram, solved, following, moving, first, near, new_slot, row, terms[-1], flags, *terms)


def add_kernel(count, *refs):
    total = refs[0][...]
    for ref in refs[1:count]:
        total = total + ref[...]
    refs[-1][...] = total


def add_upper(terms, rows, *earlier):
    shape = (rows,) + terms[0].shape[1:]
    block = pl.BlockSpec(shape, lambda s: (1, 0, 0))
    return pl.pallas_call(
        functools.partial(add_kernel, len(terms)),
        grid=(1,),
        out_shape=jax.ShapeDtypeStruct(shape, f32),
        in_specs=[block] * len(terms) + [anywhere] * len(earlier),
        out_specs=vmem,
        compiler_params=params(),
        name="add_upper",
    )(*terms, *earlier)


def add_with_row_kernel(step, count, row, other, flags, *refs):
    terms, out, held = refs[:count], refs[-2], refs[-1]
    total = terms[0][...]
    for ref in terms[1:]:
        total = total + ref[...]
    out[: total.shape[0]] = total
    value = row[...]
    if step > 1:
        value = jnp.where(flags[8 * step : 8 * step + 1] > 0.5, other[0], value)
    out[total.shape[0]] = value
    held[...] = value


def add_with_row(terms, rows, row, flags, step, *earlier):
    shape = (rows,) + terms[0].shape[1:]
    block = pl.BlockSpec(shape, lambda s: (1, 0, 0))
    last = pl.BlockSpec((1,) + shape[1:], lambda s: (terms[-1].shape[0] - 1, 0, 0))
    return pl.pallas_call(
        functools.partial(add_with_row_kernel, step, len(terms)),
        grid=(1,),
        out_shape=[
            jax.ShapeDtypeStruct((rows + 1,) + shape[1:], f32),
            jax.ShapeDtypeStruct(row.shape, f32),
        ],
        in_specs=[vmem, last, vmem] + [block] * len(terms) + [anywhere] * len(earlier),
        out_specs=[vmem] * 2,
        compiler_params=params(),
        name="add_with_row",
    )(row, terms[-1], flags, *terms, *earlier)


def settle_kernel(index, sums, extra, partner, flags, *refs):
    out = refs[-1]
    out[:sums] = extra[:sums] + partner[:sums]
    if extra.shape[0] > sums:
        chosen = flags[8 * index : 8 * index + 1] > 0.5
        out[sums:] = jnp.where(chosen, partner[sums:], extra[sums:])


def settle(extra, partner, flags, index, sums, *earlier):
    return pl.pallas_call(
        functools.partial(settle_kernel, index, sums),
        out_shape=jax.ShapeDtypeStruct(extra.shape, f32),
        in_specs=[vmem] * 3 + [anywhere] * len(earlier),
        out_specs=vmem,
        compiler_params=params(),
        name="settle",
    )(extra, partner, flags, *earlier)


def leave_row_kernel(sums, extra, partner, flags, out, row):
    out[...] = extra[:sums] + partner[:sums]
    row[...] = jnp.where(flags[8:9] > 0.5, partner[sums:], extra[sums:])


def leave_row(extra, partner, flags, sums):
    order = extra.shape[1]
    return pl.pallas_call(
        functools.partial(leave_row_kernel, sums),
        out_shape=[
            jax.ShapeDtypeStruct((sums, order), f32),
            jax.ShapeDtypeStruct((extra.shape[0] - sums, order), f32),
        ],
        in_specs=[vmem] * 3,
        out_specs=[vmem] * 2,
        compiler_params=params(),
        name="leave_row",
    )(extra, partner, flags)


def last_gram_kernel(sums, partner, out, gram):
    total = sums[...] + partner[...]
    out[...] = total
    gram[...] = pack(grams_of(total)[3])


def last_gram(sums, partner):
    rows, order = sums.shape
    return pl.pallas_call(
        last_gram_kernel,
        out_shape=[
            jax.ShapeDtypeStruct((rows, order), f32),
            jax.ShapeDtypeStruct((order // 4, order), f32),
        ],
        in_specs=[vmem] * 2,
        out_specs=[vmem] * 2,
        compiler_params=params(),
        name="last_gram",
    )(sums, partner)


def add_whole(left, right, *earlier):
    return pl.pallas_call(
        functools.partial(add_kernel, 2),
        out_shape=jax.ShapeDtypeStruct(left.shape, f32),
        in_specs=[vmem] * 2 + [anywhere] * len(earlier),
        out_specs=vmem,
        compiler_params=params(),
        name="add_whole",
    )(left, right, *earlier)


def join_kernel(count, *refs):
    out = refs[-1]
    rows = refs[0].shape[0]
    for index, ref in enumerate(refs[:count]):
        out[index * rows : (index + 1) * rows] = ref[...]


def join(pieces, *earlier):
    rows, order = pieces[0].shape
    return pl.pallas_call(
        functools.partial(join_kernel, len(pieces)),
        out_shape=jax.ShapeDtypeStruct((len(pieces) * rows, order), f32),
        in_specs=[vmem] * len(pieces) + [anywhere] * len(earlier),
        out_specs=vmem,
        compiler_params=params(),
        name="join",
    )(*pieces, *earlier)


def merge_kernel(edge, mine, other, *refs):
    out = refs[-1]
    out[:edge] = mine[:edge]
    out[edge : 2 * edge] = other[:edge]
    if mine.shape[0] > edge:
        out[2 * edge :] = mine[edge:] + other[edge:]


def merge_side(side, other, edge, *earlier):
    return pl.pallas_call(
        functools.partial(merge_kernel, edge),
        out_shape=jax.ShapeDtypeStruct((side.shape[0] + edge, side.shape[1]), f32),
        in_specs=[vmem] * 2 + [anywhere] * len(earlier),
        out_specs=vmem,
        compiler_params=params(),
        name="merge_side",
    )(side, other, *earlier)


def share_side(side, edge, part_count):
    mask = 1
    while 2 * mask < part_count:
        side = merge_side(side, swap(side, "group", mask), mask * edge)
        mask *= 2
    return side, swap(side, "group", mask)


def share_panel(piece, bulk_count, *earlier):
    own = [piece] + [swap(piece, "bulk", rel) for rel in range(2, bulk_count, 2)]
    middle = len(own) // 2
    joined = [join(own[:middle]), join(own[middle:], *earlier)]
    return own + [swap(one, "bulk", 1) for one in joined], joined[-1]


def local(rhs, diag_tiles, offdiag_blocks, coupling, col_index, load, new_slot):
    row_count, count, order = rhs.shape
    edge_rows, part_count = coupling.shape[:2]
    bulk_count = lax.axis_size("bulk")
    steps = bulk_count.bit_length() - 1
    masks = far_masks(bulk_count)[::-1]
    edge = edge_rows * count
    half_edges = part_count // 2 * edge
    indices = (col_index.T, load, new_slot)

    flat = rhs.reshape(row_count * count, order)
    side, other_side = share_side(flat[:edge], edge, part_count)
    keep, send = returned(rhs, offdiag_blocks, *indices, bulk_count, False)
    panel, joined = share_panel(flat, bulk_count, side)
    terms = [keep, swap(send, "bulk", 1)]
    rows = bulk_count // 2 * row_count
    for step, mask in enumerate(masks):
        rows //= 2
        total = add_upper(terms, rows, *([joined] if step else []))
        terms.append(swap(total, "bulk", mask))
    near, moving, packed, flags = near_part(
        panel, rhs, offdiag_blocks, diag_tiles, *indices, False
    )
    side = merge_side(side, other_side, half_edges, near)
    first, side = gather_first(rhs, near, terms, coupling, side, packed)

    side, other_side = share_side(side, edge, part_count)
    keep, send = returned(first, offdiag_blocks, *indices, bulk_count, True)
    panel, joined = share_panel(
        first.reshape(row_count * count, order), bulk_count, side, keep
    )
    terms = [keep, swap(send, "bulk", 1)]
    rows = bulk_count // 4 * row_count
    terms.append(swap(add_upper(terms, rows, joined), "bulk", masks[0]))
    near, moved, packed = near_part(panel, first, offdiag_blocks, diag_tiles, *indices, True)
    side = merge_side(side, other_side, half_edges, near)
    near, extra = edge_second(first, near, packed, coupling, side, new_slot)

    sums = count + 8
    extra = settle(extra, swap(extra, "bulk", 1), flags, 0, sums, terms[-1])
    extra, row = leave_row(extra, swap(extra, "bulk", masks[0]), flags, sums)
    mask = 4
    while 2 * mask < bulk_count:
        extra = settle(extra, swap(extra, "bulk", mask), flags, 0, sums)
        mask *= 2
    extra, gram = last_gram(extra, swap(extra, "bulk", mask))
    for step in range(1, steps - 1):
        rows //= 2
        total, row = add_with_row(terms, rows, row, flags, step, extra)
        terms.append(swap(total, "bulk", masks[step]))
    solved = small_call(first_solves_kernel, count, 2, "first_solves", extra)
    following = small_call(next_gram_kernel, count, 3, "next_gram", extra, solved)
    mask = 1
    while mask < part_count:
        partner = swap(gram, "group", mask)
        gram = add_whole(gram, partner, *([solved] if mask == 1 else []))
        mask *= 2
    return tuple(
        final(gram, solved, following, moving, moved, near, new_slot, row, flags, terms)
    )


def solution(mesh):
    rows = P(("group", "bulk"))
    return jax.shard_map(
        local,
        mesh=mesh,
        in_specs=(rows, rows, rows, rows, P(), P(), P()),
        out_specs=(rows, rows),
        check_vma=False,
    )
```

time: 103 us -> 88.9 us (0.86)
  starting transfers between devices: 36.5 us -> 28.6 us
  waiting for transfers between devices: 36 us -> 28.8 us
  local copies, waits for them, and re-layouts: 0.05 us -> 2.12 us
  other arithmetic: 1.42 us -> 0 us
    ppermute x31 -> x25, starting transfers between devices: 36.5 us -> 28.6 us  [swap(): return lax.ppermute(value, axis, pairs)]
    ppermute x31 -> x25, waiting for transfers between devices: 36 us -> 28.8 us  [swap(): return lax.ppermute(value, axis, pairs)]
    unnamed x16 -> x20, local copies, waits for them, and re-layouts: 0.03 us -> 2.12 us
    add x5 -> x0, other arithmetic: 1.2 us -> none  [the longest x2 1.18 us: give_back(): received.append(swap(keep[rows] + from_core[rows], 'bulk', 2 * z))]
    pallas_call x4 -> x23, Pallas kernels: 19.8 us -> 20 us  [the longest x2 8.64 us: near_part(): pl.pallas_call(functools.partial(near_kernel, bulk_count, len(panel), sec...]
  transfers between devices with their start and end apart: 31 -> 25, of which waited for: 12 -> 11; matrix products, arithmetic and copies ran while one was open for 1% -> 0% of each run, Pallas kernels for 10% -> 17%
where the time goes in v5:
time: 88.9 us; the launch traced here: 88.6 us
  waiting for transfers between devices  28.8 us (32%)
  starting transfers between devices  28.6 us (32%)
  Pallas kernels  28.2 us (32%)
  local copies, waits for them, and re-layouts  2.12 us (2%)
  between operations  0.92 us (1%)
    ppermute x25, waiting for transfers between devices, swap(): return lax.ppermute(value, axis, pairs)  28.8 us
    ppermute x25, starting transfers between devices, swap(): return lax.ppermute(value, axis, pairs)  28.6 us
    pallas_call x2, Pallas kernels, near_part(): pl.pallas_call(functools.partial(near_kernel, bulk_count, len(panel), sec...  8.64 us
    pallas_call x2, Pallas kernels, returned(): pl.pallas_call(functools.partial(returned_kernel, bulk_count, moved), gri...  7.05 us
    pallas_call x1, Pallas kernels, final(): pl.pallas_call(final_kernel, grid=(1,), out_shape=[jax.ShapeDtypeStruct(n...  4.81 us
    pallas_call x2, Pallas kernels, small_call(): pl.pallas_call(kernel, out_shape=jax.ShapeDtypeStruct((matrices, count, c...  4.32 us
    unnamed x20, local copies, waits for them, and re-layouts  2.12 us
  transfers between devices with their start and end apart: 25, of which 11 were waited for; matrix products, arithmetic and copies ran while one was open for 0% of the time, Pallas kernels for 17%

profile of v5, /device:TPU:0, one launch (start us, length us, event | category | flops | bytes accessed | tf_op | source)
XLA Modules:
  0.0 88.6 jit_solution(8170327581666981977)
XLA Ops:
  0.7 4.7 %returned.1 = (f32[16,64,128]{2,1,0:T(8,128)}, f32[16,64,128]{2,1,0:T(8,128)}) custom-call(f32[4,64,128]{2,1,0:T(8,128)} %vectors.3, f32[4,11,128,128]{3,2,1,0:T(8,128)} %refs_7_.3, s32[11,128]{1,0:T(8,128)} %bitcast.16, s32[128]{0:T(128)} %refs_10_.3, s32[128]{0:T(128)} %new_slot.7), custom_call_target="tpu_custom_call" | custom-call | tf_op jit(solution)/shard_map/returned/pallas_call | solution.py:164
  5.4 0.5 collective-permute-start.6
  5.8 3.7 %collective-permute-start.1 = (f32[256,128]{1,0:T(8,128)S(1)}, f32[256,128]{1,0:T(8,128)S(1)}, u32[]{:S(2)}, u32[]{:S(2)}) collective-permute-start(f32[256,128]{1,0:T(8,128)S(1)} %bitcast.4), channel_id=1, source_target_pairs={{0,4},{1,5},{2,6},{3,7},{4,0},{5,1},{6,2},{7,3},{8,12},{9,13},{10,... | collective-permute-start | bytes 393224 | tf_op jit(solution)/shard_map/ppermute | solution.py:29
  9.5 1.3 %collective-permute-start.2 = (f32[256,128]{1,0:T(8,128)S(1)}, f32[256,128]{1,0:T(8,128)S(1)}, u32[]{:S(2)}, u32[]{:S(2)}) collective-permute-start(f32[256,128]{1,0:T(8,128)S(1)} %bitcast.5), channel_id=1, source_target_pairs={{0,6},{1,7},{2,4},{3,5},{4,2},{5,3},{6,0},{7,1},{8,14},{9,15},{10,... | collective-permute-start | bytes 393224 | tf_op jit(solution)/shard_map/ppermute | solution.py:29
  10.8 0.2 collective-permute-start
  11.1 1.0 %copy-done.1 = f32[16,64,128]{2,1,0:T(8,128)S(1)} copy-done((f32[16,64,128]{2,1,0:T(8,128)S(1)}, f32[16,64,128]{2,1,0:T(8,128)}, u32[]{:S(2)}) %copy-start.1) | copy-done | bytes 524312
  12.1 1.9 %collective-permute-start.7 = (f32[8,64,128]{2,1,0:T(8,128)S(1)}, f32[8,64,128]{2,1,0:T(8,128)S(1)}, u32[]{:S(2)}, u32[]{:S(2)}) collective-permute-start(f32[8,64,128]{2,1,0:T(8,128)S(1)} %add_upper.3), channel_id=1, source_target_pairs={{0,2},{1,3},{2,0},{3,1},{4,6},{5,7},{6,4},{7,5},{8,10},{9,11},{10,... | collective-permute-start | bytes 786440 | tf_op jit(solution)/shard_map/ppermute | solution.py:29
  14.0 1.5 %collective-permute-start.4 = (f32[128,128]{1,0:T(8,128)S(1)}, f32[128,128]{1,0:T(8,128)S(1)}, u32[]{:S(2)}, u32[]{:S(2)}) collective-permute-start(f32[128,128]{1,0:T(8,128)S(1)} %bitcast.14), channel_id=1, source_target_pairs={{0,8},{8,0},{16,24},{24,16},{1,9},{9,1},{17,25},{25,17},{2,10},{10... | collective-permute-start | bytes 196616 | tf_op jit(solution)/shard_map/ppermute | solution.py:29
  15.5 2.8 %collective-permute-done.4.other = f32[128,128]{1,0:T(8,128)S(1)} collective-permute-done((f32[128,128]{1,0:T(8,128)S(1)}, f32[128,128]{1,0:T(8,128)S(1)}, u32[]{:S(2)}, u32[]{:S(2)}) %collective-permute-start.4) | collective-permute-done | bytes 65568 | tf_op jit(solution)/shard_map/ppermute | solution.py:29
  18.3 1.2 %collective-permute-done.1.refs_0_.refs_2_ = f32[256,128]{1,0:T(8,128)S(1)} collective-permute-done((f32[256,128]{1,0:T(8,128)S(1)}, f32[256,128]{1,0:T(8,128)S(1)}, u32[]{:S(2)}, u32[]{:S(2)}) %collective-permute-start.1) | collective-permute-done | bytes 131104 | tf_op jit(solution)/shard_map/ppermute | solution.py:29
  19.5 0.1 collective-permute-start.5
  19.6 2.0 %collective-permute-done.refs_1_ = f32[256,128]{1,0:T(8,128)S(1)} collective-permute-done((f32[256,128]{1,0:T(8,128)S(1)}, f32[256,128]{1,0:T(8,128)S(1)}, u32[]{:S(2)}, u32[]{:S(2)}) %collective-permute-start) | collective-permute-done | bytes 131104 | tf_op jit(solution)/shard_map/ppermute | solution.py:29
  21.6 0.1 collective-permute-start.3
  21.7 1.6 %collective-permute-start.9 = (f32[256,128]{1,0:T(8,128)S(1)}, f32[256,128]{1,0:T(8,128)S(1)}, u32[]{:S(2)}, u32[]{:S(2)}) collective-permute-start(f32[256,128]{1,0:T(8,128)S(1)} %merge_side.4.refs_2_.mine), channel_id=1, source_target_pairs={{0,16},{8,24},{16,0},{24,8},{1,17},{9,25},{17,1},{25,9},{2,18},{10... | collective-permute-start | bytes 393224 | tf_op jit(solution)/shard_map/ppermute | solution.py:29
  23.4 2.8 %collective-permute-done.7.refs_2_.refs_1_ = f32[8,64,128]{2,1,0:T(8,128)S(1)} collective-permute-done((f32[8,64,128]{2,1,0:T(8,128)S(1)}, f32[8,64,128]{2,1,0:T(8,128)S(1)}, u32[]{:S(2)}, u32[]{:S(2)}) %collective-permute-start.7) | collective-permute-done | bytes 262176 | tf_op jit(solution)/shard_map/ppermute | solution.py:29
  26.2 1.0 %copy-done.2 = f32[16,64,128]{2,1,0:T(8,128)S(1)} copy-done((f32[16,64,128]{2,1,0:T(8,128)S(1)}, f32[16,64,128]{2,1,0:T(8,128)}, u32[]{:S(2)}) %copy-start.2) | copy-done | bytes 524312
  27.3 3.6 %collective-permute-start.8 = (f32[4,64,128]{2,1,0:T(8,128)S(1)}, f32[4,64,128]{2,1,0:T(8,128)S(1)}, u32[]{:S(2)}, u32[]{:S(2)}) collective-permute-start(f32[4,64,128]{2,1,0:T(8,128)S(1)} %add_upper.4), channel_id=1, source_target_pairs={{0,6},{1,7},{2,4},{3,5},{4,2},{5,3},{6,0},{7,1},{8,14},{9,15},{10,... | collective-permute-start | bytes 393224 | tf_op jit(solution)/shard_map/ppermute | solution.py:29
  30.9 4.0 %near_first.1 = (f32[4,64,128]{2,1,0:T(8,128)S(1)}, f32[4,64,128]{2,1,0:T(8,128)S(1)}, f32[32,128]{1,0:T(8,128)S(1)}, f32[24,128]{1,0:T(8,128)S(1)}) custom-call(f32[256,128]{1,0:T(8,128)S(1)} %bitcast.8, f32[256,128]{1,0:T(8,128)S(1)} %collective-permute-done.refs_1_, f32[256,128]{1,0:T(8,128)S(1)} %collective-permute-done.1.refs_0_.refs_2_, ...), custom_call_target="tpu_custom_call" | custom-call | tf_op jit(solution)/shard_map/near_first/pallas_call | solution.py:258
  35.0 1.1 %gather_first.1 = (f32[4,64,128]{2,1,0:T(8,128)S(1)}, f32[200,128]{1,0:T(8,128)S(1)}) custom-call(f32[4,64,128]{2,1,0:T(8,128)S(1)} %copy-done.4, f32[4,64,128]{2,1,0:T(8,128)S(1)} %get-tuple-element.23.refs_0_.near, f32[16,64,128]{2,1,0:T(8,128)S(1)} %copy-done.3, f32[16,64,128]{2,1,0:T(8,128)S(1)} %collective-permute-done.6.refs_1_.refs_0_, ...), custom_call_target="tpu_custom_call" | custom-call | tf_op jit(solution)/shard_map/gather_first/pallas_call | solution.py:325
  36.1 2.4 %returned_moved.1 = (f32[16,64,128]{2,1,0:T(8,128)S(1)}, f32[16,64,128]{2,1,0:T(8,128)S(1)}) custom-call(f32[4,64,128]{2,1,0:T(8,128)S(1)} %get-tuple-element.27.vectors.refs_6_.first, f32[4,11,128,128]{3,2,1,0:T(8,128)S(1)} %copy-done, s32[11,128]{1,0:T(8,128)S(1)} %bitcast.18, s32[128]{0:T(128)S(1)} %copy-done.9, s32[128]{0:T(128)S(1)} %copy-done.8), custom_call_target="tpu_custom_call" | custom-call | tf_op jit(solution)/shard_map/returned_moved/pallas_call | solution.py:164
  38.5 0.1 collective-permute-start.18
  38.6 0.4 collective-permute-start.11
  39.0 2.7 %collective-permute-start.12 = (f32[256,128]{1,0:T(8,128)S(1)}, f32[256,128]{1,0:T(8,128)S(1)}, u32[]{:S(2)}, u32[]{:S(2)}) collective-permute-start(f32[256,128]{1,0:T(8,128)S(1)} %bitcast.10), channel_id=1, source_target_pairs={{0,6},{1,7},{2,4},{3,5},{4,2},{5,3},{6,0},{7,1},{8,14},{9,15},{10,... | collective-permute-start | bytes 393224 | tf_op jit(solution)/shard_map/ppermute | solution.py:29
  41.7 0.5 collective-permute-start.10
  42.2 1.5 %collective-permute-start.14 = (f32[200,128]{1,0:T(8,128)S(1)}, f32[200,128]{1,0:T(8,128)S(1)}, u32[]{:S(2)}, u32[]{:S(2)}) collective-permute-start(f32[200,128]{1,0:T(8,128)S(1)} %get-tuple-element.28.mine), channel_id=1, source_target_pairs={{0,8},{8,0},{16,24},{24,16},{1,9},{9,1},{17,25},{25,17},{2,10},{10... | collective-permute-start | bytes 307208 | tf_op jit(solution)/shard_map/ppermute | solution.py:29
  43.6 3.2 %collective-permute-done.14.other = f32[200,128]{1,0:T(8,128)S(1)} collective-permute-done((f32[200,128]{1,0:T(8,128)S(1)}, f32[200,128]{1,0:T(8,128)S(1)}, u32[]{:S(2)}, u32[]{:S(2)}) %collective-permute-start.14) | collective-permute-done | bytes 102432 | tf_op jit(solution)/shard_map/ppermute | solution.py:29
  46.8 4.5 %collective-permute-done.11.refs_0_.refs_2_ = f32[256,128]{1,0:T(8,128)S(1)} collective-permute-done((f32[256,128]{1,0:T(8,128)S(1)}, f32[256,128]{1,0:T(8,128)S(1)}, u32[]{:S(2)}, u32[]{:S(2)}) %collective-permute-start.11) | collective-permute-done | bytes 131104 | tf_op jit(solution)/shard_map/ppermute | solution.py:29
  51.3 0.1 collective-permute-start.15
  51.4 1.0 %collective-permute-done.10.refs_1_ = f32[256,128]{1,0:T(8,128)S(1)} collective-permute-done((f32[256,128]{1,0:T(8,128)S(1)}, f32[256,128]{1,0:T(8,128)S(1)}, u32[]{:S(2)}, u32[]{:S(2)}) %collective-permute-start.10) | collective-permute-done | bytes 131104 | tf_op jit(solution)/shard_map/ppermute | solution.py:29
  52.4 0.1 collective-permute-start.13
  52.5 2.7 %collective-permute-start.19 = (f32[8,64,128]{2,1,0:T(8,128)S(1)}, f32[8,64,128]{2,1,0:T(8,128)S(1)}, u32[]{:S(2)}, u32[]{:S(2)}) collective-permute-start(f32[8,64,128]{2,1,0:T(8,128)S(1)} %add_upper.5), channel_id=1, source_target_pairs={{0,2},{1,3},{2,0},{3,1},{4,6},{5,7},{6,4},{7,5},{8,10},{9,11},{10,... | collective-permute-start | bytes 786440 | tf_op jit(solution)/shard_map/ppermute | solution.py:29
  55.2 1.5 %collective-permute-start.16 = (f32[328,128]{1,0:T(8,128)S(1)}, f32[328,128]{1,0:T(8,128)S(1)}, u32[]{:S(2)}, u32[]{:S(2)}) collective-permute-start(f32[328,128]{1,0:T(8,128)S(1)} %merge_side.6.refs_2_.mine), channel_id=1, source_target_pairs={{0,16},{8,24},{16,0},{24,8},{1,17},{9,25},{17,1},{25,9},{2,18},{10... | collective-permute-start | bytes 503816 | tf_op jit(solution)/shard_map/ppermute | solution.py:29
  56.8 4.6 %near_second.1 = (f32[4,64,128]{2,1,0:T(8,128)S(1)}, f32[4,64,128]{2,1,0:T(8,128)S(1)}, f32[32,128]{1,0:T(8,128)S(1)}) custom-call(f32[256,128]{1,0:T(8,128)S(1)} %bitcast.13, f32[256,128]{1,0:T(8,128)S(1)} %collective-permute-done.10.refs_1_, f32[256,128]{1,0:T(8,128)S(1)} %collective-permute-done.11.refs_0_.refs_2_, ...), custom_call_target="tpu_custom_call" | custom-call | tf_op jit(solution)/shard_map/near_second/pallas_call | solution.py:258
  61.4 1.7 %edge_second.1 = (f32[4,64,128]{2,1,0:T(8,128)S(1)}, f32[136,128]{1,0:T(8,128)S(1)}) custom-call(f32[4,64,128]{2,1,0:T(8,128)S(1)} %get-tuple-element.27.vectors.refs_6_.first, f32[4,64,128]{2,1,0:T(8,128)S(1)} %get-tuple-element.30.refs_0_.near, f32[32,128]{1,0:T(8,128)S(1)} %get-tuple-element.31.packed, f32[2,4,128,128]{3,2,1,0:T(8,128)S(1)} %copy-done.5, ...), custom_call_target="tpu_custom_call" | custom-call | tf_op jit(solution)/shard_map/edge_second/pallas_call | solution.py:364
  63.2 0.1 collective-permute-start.17
  63.3 1.2 %collective-permute-done.17.partner = f32[136,128]{1,0:T(8,128)S(1)} collective-permute-done((f32[136,128]{1,0:T(8,128)S(1)}, f32[136,128]{1,0:T(8,128)S(1)}, u32[]{:S(2)}, u32[]{:S(2)}) %collective-permute-start.17) | collective-permute-done | bytes 69664 | tf_op jit(solution)/shard_map/ppermute | solution.py:29
  64.5 0.2 collective-permute-start.20
  64.7 4.2 %collective-permute-done.20.partner = f32[136,128]{1,0:T(8,128)S(1)} collective-permute-done((f32[136,128]{1,0:T(8,128)S(1)}, f32[136,128]{1,0:T(8,128)S(1)}, u32[]{:S(2)}, u32[]{:S(2)}) %collective-permute-start.20) | collective-permute-done | bytes 69664 | tf_op jit(solution)/shard_map/ppermute | solution.py:29
  68.9 0.1 collective-permute-start.21
  69.0 4.9 %collective-permute-done.21.partner = f32[72,128]{1,0:T(8,128)S(1)} collective-permute-done((f32[72,128]{1,0:T(8,128)S(1)}, f32[72,128]{1,0:T(8,128)S(1)}, u32[]{:S(2)}, u32[]{:S(2)}) %collective-permute-start.21) | collective-permute-done | bytes 36896 | tf_op jit(solution)/shard_map/ppermute | solution.py:29
  73.9 0.2 last_gram.1
  74.1 1.3 %collective-permute-start.24 = (f32[5,64,128]{2,1,0:T(8,128)S(1)}, f32[5,64,128]{2,1,0:T(8,128)S(1)}, u32[]{:S(2)}, u32[]{:S(2)}) collective-permute-start(f32[5,64,128]{2,1,0:T(8,128)S(1)} %get-tuple-element.43), channel_id=1, source_target_pairs={{0,6},{1,7},{2,4},{3,5},{4,2},{5,3},{6,0},{7,1},{8,14},{9,15},{10,... | collective-permute-start | bytes 491528 | tf_op jit(solution)/shard_map/ppermute | solution.py:29
  75.5 1.5 %collective-permute-start.22 = (f32[32,128]{1,0:T(8,128)S(1)}, f32[32,128]{1,0:T(8,128)S(1)}, u32[]{:S(2)}, u32[]{:S(2)}) collective-permute-start(f32[32,128]{1,0:T(8,128)S(1)} %get-tuple-element.36.refs_0_), channel_id=1, source_target_pairs={{0,8},{8,0},{16,24},{24,16},{1,9},{9,1},{17,25},{25,17},{2,10},{10... | collective-permute-start | bytes 49160 | tf_op jit(solution)/shard_map/ppermute | solution.py:29
  76.9 3.0 %first_solves.1.refs_2_.solved = f32[2,64,64]{2,1,0:T(8,128)S(1)} custom-call(f32[72,128]{1,0:T(8,128)S(1)} %get-tuple-element.37.extra.refs_3_), custom_call_target="tpu_custom_call" | custom-call | tf_op jit(solution)/shard_map/first_solves/pallas_call | solution.py:468
  80.0 1.5 %collective-permute-start.23 = (f32[32,128]{1,0:T(8,128)S(1)}, f32[32,128]{1,0:T(8,128)S(1)}, u32[]{:S(2)}, u32[]{:S(2)}) collective-permute-start(f32[32,128]{1,0:T(8,128)S(1)} %add_whole.2.refs_0_), channel_id=1, source_target_pairs={{0,16},{8,24},{16,0},{24,8},{1,17},{9,25},{17,1},{25,9},{2,18},{10... | collective-permute-start | bytes 49160 | tf_op jit(solution)/shard_map/ppermute | solution.py:29
  81.5 1.3 %next_gram.1.following = f32[3,64,64]{2,1,0:T(8,128)S(1)} custom-call(f32[72,128]{1,0:T(8,128)S(1)} %get-tuple-element.37.extra.refs_3_, f32[2,64,64]{2,1,0:T(8,128)S(1)} %first_solves.1.refs_2_.solved), custom_call_target="tpu_custom_call" | custom-call | tf_op jit(solution)/shard_map/next_gram/pallas_call | solution.py:468
  82.8 1.0 %collective-permute-done.23.refs_1_ = f32[32,128]{1,0:T(8,128)S(1)} collective-permute-done((f32[32,128]{1,0:T(8,128)S(1)}, f32[32,128]{1,0:T(8,128)S(1)}, u32[]{:S(2)}, u32[]{:S(2)}) %collective-permute-start.23) | collective-permute-done | bytes 16416 | tf_op jit(solution)/shard_map/ppermute | solution.py:29
  83.8 4.8 %final.1 = (f32[4,64,128]{2,1,0:T(8,128)}, f32[4,64,128]{2,1,0:T(8,128)}) custom-call(f32[32,128]{1,0:T(8,128)S(1)} %add_whole.3.gram, f32[2,64,64]{2,1,0:T(8,128)S(1)} %first_solves.1.refs_2_.solved, f32[3,64,64]{2,1,0:T(8,128)S(1)} %next_gram.1.following, f32[4,64,128]{2,1,0:T(8,128)S(1)} %get-tuple-element.38.moving, ...), custom_call_target="tpu_custom_call" | custom-call | tf_op jit(solution)/shard_map/final/pallas_call | solution.py:511
  (49 shorter events, 0.4 us)
Async XLA Ops:
  0.6 5.2 %copy-start.4 = (f32[4,64,128]{2,1,0:T(8,128)S(1)}, f32[4,64,128]{2,1,0:T(8,128)}, u32[]{:S(2)}) copy-start(f32[4,64,128]{2,1,0:T(8,128)} %vectors.3) | copy-start | bytes 393220
  0.6 30.3 %copy-start.6 = (f32[4,128,128]{2,1,0:T(8,128)S(1)}, f32[4,128,128]{2,1,0:T(8,128)}, u32[]{:S(2)}) copy-start(f32[4,128,128]{2,1,0:T(8,128)} %refs_8_.3) | copy-start | bytes 786436
  0.7 30.3 %copy-start.7 = (s32[128,11]{0,1:T(8,128)S(1)}, s32[128,11]{0,1:T(8,128)}, u32[]{:S(2)}) copy-start(s32[128,11]{0,1:T(8,128)} %param.11) | copy-start | bytes 16900
  0.7 30.3 %copy-start.8 = (s32[128]{0:T(128)S(1)}, s32[128]{0:T(128)}, u32[]{:S(2)}) copy-start(s32[128]{0:T(128)} %new_slot.7) | copy-start | bytes 1540
  0.7 30.3 %copy-start.9 = (s32[128]{0:T(128)S(1)}, s32[128]{0:T(128)}, u32[]{:S(2)}) copy-start(s32[128]{0:T(128)} %refs_10_.3) | copy-start | bytes 1540
  5.4 25.6 %copy-start = (f32[4,11,128,128]{3,2,1,0:T(8,128)S(1)}, f32[4,11,128,128]{3,2,1,0:T(8,128)}, u32[]{:S(2)}) copy-start(f32[4,11,128,128]{3,2,1,0:T(8,128)} %refs_7_.3) | copy-start | bytes 8650756
  5.4 5.7 %collective-permute-start.6 = (f32[16,64,128]{2,1,0:T(8,128)}, f32[16,64,128]{2,1,0:T(8,128)S(1)}, u32[]{:S(2)}, u32[]{:S(2)}) collective-permute-start(f32[16,64,128]{2,1,0:T(8,128)} %get-tuple-element.25), channel_id=1, source_target_pairs={{0,1},{1,0},{2,3},{3,2},{4,5},{5,4},{6,7},{7,6},{8,9},{9,8},{10,11... | collective-permute-start | bytes 1572872 | tf_op jit(solution)/shard_map/ppermute | solution.py:29
  5.8 13.7 %collective-permute-start.1 = (f32[256,128]{1,0:T(8,128)S(1)}, f32[256,128]{1,0:T(8,128)S(1)}, u32[]{:S(2)}, u32[]{:S(2)}) collective-permute-start(f32[256,128]{1,0:T(8,128)S(1)} %bitcast.4), channel_id=1, source_target_pairs={{0,4},{1,5},{2,6},{3,7},{4,0},{5,1},{6,2},{7,3},{8,12},{9,13},{10,... | collective-permute-start | bytes 393224 | tf_op jit(solution)/shard_map/ppermute | solution.py:29
  9.5 10.0 %collective-permute-start.2 = (f32[256,128]{1,0:T(8,128)S(1)}, f32[256,128]{1,0:T(8,128)S(1)}, u32[]{:S(2)}, u32[]{:S(2)}) collective-permute-start(f32[256,128]{1,0:T(8,128)S(1)} %bitcast.5), channel_id=1, source_target_pairs={{0,6},{1,7},{2,4},{3,5},{4,2},{5,3},{6,0},{7,1},{8,14},{9,15},{10,... | collective-permute-start | bytes 393224 | tf_op jit(solution)/shard_map/ppermute | solution.py:29
  10.8 10.8 %collective-permute-start = (f32[256,128]{1,0:T(8,128)S(1)}, f32[256,128]{1,0:T(8,128)S(1)}, u32[]{:S(2)}, u32[]{:S(2)}) collective-permute-start(f32[256,128]{1,0:T(8,128)S(1)} %bitcast.6), channel_id=1, source_target_pairs={{0,2},{1,3},{2,0},{3,1},{4,6},{5,7},{6,4},{7,5},{8,10},{9,11},{10,... | collective-permute-start | bytes 393224 | tf_op jit(solution)/shard_map/ppermute | solution.py:29
  11.1 1.0 %copy-start.1 = (f32[16,64,128]{2,1,0:T(8,128)S(1)}, f32[16,64,128]{2,1,0:T(8,128)}, u32[]{:S(2)}) copy-start(f32[16,64,128]{2,1,0:T(8,128)} %get-tuple-element.24.refs_0_.keep) | copy-start | bytes 1572868
  12.1 14.0 %collective-permute-start.7 = (f32[8,64,128]{2,1,0:T(8,128)S(1)}, f32[8,64,128]{2,1,0:T(8,128)S(1)}, u32[]{:S(2)}, u32[]{:S(2)}) collective-permute-start(f32[8,64,128]{2,1,0:T(8,128)S(1)} %add_upper.3), channel_id=1, source_target_pairs={{0,2},{1,3},{2,0},{3,1},{4,6},{5,7},{6,4},{7,5},{8,10},{9,11},{10,... | collective-permute-start | bytes 786440 | tf_op jit(solution)/shard_map/ppermute | solution.py:29
  14.0 4.3 %collective-permute-start.4 = (f32[128,128]{1,0:T(8,128)S(1)}, f32[128,128]{1,0:T(8,128)S(1)}, u32[]{:S(2)}, u32[]{:S(2)}) collective-permute-start(f32[128,128]{1,0:T(8,128)S(1)} %bitcast.14), channel_id=1, source_target_pairs={{0,8},{8,0},{16,24},{24,16},{1,9},{9,1},{17,25},{25,17},{2,10},{10... | collective-permute-start | bytes 196616 | tf_op jit(solution)/shard_map/ppermute | solution.py:29
  19.5 11.4 %collective-permute-start.5 = (f32[512,128]{1,0:T(8,128)S(1)}, f32[512,128]{1,0:T(8,128)S(1)}, u32[]{:S(2)}, u32[]{:S(2)}) collective-permute-start(f32[512,128]{1,0:T(8,128)S(1)} %join.5.refs_3_), channel_id=1, source_target_pairs={{0,1},{1,0},{2,3},{3,2},{4,5},{5,4},{6,7},{7,6},{8,9},{9,8},{10,11... | collective-permute-start | bytes 786440 | tf_op jit(solution)/shard_map/ppermute | solution.py:29
  21.6 9.3 %collective-permute-start.3 = (f32[512,128]{1,0:T(8,128)S(1)}, f32[512,128]{1,0:T(8,128)S(1)}, u32[]{:S(2)}, u32[]{:S(2)}) collective-permute-start(f32[512,128]{1,0:T(8,128)S(1)} %join.4), channel_id=1, source_target_pairs={{0,1},{1,0},{2,3},{3,2},{4,5},{5,4},{6,7},{7,6},{8,9},{9,8},{10,11... | collective-permute-start | bytes 786440 | tf_op jit(solution)/shard_map/ppermute | solution.py:29
  21.7 13.2 %collective-permute-start.9 = (f32[256,128]{1,0:T(8,128)S(1)}, f32[256,128]{1,0:T(8,128)S(1)}, u32[]{:S(2)}, u32[]{:S(2)}) collective-permute-start(f32[256,128]{1,0:T(8,128)S(1)} %merge_side.4.refs_2_.mine), channel_id=1, source_target_pairs={{0,16},{8,24},{16,0},{24,8},{1,17},{9,25},{17,1},{25,9},{2,18},{10... | collective-permute-start | bytes 393224 | tf_op jit(solution)/shard_map/ppermute | solution.py:29
  26.2 1.0 %copy-start.2 = (f32[16,64,128]{2,1,0:T(8,128)S(1)}, f32[16,64,128]{2,1,0:T(8,128)}, u32[]{:S(2)}) copy-start(f32[16,64,128]{2,1,0:T(8,128)} %get-tuple-element.24.refs_0_.keep) | copy-start | bytes 1572868
  27.2 7.7 %copy-start.3 = (f32[16,64,128]{2,1,0:T(8,128)S(1)}, f32[16,64,128]{2,1,0:T(8,128)}, u32[]{:S(2)}) copy-start(f32[16,64,128]{2,1,0:T(8,128)} %get-tuple-element.24.refs_0_.keep) | copy-start | bytes 1572868
  27.3 7.7 %copy-start.5 = (f32[2,4,128,128]{3,2,1,0:T(8,128)S(1)}, f32[2,4,128,128]{3,2,1,0:T(8,128)}, u32[]{:S(2)}) copy-start(f32[2,4,128,128]{3,2,1,0:T(8,128)} %coupling.1) | copy-start | bytes 1572868
  27.3 7.7 %collective-permute-start.8 = (f32[4,64,128]{2,1,0:T(8,128)S(1)}, f32[4,64,128]{2,1,0:T(8,128)S(1)}, u32[]{:S(2)}, u32[]{:S(2)}) collective-permute-start(f32[4,64,128]{2,1,0:T(8,128)S(1)} %add_upper.4), channel_id=1, source_target_pairs={{0,6},{1,7},{2,4},{3,5},{4,2},{5,3},{6,0},{7,1},{8,14},{9,15},{10,... | collective-permute-start | bytes 393224 | tf_op jit(solution)/shard_map/ppermute | solution.py:29
  38.5 14.0 %collective-permute-start.18 = (f32[16,64,128]{2,1,0:T(8,128)S(1)}, f32[16,64,128]{2,1,0:T(8,128)S(1)}, u32[]{:S(2)}, u32[]{:S(2)}) collective-permute-start(f32[16,64,128]{2,1,0:T(8,128)S(1)} %get-tuple-element.34), channel_id=1, source_target_pairs={{0,1},{1,0},{2,3},{3,2},{4,5},{5,4},{6,7},{7,6},{8,9},{9,8},{10,11... | collective-permute-start | bytes 1572872 | tf_op jit(solution)/shard_map/ppermute | solution.py:29
  38.6 12.7 %collective-permute-start.11 = (f32[256,128]{1,0:T(8,128)S(1)}, f32[256,128]{1,0:T(8,128)S(1)}, u32[]{:S(2)}, u32[]{:S(2)}) collective-permute-start(f32[256,128]{1,0:T(8,128)S(1)} %bitcast.9), channel_id=1, source_target_pairs={{0,4},{1,5},{2,6},{3,7},{4,0},{5,1},{6,2},{7,3},{8,12},{9,13},{10,... | collective-permute-start | bytes 393224 | tf_op jit(solution)/shard_map/ppermute | solution.py:29
  39.0 12.3 %collective-permute-start.12 = (f32[256,128]{1,0:T(8,128)S(1)}, f32[256,128]{1,0:T(8,128)S(1)}, u32[]{:S(2)}, u32[]{:S(2)}) collective-permute-start(f32[256,128]{1,0:T(8,128)S(1)} %bitcast.10), channel_id=1, source_target_pairs={{0,6},{1,7},{2,4},{3,5},{4,2},{5,3},{6,0},{7,1},{8,14},{9,15},{10,... | collective-permute-start | bytes 393224 | tf_op jit(solution)/shard_map/ppermute | solution.py:29
  41.7 10.7 %collective-permute-start.10 = (f32[256,128]{1,0:T(8,128)S(1)}, f32[256,128]{1,0:T(8,128)S(1)}, u32[]{:S(2)}, u32[]{:S(2)}) collective-permute-start(f32[256,128]{1,0:T(8,128)S(1)} %bitcast.11), channel_id=1, source_target_pairs={{0,2},{1,3},{2,0},{3,1},{4,6},{5,7},{6,4},{7,5},{8,10},{9,11},{10,... | collective-permute-start | bytes 393224 | tf_op jit(solution)/shard_map/ppermute | solution.py:29
  42.2 4.7 %collective-permute-start.14 = (f32[200,128]{1,0:T(8,128)S(1)}, f32[200,128]{1,0:T(8,128)S(1)}, u32[]{:S(2)}, u32[]{:S(2)}) collective-permute-start(f32[200,128]{1,0:T(8,128)S(1)} %get-tuple-element.28.mine), channel_id=1, source_target_pairs={{0,8},{8,0},{16,24},{24,16},{1,9},{9,1},{17,25},{25,17},{2,10},{10... | collective-permute-start | bytes 307208 | tf_op jit(solution)/shard_map/ppermute | solution.py:29
  51.3 5.4 %collective-permute-start.15 = (f32[512,128]{1,0:T(8,128)S(1)}, f32[512,128]{1,0:T(8,128)S(1)}, u32[]{:S(2)}, u32[]{:S(2)}) collective-permute-start(f32[512,128]{1,0:T(8,128)S(1)} %join.7.refs_2_), channel_id=1, source_target_pairs={{0,1},{1,0},{2,3},{3,2},{4,5},{5,4},{6,7},{7,6},{8,9},{9,8},{10,11... | collective-permute-start | bytes 786440 | tf_op jit(solution)/shard_map/ppermute | solution.py:29
  52.4 4.3 %collective-permute-start.13 = (f32[512,128]{1,0:T(8,128)S(1)}, f32[512,128]{1,0:T(8,128)S(1)}, u32[]{:S(2)}, u32[]{:S(2)}) collective-permute-start(f32[512,128]{1,0:T(8,128)S(1)} %join.6), channel_id=1, source_target_pairs={{0,1},{1,0},{2,3},{3,2},{4,5},{5,4},{6,7},{7,6},{8,9},{9,8},{10,11... | collective-permute-start | bytes 786440 | tf_op jit(solution)/shard_map/ppermute | solution.py:29
  52.5 12.0 %collective-permute-start.19 = (f32[8,64,128]{2,1,0:T(8,128)S(1)}, f32[8,64,128]{2,1,0:T(8,128)S(1)}, u32[]{:S(2)}, u32[]{:S(2)}) collective-permute-start(f32[8,64,128]{2,1,0:T(8,128)S(1)} %add_upper.5), channel_id=1, source_target_pairs={{0,2},{1,3},{2,0},{3,1},{4,6},{5,7},{6,4},{7,5},{8,10},{9,11},{10,... | collective-permute-start | bytes 786440 | tf_op jit(solution)/shard_map/ppermute | solution.py:29
  55.2 6.2 %collective-permute-start.16 = (f32[328,128]{1,0:T(8,128)S(1)}, f32[328,128]{1,0:T(8,128)S(1)}, u32[]{:S(2)}, u32[]{:S(2)}) collective-permute-start(f32[328,128]{1,0:T(8,128)S(1)} %merge_side.6.refs_2_.mine), channel_id=1, source_target_pairs={{0,16},{8,24},{16,0},{24,8},{1,17},{9,25},{17,1},{25,9},{2,18},{10... | collective-permute-start | bytes 503816 | tf_op jit(solution)/shard_map/ppermute | solution.py:29
  63.2 1.3 %collective-permute-start.17 = (f32[136,128]{1,0:T(8,128)S(1)}, f32[136,128]{1,0:T(8,128)S(1)}, u32[]{:S(2)}, u32[]{:S(2)}) collective-permute-start(f32[136,128]{1,0:T(8,128)S(1)} %get-tuple-element.32.extra), channel_id=1, source_target_pairs={{0,1},{1,0},{2,3},{3,2},{4,5},{5,4},{6,7},{7,6},{8,9},{9,8},{10,11... | collective-permute-start | bytes 208904 | tf_op jit(solution)/shard_map/ppermute | solution.py:29
  64.5 4.4 %collective-permute-start.20 = (f32[136,128]{1,0:T(8,128)S(1)}, f32[136,128]{1,0:T(8,128)S(1)}, u32[]{:S(2)}, u32[]{:S(2)}) collective-permute-start(f32[136,128]{1,0:T(8,128)S(1)} %settle.1.extra), channel_id=1, source_target_pairs={{0,2},{1,3},{2,0},{3,1},{4,6},{5,7},{6,4},{7,5},{8,10},{9,11},{10,... | collective-permute-start | bytes 208904 | tf_op jit(solution)/shard_map/ppermute | solution.py:29
  68.9 5.0 %collective-permute-start.21 = (f32[72,128]{1,0:T(8,128)S(1)}, f32[72,128]{1,0:T(8,128)S(1)}, u32[]{:S(2)}, u32[]{:S(2)}) collective-permute-start(f32[72,128]{1,0:T(8,128)S(1)} %get-tuple-element.35.sums), channel_id=1, source_target_pairs={{0,4},{1,5},{2,6},{3,7},{4,0},{5,1},{6,2},{7,3},{8,12},{9,13},{10,... | collective-permute-start | bytes 110600 | tf_op jit(solution)/shard_map/ppermute | solution.py:29
  74.1 9.7 %collective-permute-start.24 = (f32[5,64,128]{2,1,0:T(8,128)S(1)}, f32[5,64,128]{2,1,0:T(8,128)S(1)}, u32[]{:S(2)}, u32[]{:S(2)}) collective-permute-start(f32[5,64,128]{2,1,0:T(8,128)S(1)} %get-tuple-element.43), channel_id=1, source_target_pairs={{0,6},{1,7},{2,4},{3,5},{4,2},{5,3},{6,0},{7,1},{8,14},{9,15},{10,... | collective-permute-start | bytes 491528 | tf_op jit(solution)/shard_map/ppermute | solution.py:29
  75.5 4.5 %collective-permute-start.22 = (f32[32,128]{1,0:T(8,128)S(1)}, f32[32,128]{1,0:T(8,128)S(1)}, u32[]{:S(2)}, u32[]{:S(2)}) collective-permute-start(f32[32,128]{1,0:T(8,128)S(1)} %get-tuple-element.36.refs_0_), channel_id=1, source_target_pairs={{0,8},{8,0},{16,24},{24,16},{1,9},{9,1},{17,25},{25,17},{2,10},{10... | collective-permute-start | bytes 49160 | tf_op jit(solution)/shard_map/ppermute | solution.py:29
  80.0 3.8 %collective-permute-start.23 = (f32[32,128]{1,0:T(8,128)S(1)}, f32[32,128]{1,0:T(8,128)S(1)}, u32[]{:S(2)}, u32[]{:S(2)}) collective-permute-start(f32[32,128]{1,0:T(8,128)S(1)} %add_whole.2.refs_0_), channel_id=1, source_target_pairs={{0,16},{8,24},{16,0},{24,8},{1,17},{9,25},{17,1},{25,9},{2,18},{10... | collective-permute-start | bytes 49160 | tf_op jit(solution)/shard_map/ppermute | solution.py:29

commit v6 on v5

--- a/solution.py
+++ b/solution.py
@@ -642,6 +642,17 @@
     )(left, right, *earlier)
 
 
+def pass_on(value, *earlier):
+    return pl.pallas_call(
+        functools.partial(add_kernel, 1),
+        out_shape=jax.ShapeDtypeStruct(value.shape, f32),
+        in_specs=[vmem] + [anywhere] * len(earlier),
+        out_specs=vmem,
+        compiler_params=params(),
+        name="pass_on",
+    )(value, *earlier)
+
+
 def join_kernel(count, *refs):
     out = refs[-1]
     rows = refs[0].shape[0]
@@ -688,10 +699,11 @@
     return side, swap(side, "group", mask)
 
 
-def share_panel(piece, bulk_count, *earlier):
+def share_panel(piece, bulk_count, pieces, *earlier):
     own = [piece] + [swap(piece, "bulk", rel) for rel in range(2, bulk_count, 2)]
-    middle = len(own) // 2
-    joined = [join(own[:middle]), join(own[middle:], *earlier)]
+    size = len(own) // pieces
+    joined = [join(own[i * size : (i + 1) * size]) for i in range(pieces - 1)]
+    joined.append(join(own[(pieces - 1) * size :], *earlier))
     return own + [swap(one, "bulk", 1) for one in joined], joined[-1]
 
 
@@ -708,7 +720,7 @@
     flat = rhs.reshape(row_count * count, order)
     side, other_side = share_side(flat[:edge], edge, part_count)
     keep, send = returned(rhs, offdiag_blocks, *indices, bulk_count, False)
-    panel, joined = share_panel(flat, bulk_count, side)
+    panel, joined = share_panel(flat, bulk_count, 2, side)
     terms = [keep, swap(send, "bulk", 1)]
     rows = bulk_count // 2 * row_count
     for step, mask in enumerate(masks):
@@ -724,11 +736,11 @@
     side, other_side = share_side(side, edge, part_count)
     keep, send = returned(first, offdiag_blocks, *indices, bulk_count, True)
     panel, joined = share_panel(
-        first.reshape(row_count * count, order), bulk_count, side, keep
+        first.reshape(row_count * count, order), bulk_count, 1, side, keep
     )
-    terms = [keep, swap(send, "bulk", 1)]
+    terms = [keep, swap(pass_on(send, joined), "bulk", 1)]
     rows = bulk_count // 4 * row_count
-    terms.append(swap(add_upper(terms, rows, joined), "bulk", masks[0]))
+    terms.append(swap(add_upper(terms, rows), "bulk", masks[0]))
     near, moved, packed = near_part(panel, first, offdiag_blocks, diag_tiles, *indices, True)
     side = merge_side(side, other_side, half_edges, near)
     near, extra = edge_second(first, near, packed, coupling, side, new_slot)

time: 88.9 us -> 86.8 us (0.976)
  waiting for transfers between devices: 28.8 us -> 24.7 us
  starting transfers between devices: 28.6 us -> 30.7 us
    ppermute x25 -> x24, waiting for transfers between devices: 28.8 us -> 24.7 us  [swap(): return lax.ppermute(value, axis, pairs)]
    ppermute x25 -> x24, starting transfers between devices: 28.6 us -> 30.7 us  [swap(): return lax.ppermute(value, axis, pairs)]
  transfers between devices with their start and end apart: 25 -> 24, of which waited for: 11 -> 11; matrix products, arithmetic and copies ran while one was open for 0% -> 0% of each run, Pallas kernels for 17% -> 20%
where the time goes in v6:
time: 86.8 us; the launch traced here: 86.6 us
  starting transfers between devices  30.7 us (35%)
  Pallas kernels  28.2 us (32%)
  waiting for transfers between devices  24.7 us (28%)
  local copies, waits for them, and re-layouts  2.12 us (2%)
  between operations  0.9 us (1%)
    ppermute x24, starting transfers between devices, swap(): return lax.ppermute(value, axis, pairs)  30.7 us
    ppermute x24, waiting for transfers between devices, swap(): return lax.ppermute(value, axis, pairs)  24.7 us
    pallas_call x2, Pallas kernels, near_part(): pl.pallas_call(functools.partial(near_kernel, bulk_count, len(panel), sec...  8.61 us
    pallas_call x2, Pallas kernels, returned(): pl.pallas_call(functools.partial(returned_kernel, bulk_count, moved), gri...  7.05 us
    pallas_call x1, Pallas kernels, final(): pl.pallas_call(final_kernel, grid=(1,), out_shape=[jax.ShapeDtypeStruct(n...  4.81 us
    pallas_call x2, Pallas kernels, small_call(): pl.pallas_call(kernel, out_shape=jax.ShapeDtypeStruct((matrices, count, c...  4.32 us
    unnamed x20, local copies, waits for them, and re-layouts  2.12 us
  transfers between devices with their start and end apart: 24, of which 11 were waited for; matrix products, arithmetic and copies ran while one was open for 0% of the time, Pallas kernels for 20%

profile of v6, /device:TPU:0, one launch (start us, length us, event | category | flops | bytes accessed | tf_op | source)
XLA Modules:
  0.0 86.6 jit_solution(13833788618428254465)
XLA Ops:
  0.7 4.7 %returned.1 = (f32[16,64,128]{2,1,0:T(8,128)}, f32[16,64,128]{2,1,0:T(8,128)}) custom-call(f32[4,64,128]{2,1,0:T(8,128)} %vectors.3, f32[4,11,128,128]{3,2,1,0:T(8,128)} %refs_6_.3, s32[11,128]{1,0:T(8,128)} %bitcast.16, s32[128]{0:T(128)} %refs_9_.1, s32[128]{0:T(128)} %new_slot.7), custom_call_target="tpu_custom_call" | custom-call | tf_op jit(solution)/shard_map/returned/pallas_call | solution.py:164
  5.4 0.5 collective-permute-start.6
  5.8 3.7 %collective-permute-start.1 = (f32[256,128]{1,0:T(8,128)S(1)}, f32[256,128]{1,0:T(8,128)S(1)}, u32[]{:S(2)}, u32[]{:S(2)}) collective-permute-start(f32[256,128]{1,0:T(8,128)S(1)} %bitcast.4), channel_id=1, source_target_pairs={{0,4},{1,5},{2,6},{3,7},{4,0},{5,1},{6,2},{7,3},{8,12},{9,13},{10,... | collective-permute-start | bytes 393224 | tf_op jit(solution)/shard_map/ppermute | solution.py:29
  9.5 1.3 %collective-permute-start.2 = (f32[256,128]{1,0:T(8,128)S(1)}, f32[256,128]{1,0:T(8,128)S(1)}, u32[]{:S(2)}, u32[]{:S(2)}) collective-permute-start(f32[256,128]{1,0:T(8,128)S(1)} %bitcast.5), channel_id=1, source_target_pairs={{0,6},{1,7},{2,4},{3,5},{4,2},{5,3},{6,0},{7,1},{8,14},{9,15},{10,... | collective-permute-start | bytes 393224 | tf_op jit(solution)/shard_map/ppermute | solution.py:29
  10.8 0.2 collective-permute-start
  11.1 1.0 %copy-done.1 = f32[16,64,128]{2,1,0:T(8,128)S(1)} copy-done((f32[16,64,128]{2,1,0:T(8,128)S(1)}, f32[16,64,128]{2,1,0:T(8,128)}, u32[]{:S(2)}) %copy-start.1) | copy-done | bytes 524312
  12.2 1.9 %collective-permute-start.7 = (f32[8,64,128]{2,1,0:T(8,128)S(1)}, f32[8,64,128]{2,1,0:T(8,128)S(1)}, u32[]{:S(2)}, u32[]{:S(2)}) collective-permute-start(f32[8,64,128]{2,1,0:T(8,128)S(1)} %add_upper.3), channel_id=1, source_target_pairs={{0,2},{1,3},{2,0},{3,1},{4,6},{5,7},{6,4},{7,5},{8,10},{9,11},{10,... | collective-permute-start | bytes 786440 | tf_op jit(solution)/shard_map/ppermute | solution.py:29
  14.0 1.5 %collective-permute-start.4 = (f32[128,128]{1,0:T(8,128)S(1)}, f32[128,128]{1,0:T(8,128)S(1)}, u32[]{:S(2)}, u32[]{:S(2)}) collective-permute-start(f32[128,128]{1,0:T(8,128)S(1)} %bitcast.14), channel_id=1, source_target_pairs={{0,8},{8,0},{16,24},{24,16},{1,9},{9,1},{17,25},{25,17},{2,10},{10... | collective-permute-start | bytes 196616 | tf_op jit(solution)/shard_map/ppermute | solution.py:29
  15.5 2.8 %collective-permute-done.4.other = f32[128,128]{1,0:T(8,128)S(1)} collective-permute-done((f32[128,128]{1,0:T(8,128)S(1)}, f32[128,128]{1,0:T(8,128)S(1)}, u32[]{:S(2)}, u32[]{:S(2)}) %collective-permute-start.4) | collective-permute-done | bytes 65568 | tf_op jit(solution)/shard_map/ppermute | solution.py:29
  18.3 1.2 %collective-permute-done.1.refs_0_.refs_2_ = f32[256,128]{1,0:T(8,128)S(1)} collective-permute-done((f32[256,128]{1,0:T(8,128)S(1)}, f32[256,128]{1,0:T(8,128)S(1)}, u32[]{:S(2)}, u32[]{:S(2)}) %collective-permute-start.1) | collective-permute-done | bytes 131104 | tf_op jit(solution)/shard_map/ppermute | solution.py:29
  19.5 0.1 collective-permute-start.5
  19.6 2.0 %collective-permute-done.refs_1_ = f32[256,128]{1,0:T(8,128)S(1)} collective-permute-done((f32[256,128]{1,0:T(8,128)S(1)}, f32[256,128]{1,0:T(8,128)S(1)}, u32[]{:S(2)}, u32[]{:S(2)}) %collective-permute-start) | collective-permute-done | bytes 131104 | tf_op jit(solution)/shard_map/ppermute | solution.py:29
  21.6 0.1 collective-permute-start.3
  21.7 1.6 %collective-permute-start.9 = (f32[256,128]{1,0:T(8,128)S(1)}, f32[256,128]{1,0:T(8,128)S(1)}, u32[]{:S(2)}, u32[]{:S(2)}) collective-permute-start(f32[256,128]{1,0:T(8,128)S(1)} %merge_side.4.refs_2_.mine), channel_id=1, source_target_pairs={{0,16},{8,24},{16,0},{24,8},{1,17},{9,25},{17,1},{25,9},{2,18},{10... | collective-permute-start | bytes 393224 | tf_op jit(solution)/shard_map/ppermute | solution.py:29
  23.4 2.8 %collective-permute-done.7.refs_2_.refs_1_ = f32[8,64,128]{2,1,0:T(8,128)S(1)} collective-permute-done((f32[8,64,128]{2,1,0:T(8,128)S(1)}, f32[8,64,128]{2,1,0:T(8,128)S(1)}, u32[]{:S(2)}, u32[]{:S(2)}) %collective-permute-start.7) | collective-permute-done | bytes 262176 | tf_op jit(solution)/shard_map/ppermute | solution.py:29
  26.2 1.0 %copy-done.2 = f32[16,64,128]{2,1,0:T(8,128)S(1)} copy-done((f32[16,64,128]{2,1,0:T(8,128)S(1)}, f32[16,64,128]{2,1,0:T(8,128)}, u32[]{:S(2)}) %copy-start.2) | copy-done | bytes 524312
  27.3 0.0 copy-start.5
  27.3 3.6 %collective-permute-start.8 = (f32[4,64,128]{2,1,0:T(8,128)S(1)}, f32[4,64,128]{2,1,0:T(8,128)S(1)}, u32[]{:S(2)}, u32[]{:S(2)}) collective-permute-start(f32[4,64,128]{2,1,0:T(8,128)S(1)} %add_upper.4), channel_id=1, source_target_pairs={{0,6},{1,7},{2,4},{3,5},{4,2},{5,3},{6,0},{7,1},{8,14},{9,15},{10,... | collective-permute-start | bytes 393224 | tf_op jit(solution)/shard_map/ppermute | solution.py:29
  30.9 4.0 %near_first.1 = (f32[4,64,128]{2,1,0:T(8,128)S(1)}, f32[4,64,128]{2,1,0:T(8,128)S(1)}, f32[32,128]{1,0:T(8,128)S(1)}, f32[24,128]{1,0:T(8,128)S(1)}) custom-call(f32[256,128]{1,0:T(8,128)S(1)} %bitcast.8, f32[256,128]{1,0:T(8,128)S(1)} %collective-permute-done.refs_1_, f32[256,128]{1,0:T(8,128)S(1)} %collective-permute-done.1.refs_0_.refs_2_, ...), custom_call_target="tpu_custom_call" | custom-call | tf_op jit(solution)/shard_map/near_first/pallas_call | solution.py:258
  35.0 1.1 %gather_first.1 = (f32[4,64,128]{2,1,0:T(8,128)S(1)}, f32[200,128]{1,0:T(8,128)S(1)}) custom-call(f32[4,64,128]{2,1,0:T(8,128)S(1)} %copy-done.4, f32[4,64,128]{2,1,0:T(8,128)S(1)} %get-tuple-element.23.refs_0_.near, f32[16,64,128]{2,1,0:T(8,128)S(1)} %copy-done.3, f32[16,64,128]{2,1,0:T(8,128)S(1)} %collective-permute-done.6.refs_1_.refs_0_, ...), custom_call_target="tpu_custom_call" | custom-call | tf_op jit(solution)/shard_map/gather_first/pallas_call | solution.py:325
  36.1 0.7 collective-permute-start.10
  36.8 2.6 %collective-permute-start.11 = (f32[256,128]{1,0:T(8,128)S(1)}, f32[256,128]{1,0:T(8,128)S(1)}, u32[]{:S(2)}, u32[]{:S(2)}) collective-permute-start(f32[256,128]{1,0:T(8,128)S(1)} %bitcast.10), channel_id=1, source_target_pairs={{0,4},{1,5},{2,6},{3,7},{4,0},{5,1},{6,2},{7,3},{8,12},{9,13},{10,... | collective-permute-start | bytes 393224 | tf_op jit(solution)/shard_map/ppermute | solution.py:29
  39.4 1.2 %collective-permute-start.12 = (f32[256,128]{1,0:T(8,128)S(1)}, f32[256,128]{1,0:T(8,128)S(1)}, u32[]{:S(2)}, u32[]{:S(2)}) collective-permute-start(f32[256,128]{1,0:T(8,128)S(1)} %bitcast.11), channel_id=1, source_target_pairs={{0,6},{1,7},{2,4},{3,5},{4,2},{5,3},{6,0},{7,1},{8,14},{9,15},{10,... | collective-permute-start | bytes 393224 | tf_op jit(solution)/shard_map/ppermute | solution.py:29
  40.5 1.5 %collective-permute-start.13 = (f32[200,128]{1,0:T(8,128)S(1)}, f32[200,128]{1,0:T(8,128)S(1)}, u32[]{:S(2)}, u32[]{:S(2)}) collective-permute-start(f32[200,128]{1,0:T(8,128)S(1)} %get-tuple-element.28.mine), channel_id=1, source_target_pairs={{0,8},{8,0},{16,24},{24,16},{1,9},{9,1},{17,25},{25,17},{2,10},{10... | collective-permute-start | bytes 307208 | tf_op jit(solution)/shard_map/ppermute | solution.py:29
  42.0 2.4 %returned_moved.1 = (f32[16,64,128]{2,1,0:T(8,128)S(1)}, f32[16,64,128]{2,1,0:T(8,128)S(1)}) custom-call(f32[4,64,128]{2,1,0:T(8,128)S(1)} %get-tuple-element.27.vectors.refs_5_.first, f32[4,11,128,128]{3,2,1,0:T(8,128)S(1)} %copy-done, s32[11,128]{1,0:T(8,128)S(1)} %bitcast.18, s32[128]{0:T(128)S(1)} %copy-done.9, s32[128]{0:T(128)S(1)} %copy-done.8), custom_call_target="tpu_custom_call" | custom-call | tf_op jit(solution)/shard_map/returned_moved/pallas_call | solution.py:164
  44.4 0.8 collective-permute-done.13.other
  45.2 3.2 %collective-permute-done.11.refs_2_ = f32[256,128]{1,0:T(8,128)S(1)} collective-permute-done((f32[256,128]{1,0:T(8,128)S(1)}, f32[256,128]{1,0:T(8,128)S(1)}, u32[]{:S(2)}, u32[]{:S(2)}) %collective-permute-start.11) | collective-permute-done | bytes 131104 | tf_op jit(solution)/shard_map/ppermute | solution.py:29
  48.5 0.1 collective-permute-start.17
  48.6 0.5 collective-permute-start.14
  49.1 1.4 %collective-permute-done.17.refs_1_.refs_3_ = f32[16,64,128]{2,1,0:T(8,128)S(1)} collective-permute-done((f32[16,64,128]{2,1,0:T(8,128)S(1)}, f32[16,64,128]{2,1,0:T(8,128)S(1)}, u32[]{:S(2)}, u32[]{:S(2)}) %collective-permute-start.17) | collective-permute-done | bytes 524320 | tf_op jit(solution)/shard_map/ppermute | solution.py:29
  50.5 2.0 %collective-permute-start.18 = (f32[8,64,128]{2,1,0:T(8,128)S(1)}, f32[8,64,128]{2,1,0:T(8,128)S(1)}, u32[]{:S(2)}, u32[]{:S(2)}) collective-permute-start(f32[8,64,128]{2,1,0:T(8,128)S(1)} %add_upper.5), channel_id=1, source_target_pairs={{0,2},{1,3},{2,0},{3,1},{4,6},{5,7},{6,4},{7,5},{8,10},{9,11},{10,... | collective-permute-start | bytes 786440 | tf_op jit(solution)/shard_map/ppermute | solution.py:29
  52.5 1.5 %collective-permute-start.15 = (f32[328,128]{1,0:T(8,128)S(1)}, f32[328,128]{1,0:T(8,128)S(1)}, u32[]{:S(2)}, u32[]{:S(2)}) collective-permute-start(f32[328,128]{1,0:T(8,128)S(1)} %merge_side.6.refs_4_.mine), channel_id=1, source_target_pairs={{0,16},{8,24},{16,0},{24,8},{1,17},{9,25},{17,1},{25,9},{2,18},{10... | collective-permute-start | bytes 503816 | tf_op jit(solution)/shard_map/ppermute | solution.py:29
  54.0 4.6 %near_second.1 = (f32[4,64,128]{2,1,0:T(8,128)S(1)}, f32[4,64,128]{2,1,0:T(8,128)S(1)}, f32[32,128]{1,0:T(8,128)S(1)}) custom-call(f32[256,128]{1,0:T(8,128)S(1)} %bitcast.13, f32[256,128]{1,0:T(8,128)S(1)} %collective-permute-done.10.refs_1_, f32[256,128]{1,0:T(8,128)S(1)} %collective-permute-done.11.refs_2_, ...), custom_call_target="tpu_custom_call" | custom-call | tf_op jit(solution)/shard_map/near_second/pallas_call | solution.py:258
  58.7 1.7 %edge_second.1 = (f32[4,64,128]{2,1,0:T(8,128)S(1)}, f32[136,128]{1,0:T(8,128)S(1)}) custom-call(f32[4,64,128]{2,1,0:T(8,128)S(1)} %get-tuple-element.27.vectors.refs_5_.first, f32[4,64,128]{2,1,0:T(8,128)S(1)} %get-tuple-element.30.refs_0_.near, f32[32,128]{1,0:T(8,128)S(1)} %get-tuple-element.31.packed, f32[2,4,128,128]{3,2,1,0:T(8,128)S(1)} %copy-done.5, ...), custom_call_target="tpu_custom_call" | custom-call | tf_op jit(solution)/shard_map/edge_second/pallas_call | solution.py:364
  60.4 0.1 collective-permute-start.16
  60.5 1.2 %collective-permute-done.16.partner = f32[136,128]{1,0:T(8,128)S(1)} collective-permute-done((f32[136,128]{1,0:T(8,128)S(1)}, f32[136,128]{1,0:T(8,128)S(1)}, u32[]{:S(2)}, u32[]{:S(2)}) %collective-permute-start.16) | collective-permute-done | bytes 69664 | tf_op jit(solution)/shard_map/ppermute | solution.py:29
  61.8 0.3 collective-permute-start.19
  62.1 4.0 %collective-permute-done.19.partner = f32[136,128]{1,0:T(8,128)S(1)} collective-permute-done((f32[136,128]{1,0:T(8,128)S(1)}, f32[136,128]{1,0:T(8,128)S(1)}, u32[]{:S(2)}, u32[]{:S(2)}) %collective-permute-start.19) | collective-permute-done | bytes 69664 | tf_op jit(solution)/shard_map/ppermute | solution.py:29
  66.2 0.8 collective-permute-start.20
  66.9 4.3 %collective-permute-done.20.partner = f32[72,128]{1,0:T(8,128)S(1)} collective-permute-done((f32[72,128]{1,0:T(8,128)S(1)}, f32[72,128]{1,0:T(8,128)S(1)}, u32[]{:S(2)}, u32[]{:S(2)}) %collective-permute-start.20) | collective-permute-done | bytes 36896 | tf_op jit(solution)/shard_map/ppermute | solution.py:29
  71.2 0.2 last_gram.1
  71.4 2.0 %collective-permute-start.23 = (f32[5,64,128]{2,1,0:T(8,128)S(1)}, f32[5,64,128]{2,1,0:T(8,128)S(1)}, u32[]{:S(2)}, u32[]{:S(2)}) collective-permute-start(f32[5,64,128]{2,1,0:T(8,128)S(1)} %get-tuple-element.43), channel_id=1, source_target_pairs={{0,6},{1,7},{2,4},{3,5},{4,2},{5,3},{6,0},{7,1},{8,14},{9,15},{10,... | collective-permute-start | bytes 491528 | tf_op jit(solution)/shard_map/ppermute | solution.py:29
  73.4 1.5 %collective-permute-start.21 = (f32[32,128]{1,0:T(8,128)S(1)}, f32[32,128]{1,0:T(8,128)S(1)}, u32[]{:S(2)}, u32[]{:S(2)}) collective-permute-start(f32[32,128]{1,0:T(8,128)S(1)} %get-tuple-element.36.refs_0_), channel_id=1, source_target_pairs={{0,8},{8,0},{16,24},{24,16},{1,9},{9,1},{17,25},{25,17},{2,10},{10... | collective-permute-start | bytes 49160 | tf_op jit(solution)/shard_map/ppermute | solution.py:29
  74.9 3.0 %first_solves.1.refs_2_.solved = f32[2,64,64]{2,1,0:T(8,128)S(1)} custom-call(f32[72,128]{1,0:T(8,128)S(1)} %get-tuple-element.37.extra.refs_3_), custom_call_target="tpu_custom_call" | custom-call | tf_op jit(solution)/shard_map/first_solves/pallas_call | solution.py:468
  77.9 1.6 %collective-permute-start.22 = (f32[32,128]{1,0:T(8,128)S(1)}, f32[32,128]{1,0:T(8,128)S(1)}, u32[]{:S(2)}, u32[]{:S(2)}) collective-permute-start(f32[32,128]{1,0:T(8,128)S(1)} %add_whole.2.refs_0_), channel_id=1, source_target_pairs={{0,16},{8,24},{16,0},{24,8},{1,17},{9,25},{17,1},{25,9},{2,18},{10... | collective-permute-start | bytes 49160 | tf_op jit(solution)/shard_map/ppermute | solution.py:29
  79.5 1.3 %next_gram.1.following = f32[3,64,64]{2,1,0:T(8,128)S(1)} custom-call(f32[72,128]{1,0:T(8,128)S(1)} %get-tuple-element.37.extra.refs_3_, f32[2,64,64]{2,1,0:T(8,128)S(1)} %first_solves.1.refs_2_.solved), custom_call_target="tpu_custom_call" | custom-call | tf_op jit(solution)/shard_map/next_gram/pallas_call | solution.py:468
  80.8 0.9 %collective-permute-done.22.refs_1_ = f32[32,128]{1,0:T(8,128)S(1)} collective-permute-done((f32[32,128]{1,0:T(8,128)S(1)}, f32[32,128]{1,0:T(8,128)S(1)}, u32[]{:S(2)}, u32[]{:S(2)}) %collective-permute-start.22) | collective-permute-done | bytes 16416 | tf_op jit(solution)/shard_map/ppermute | solution.py:29
  81.8 4.8 %final.1 = (f32[4,64,128]{2,1,0:T(8,128)}, f32[4,64,128]{2,1,0:T(8,128)}) custom-call(f32[32,128]{1,0:T(8,128)S(1)} %add_whole.3.gram, f32[2,64,64]{2,1,0:T(8,128)S(1)} %first_solves.1.refs_2_.solved, f32[3,64,64]{2,1,0:T(8,128)S(1)} %next_gram.1.following, f32[4,64,128]{2,1,0:T(8,128)S(1)} %get-tuple-element.38.moving, ...), custom_call_target="tpu_custom_call" | custom-call | tf_op jit(solution)/shard_map/final/pallas_call | solution.py:511
  (47 shorter events, 0.4 us)
Async XLA Ops:
  0.6 5.2 %copy-start.4 = (f32[4,64,128]{2,1,0:T(8,128)S(1)}, f32[4,64,128]{2,1,0:T(8,128)}, u32[]{:S(2)}) copy-start(f32[4,64,128]{2,1,0:T(8,128)} %vectors.3) | copy-start | bytes 393220
  0.6 30.3 %copy-start.6 = (f32[4,128,128]{2,1,0:T(8,128)S(1)}, f32[4,128,128]{2,1,0:T(8,128)}, u32[]{:S(2)}) copy-start(f32[4,128,128]{2,1,0:T(8,128)} %refs_7_.3) | copy-start | bytes 786436
  0.7 30.3 %copy-start.7 = (s32[128,11]{0,1:T(8,128)S(1)}, s32[128,11]{0,1:T(8,128)}, u32[]{:S(2)}) copy-start(s32[128,11]{0,1:T(8,128)} %param.11) | copy-start | bytes 16900
  0.7 30.3 %copy-start.8 = (s32[128]{0:T(128)S(1)}, s32[128]{0:T(128)}, u32[]{:S(2)}) copy-start(s32[128]{0:T(128)} %new_slot.7) | copy-start | bytes 1540
  0.7 30.3 %copy-start.9 = (s32[128]{0:T(128)S(1)}, s32[128]{0:T(128)}, u32[]{:S(2)}) copy-start(s32[128]{0:T(128)} %refs_9_.1) | copy-start | bytes 1540
  5.4 25.6 %copy-start = (f32[4,11,128,128]{3,2,1,0:T(8,128)S(1)}, f32[4,11,128,128]{3,2,1,0:T(8,128)}, u32[]{:S(2)}) copy-start(f32[4,11,128,128]{3,2,1,0:T(8,128)} %refs_6_.3) | copy-start | bytes 8650756
  5.4 5.7 %collective-permute-start.6 = (f32[16,64,128]{2,1,0:T(8,128)}, f32[16,64,128]{2,1,0:T(8,128)S(1)}, u32[]{:S(2)}, u32[]{:S(2)}) collective-permute-start(f32[16,64,128]{2,1,0:T(8,128)} %get-tuple-element.25), channel_id=1, source_target_pairs={{0,1},{1,0},{2,3},{3,2},{4,5},{5,4},{6,7},{7,6},{8,9},{9,8},{10,11... | collective-permute-start | bytes 1572872 | tf_op jit(solution)/shard_map/ppermute | solution.py:29
  5.8 13.7 %collective-permute-start.1 = (f32[256,128]{1,0:T(8,128)S(1)}, f32[256,128]{1,0:T(8,128)S(1)}, u32[]{:S(2)}, u32[]{:S(2)}) collective-permute-start(f32[256,128]{1,0:T(8,128)S(1)} %bitcast.4), channel_id=1, source_target_pairs={{0,4},{1,5},{2,6},{3,7},{4,0},{5,1},{6,2},{7,3},{8,12},{9,13},{10,... | collective-permute-start | bytes 393224 | tf_op jit(solution)/shard_map/ppermute | solution.py:29
  9.5 10.0 %collective-permute-start.2 = (f32[256,128]{1,0:T(8,128)S(1)}, f32[256,128]{1,0:T(8,128)S(1)}, u32[]{:S(2)}, u32[]{:S(2)}) collective-permute-start(f32[256,128]{1,0:T(8,128)S(1)} %bitcast.5), channel_id=1, source_target_pairs={{0,6},{1,7},{2,4},{3,5},{4,2},{5,3},{6,0},{7,1},{8,14},{9,15},{10,... | collective-permute-start | bytes 393224 | tf_op jit(solution)/shard_map/ppermute | solution.py:29
  10.8 10.8 %collective-permute-start = (f32[256,128]{1,0:T(8,128)S(1)}, f32[256,128]{1,0:T(8,128)S(1)}, u32[]{:S(2)}, u32[]{:S(2)}) collective-permute-start(f32[256,128]{1,0:T(8,128)S(1)} %bitcast.6), channel_id=1, source_target_pairs={{0,2},{1,3},{2,0},{3,1},{4,6},{5,7},{6,4},{7,5},{8,10},{9,11},{10,... | collective-permute-start | bytes 393224 | tf_op jit(solution)/shard_map/ppermute | solution.py:29
  11.1 1.0 %copy-start.1 = (f32[16,64,128]{2,1,0:T(8,128)S(1)}, f32[16,64,128]{2,1,0:T(8,128)}, u32[]{:S(2)}) copy-start(f32[16,64,128]{2,1,0:T(8,128)} %get-tuple-element.24.refs_0_.keep) | copy-start | bytes 1572868
  12.2 14.0 %collective-permute-start.7 = (f32[8,64,128]{2,1,0:T(8,128)S(1)}, f32[8,64,128]{2,1,0:T(8,128)S(1)}, u32[]{:S(2)}, u32[]{:S(2)}) collective-permute-start(f32[8,64,128]{2,1,0:T(8,128)S(1)} %add_upper.3), channel_id=1, source_target_pairs={{0,2},{1,3},{2,0},{3,1},{4,6},{5,7},{6,4},{7,5},{8,10},{9,11},{10,... | collective-permute-start | bytes 786440 | tf_op jit(solution)/shard_map/ppermute | solution.py:29
  14.0 4.3 %collective-permute-start.4 = (f32[128,128]{1,0:T(8,128)S(1)}, f32[128,128]{1,0:T(8,128)S(1)}, u32[]{:S(2)}, u32[]{:S(2)}) collective-permute-start(f32[128,128]{1,0:T(8,128)S(1)} %bitcast.14), channel_id=1, source_target_pairs={{0,8},{8,0},{16,24},{24,16},{1,9},{9,1},{17,25},{25,17},{2,10},{10... | collective-permute-start | bytes 196616 | tf_op jit(solution)/shard_map/ppermute | solution.py:29
  19.5 11.4 %collective-permute-start.5 = (f32[512,128]{1,0:T(8,128)S(1)}, f32[512,128]{1,0:T(8,128)S(1)}, u32[]{:S(2)}, u32[]{:S(2)}) collective-permute-start(f32[512,128]{1,0:T(8,128)S(1)} %join.4.refs_3_), channel_id=1, source_target_pairs={{0,1},{1,0},{2,3},{3,2},{4,5},{5,4},{6,7},{7,6},{8,9},{9,8},{10,11... | collective-permute-start | bytes 786440 | tf_op jit(solution)/shard_map/ppermute | solution.py:29
  21.6 9.3 %collective-permute-start.3 = (f32[512,128]{1,0:T(8,128)S(1)}, f32[512,128]{1,0:T(8,128)S(1)}, u32[]{:S(2)}, u32[]{:S(2)}) collective-permute-start(f32[512,128]{1,0:T(8,128)S(1)} %join.3), channel_id=1, source_target_pairs={{0,1},{1,0},{2,3},{3,2},{4,5},{5,4},{6,7},{7,6},{8,9},{9,8},{10,11... | collective-permute-start | bytes 786440 | tf_op jit(solution)/shard_map/ppermute | solution.py:29
  21.7 13.2 %collective-permute-start.9 = (f32[256,128]{1,0:T(8,128)S(1)}, f32[256,128]{1,0:T(8,128)S(1)}, u32[]{:S(2)}, u32[]{:S(2)}) collective-permute-start(f32[256,128]{1,0:T(8,128)S(1)} %merge_side.4.refs_2_.mine), channel_id=1, source_target_pairs={{0,16},{8,24},{16,0},{24,8},{1,17},{9,25},{17,1},{25,9},{2,18},{10... | collective-permute-start | bytes 393224 | tf_op jit(solution)/shard_map/ppermute | solution.py:29
  26.2 1.0 %copy-start.2 = (f32[16,64,128]{2,1,0:T(8,128)S(1)}, f32[16,64,128]{2,1,0:T(8,128)}, u32[]{:S(2)}) copy-start(f32[16,64,128]{2,1,0:T(8,128)} %get-tuple-element.24.refs_0_.keep) | copy-start | bytes 1572868
  27.3 7.7 %copy-start.3 = (f32[16,64,128]{2,1,0:T(8,128)S(1)}, f32[16,64,128]{2,1,0:T(8,128)}, u32[]{:S(2)}) copy-start(f32[16,64,128]{2,1,0:T(8,128)} %get-tuple-element.24.refs_0_.keep) | copy-start | bytes 1572868
  27.3 7.7 %copy-start.5 = (f32[2,4,128,128]{3,2,1,0:T(8,128)S(1)}, f32[2,4,128,128]{3,2,1,0:T(8,128)}, u32[]{:S(2)}) copy-start(f32[2,4,128,128]{3,2,1,0:T(8,128)} %coupling.1) | copy-start | bytes 1572868
  27.3 7.7 %collective-permute-start.8 = (f32[4,64,128]{2,1,0:T(8,128)S(1)}, f32[4,64,128]{2,1,0:T(8,128)S(1)}, u32[]{:S(2)}, u32[]{:S(2)}) collective-permute-start(f32[4,64,128]{2,1,0:T(8,128)S(1)} %add_upper.4), channel_id=1, source_target_pairs={{0,6},{1,7},{2,4},{3,5},{4,2},{5,3},{6,0},{7,1},{8,14},{9,15},{10,... | collective-permute-start | bytes 393224 | tf_op jit(solution)/shard_map/ppermute | solution.py:29
  36.1 9.1 %collective-permute-start.10 = (f32[256,128]{1,0:T(8,128)S(1)}, f32[256,128]{1,0:T(8,128)S(1)}, u32[]{:S(2)}, u32[]{:S(2)}) collective-permute-start(f32[256,128]{1,0:T(8,128)S(1)} %bitcast.9), channel_id=1, source_target_pairs={{0,2},{1,3},{2,0},{3,1},{4,6},{5,7},{6,4},{7,5},{8,10},{9,11},{10,... | collective-permute-start | bytes 393224 | tf_op jit(solution)/shard_map/ppermute | solution.py:29
  36.8 11.6 %collective-permute-start.11 = (f32[256,128]{1,0:T(8,128)S(1)}, f32[256,128]{1,0:T(8,128)S(1)}, u32[]{:S(2)}, u32[]{:S(2)}) collective-permute-start(f32[256,128]{1,0:T(8,128)S(1)} %bitcast.10), channel_id=1, source_target_pairs={{0,4},{1,5},{2,6},{3,7},{4,0},{5,1},{6,2},{7,3},{8,12},{9,13},{10,... | collective-permute-start | bytes 393224 | tf_op jit(solution)/shard_map/ppermute | solution.py:29
  39.4 9.0 %collective-permute-start.12 = (f32[256,128]{1,0:T(8,128)S(1)}, f32[256,128]{1,0:T(8,128)S(1)}, u32[]{:S(2)}, u32[]{:S(2)}) collective-permute-start(f32[256,128]{1,0:T(8,128)S(1)} %bitcast.11), channel_id=1, source_target_pairs={{0,6},{1,7},{2,4},{3,5},{4,2},{5,3},{6,0},{7,1},{8,14},{9,15},{10,... | collective-permute-start | bytes 393224 | tf_op jit(solution)/shard_map/ppermute | solution.py:29
  40.5 4.7 %collective-permute-start.13 = (f32[200,128]{1,0:T(8,128)S(1)}, f32[200,128]{1,0:T(8,128)S(1)}, u32[]{:S(2)}, u32[]{:S(2)}) collective-permute-start(f32[200,128]{1,0:T(8,128)S(1)} %get-tuple-element.28.mine), channel_id=1, source_target_pairs={{0,8},{8,0},{16,24},{24,16},{1,9},{9,1},{17,25},{25,17},{2,10},{10... | collective-permute-start | bytes 307208 | tf_op jit(solution)/shard_map/ppermute | solution.py:29
  48.5 2.0 %collective-permute-start.17 = (f32[16,64,128]{2,1,0:T(8,128)S(1)}, f32[16,64,128]{2,1,0:T(8,128)S(1)}, u32[]{:S(2)}, u32[]{:S(2)}) collective-permute-start(f32[16,64,128]{2,1,0:T(8,128)S(1)} %pass_on.1), channel_id=1, source_target_pairs={{0,1},{1,0},{2,3},{3,2},{4,5},{5,4},{6,7},{7,6},{8,9},{9,8},{10,11... | collective-permute-start | bytes 1572872 | tf_op jit(solution)/shard_map/ppermute | solution.py:29
  48.6 5.5 %collective-permute-start.14 = (f32[1024,128]{1,0:T(8,128)S(1)}, f32[1024,128]{1,0:T(8,128)S(1)}, u32[]{:S(2)}, u32[]{:S(2)}) collective-permute-start(f32[1024,128]{1,0:T(8,128)S(1)} %join.5.refs_1_), channel_id=1, source_target_pairs={{0,1},{1,0},{2,3},{3,2},{4,5},{5,4},{6,7},{7,6},{8,9},{9,8},{10,11... | collective-permute-start | bytes 1572872 | tf_op jit(solution)/shard_map/ppermute | solution.py:29
  50.5 11.3 %collective-permute-start.18 = (f32[8,64,128]{2,1,0:T(8,128)S(1)}, f32[8,64,128]{2,1,0:T(8,128)S(1)}, u32[]{:S(2)}, u32[]{:S(2)}) collective-permute-start(f32[8,64,128]{2,1,0:T(8,128)S(1)} %add_upper.5), channel_id=1, source_target_pairs={{0,2},{1,3},{2,0},{3,1},{4,6},{5,7},{6,4},{7,5},{8,10},{9,11},{10,... | collective-permute-start | bytes 786440 | tf_op jit(solution)/shard_map/ppermute | solution.py:29
  52.5 6.1 %collective-permute-start.15 = (f32[328,128]{1,0:T(8,128)S(1)}, f32[328,128]{1,0:T(8,128)S(1)}, u32[]{:S(2)}, u32[]{:S(2)}) collective-permute-start(f32[328,128]{1,0:T(8,128)S(1)} %merge_side.6.refs_4_.mine), channel_id=1, source_target_pairs={{0,16},{8,24},{16,0},{24,8},{1,17},{9,25},{17,1},{25,9},{2,18},{10... | collective-permute-start | bytes 503816 | tf_op jit(solution)/shard_map/ppermute | solution.py:29
  60.4 1.3 %collective-permute-start.16 = (f32[136,128]{1,0:T(8,128)S(1)}, f32[136,128]{1,0:T(8,128)S(1)}, u32[]{:S(2)}, u32[]{:S(2)}) collective-permute-start(f32[136,128]{1,0:T(8,128)S(1)} %get-tuple-element.32.extra), channel_id=1, source_target_pairs={{0,1},{1,0},{2,3},{3,2},{4,5},{5,4},{6,7},{7,6},{8,9},{9,8},{10,11... | collective-permute-start | bytes 208904 | tf_op jit(solution)/shard_map/ppermute | solution.py:29
  61.8 4.4 %collective-permute-start.19 = (f32[136,128]{1,0:T(8,128)S(1)}, f32[136,128]{1,0:T(8,128)S(1)}, u32[]{:S(2)}, u32[]{:S(2)}) collective-permute-start(f32[136,128]{1,0:T(8,128)S(1)} %settle.1.extra), channel_id=1, source_target_pairs={{0,2},{1,3},{2,0},{3,1},{4,6},{5,7},{6,4},{7,5},{8,10},{9,11},{10,... | collective-permute-start | bytes 208904 | tf_op jit(solution)/shard_map/ppermute | solution.py:29
  66.2 5.0 %collective-permute-start.20 = (f32[72,128]{1,0:T(8,128)S(1)}, f32[72,128]{1,0:T(8,128)S(1)}, u32[]{:S(2)}, u32[]{:S(2)}) collective-permute-start(f32[72,128]{1,0:T(8,128)S(1)} %get-tuple-element.35.sums), channel_id=1, source_target_pairs={{0,4},{1,5},{2,6},{3,7},{4,0},{5,1},{6,2},{7,3},{8,12},{9,13},{10,... | collective-permute-start | bytes 110600 | tf_op jit(solution)/shard_map/ppermute | solution.py:29
  71.4 10.3 %collective-permute-start.23 = (f32[5,64,128]{2,1,0:T(8,128)S(1)}, f32[5,64,128]{2,1,0:T(8,128)S(1)}, u32[]{:S(2)}, u32[]{:S(2)}) collective-permute-start(f32[5,64,128]{2,1,0:T(8,128)S(1)} %get-tuple-element.43), channel_id=1, source_target_pairs={{0,6},{1,7},{2,4},{3,5},{4,2},{5,3},{6,0},{7,1},{8,14},{9,15},{10,... | collective-permute-start | bytes 491528 | tf_op jit(solution)/shard_map/ppermute | solution.py:29
  73.4 4.5 %collective-permute-start.21 = (f32[32,128]{1,0:T(8,128)S(1)}, f32[32,128]{1,0:T(8,128)S(1)}, u32[]{:S(2)}, u32[]{:S(2)}) collective-permute-start(f32[32,128]{1,0:T(8,128)S(1)} %get-tuple-element.36.refs_0_), channel_id=1, source_target_pairs={{0,8},{8,0},{16,24},{24,16},{1,9},{9,1},{17,25},{25,17},{2,10},{10... | collective-permute-start | bytes 49160 | tf_op jit(solution)/shard_map/ppermute | solution.py:29
  77.9 3.8 %collective-permute-start.22 = (f32[32,128]{1,0:T(8,128)S(1)}, f32[32,128]{1,0:T(8,128)S(1)}, u32[]{:S(2)}, u32[]{:S(2)}) collective-permute-start(f32[32,128]{1,0:T(8,128)S(1)} %add_whole.2.refs_0_), channel_id=1, source_target_pairs={{0,16},{8,24},{16,0},{24,8},{1,17},{9,25},{17,1},{25,9},{2,18},{10... | collective-permute-start | bytes 49160 | tf_op jit(solution)/shard_map/ppermute | solution.py:29

commit v7 on v6

--- a/solution.py
+++ b/solution.py
@@ -52,8 +52,15 @@
 def times_tile(rows, tile, dims):
     count = rows.shape[0] // 2
     high, low = split(tile)
-    both = dot16(rows, high, dims)
-    return both[:count] + both[count:] + dot16(rows[:count], low, dims)
+    left = jnp.concatenate([rows[:count], rows[count:], rows[:count]], axis=1)
+    return dot16(left, jnp.concatenate([high, high, low], axis=dims[0][1][0]), dims)
+
+
+def dot24(left, right):
+    high, low = split(left)
+    other_high, other_low = split(right)
+    left = jnp.concatenate([high, low, high], axis=1)
+    return dot16(left, jnp.concatenate([other_high, other_high, other_low], axis=1), right_t)
 
 
 def pack(gram):
@@ -206,22 +213,21 @@
                 rows_of[first + k] = split_rows(piece[k * count : (k + 1) * count])
         gram[...] = jnp.zeros_like(gram)
 
-    direct = None
+    left, right = [], []
     for t in range(tiles.shape[1]):
         rows = rows_of[place_of(col[t, slot])]
+        rows = jnp.where(t < load[slot], rows, jnp.zeros_like(rows))
         high, low = split(tiles[0, t])
-        alive = live(load, slot, t)
-        both = alive * dot16(rows, high, right_t)
-        rest = alive * dot16(rows[:count], low, right_t)
-        direct = (both, rest) if direct is None else (direct[0] + both, direct[1] + rest)
-    direct = direct[0][:count] + direct[0][count:] + direct[1]
+        left += [rows[:count], rows[count:], rows[:count]]
+        right += [high, high, low]
+    direct = dot16(jnp.concatenate(left, axis=1), jnp.concatenate(right, axis=1), right_t)
     value = vectors[s]
     near_value = times_tile(split_rows(value), diag[0], right_t)
     near[s] = near_value + direct
     if second:
-        gram[...] += dot32(value, near_value + 2.0 * direct, right_t)
+        gram[...] += dot24(value, near_value + 2.0 * direct)
     else:
-        gram[...] += dot32(value, value, right_t)
+        gram[...] += dot24(value, value)
 
     arriving = new_slot[slot]
     incoming = place_of(arriving)
@@ -307,7 +313,7 @@
         first[k] = value
         if k < edge_rows:
             side[k * count : (k + 1) * count] = value
-        terms = (dot32(vectors[k], value, right_t), dot32(value, value, right_t))
+        terms = (dot24(vectors[k], value), dot24(value, value))
         grams = [term if old is None else old + term for old, term in zip(grams, terms)]
     start = edge_rows * count
     joined, row = join_symmetric(unpack(packed[...]), grams[1])
@@ -333,34 +339,31 @@
     )(vectors, near, *terms, coupling, old_side, packed)
 
 
-def edge_second_kernel(first, near, packed, coupling, side, new_slot, out, extra):
+def edge_second_kernel(first, near, packed, coupling, side, new_slot, more, extra):
     row_count, count = first.shape[:2]
     edge_rows, part_count = coupling.shape[:2]
     half = count // 2
     gram = unpack(packed[...])
-    for k in range(row_count):
-        value = near[k]
-        if k < edge_rows:
-            more = crossed(side, coupling, k)
-            gram = gram + dot32(first[k], more, right_t)
-            value = value + more
-        out[k] = value
+    for k in range(edge_rows):
+        value = crossed(side, coupling, k)
+        gram = gram + dot24(first[k], value)
+        more[k] = value
     start = part_count * edge_rows * count
     joined, row = join_symmetric(unpack(side[start + half : start + 2 * half]), sym(gram))
     extra[:count] = jnp.concatenate([unpack(side[start : start + half]), joined], axis=1)
     row = jnp.concatenate([jnp.zeros_like(row), row], axis=1)
     extra[count : count + 8] = side[start + 2 * half :] + jnp.broadcast_to(row, (8, 2 * count))
     slot = first_slot(row_count)
-    for k in range(row_count):
+    for k in range(edge_rows, row_count):
 
         @pl.when(new_slot[slot + k] != slot + k)
         def _(k=k):
-            extra[count + 8 :] = out[k]
+            extra[count + 8 :] = near[k]
 
 
 def edge_second(first, near, packed, coupling, side, new_slot):
     count, order = first.shape[1:]
-    shapes = [near.shape, (2 * count + 8, order)]
+    shapes = [(coupling.shape[0], count, order), (2 * count + 8, order)]
     return pl.pallas_call(
         edge_second_kernel,
         out_shape=[jax.ShapeDtypeStruct(shape, f32) for shape in shapes],
@@ -475,7 +478,7 @@
     )(*operands)
 
 
-def final_kernel(gram, solved, following, moving, first, near, new_slot, row, *refs):
+def final_kernel(gram, solved, following, moving, first, near, more, new_slot, row, *refs):
     last_row, flags, *terms, solution, resid = refs
     row_count, count = moving.shape[:2]
     arrived = jnp.where(flags[flags.shape[0] - 8 :][:1] > 0.5, last_row[0], row[...])
@@ -495,6 +498,8 @@
     for k in range(row_count):
         stays = new_slot[slot + k] == slot + k
         second = jnp.where(stays, near[k], arrived)
+        if k < more.shape[0]:
+            second = second + more[k]
         for ref in terms:
             second = second + ref[k]
         basis.append(jnp.concatenate([moving[k], first[k], second], axis=0))
@@ -505,18 +510,18 @@
         resid[k] = both[count:, k * order : (k + 1) * order]
 
 
-def final(gram, solved, following, moving, first, near, new_slot, row, flags, terms):
+def final(gram, solved, following, moving, first, near, more, new_slot, row, flags, terms):
     block = pl.BlockSpec(near.shape, lambda s: (0, 0, 0))
     last = pl.BlockSpec((1,) + near.shape[1:], lambda s: (terms[-1].shape[0] - 1, 0, 0))
     return pl.pallas_call(
         final_kernel,
         grid=(1,),
         out_shape=[jax.ShapeDtypeStruct(near.shape, f32)] * 2,
-        in_specs=[vmem] * 6 + [smem, vmem, last, vmem] + [block] * len(terms),
+        in_specs=[vmem] * 7 + [smem, vmem, last, vmem] + [block] * len(terms),
         out_specs=[vmem] * 2,
         compiler_params=params(),
         name="final",
-    )(gram, solved, following, moving, first, near, new_slot, row, terms[-1], flags, *terms)
+    )(gram, solved, following, moving, first, near, more, new_slot, row, terms[-1], flags, *terms)
 
 
 def add_kernel(count, *refs):
@@ -743,7 +748,7 @@
     terms.append(swap(add_upper(terms, rows), "bulk", masks[0]))
     near, moved, packed = near_part(panel, first, offdiag_blocks, diag_tiles, *indices, True)
     side = merge_side(side, other_side, half_edges, near)
-    near, extra = edge_second(first, near, packed, coupling, side, new_slot)
+    more, extra = edge_second(first, near, packed, coupling, side, new_slot)
 
     sums = count + 8
     extra = settle(extra, swap(extra, "bulk", 1), flags, 0, sums, terms[-1])
@@ -765,7 +770,7 @@
         gram = add_whole(gram, partner, *([solved] if mask == 1 else []))
         mask *= 2
     return tuple(
-        final(gram, solved, following, moving, moved, near, new_slot, row, flags, terms)
+        final(gram, solved, following, moving, moved, near, more, new_slot, row, flags, terms)
     )
 
 

time: 86.8 us -> 86.3 us (level)
  Pallas kernels: 28.2 us -> 26.3 us
  starting transfers between devices: 30.7 us -> 31.9 us
    ppermute x24, starting transfers between devices: 30.7 us -> 31.9 us  [swap(): return lax.ppermute(value, axis, pairs)]
    pallas_call x2, Pallas kernels: 8.61 us -> 7.36 us  [near_part(): pl.pallas_call(functools.partial(near_kernel, bulk_count, len(panel), sec...]
  transfers between devices with their start and end apart: 24 -> 24, of which waited for: 11 -> 12; matrix products, arithmetic and copies ran while one was open for 0% -> 0% of each run, Pallas kernels for 20% -> 18%
where the time goes in v7:
time: 86.3 us; the launch traced here: 86 us
  starting transfers between devices  31.9 us (37%)
  Pallas kernels  26.3 us (30%)
  waiting for transfers between devices  24.7 us (29%)
  local copies, waits for them, and re-layouts  2.12 us (2%)
  between operations  0.9 us (1%)
    ppermute x24, starting transfers between devices, swap(): return lax.ppermute(value, axis, pairs)  31.9 us
    ppermute x24, waiting for transfers between devices, swap(): return lax.ppermute(value, axis, pairs)  24.7 us
    pallas_call x2, Pallas kernels, near_part(): pl.pallas_call(functools.partial(near_kernel, bulk_count, len(panel), sec...  7.36 us
    pallas_call x2, Pallas kernels, returned(): pl.pallas_call(functools.partial(returned_kernel, bulk_count, moved), gri...  6.89 us
    pallas_call x1, Pallas kernels, final(): pl.pallas_call(final_kernel, grid=(1,), out_shape=[jax.ShapeDtypeStruct(n...  4.81 us
    pallas_call x2, Pallas kernels, small_call(): pl.pallas_call(kernel, out_shape=jax.ShapeDtypeStruct((matrices, count, c...  4.32 us
    unnamed x20, local copies, waits for them, and re-layouts  2.12 us
  transfers between devices with their start and end apart: 24, of which 12 were waited for; matrix products, arithmetic and copies ran while one was open for 0% of the time, Pallas kernels for 18%

profile of v7, /device:TPU:0, one launch (start us, length us, event | category | flops | bytes accessed | tf_op | source)
XLA Modules:
  0.0 86.0 jit_solution(3048070855807392444)
XLA Ops:
  0.7 4.6 %returned.1 = (f32[16,64,128]{2,1,0:T(8,128)}, f32[16,64,128]{2,1,0:T(8,128)}) custom-call(f32[4,64,128]{2,1,0:T(8,128)} %vectors.3, f32[4,11,128,128]{3,2,1,0:T(8,128)} %refs_6_.3, s32[11,128]{1,0:T(8,128)} %bitcast.16, s32[128]{0:T(128)} %refs_9_.1, s32[128]{0:T(128)} %new_slot.7), custom_call_target="tpu_custom_call" | custom-call | tf_op jit(solution)/shard_map/returned/pallas_call | solution.py:171
  5.3 0.5 collective-permute-start.6
  5.8 3.7 %collective-permute-start.1 = (f32[256,128]{1,0:T(8,128)S(1)}, f32[256,128]{1,0:T(8,128)S(1)}, u32[]{:S(2)}, u32[]{:S(2)}) collective-permute-start(f32[256,128]{1,0:T(8,128)S(1)} %bitcast.4), channel_id=1, source_target_pairs={{0,4},{1,5},{2,6},{3,7},{4,0},{5,1},{6,2},{7,3},{8,12},{9,13},{10,... | collective-permute-start | bytes 393224 | tf_op jit(solution)/shard_map/ppermute | solution.py:29
  9.4 1.3 %collective-permute-start.2 = (f32[256,128]{1,0:T(8,128)S(1)}, f32[256,128]{1,0:T(8,128)S(1)}, u32[]{:S(2)}, u32[]{:S(2)}) collective-permute-start(f32[256,128]{1,0:T(8,128)S(1)} %bitcast.5), channel_id=1, source_target_pairs={{0,6},{1,7},{2,4},{3,5},{4,2},{5,3},{6,0},{7,1},{8,14},{9,15},{10,... | collective-permute-start | bytes 393224 | tf_op jit(solution)/shard_map/ppermute | solution.py:29
  10.8 0.2 collective-permute-start
  11.0 1.0 %copy-done.1 = f32[16,64,128]{2,1,0:T(8,128)S(1)} copy-done((f32[16,64,128]{2,1,0:T(8,128)S(1)}, f32[16,64,128]{2,1,0:T(8,128)}, u32[]{:S(2)}) %copy-start.1) | copy-done | bytes 524312
  12.1 1.9 %collective-permute-start.7 = (f32[8,64,128]{2,1,0:T(8,128)S(1)}, f32[8,64,128]{2,1,0:T(8,128)S(1)}, u32[]{:S(2)}, u32[]{:S(2)}) collective-permute-start(f32[8,64,128]{2,1,0:T(8,128)S(1)} %add_upper.3), channel_id=1, source_target_pairs={{0,2},{1,3},{2,0},{3,1},{4,6},{5,7},{6,4},{7,5},{8,10},{9,11},{10,... | collective-permute-start | bytes 786440 | tf_op jit(solution)/shard_map/ppermute | solution.py:29
  13.9 1.5 %collective-permute-start.4 = (f32[128,128]{1,0:T(8,128)S(1)}, f32[128,128]{1,0:T(8,128)S(1)}, u32[]{:S(2)}, u32[]{:S(2)}) collective-permute-start(f32[128,128]{1,0:T(8,128)S(1)} %bitcast.14), channel_id=1, source_target_pairs={{0,8},{8,0},{16,24},{24,16},{1,9},{9,1},{17,25},{25,17},{2,10},{10... | collective-permute-start | bytes 196616 | tf_op jit(solution)/shard_map/ppermute | solution.py:29
  15.4 2.8 %collective-permute-done.4.other = f32[128,128]{1,0:T(8,128)S(1)} collective-permute-done((f32[128,128]{1,0:T(8,128)S(1)}, f32[128,128]{1,0:T(8,128)S(1)}, u32[]{:S(2)}, u32[]{:S(2)}) %collective-permute-start.4) | collective-permute-done | bytes 65568 | tf_op jit(solution)/shard_map/ppermute | solution.py:29
  18.2 1.2 %collective-permute-done.1.refs_0_.refs_2_ = f32[256,128]{1,0:T(8,128)S(1)} collective-permute-done((f32[256,128]{1,0:T(8,128)S(1)}, f32[256,128]{1,0:T(8,128)S(1)}, u32[]{:S(2)}, u32[]{:S(2)}) %collective-permute-start.1) | collective-permute-done | bytes 131104 | tf_op jit(solution)/shard_map/ppermute | solution.py:29
  19.4 0.1 collective-permute-start.5
  19.5 2.0 %collective-permute-done.refs_1_ = f32[256,128]{1,0:T(8,128)S(1)} collective-permute-done((f32[256,128]{1,0:T(8,128)S(1)}, f32[256,128]{1,0:T(8,128)S(1)}, u32[]{:S(2)}, u32[]{:S(2)}) %collective-permute-start) | collective-permute-done | bytes 131104 | tf_op jit(solution)/shard_map/ppermute | solution.py:29
  21.6 0.1 collective-permute-start.3
  21.6 1.7 %collective-permute-start.9 = (f32[256,128]{1,0:T(8,128)S(1)}, f32[256,128]{1,0:T(8,128)S(1)}, u32[]{:S(2)}, u32[]{:S(2)}) collective-permute-start(f32[256,128]{1,0:T(8,128)S(1)} %merge_side.4.refs_2_.mine), channel_id=1, source_target_pairs={{0,16},{8,24},{16,0},{24,8},{1,17},{9,25},{17,1},{25,9},{2,18},{10... | collective-permute-start | bytes 393224 | tf_op jit(solution)/shard_map/ppermute | solution.py:29
  23.3 2.8 %collective-permute-done.7.refs_2_.refs_1_ = f32[8,64,128]{2,1,0:T(8,128)S(1)} collective-permute-done((f32[8,64,128]{2,1,0:T(8,128)S(1)}, f32[8,64,128]{2,1,0:T(8,128)S(1)}, u32[]{:S(2)}, u32[]{:S(2)}) %collective-permute-start.7) | collective-permute-done | bytes 262176 | tf_op jit(solution)/shard_map/ppermute | solution.py:29
  26.1 1.0 %copy-done.2 = f32[16,64,128]{2,1,0:T(8,128)S(1)} copy-done((f32[16,64,128]{2,1,0:T(8,128)S(1)}, f32[16,64,128]{2,1,0:T(8,128)}, u32[]{:S(2)}) %copy-start.2) | copy-done | bytes 524312
  27.2 3.6 %collective-permute-start.8 = (f32[4,64,128]{2,1,0:T(8,128)S(1)}, f32[4,64,128]{2,1,0:T(8,128)S(1)}, u32[]{:S(2)}, u32[]{:S(2)}) collective-permute-start(f32[4,64,128]{2,1,0:T(8,128)S(1)} %add_upper.4), channel_id=1, source_target_pairs={{0,6},{1,7},{2,4},{3,5},{4,2},{5,3},{6,0},{7,1},{8,14},{9,15},{10,... | collective-permute-start | bytes 393224 | tf_op jit(solution)/shard_map/ppermute | solution.py:29
  30.9 3.4 %near_first.1 = (f32[4,64,128]{2,1,0:T(8,128)S(1)}, f32[4,64,128]{2,1,0:T(8,128)S(1)}, f32[32,128]{1,0:T(8,128)S(1)}, f32[24,128]{1,0:T(8,128)S(1)}) custom-call(f32[256,128]{1,0:T(8,128)S(1)} %bitcast.8, f32[256,128]{1,0:T(8,128)S(1)} %collective-permute-done.refs_1_, f32[256,128]{1,0:T(8,128)S(1)} %collective-permute-done.1.refs_0_.refs_2_, ...), custom_call_target="tpu_custom_call" | custom-call | tf_op jit(solution)/shard_map/near_first/pallas_call | solution.py:264
  34.4 0.9 %gather_first.1 = (f32[4,64,128]{2,1,0:T(8,128)S(1)}, f32[200,128]{1,0:T(8,128)S(1)}) custom-call(f32[4,64,128]{2,1,0:T(8,128)S(1)} %copy-done.4, f32[4,64,128]{2,1,0:T(8,128)S(1)} %get-tuple-element.23.refs_0_.near, f32[16,64,128]{2,1,0:T(8,128)S(1)} %copy-done.3, f32[16,64,128]{2,1,0:T(8,128)S(1)} %collective-permute-done.6.refs_1_.refs_0_, ...), custom_call_target="tpu_custom_call" | custom-call | tf_op jit(solution)/shard_map/gather_first/pallas_call | solution.py:331
  35.3 1.3 %collective-permute-start.10 = (f32[256,128]{1,0:T(8,128)S(1)}, f32[256,128]{1,0:T(8,128)S(1)}, u32[]{:S(2)}, u32[]{:S(2)}) collective-permute-start(f32[256,128]{1,0:T(8,128)S(1)} %bitcast.9), channel_id=1, source_target_pairs={{0,2},{1,3},{2,0},{3,1},{4,6},{5,7},{6,4},{7,5},{8,10},{9,11},{10,... | collective-permute-start | bytes 393224 | tf_op jit(solution)/shard_map/ppermute | solution.py:29
  36.5 2.6 %collective-permute-start.11 = (f32[256,128]{1,0:T(8,128)S(1)}, f32[256,128]{1,0:T(8,128)S(1)}, u32[]{:S(2)}, u32[]{:S(2)}) collective-permute-start(f32[256,128]{1,0:T(8,128)S(1)} %bitcast.10), channel_id=1, source_target_pairs={{0,4},{1,5},{2,6},{3,7},{4,0},{5,1},{6,2},{7,3},{8,12},{9,13},{10,... | collective-permute-start | bytes 393224 | tf_op jit(solution)/shard_map/ppermute | solution.py:29
  39.1 0.6 collective-permute-start.12
  39.7 1.5 %collective-permute-start.13 = (f32[200,128]{1,0:T(8,128)S(1)}, f32[200,128]{1,0:T(8,128)S(1)}, u32[]{:S(2)}, u32[]{:S(2)}) collective-permute-start(f32[200,128]{1,0:T(8,128)S(1)} %get-tuple-element.28.mine), channel_id=1, source_target_pairs={{0,8},{8,0},{16,24},{24,16},{1,9},{9,1},{17,25},{25,17},{2,10},{10... | collective-permute-start | bytes 307208 | tf_op jit(solution)/shard_map/ppermute | solution.py:29
  41.2 2.3 %returned_moved.1 = (f32[16,64,128]{2,1,0:T(8,128)S(1)}, f32[16,64,128]{2,1,0:T(8,128)S(1)}) custom-call(f32[4,64,128]{2,1,0:T(8,128)S(1)} %get-tuple-element.27.vectors.refs_5_.first, f32[4,11,128,128]{3,2,1,0:T(8,128)S(1)} %copy-done, s32[11,128]{1,0:T(8,128)S(1)} %bitcast.18, s32[128]{0:T(128)S(1)} %copy-done.9, s32[128]{0:T(128)S(1)} %copy-done.8), custom_call_target="tpu_custom_call" | custom-call | tf_op jit(solution)/shard_map/returned_moved/pallas_call | solution.py:171
  43.5 0.9 %collective-permute-done.13.other = f32[200,128]{1,0:T(8,128)S(1)} collective-permute-done((f32[200,128]{1,0:T(8,128)S(1)}, f32[200,128]{1,0:T(8,128)S(1)}, u32[]{:S(2)}, u32[]{:S(2)}) %collective-permute-start.13) | collective-permute-done | bytes 102432 | tf_op jit(solution)/shard_map/ppermute | solution.py:29
  44.4 3.2 %collective-permute-done.11.refs_2_ = f32[256,128]{1,0:T(8,128)S(1)} collective-permute-done((f32[256,128]{1,0:T(8,128)S(1)}, f32[256,128]{1,0:T(8,128)S(1)}, u32[]{:S(2)}, u32[]{:S(2)}) %collective-permute-start.11) | collective-permute-done | bytes 131104 | tf_op jit(solution)/shard_map/ppermute | solution.py:29
  47.6 0.1 collective-permute-start.17
  47.7 0.5 collective-permute-start.14
  48.2 1.4 %collective-permute-done.17.refs_1_.refs_3_ = f32[16,64,128]{2,1,0:T(8,128)S(1)} collective-permute-done((f32[16,64,128]{2,1,0:T(8,128)S(1)}, f32[16,64,128]{2,1,0:T(8,128)S(1)}, u32[]{:S(2)}, u32[]{:S(2)}) %collective-permute-start.17) | collective-permute-done | bytes 524320 | tf_op jit(solution)/shard_map/ppermute | solution.py:29
  49.6 2.0 %collective-permute-start.18 = (f32[8,64,128]{2,1,0:T(8,128)S(1)}, f32[8,64,128]{2,1,0:T(8,128)S(1)}, u32[]{:S(2)}, u32[]{:S(2)}) collective-permute-start(f32[8,64,128]{2,1,0:T(8,128)S(1)} %add_upper.5), channel_id=1, source_target_pairs={{0,2},{1,3},{2,0},{3,1},{4,6},{5,7},{6,4},{7,5},{8,10},{9,11},{10,... | collective-permute-start | bytes 786440 | tf_op jit(solution)/shard_map/ppermute | solution.py:29
  51.7 1.5 %collective-permute-start.15 = (f32[328,128]{1,0:T(8,128)S(1)}, f32[328,128]{1,0:T(8,128)S(1)}, u32[]{:S(2)}, u32[]{:S(2)}) collective-permute-start(f32[328,128]{1,0:T(8,128)S(1)} %merge_side.6.refs_4_.mine), channel_id=1, source_target_pairs={{0,16},{8,24},{16,0},{24,8},{1,17},{9,25},{17,1},{25,9},{2,18},{10... | collective-permute-start | bytes 503816 | tf_op jit(solution)/shard_map/ppermute | solution.py:29
  53.2 3.9 %near_second.1 = (f32[4,64,128]{2,1,0:T(8,128)S(1)}, f32[4,64,128]{2,1,0:T(8,128)S(1)}, f32[32,128]{1,0:T(8,128)S(1)}) custom-call(f32[256,128]{1,0:T(8,128)S(1)} %bitcast.13, f32[256,128]{1,0:T(8,128)S(1)} %collective-permute-done.10.refs_1_, f32[256,128]{1,0:T(8,128)S(1)} %collective-permute-done.11.refs_2_, ...), custom_call_target="tpu_custom_call" | custom-call | tf_op jit(solution)/shard_map/near_second/pallas_call | solution.py:264
  57.1 0.6 collective-permute-done.15.other
  57.7 1.5 %edge_second.1 = (f32[2,64,128]{2,1,0:T(8,128)S(1)}, f32[136,128]{1,0:T(8,128)S(1)}) custom-call(f32[4,64,128]{2,1,0:T(8,128)S(1)} %get-tuple-element.27.vectors.refs_5_.first, f32[4,64,128]{2,1,0:T(8,128)S(1)} %get-tuple-element.30.refs_0_.near, f32[32,128]{1,0:T(8,128)S(1)} %get-tuple-element.31.packed, f32[2,4,128,128]{3,2,1,0:T(8,128)S(1)} %copy-done.5, ...), custom_call_target="tpu_custom_call" | custom-call | tf_op jit(solution)/shard_map/edge_second/pallas_call | solution.py:367
  59.2 0.1 collective-permute-start.16
  59.3 1.2 %collective-permute-done.16.partner = f32[136,128]{1,0:T(8,128)S(1)} collective-permute-done((f32[136,128]{1,0:T(8,128)S(1)}, f32[136,128]{1,0:T(8,128)S(1)}, u32[]{:S(2)}, u32[]{:S(2)}) %collective-permute-start.16) | collective-permute-done | bytes 69664 | tf_op jit(solution)/shard_map/ppermute | solution.py:29
  60.6 0.4 collective-permute-start.19
  61.0 4.0 %collective-permute-done.19.partner = f32[136,128]{1,0:T(8,128)S(1)} collective-permute-done((f32[136,128]{1,0:T(8,128)S(1)}, f32[136,128]{1,0:T(8,128)S(1)}, u32[]{:S(2)}, u32[]{:S(2)}) %collective-permute-start.19) | collective-permute-done | bytes 69664 | tf_op jit(solution)/shard_map/ppermute | solution.py:29
  64.9 1.4 %collective-permute-start.20 = (f32[72,128]{1,0:T(8,128)S(1)}, f32[72,128]{1,0:T(8,128)S(1)}, u32[]{:S(2)}, u32[]{:S(2)}) collective-permute-start(f32[72,128]{1,0:T(8,128)S(1)} %get-tuple-element.35.sums), channel_id=1, source_target_pairs={{0,4},{1,5},{2,6},{3,7},{4,0},{5,1},{6,2},{7,3},{8,12},{9,13},{10,... | collective-permute-start | bytes 110600 | tf_op jit(solution)/shard_map/ppermute | solution.py:29
  66.3 3.7 %collective-permute-done.20.partner = f32[72,128]{1,0:T(8,128)S(1)} collective-permute-done((f32[72,128]{1,0:T(8,128)S(1)}, f32[72,128]{1,0:T(8,128)S(1)}, u32[]{:S(2)}, u32[]{:S(2)}) %collective-permute-start.20) | collective-permute-done | bytes 36896 | tf_op jit(solution)/shard_map/ppermute | solution.py:29
  70.1 0.2 last_gram.1
  70.3 2.5 %collective-permute-start.23 = (f32[5,64,128]{2,1,0:T(8,128)S(1)}, f32[5,64,128]{2,1,0:T(8,128)S(1)}, u32[]{:S(2)}, u32[]{:S(2)}) collective-permute-start(f32[5,64,128]{2,1,0:T(8,128)S(1)} %get-tuple-element.43), channel_id=1, source_target_pairs={{0,6},{1,7},{2,4},{3,5},{4,2},{5,3},{6,0},{7,1},{8,14},{9,15},{10,... | collective-permute-start | bytes 491528 | tf_op jit(solution)/shard_map/ppermute | solution.py:29
  72.8 1.5 %collective-permute-start.21 = (f32[32,128]{1,0:T(8,128)S(1)}, f32[32,128]{1,0:T(8,128)S(1)}, u32[]{:S(2)}, u32[]{:S(2)}) collective-permute-start(f32[32,128]{1,0:T(8,128)S(1)} %get-tuple-element.36.refs_0_), channel_id=1, source_target_pairs={{0,8},{8,0},{16,24},{24,16},{1,9},{9,1},{17,25},{25,17},{2,10},{10... | collective-permute-start | bytes 49160 | tf_op jit(solution)/shard_map/ppermute | solution.py:29
  74.3 3.0 %first_solves.1.refs_2_.solved = f32[2,64,64]{2,1,0:T(8,128)S(1)} custom-call(f32[72,128]{1,0:T(8,128)S(1)} %get-tuple-element.37.extra.refs_3_), custom_call_target="tpu_custom_call" | custom-call | tf_op jit(solution)/shard_map/first_solves/pallas_call | solution.py:471
  77.4 1.6 %collective-permute-start.22 = (f32[32,128]{1,0:T(8,128)S(1)}, f32[32,128]{1,0:T(8,128)S(1)}, u32[]{:S(2)}, u32[]{:S(2)}) collective-permute-start(f32[32,128]{1,0:T(8,128)S(1)} %add_whole.2.refs_0_), channel_id=1, source_target_pairs={{0,16},{8,24},{16,0},{24,8},{1,17},{9,25},{17,1},{25,9},{2,18},{10... | collective-permute-start | bytes 49160 | tf_op jit(solution)/shard_map/ppermute | solution.py:29
  79.0 1.3 %next_gram.1.following = f32[3,64,64]{2,1,0:T(8,128)S(1)} custom-call(f32[72,128]{1,0:T(8,128)S(1)} %get-tuple-element.37.extra.refs_3_, f32[2,64,64]{2,1,0:T(8,128)S(1)} %first_solves.1.refs_2_.solved), custom_call_target="tpu_custom_call" | custom-call | tf_op jit(solution)/shard_map/next_gram/pallas_call | solution.py:471
  80.2 0.9 %collective-permute-done.22.refs_1_ = f32[32,128]{1,0:T(8,128)S(1)} collective-permute-done((f32[32,128]{1,0:T(8,128)S(1)}, f32[32,128]{1,0:T(8,128)S(1)}, u32[]{:S(2)}, u32[]{:S(2)}) %collective-permute-start.22) | collective-permute-done | bytes 16416 | tf_op jit(solution)/shard_map/ppermute | solution.py:29
  81.2 4.8 %final.1 = (f32[4,64,128]{2,1,0:T(8,128)}, f32[4,64,128]{2,1,0:T(8,128)}) custom-call(f32[32,128]{1,0:T(8,128)S(1)} %add_whole.3.gram, f32[2,64,64]{2,1,0:T(8,128)S(1)} %first_solves.1.refs_2_.solved, f32[3,64,64]{2,1,0:T(8,128)S(1)} %next_gram.1.following, f32[4,64,128]{2,1,0:T(8,128)S(1)} %get-tuple-element.38.moving, ...), custom_call_target="tpu_custom_call" | custom-call | tf_op jit(solution)/shard_map/final/pallas_call | solution.py:516
  (47 shorter events, 0.4 us)
Async XLA Ops:
  0.6 5.1 %copy-start.4 = (f32[4,64,128]{2,1,0:T(8,128)S(1)}, f32[4,64,128]{2,1,0:T(8,128)}, u32[]{:S(2)}) copy-start(f32[4,64,128]{2,1,0:T(8,128)} %vectors.3) | copy-start | bytes 393220
  0.6 30.2 %copy-start.6 = (f32[4,128,128]{2,1,0:T(8,128)S(1)}, f32[4,128,128]{2,1,0:T(8,128)}, u32[]{:S(2)}) copy-start(f32[4,128,128]{2,1,0:T(8,128)} %refs_7_.3) | copy-start | bytes 786436
  0.7 30.2 %copy-start.7 = (s32[128,11]{0,1:T(8,128)S(1)}, s32[128,11]{0,1:T(8,128)}, u32[]{:S(2)}) copy-start(s32[128,11]{0,1:T(8,128)} %param.11) | copy-start | bytes 16900
  0.7 30.2 %copy-start.8 = (s32[128]{0:T(128)S(1)}, s32[128]{0:T(128)}, u32[]{:S(2)}) copy-start(s32[128]{0:T(128)} %new_slot.7) | copy-start | bytes 1540
  0.7 30.2 %copy-start.9 = (s32[128]{0:T(128)S(1)}, s32[128]{0:T(128)}, u32[]{:S(2)}) copy-start(s32[128]{0:T(128)} %refs_9_.1) | copy-start | bytes 1540
  5.3 25.6 %copy-start = (f32[4,11,128,128]{3,2,1,0:T(8,128)S(1)}, f32[4,11,128,128]{3,2,1,0:T(8,128)}, u32[]{:S(2)}) copy-start(f32[4,11,128,128]{3,2,1,0:T(8,128)} %refs_6_.3) | copy-start | bytes 8650756
  5.3 5.7 %collective-permute-start.6 = (f32[16,64,128]{2,1,0:T(8,128)}, f32[16,64,128]{2,1,0:T(8,128)S(1)}, u32[]{:S(2)}, u32[]{:S(2)}) collective-permute-start(f32[16,64,128]{2,1,0:T(8,128)} %get-tuple-element.25), channel_id=1, source_target_pairs={{0,1},{1,0},{2,3},{3,2},{4,5},{5,4},{6,7},{7,6},{8,9},{9,8},{10,11... | collective-permute-start | bytes 1572872 | tf_op jit(solution)/shard_map/ppermute | solution.py:29
  5.8 13.7 %collective-permute-start.1 = (f32[256,128]{1,0:T(8,128)S(1)}, f32[256,128]{1,0:T(8,128)S(1)}, u32[]{:S(2)}, u32[]{:S(2)}) collective-permute-start(f32[256,128]{1,0:T(8,128)S(1)} %bitcast.4), channel_id=1, source_target_pairs={{0,4},{1,5},{2,6},{3,7},{4,0},{5,1},{6,2},{7,3},{8,12},{9,13},{10,... | collective-permute-start | bytes 393224 | tf_op jit(solution)/shard_map/ppermute | solution.py:29
  9.4 10.0 %collective-permute-start.2 = (f32[256,128]{1,0:T(8,128)S(1)}, f32[256,128]{1,0:T(8,128)S(1)}, u32[]{:S(2)}, u32[]{:S(2)}) collective-permute-start(f32[256,128]{1,0:T(8,128)S(1)} %bitcast.5), channel_id=1, source_target_pairs={{0,6},{1,7},{2,4},{3,5},{4,2},{5,3},{6,0},{7,1},{8,14},{9,15},{10,... | collective-permute-start | bytes 393224 | tf_op jit(solution)/shard_map/ppermute | solution.py:29
  10.8 10.8 %collective-permute-start = (f32[256,128]{1,0:T(8,128)S(1)}, f32[256,128]{1,0:T(8,128)S(1)}, u32[]{:S(2)}, u32[]{:S(2)}) collective-permute-start(f32[256,128]{1,0:T(8,128)S(1)} %bitcast.6), channel_id=1, source_target_pairs={{0,2},{1,3},{2,0},{3,1},{4,6},{5,7},{6,4},{7,5},{8,10},{9,11},{10,... | collective-permute-start | bytes 393224 | tf_op jit(solution)/shard_map/ppermute | solution.py:29
  11.0 1.0 %copy-start.1 = (f32[16,64,128]{2,1,0:T(8,128)S(1)}, f32[16,64,128]{2,1,0:T(8,128)}, u32[]{:S(2)}) copy-start(f32[16,64,128]{2,1,0:T(8,128)} %get-tuple-element.24.refs_0_.keep) | copy-start | bytes 1572868
  12.1 14.0 %collective-permute-start.7 = (f32[8,64,128]{2,1,0:T(8,128)S(1)}, f32[8,64,128]{2,1,0:T(8,128)S(1)}, u32[]{:S(2)}, u32[]{:S(2)}) collective-permute-start(f32[8,64,128]{2,1,0:T(8,128)S(1)} %add_upper.3), channel_id=1, source_target_pairs={{0,2},{1,3},{2,0},{3,1},{4,6},{5,7},{6,4},{7,5},{8,10},{9,11},{10,... | collective-permute-start | bytes 786440 | tf_op jit(solution)/shard_map/ppermute | solution.py:29
  13.9 4.3 %collective-permute-start.4 = (f32[128,128]{1,0:T(8,128)S(1)}, f32[128,128]{1,0:T(8,128)S(1)}, u32[]{:S(2)}, u32[]{:S(2)}) collective-permute-start(f32[128,128]{1,0:T(8,128)S(1)} %bitcast.14), channel_id=1, source_target_pairs={{0,8},{8,0},{16,24},{24,16},{1,9},{9,1},{17,25},{25,17},{2,10},{10... | collective-permute-start | bytes 196616 | tf_op jit(solution)/shard_map/ppermute | solution.py:29
  19.4 11.4 %collective-permute-start.5 = (f32[512,128]{1,0:T(8,128)S(1)}, f32[512,128]{1,0:T(8,128)S(1)}, u32[]{:S(2)}, u32[]{:S(2)}) collective-permute-start(f32[512,128]{1,0:T(8,128)S(1)} %join.4.refs_3_), channel_id=1, source_target_pairs={{0,1},{1,0},{2,3},{3,2},{4,5},{5,4},{6,7},{7,6},{8,9},{9,8},{10,11... | collective-permute-start | bytes 786440 | tf_op jit(solution)/shard_map/ppermute | solution.py:29
  21.6 9.3 %collective-permute-start.3 = (f32[512,128]{1,0:T(8,128)S(1)}, f32[512,128]{1,0:T(8,128)S(1)}, u32[]{:S(2)}, u32[]{:S(2)}) collective-permute-start(f32[512,128]{1,0:T(8,128)S(1)} %join.3), channel_id=1, source_target_pairs={{0,1},{1,0},{2,3},{3,2},{4,5},{5,4},{6,7},{7,6},{8,9},{9,8},{10,11... | collective-permute-start | bytes 786440 | tf_op jit(solution)/shard_map/ppermute | solution.py:29
  21.6 12.7 %collective-permute-start.9 = (f32[256,128]{1,0:T(8,128)S(1)}, f32[256,128]{1,0:T(8,128)S(1)}, u32[]{:S(2)}, u32[]{:S(2)}) collective-permute-start(f32[256,128]{1,0:T(8,128)S(1)} %merge_side.4.refs_2_.mine), channel_id=1, source_target_pairs={{0,16},{8,24},{16,0},{24,8},{1,17},{9,25},{17,1},{25,9},{2,18},{10... | collective-permute-start | bytes 393224 | tf_op jit(solution)/shard_map/ppermute | solution.py:29
  26.1 1.0 %copy-start.2 = (f32[16,64,128]{2,1,0:T(8,128)S(1)}, f32[16,64,128]{2,1,0:T(8,128)}, u32[]{:S(2)}) copy-start(f32[16,64,128]{2,1,0:T(8,128)} %get-tuple-element.24.refs_0_.keep) | copy-start | bytes 1572868
  27.2 7.2 %copy-start.3 = (f32[16,64,128]{2,1,0:T(8,128)S(1)}, f32[16,64,128]{2,1,0:T(8,128)}, u32[]{:S(2)}) copy-start(f32[16,64,128]{2,1,0:T(8,128)} %get-tuple-element.24.refs_0_.keep) | copy-start | bytes 1572868
  27.2 7.2 %copy-start.5 = (f32[2,4,128,128]{3,2,1,0:T(8,128)S(1)}, f32[2,4,128,128]{3,2,1,0:T(8,128)}, u32[]{:S(2)}) copy-start(f32[2,4,128,128]{3,2,1,0:T(8,128)} %coupling.1) | copy-start | bytes 1572868
  27.2 7.1 %collective-permute-start.8 = (f32[4,64,128]{2,1,0:T(8,128)S(1)}, f32[4,64,128]{2,1,0:T(8,128)S(1)}, u32[]{:S(2)}, u32[]{:S(2)}) collective-permute-start(f32[4,64,128]{2,1,0:T(8,128)S(1)} %add_upper.4), channel_id=1, source_target_pairs={{0,6},{1,7},{2,4},{3,5},{4,2},{5,3},{6,0},{7,1},{8,14},{9,15},{10,... | collective-permute-start | bytes 393224 | tf_op jit(solution)/shard_map/ppermute | solution.py:29
  35.3 9.1 %collective-permute-start.10 = (f32[256,128]{1,0:T(8,128)S(1)}, f32[256,128]{1,0:T(8,128)S(1)}, u32[]{:S(2)}, u32[]{:S(2)}) collective-permute-start(f32[256,128]{1,0:T(8,128)S(1)} %bitcast.9), channel_id=1, source_target_pairs={{0,2},{1,3},{2,0},{3,1},{4,6},{5,7},{6,4},{7,5},{8,10},{9,11},{10,... | collective-permute-start | bytes 393224 | tf_op jit(solution)/shard_map/ppermute | solution.py:29
  36.5 11.0 %collective-permute-start.11 = (f32[256,128]{1,0:T(8,128)S(1)}, f32[256,128]{1,0:T(8,128)S(1)}, u32[]{:S(2)}, u32[]{:S(2)}) collective-permute-start(f32[256,128]{1,0:T(8,128)S(1)} %bitcast.10), channel_id=1, source_target_pairs={{0,4},{1,5},{2,6},{3,7},{4,0},{5,1},{6,2},{7,3},{8,12},{9,13},{10,... | collective-permute-start | bytes 393224 | tf_op jit(solution)/shard_map/ppermute | solution.py:29
  39.1 8.5 %collective-permute-start.12 = (f32[256,128]{1,0:T(8,128)S(1)}, f32[256,128]{1,0:T(8,128)S(1)}, u32[]{:S(2)}, u32[]{:S(2)}) collective-permute-start(f32[256,128]{1,0:T(8,128)S(1)} %bitcast.11), channel_id=1, source_target_pairs={{0,6},{1,7},{2,4},{3,5},{4,2},{5,3},{6,0},{7,1},{8,14},{9,15},{10,... | collective-permute-start | bytes 393224 | tf_op jit(solution)/shard_map/ppermute | solution.py:29
  39.7 4.7 %collective-permute-start.13 = (f32[200,128]{1,0:T(8,128)S(1)}, f32[200,128]{1,0:T(8,128)S(1)}, u32[]{:S(2)}, u32[]{:S(2)}) collective-permute-start(f32[200,128]{1,0:T(8,128)S(1)} %get-tuple-element.28.mine), channel_id=1, source_target_pairs={{0,8},{8,0},{16,24},{24,16},{1,9},{9,1},{17,25},{25,17},{2,10},{10... | collective-permute-start | bytes 307208 | tf_op jit(solution)/shard_map/ppermute | solution.py:29
  47.6 2.0 %collective-permute-start.17 = (f32[16,64,128]{2,1,0:T(8,128)S(1)}, f32[16,64,128]{2,1,0:T(8,128)S(1)}, u32[]{:S(2)}, u32[]{:S(2)}) collective-permute-start(f32[16,64,128]{2,1,0:T(8,128)S(1)} %pass_on.1), channel_id=1, source_target_pairs={{0,1},{1,0},{2,3},{3,2},{4,5},{5,4},{6,7},{7,6},{8,9},{9,8},{10,11... | collective-permute-start | bytes 1572872 | tf_op jit(solution)/shard_map/ppermute | solution.py:29
  47.7 5.5 %collective-permute-start.14 = (f32[1024,128]{1,0:T(8,128)S(1)}, f32[1024,128]{1,0:T(8,128)S(1)}, u32[]{:S(2)}, u32[]{:S(2)}) collective-permute-start(f32[1024,128]{1,0:T(8,128)S(1)} %join.5.refs_1_), channel_id=1, source_target_pairs={{0,1},{1,0},{2,3},{3,2},{4,5},{5,4},{6,7},{7,6},{8,9},{9,8},{10,11... | collective-permute-start | bytes 1572872 | tf_op jit(solution)/shard_map/ppermute | solution.py:29
  49.6 10.9 %collective-permute-start.18 = (f32[8,64,128]{2,1,0:T(8,128)S(1)}, f32[8,64,128]{2,1,0:T(8,128)S(1)}, u32[]{:S(2)}, u32[]{:S(2)}) collective-permute-start(f32[8,64,128]{2,1,0:T(8,128)S(1)} %add_upper.5), channel_id=1, source_target_pairs={{0,2},{1,3},{2,0},{3,1},{4,6},{5,7},{6,4},{7,5},{8,10},{9,11},{10,... | collective-permute-start | bytes 786440 | tf_op jit(solution)/shard_map/ppermute | solution.py:29
  51.7 6.0 %collective-permute-start.15 = (f32[328,128]{1,0:T(8,128)S(1)}, f32[328,128]{1,0:T(8,128)S(1)}, u32[]{:S(2)}, u32[]{:S(2)}) collective-permute-start(f32[328,128]{1,0:T(8,128)S(1)} %merge_side.6.refs_4_.mine), channel_id=1, source_target_pairs={{0,16},{8,24},{16,0},{24,8},{1,17},{9,25},{17,1},{25,9},{2,18},{10... | collective-permute-start | bytes 503816 | tf_op jit(solution)/shard_map/ppermute | solution.py:29
  59.2 1.3 %collective-permute-start.16 = (f32[136,128]{1,0:T(8,128)S(1)}, f32[136,128]{1,0:T(8,128)S(1)}, u32[]{:S(2)}, u32[]{:S(2)}) collective-permute-start(f32[136,128]{1,0:T(8,128)S(1)} %get-tuple-element.32.extra), channel_id=1, source_target_pairs={{0,1},{1,0},{2,3},{3,2},{4,5},{5,4},{6,7},{7,6},{8,9},{9,8},{10,11... | collective-permute-start | bytes 208904 | tf_op jit(solution)/shard_map/ppermute | solution.py:29
  60.6 4.4 %collective-permute-start.19 = (f32[136,128]{1,0:T(8,128)S(1)}, f32[136,128]{1,0:T(8,128)S(1)}, u32[]{:S(2)}, u32[]{:S(2)}) collective-permute-start(f32[136,128]{1,0:T(8,128)S(1)} %settle.1.extra), channel_id=1, source_target_pairs={{0,2},{1,3},{2,0},{3,1},{4,6},{5,7},{6,4},{7,5},{8,10},{9,11},{10,... | collective-permute-start | bytes 208904 | tf_op jit(solution)/shard_map/ppermute | solution.py:29
  64.9 5.1 %collective-permute-start.20 = (f32[72,128]{1,0:T(8,128)S(1)}, f32[72,128]{1,0:T(8,128)S(1)}, u32[]{:S(2)}, u32[]{:S(2)}) collective-permute-start(f32[72,128]{1,0:T(8,128)S(1)} %get-tuple-element.35.sums), channel_id=1, source_target_pairs={{0,4},{1,5},{2,6},{3,7},{4,0},{5,1},{6,2},{7,3},{8,12},{9,13},{10,... | collective-permute-start | bytes 110600 | tf_op jit(solution)/shard_map/ppermute | solution.py:29
  70.3 10.9 %collective-permute-start.23 = (f32[5,64,128]{2,1,0:T(8,128)S(1)}, f32[5,64,128]{2,1,0:T(8,128)S(1)}, u32[]{:S(2)}, u32[]{:S(2)}) collective-permute-start(f32[5,64,128]{2,1,0:T(8,128)S(1)} %get-tuple-element.43), channel_id=1, source_target_pairs={{0,6},{1,7},{2,4},{3,5},{4,2},{5,3},{6,0},{7,1},{8,14},{9,15},{10,... | collective-permute-start | bytes 491528 | tf_op jit(solution)/shard_map/ppermute | solution.py:29
  72.8 4.5 %collective-permute-start.21 = (f32[32,128]{1,0:T(8,128)S(1)}, f32[32,128]{1,0:T(8,128)S(1)}, u32[]{:S(2)}, u32[]{:S(2)}) collective-permute-start(f32[32,128]{1,0:T(8,128)S(1)} %get-tuple-element.36.refs_0_), channel_id=1, source_target_pairs={{0,8},{8,0},{16,24},{24,16},{1,9},{9,1},{17,25},{25,17},{2,10},{10... | collective-permute-start | bytes 49160 | tf_op jit(solution)/shard_map/ppermute | solution.py:29
  77.4 3.8 %collective-permute-start.22 = (f32[32,128]{1,0:T(8,128)S(1)}, f32[32,128]{1,0:T(8,128)S(1)}, u32[]{:S(2)}, u32[]{:S(2)}) collective-permute-start(f32[32,128]{1,0:T(8,128)S(1)} %add_whole.2.refs_0_), channel_id=1, source_target_pairs={{0,16},{8,24},{16,0},{24,8},{1,17},{9,25},{17,1},{25,9},{2,18},{10... | collective-permute-start | bytes 49160 | tf_op jit(solution)/shard_map/ppermute | solution.py:29

commit v8 on v7

--- a/solution.py
+++ b/solution.py
@@ -17,7 +17,7 @@
 smem = pl.BlockSpec(memory_space=pltpu.SMEM)
 anywhere = pl.BlockSpec(memory_space=pl.ANY)
 vmem_bytes = 40 * 2**20
-all_vmem = 60 * 2**20
+all_vmem = 56 * 2**20
 
 
 def params(limit=vmem_bytes):
@@ -171,7 +171,7 @@
     return pl.pallas_call(
         functools.partial(returned_kernel, bulk_count, moved),
         grid=(row_count,),
-        out_shape=[jax.ShapeDtypeStruct(half, f32)] * 2,
+        out_shape=[jax.ShapeDtypeStruct(half, f32) if moved else pltpu.VMEM(half, f32)] * 2,
         in_specs=[
             vmem,
             pl.BlockSpec((1, tile_count, order, order), lambda s: (s, 0, 0, 0)),

time: 86.3 us -> 84.2 us (0.976)
  local copies, waits for them, and re-layouts: 2.12 us -> 0.05 us
  waiting for transfers between devices: 24.7 us -> 25.8 us
  Pallas kernels: 26.3 us -> 25.3 us
    unnamed x20 -> x14, local copies, waits for them, and re-layouts: 2.12 us -> 0.04 us
    ppermute x24, waiting for transfers between devices: 24.7 us -> 25.8 us  [swap(): return lax.ppermute(value, axis, pairs)]
    pallas_call x2, Pallas kernels: 6.89 us -> 5.88 us  [returned(): pl.pallas_call(functools.partial(returned_kernel, bulk_count, moved), gri...]
  transfers between devices with their start and end apart: 24 -> 24, of which waited for: 12 -> 12; matrix products, arithmetic and copies ran while one was open for 0% -> 0% of each run, Pallas kernels for 18% -> 19%
where the time goes in v8:
time: 84.2 us; the launch traced here: 84 us
  starting transfers between devices  32 us (38%)
  waiting for transfers between devices  25.8 us (31%)
  Pallas kernels  25.3 us (30%)
  between operations  0.9 us (1%)
    ppermute x24, starting transfers between devices, swap(): return lax.ppermute(value, axis, pairs)  32 us
    ppermute x24, waiting for transfers between devices, swap(): return lax.ppermute(value, axis, pairs)  25.8 us
    pallas_call x2, Pallas kernels, near_part(): pl.pallas_call(functools.partial(near_kernel, bulk_count, len(panel), sec...  7.36 us
    pallas_call x2, Pallas kernels, returned(): pl.pallas_call(functools.partial(returned_kernel, bulk_count, moved), gri...  5.88 us
    pallas_call x1, Pallas kernels, final(): pl.pallas_call(final_kernel, grid=(1,), out_shape=[jax.ShapeDtypeStruct(n...  4.8 us
    pallas_call x2, Pallas kernels, small_call(): pl.pallas_call(kernel, out_shape=jax.ShapeDtypeStruct((matrices, count, c...  4.32 us
  transfers between devices with their start and end apart: 24, of which 12 were waited for; matrix products, arithmetic and copies ran while one was open for 0% of the time, Pallas kernels for 19%

profile of v8, /device:TPU:0, one launch (start us, length us, event | category | flops | bytes accessed | tf_op | source)
XLA Modules:
  0.0 84.0 jit_solution(3525426703330016929)
XLA Ops:
  0.6 3.6 %returned.1 = (f32[16,64,128]{2,1,0:T(8,128)S(1)}, f32[16,64,128]{2,1,0:T(8,128)S(1)}) custom-call(f32[4,64,128]{2,1,0:T(8,128)} %vectors.3, f32[4,11,128,128]{3,2,1,0:T(8,128)} %refs_6_.3, s32[11,128]{1,0:T(8,128)} %bitcast.16, s32[128]{0:T(128)} %refs_9_.1, s32[128]{0:T(128)} %new_slot.7), custom_call_target="tpu_custom_call" | custom-call | tf_op jit(solution)/shard_map/returned/pallas_call | solution.py:171
  4.3 0.0 copy-start.3
  4.3 0.0 copy-start.4
  4.3 0.5 collective-permute-start.6
  4.8 3.7 %collective-permute-start.1 = (f32[256,128]{1,0:T(8,128)S(1)}, f32[256,128]{1,0:T(8,128)S(1)}, u32[]{:S(2)}, u32[]{:S(2)}) collective-permute-start(f32[256,128]{1,0:T(8,128)S(1)} %bitcast.4), channel_id=1, source_target_pairs={{0,4},{1,5},{2,6},{3,7},{4,0},{5,1},{6,2},{7,3},{8,12},{9,13},{10,... | collective-permute-start | bytes 393224 | tf_op jit(solution)/shard_map/ppermute | solution.py:29
  8.5 1.3 %collective-permute-start.2 = (f32[256,128]{1,0:T(8,128)S(1)}, f32[256,128]{1,0:T(8,128)S(1)}, u32[]{:S(2)}, u32[]{:S(2)}) collective-permute-start(f32[256,128]{1,0:T(8,128)S(1)} %bitcast.5), channel_id=1, source_target_pairs={{0,6},{1,7},{2,4},{3,5},{4,2},{5,3},{6,0},{7,1},{8,14},{9,15},{10,... | collective-permute-start | bytes 393224 | tf_op jit(solution)/shard_map/ppermute | solution.py:29
  9.8 0.2 collective-permute-start
  10.1 1.9 %collective-permute-start.7 = (f32[8,64,128]{2,1,0:T(8,128)S(1)}, f32[8,64,128]{2,1,0:T(8,128)S(1)}, u32[]{:S(2)}, u32[]{:S(2)}) collective-permute-start(f32[8,64,128]{2,1,0:T(8,128)S(1)} %add_upper.3), channel_id=1, source_target_pairs={{0,2},{1,3},{2,0},{3,1},{4,6},{5,7},{6,4},{7,5},{8,10},{9,11},{10,... | collective-permute-start | bytes 786440 | tf_op jit(solution)/shard_map/ppermute | solution.py:29
  12.0 1.5 %collective-permute-start.4 = (f32[128,128]{1,0:T(8,128)S(1)}, f32[128,128]{1,0:T(8,128)S(1)}, u32[]{:S(2)}, u32[]{:S(2)}) collective-permute-start(f32[128,128]{1,0:T(8,128)S(1)} %bitcast.14), channel_id=1, source_target_pairs={{0,8},{8,0},{16,24},{24,16},{1,9},{9,1},{17,25},{25,17},{2,10},{10... | collective-permute-start | bytes 196616 | tf_op jit(solution)/shard_map/ppermute | solution.py:29
  13.5 2.8 %collective-permute-done.4.other = f32[128,128]{1,0:T(8,128)S(1)} collective-permute-done((f32[128,128]{1,0:T(8,128)S(1)}, f32[128,128]{1,0:T(8,128)S(1)}, u32[]{:S(2)}, u32[]{:S(2)}) %collective-permute-start.4) | collective-permute-done | bytes 65568 | tf_op jit(solution)/shard_map/ppermute | solution.py:29
  16.3 2.2 %collective-permute-done.1.refs_0_.refs_2_ = f32[256,128]{1,0:T(8,128)S(1)} collective-permute-done((f32[256,128]{1,0:T(8,128)S(1)}, f32[256,128]{1,0:T(8,128)S(1)}, u32[]{:S(2)}, u32[]{:S(2)}) %collective-permute-start.1) | collective-permute-done | bytes 131104 | tf_op jit(solution)/shard_map/ppermute | solution.py:29
  18.5 0.1 collective-permute-start.5
  18.6 2.0 %collective-permute-done.refs_1_ = f32[256,128]{1,0:T(8,128)S(1)} collective-permute-done((f32[256,128]{1,0:T(8,128)S(1)}, f32[256,128]{1,0:T(8,128)S(1)}, u32[]{:S(2)}, u32[]{:S(2)}) %collective-permute-start) | collective-permute-done | bytes 131104 | tf_op jit(solution)/shard_map/ppermute | solution.py:29
  20.6 0.1 collective-permute-start.3
  20.7 1.7 %collective-permute-start.9 = (f32[256,128]{1,0:T(8,128)S(1)}, f32[256,128]{1,0:T(8,128)S(1)}, u32[]{:S(2)}, u32[]{:S(2)}) collective-permute-start(f32[256,128]{1,0:T(8,128)S(1)} %merge_side.4.refs_2_.mine), channel_id=1, source_target_pairs={{0,16},{8,24},{16,0},{24,8},{1,17},{9,25},{17,1},{25,9},{2,18},{10... | collective-permute-start | bytes 393224 | tf_op jit(solution)/shard_map/ppermute | solution.py:29
  22.4 2.8 %collective-permute-done.7.refs_2_.refs_1_ = f32[8,64,128]{2,1,0:T(8,128)S(1)} collective-permute-done((f32[8,64,128]{2,1,0:T(8,128)S(1)}, f32[8,64,128]{2,1,0:T(8,128)S(1)}, u32[]{:S(2)}, u32[]{:S(2)}) %collective-permute-start.7) | collective-permute-done | bytes 262176 | tf_op jit(solution)/shard_map/ppermute | solution.py:29
  25.2 3.6 %collective-permute-start.8 = (f32[4,64,128]{2,1,0:T(8,128)S(1)}, f32[4,64,128]{2,1,0:T(8,128)S(1)}, u32[]{:S(2)}, u32[]{:S(2)}) collective-permute-start(f32[4,64,128]{2,1,0:T(8,128)S(1)} %add_upper.4), channel_id=1, source_target_pairs={{0,6},{1,7},{2,4},{3,5},{4,2},{5,3},{6,0},{7,1},{8,14},{9,15},{10,... | collective-permute-start | bytes 393224 | tf_op jit(solution)/shard_map/ppermute | solution.py:29
  28.9 3.4 %near_first.1 = (f32[4,64,128]{2,1,0:T(8,128)S(1)}, f32[4,64,128]{2,1,0:T(8,128)S(1)}, f32[32,128]{1,0:T(8,128)S(1)}, f32[24,128]{1,0:T(8,128)S(1)}) custom-call(f32[256,128]{1,0:T(8,128)S(1)} %bitcast.8, f32[256,128]{1,0:T(8,128)S(1)} %collective-permute-done.refs_1_, f32[256,128]{1,0:T(8,128)S(1)} %collective-permute-done.1.refs_0_.refs_2_, ...), custom_call_target="tpu_custom_call" | custom-call | tf_op jit(solution)/shard_map/near_first/pallas_call | solution.py:264
  32.4 0.9 %gather_first.1 = (f32[4,64,128]{2,1,0:T(8,128)S(1)}, f32[200,128]{1,0:T(8,128)S(1)}) custom-call(f32[4,64,128]{2,1,0:T(8,128)S(1)} %copy-done.1, f32[4,64,128]{2,1,0:T(8,128)S(1)} %get-tuple-element.23.refs_0_.near, f32[16,64,128]{2,1,0:T(8,128)S(1)} %get-tuple-element.24.refs_0_.keep, f32[16,64,128]{2,1,0:T(8,128)S(1)} %collective-permute-done.6.refs_1_.refs_0_, ...), custom_call_target="tpu_custom_call" | custom-call | tf_op jit(solution)/shard_map/gather_first/pallas_call | solution.py:331
  33.3 1.2 %collective-permute-start.10 = (f32[256,128]{1,0:T(8,128)S(1)}, f32[256,128]{1,0:T(8,128)S(1)}, u32[]{:S(2)}, u32[]{:S(2)}) collective-permute-start(f32[256,128]{1,0:T(8,128)S(1)} %bitcast.9), channel_id=1, source_target_pairs={{0,2},{1,3},{2,0},{3,1},{4,6},{5,7},{6,4},{7,5},{8,10},{9,11},{10,... | collective-permute-start | bytes 393224 | tf_op jit(solution)/shard_map/ppermute | solution.py:29
  34.5 2.6 %collective-permute-start.11 = (f32[256,128]{1,0:T(8,128)S(1)}, f32[256,128]{1,0:T(8,128)S(1)}, u32[]{:S(2)}, u32[]{:S(2)}) collective-permute-start(f32[256,128]{1,0:T(8,128)S(1)} %bitcast.10), channel_id=1, source_target_pairs={{0,4},{1,5},{2,6},{3,7},{4,0},{5,1},{6,2},{7,3},{8,12},{9,13},{10,... | collective-permute-start | bytes 393224 | tf_op jit(solution)/shard_map/ppermute | solution.py:29
  37.1 0.6 collective-permute-start.12
  37.7 1.5 %collective-permute-start.13 = (f32[200,128]{1,0:T(8,128)S(1)}, f32[200,128]{1,0:T(8,128)S(1)}, u32[]{:S(2)}, u32[]{:S(2)}) collective-permute-start(f32[200,128]{1,0:T(8,128)S(1)} %get-tuple-element.28.mine), channel_id=1, source_target_pairs={{0,8},{8,0},{16,24},{24,16},{1,9},{9,1},{17,25},{25,17},{2,10},{10... | collective-permute-start | bytes 307208 | tf_op jit(solution)/shard_map/ppermute | solution.py:29
  39.2 2.3 %returned_moved.1 = (f32[16,64,128]{2,1,0:T(8,128)S(1)}, f32[16,64,128]{2,1,0:T(8,128)S(1)}) custom-call(f32[4,64,128]{2,1,0:T(8,128)S(1)} %get-tuple-element.27.vectors.refs_5_.first, f32[4,11,128,128]{3,2,1,0:T(8,128)S(1)} %copy-done, s32[11,128]{1,0:T(8,128)S(1)} %bitcast.18, s32[128]{0:T(128)S(1)} %copy-done.6, s32[128]{0:T(128)S(1)} %copy-done.5), custom_call_target="tpu_custom_call" | custom-call | tf_op jit(solution)/shard_map/returned_moved/pallas_call | solution.py:171
  41.5 0.9 %collective-permute-done.13.other = f32[200,128]{1,0:T(8,128)S(1)} collective-permute-done((f32[200,128]{1,0:T(8,128)S(1)}, f32[200,128]{1,0:T(8,128)S(1)}, u32[]{:S(2)}, u32[]{:S(2)}) %collective-permute-start.13) | collective-permute-done | bytes 102432 | tf_op jit(solution)/shard_map/ppermute | solution.py:29
  42.4 3.2 %collective-permute-done.11.refs_2_ = f32[256,128]{1,0:T(8,128)S(1)} collective-permute-done((f32[256,128]{1,0:T(8,128)S(1)}, f32[256,128]{1,0:T(8,128)S(1)}, u32[]{:S(2)}, u32[]{:S(2)}) %collective-permute-start.11) | collective-permute-done | bytes 131104 | tf_op jit(solution)/shard_map/ppermute | solution.py:29
  45.6 0.1 collective-permute-start.17
  45.7 0.5 collective-permute-start.14
  46.2 1.4 %collective-permute-done.17.refs_1_.refs_3_ = f32[16,64,128]{2,1,0:T(8,128)S(1)} collective-permute-done((f32[16,64,128]{2,1,0:T(8,128)S(1)}, f32[16,64,128]{2,1,0:T(8,128)S(1)}, u32[]{:S(2)}, u32[]{:S(2)}) %collective-permute-start.17) | collective-permute-done | bytes 524320 | tf_op jit(solution)/shard_map/ppermute | solution.py:29
  47.6 2.0 %collective-permute-start.18 = (f32[8,64,128]{2,1,0:T(8,128)S(1)}, f32[8,64,128]{2,1,0:T(8,128)S(1)}, u32[]{:S(2)}, u32[]{:S(2)}) collective-permute-start(f32[8,64,128]{2,1,0:T(8,128)S(1)} %add_upper.5), channel_id=1, source_target_pairs={{0,2},{1,3},{2,0},{3,1},{4,6},{5,7},{6,4},{7,5},{8,10},{9,11},{10,... | collective-permute-start | bytes 786440 | tf_op jit(solution)/shard_map/ppermute | solution.py:29
  49.7 1.5 %collective-permute-start.15 = (f32[328,128]{1,0:T(8,128)S(1)}, f32[328,128]{1,0:T(8,128)S(1)}, u32[]{:S(2)}, u32[]{:S(2)}) collective-permute-start(f32[328,128]{1,0:T(8,128)S(1)} %merge_side.6.refs_4_.mine), channel_id=1, source_target_pairs={{0,16},{8,24},{16,0},{24,8},{1,17},{9,25},{17,1},{25,9},{2,18},{10... | collective-permute-start | bytes 503816 | tf_op jit(solution)/shard_map/ppermute | solution.py:29
  51.2 3.9 %near_second.1 = (f32[4,64,128]{2,1,0:T(8,128)S(1)}, f32[4,64,128]{2,1,0:T(8,128)S(1)}, f32[32,128]{1,0:T(8,128)S(1)}) custom-call(f32[256,128]{1,0:T(8,128)S(1)} %bitcast.13, f32[256,128]{1,0:T(8,128)S(1)} %collective-permute-done.10.refs_1_, f32[256,128]{1,0:T(8,128)S(1)} %collective-permute-done.11.refs_2_, ...), custom_call_target="tpu_custom_call" | custom-call | tf_op jit(solution)/shard_map/near_second/pallas_call | solution.py:264
  55.1 0.6 collective-permute-done.15.other
  55.7 1.5 %edge_second.1 = (f32[2,64,128]{2,1,0:T(8,128)S(1)}, f32[136,128]{1,0:T(8,128)S(1)}) custom-call(f32[4,64,128]{2,1,0:T(8,128)S(1)} %get-tuple-element.27.vectors.refs_5_.first, f32[4,64,128]{2,1,0:T(8,128)S(1)} %get-tuple-element.30.refs_0_.near, f32[32,128]{1,0:T(8,128)S(1)} %get-tuple-element.31.packed, f32[2,4,128,128]{3,2,1,0:T(8,128)S(1)} %copy-done.2, ...), custom_call_target="tpu_custom_call" | custom-call | tf_op jit(solution)/shard_map/edge_second/pallas_call | solution.py:367
  57.2 0.1 collective-permute-start.16
  57.3 1.2 %collective-permute-done.16.partner = f32[136,128]{1,0:T(8,128)S(1)} collective-permute-done((f32[136,128]{1,0:T(8,128)S(1)}, f32[136,128]{1,0:T(8,128)S(1)}, u32[]{:S(2)}, u32[]{:S(2)}) %collective-permute-start.16) | collective-permute-done | bytes 69664 | tf_op jit(solution)/shard_map/ppermute | solution.py:29
  58.6 0.4 collective-permute-start.19
  59.0 4.0 %collective-permute-done.19.partner = f32[136,128]{1,0:T(8,128)S(1)} collective-permute-done((f32[136,128]{1,0:T(8,128)S(1)}, f32[136,128]{1,0:T(8,128)S(1)}, u32[]{:S(2)}, u32[]{:S(2)}) %collective-permute-start.19) | collective-permute-done | bytes 69664 | tf_op jit(solution)/shard_map/ppermute | solution.py:29
  62.9 1.4 %collective-permute-start.20 = (f32[72,128]{1,0:T(8,128)S(1)}, f32[72,128]{1,0:T(8,128)S(1)}, u32[]{:S(2)}, u32[]{:S(2)}) collective-permute-start(f32[72,128]{1,0:T(8,128)S(1)} %get-tuple-element.35.sums), channel_id=1, source_target_pairs={{0,4},{1,5},{2,6},{3,7},{4,0},{5,1},{6,2},{7,3},{8,12},{9,13},{10,... | collective-permute-start | bytes 110600 | tf_op jit(solution)/shard_map/ppermute | solution.py:29
  64.3 3.7 %collective-permute-done.20.partner = f32[72,128]{1,0:T(8,128)S(1)} collective-permute-done((f32[72,128]{1,0:T(8,128)S(1)}, f32[72,128]{1,0:T(8,128)S(1)}, u32[]{:S(2)}, u32[]{:S(2)}) %collective-permute-start.20) | collective-permute-done | bytes 36896 | tf_op jit(solution)/shard_map/ppermute | solution.py:29
  68.1 0.2 last_gram.1
  68.3 2.5 %collective-permute-start.23 = (f32[5,64,128]{2,1,0:T(8,128)S(1)}, f32[5,64,128]{2,1,0:T(8,128)S(1)}, u32[]{:S(2)}, u32[]{:S(2)}) collective-permute-start(f32[5,64,128]{2,1,0:T(8,128)S(1)} %get-tuple-element.43), channel_id=1, source_target_pairs={{0,6},{1,7},{2,4},{3,5},{4,2},{5,3},{6,0},{7,1},{8,14},{9,15},{10,... | collective-permute-start | bytes 491528 | tf_op jit(solution)/shard_map/ppermute | solution.py:29
  70.8 1.5 %collective-permute-start.21 = (f32[32,128]{1,0:T(8,128)S(1)}, f32[32,128]{1,0:T(8,128)S(1)}, u32[]{:S(2)}, u32[]{:S(2)}) collective-permute-start(f32[32,128]{1,0:T(8,128)S(1)} %get-tuple-element.36.refs_0_), channel_id=1, source_target_pairs={{0,8},{8,0},{16,24},{24,16},{1,9},{9,1},{17,25},{25,17},{2,10},{10... | collective-permute-start | bytes 49160 | tf_op jit(solution)/shard_map/ppermute | solution.py:29
  72.3 3.0 %first_solves.1.refs_2_.solved = f32[2,64,64]{2,1,0:T(8,128)S(1)} custom-call(f32[72,128]{1,0:T(8,128)S(1)} %get-tuple-element.37.extra.refs_3_), custom_call_target="tpu_custom_call" | custom-call | tf_op jit(solution)/shard_map/first_solves/pallas_call | solution.py:471
  75.4 1.6 %collective-permute-start.22 = (f32[32,128]{1,0:T(8,128)S(1)}, f32[32,128]{1,0:T(8,128)S(1)}, u32[]{:S(2)}, u32[]{:S(2)}) collective-permute-start(f32[32,128]{1,0:T(8,128)S(1)} %add_whole.2.refs_0_), channel_id=1, source_target_pairs={{0,16},{8,24},{16,0},{24,8},{1,17},{9,25},{17,1},{25,9},{2,18},{10... | collective-permute-start | bytes 49160 | tf_op jit(solution)/shard_map/ppermute | solution.py:29
  77.0 1.3 %next_gram.1.following = f32[3,64,64]{2,1,0:T(8,128)S(1)} custom-call(f32[72,128]{1,0:T(8,128)S(1)} %get-tuple-element.37.extra.refs_3_, f32[2,64,64]{2,1,0:T(8,128)S(1)} %first_solves.1.refs_2_.solved), custom_call_target="tpu_custom_call" | custom-call | tf_op jit(solution)/shard_map/next_gram/pallas_call | solution.py:471
  78.2 0.9 %collective-permute-done.22.refs_1_ = f32[32,128]{1,0:T(8,128)S(1)} collective-permute-done((f32[32,128]{1,0:T(8,128)S(1)}, f32[32,128]{1,0:T(8,128)S(1)}, u32[]{:S(2)}, u32[]{:S(2)}) %collective-permute-start.22) | collective-permute-done | bytes 16416 | tf_op jit(solution)/shard_map/ppermute | solution.py:29
  79.2 4.8 %final.1 = (f32[4,64,128]{2,1,0:T(8,128)}, f32[4,64,128]{2,1,0:T(8,128)}) custom-call(f32[32,128]{1,0:T(8,128)S(1)} %add_whole.3.gram, f32[2,64,64]{2,1,0:T(8,128)S(1)} %first_solves.1.refs_2_.solved, f32[3,64,64]{2,1,0:T(8,128)S(1)} %next_gram.1.following, f32[4,64,128]{2,1,0:T(8,128)S(1)} %get-tuple-element.38.moving, ...), custom_call_target="tpu_custom_call" | custom-call | tf_op jit(solution)/shard_map/final/pallas_call | solution.py:516
  (41 shorter events, 0.4 us)
Async XLA Ops:
  0.6 4.2 %copy-start.1 = (f32[4,64,128]{2,1,0:T(8,128)S(1)}, f32[4,64,128]{2,1,0:T(8,128)}, u32[]{:S(2)}) copy-start(f32[4,64,128]{2,1,0:T(8,128)} %vectors.3) | copy-start | bytes 393220
  4.2 24.6 %copy-start = (f32[4,11,128,128]{3,2,1,0:T(8,128)S(1)}, f32[4,11,128,128]{3,2,1,0:T(8,128)}, u32[]{:S(2)}) copy-start(f32[4,11,128,128]{3,2,1,0:T(8,128)} %refs_6_.3) | copy-start | bytes 8650756
  4.3 24.6 %copy-start.3 = (f32[4,128,128]{2,1,0:T(8,128)S(1)}, f32[4,128,128]{2,1,0:T(8,128)}, u32[]{:S(2)}) copy-start(f32[4,128,128]{2,1,0:T(8,128)} %refs_7_.3) | copy-start | bytes 786436
  4.3 24.6 %copy-start.4 = (s32[128,11]{0,1:T(8,128)S(1)}, s32[128,11]{0,1:T(8,128)}, u32[]{:S(2)}) copy-start(s32[128,11]{0,1:T(8,128)} %param.11) | copy-start | bytes 16900
  4.3 24.6 %copy-start.5 = (s32[128]{0:T(128)S(1)}, s32[128]{0:T(128)}, u32[]{:S(2)}) copy-start(s32[128]{0:T(128)} %new_slot.7) | copy-start | bytes 1540
  4.3 24.6 %copy-start.6 = (s32[128]{0:T(128)S(1)}, s32[128]{0:T(128)}, u32[]{:S(2)}) copy-start(s32[128]{0:T(128)} %refs_9_.1) | copy-start | bytes 1540
  4.3 5.8 %collective-permute-start.6 = (f32[16,64,128]{2,1,0:T(8,128)S(1)}, f32[16,64,128]{2,1,0:T(8,128)S(1)}, u32[]{:S(2)}, u32[]{:S(2)}) collective-permute-start(f32[16,64,128]{2,1,0:T(8,128)S(1)} %get-tuple-element.25), channel_id=1, source_target_pairs={{0,1},{1,0},{2,3},{3,2},{4,5},{5,4},{6,7},{7,6},{8,9},{9,8},{10,11... | collective-permute-start | bytes 1572872 | tf_op jit(solution)/shard_map/ppermute | solution.py:29
  4.8 13.7 %collective-permute-start.1 = (f32[256,128]{1,0:T(8,128)S(1)}, f32[256,128]{1,0:T(8,128)S(1)}, u32[]{:S(2)}, u32[]{:S(2)}) collective-permute-start(f32[256,128]{1,0:T(8,128)S(1)} %bitcast.4), channel_id=1, source_target_pairs={{0,4},{1,5},{2,6},{3,7},{4,0},{5,1},{6,2},{7,3},{8,12},{9,13},{10,... | collective-permute-start | bytes 393224 | tf_op jit(solution)/shard_map/ppermute | solution.py:29
  8.5 10.0 %collective-permute-start.2 = (f32[256,128]{1,0:T(8,128)S(1)}, f32[256,128]{1,0:T(8,128)S(1)}, u32[]{:S(2)}, u32[]{:S(2)}) collective-permute-start(f32[256,128]{1,0:T(8,128)S(1)} %bitcast.5), channel_id=1, source_target_pairs={{0,6},{1,7},{2,4},{3,5},{4,2},{5,3},{6,0},{7,1},{8,14},{9,15},{10,... | collective-permute-start | bytes 393224 | tf_op jit(solution)/shard_map/ppermute | solution.py:29
  9.8 10.8 %collective-permute-start = (f32[256,128]{1,0:T(8,128)S(1)}, f32[256,128]{1,0:T(8,128)S(1)}, u32[]{:S(2)}, u32[]{:S(2)}) collective-permute-start(f32[256,128]{1,0:T(8,128)S(1)} %bitcast.6), channel_id=1, source_target_pairs={{0,2},{1,3},{2,0},{3,1},{4,6},{5,7},{6,4},{7,5},{8,10},{9,11},{10,... | collective-permute-start | bytes 393224 | tf_op jit(solution)/shard_map/ppermute | solution.py:29
  10.1 15.1 %collective-permute-start.7 = (f32[8,64,128]{2,1,0:T(8,128)S(1)}, f32[8,64,128]{2,1,0:T(8,128)S(1)}, u32[]{:S(2)}, u32[]{:S(2)}) collective-permute-start(f32[8,64,128]{2,1,0:T(8,128)S(1)} %add_upper.3), channel_id=1, source_target_pairs={{0,2},{1,3},{2,0},{3,1},{4,6},{5,7},{6,4},{7,5},{8,10},{9,11},{10,... | collective-permute-start | bytes 786440 | tf_op jit(solution)/shard_map/ppermute | solution.py:29
  12.0 4.3 %collective-permute-start.4 = (f32[128,128]{1,0:T(8,128)S(1)}, f32[128,128]{1,0:T(8,128)S(1)}, u32[]{:S(2)}, u32[]{:S(2)}) collective-permute-start(f32[128,128]{1,0:T(8,128)S(1)} %bitcast.14), channel_id=1, source_target_pairs={{0,8},{8,0},{16,24},{24,16},{1,9},{9,1},{17,25},{25,17},{2,10},{10... | collective-permute-start | bytes 196616 | tf_op jit(solution)/shard_map/ppermute | solution.py:29
  18.5 10.3 %collective-permute-start.5 = (f32[512,128]{1,0:T(8,128)S(1)}, f32[512,128]{1,0:T(8,128)S(1)}, u32[]{:S(2)}, u32[]{:S(2)}) collective-permute-start(f32[512,128]{1,0:T(8,128)S(1)} %join.4.refs_3_), channel_id=1, source_target_pairs={{0,1},{1,0},{2,3},{3,2},{4,5},{5,4},{6,7},{7,6},{8,9},{9,8},{10,11... | collective-permute-start | bytes 786440 | tf_op jit(solution)/shard_map/ppermute | solution.py:29
  20.6 8.2 %collective-permute-start.3 = (f32[512,128]{1,0:T(8,128)S(1)}, f32[512,128]{1,0:T(8,128)S(1)}, u32[]{:S(2)}, u32[]{:S(2)}) collective-permute-start(f32[512,128]{1,0:T(8,128)S(1)} %join.3), channel_id=1, source_target_pairs={{0,1},{1,0},{2,3},{3,2},{4,5},{5,4},{6,7},{7,6},{8,9},{9,8},{10,11... | collective-permute-start | bytes 786440 | tf_op jit(solution)/shard_map/ppermute | solution.py:29
  20.7 11.6 %collective-permute-start.9 = (f32[256,128]{1,0:T(8,128)S(1)}, f32[256,128]{1,0:T(8,128)S(1)}, u32[]{:S(2)}, u32[]{:S(2)}) collective-permute-start(f32[256,128]{1,0:T(8,128)S(1)} %merge_side.4.refs_2_.mine), channel_id=1, source_target_pairs={{0,16},{8,24},{16,0},{24,8},{1,17},{9,25},{17,1},{25,9},{2,18},{10... | collective-permute-start | bytes 393224 | tf_op jit(solution)/shard_map/ppermute | solution.py:29
  25.2 7.2 %copy-start.2 = (f32[2,4,128,128]{3,2,1,0:T(8,128)S(1)}, f32[2,4,128,128]{3,2,1,0:T(8,128)}, u32[]{:S(2)}) copy-start(f32[2,4,128,128]{3,2,1,0:T(8,128)} %coupling.1) | copy-start | bytes 1572868
  25.2 7.1 %collective-permute-start.8 = (f32[4,64,128]{2,1,0:T(8,128)S(1)}, f32[4,64,128]{2,1,0:T(8,128)S(1)}, u32[]{:S(2)}, u32[]{:S(2)}) collective-permute-start(f32[4,64,128]{2,1,0:T(8,128)S(1)} %add_upper.4), channel_id=1, source_target_pairs={{0,6},{1,7},{2,4},{3,5},{4,2},{5,3},{6,0},{7,1},{8,14},{9,15},{10,... | collective-permute-start | bytes 393224 | tf_op jit(solution)/shard_map/ppermute | solution.py:29
  33.3 9.1 %collective-permute-start.10 = (f32[256,128]{1,0:T(8,128)S(1)}, f32[256,128]{1,0:T(8,128)S(1)}, u32[]{:S(2)}, u32[]{:S(2)}) collective-permute-start(f32[256,128]{1,0:T(8,128)S(1)} %bitcast.9), channel_id=1, source_target_pairs={{0,2},{1,3},{2,0},{3,1},{4,6},{5,7},{6,4},{7,5},{8,10},{9,11},{10,... | collective-permute-start | bytes 393224 | tf_op jit(solution)/shard_map/ppermute | solution.py:29
  34.5 11.0 %collective-permute-start.11 = (f32[256,128]{1,0:T(8,128)S(1)}, f32[256,128]{1,0:T(8,128)S(1)}, u32[]{:S(2)}, u32[]{:S(2)}) collective-permute-start(f32[256,128]{1,0:T(8,128)S(1)} %bitcast.10), channel_id=1, source_target_pairs={{0,4},{1,5},{2,6},{3,7},{4,0},{5,1},{6,2},{7,3},{8,12},{9,13},{10,... | collective-permute-start | bytes 393224 | tf_op jit(solution)/shard_map/ppermute | solution.py:29
  37.1 8.5 %collective-permute-start.12 = (f32[256,128]{1,0:T(8,128)S(1)}, f32[256,128]{1,0:T(8,128)S(1)}, u32[]{:S(2)}, u32[]{:S(2)}) collective-permute-start(f32[256,128]{1,0:T(8,128)S(1)} %bitcast.11), channel_id=1, source_target_pairs={{0,6},{1,7},{2,4},{3,5},{4,2},{5,3},{6,0},{7,1},{8,14},{9,15},{10,... | collective-permute-start | bytes 393224 | tf_op jit(solution)/shard_map/ppermute | solution.py:29
  37.7 4.7 %collective-permute-start.13 = (f32[200,128]{1,0:T(8,128)S(1)}, f32[200,128]{1,0:T(8,128)S(1)}, u32[]{:S(2)}, u32[]{:S(2)}) collective-permute-start(f32[200,128]{1,0:T(8,128)S(1)} %get-tuple-element.28.mine), channel_id=1, source_target_pairs={{0,8},{8,0},{16,24},{24,16},{1,9},{9,1},{17,25},{25,17},{2,10},{10... | collective-permute-start | bytes 307208 | tf_op jit(solution)/shard_map/ppermute | solution.py:29
  45.6 2.0 %collective-permute-start.17 = (f32[16,64,128]{2,1,0:T(8,128)S(1)}, f32[16,64,128]{2,1,0:T(8,128)S(1)}, u32[]{:S(2)}, u32[]{:S(2)}) collective-permute-start(f32[16,64,128]{2,1,0:T(8,128)S(1)} %pass_on.1), channel_id=1, source_target_pairs={{0,1},{1,0},{2,3},{3,2},{4,5},{5,4},{6,7},{7,6},{8,9},{9,8},{10,11... | collective-permute-start | bytes 1572872 | tf_op jit(solution)/shard_map/ppermute | solution.py:29
  45.7 5.5 %collective-permute-start.14 = (f32[1024,128]{1,0:T(8,128)S(1)}, f32[1024,128]{1,0:T(8,128)S(1)}, u32[]{:S(2)}, u32[]{:S(2)}) collective-permute-start(f32[1024,128]{1,0:T(8,128)S(1)} %join.5.refs_1_), channel_id=1, source_target_pairs={{0,1},{1,0},{2,3},{3,2},{4,5},{5,4},{6,7},{7,6},{8,9},{9,8},{10,11... | collective-permute-start | bytes 1572872 | tf_op jit(solution)/shard_map/ppermute | solution.py:29
  47.6 10.9 %collective-permute-start.18 = (f32[8,64,128]{2,1,0:T(8,128)S(1)}, f32[8,64,128]{2,1,0:T(8,128)S(1)}, u32[]{:S(2)}, u32[]{:S(2)}) collective-permute-start(f32[8,64,128]{2,1,0:T(8,128)S(1)} %add_upper.5), channel_id=1, source_target_pairs={{0,2},{1,3},{2,0},{3,1},{4,6},{5,7},{6,4},{7,5},{8,10},{9,11},{10,... | collective-permute-start | bytes 786440 | tf_op jit(solution)/shard_map/ppermute | solution.py:29
  49.7 6.0 %collective-permute-start.15 = (f32[328,128]{1,0:T(8,128)S(1)}, f32[328,128]{1,0:T(8,128)S(1)}, u32[]{:S(2)}, u32[]{:S(2)}) collective-permute-start(f32[328,128]{1,0:T(8,128)S(1)} %merge_side.6.refs_4_.mine), channel_id=1, source_target_pairs={{0,16},{8,24},{16,0},{24,8},{1,17},{9,25},{17,1},{25,9},{2,18},{10... | collective-permute-start | bytes 503816 | tf_op jit(solution)/shard_map/ppermute | solution.py:29
  57.2 1.3 %collective-permute-start.16 = (f32[136,128]{1,0:T(8,128)S(1)}, f32[136,128]{1,0:T(8,128)S(1)}, u32[]{:S(2)}, u32[]{:S(2)}) collective-permute-start(f32[136,128]{1,0:T(8,128)S(1)} %get-tuple-element.32.extra), channel_id=1, source_target_pairs={{0,1},{1,0},{2,3},{3,2},{4,5},{5,4},{6,7},{7,6},{8,9},{9,8},{10,11... | collective-permute-start | bytes 208904 | tf_op jit(solution)/shard_map/ppermute | solution.py:29
  58.6 4.4 %collective-permute-start.19 = (f32[136,128]{1,0:T(8,128)S(1)}, f32[136,128]{1,0:T(8,128)S(1)}, u32[]{:S(2)}, u32[]{:S(2)}) collective-permute-start(f32[136,128]{1,0:T(8,128)S(1)} %settle.1.extra), channel_id=1, source_target_pairs={{0,2},{1,3},{2,0},{3,1},{4,6},{5,7},{6,4},{7,5},{8,10},{9,11},{10,... | collective-permute-start | bytes 208904 | tf_op jit(solution)/shard_map/ppermute | solution.py:29
  62.9 5.1 %collective-permute-start.20 = (f32[72,128]{1,0:T(8,128)S(1)}, f32[72,128]{1,0:T(8,128)S(1)}, u32[]{:S(2)}, u32[]{:S(2)}) collective-permute-start(f32[72,128]{1,0:T(8,128)S(1)} %get-tuple-element.35.sums), channel_id=1, source_target_pairs={{0,4},{1,5},{2,6},{3,7},{4,0},{5,1},{6,2},{7,3},{8,12},{9,13},{10,... | collective-permute-start | bytes 110600 | tf_op jit(solution)/shard_map/ppermute | solution.py:29
  68.3 10.9 %collective-permute-start.23 = (f32[5,64,128]{2,1,0:T(8,128)S(1)}, f32[5,64,128]{2,1,0:T(8,128)S(1)}, u32[]{:S(2)}, u32[]{:S(2)}) collective-permute-start(f32[5,64,128]{2,1,0:T(8,128)S(1)} %get-tuple-element.43), channel_id=1, source_target_pairs={{0,6},{1,7},{2,4},{3,5},{4,2},{5,3},{6,0},{7,1},{8,14},{9,15},{10,... | collective-permute-start | bytes 491528 | tf_op jit(solution)/shard_map/ppermute | solution.py:29
  70.8 4.5 %collective-permute-start.21 = (f32[32,128]{1,0:T(8,128)S(1)}, f32[32,128]{1,0:T(8,128)S(1)}, u32[]{:S(2)}, u32[]{:S(2)}) collective-permute-start(f32[32,128]{1,0:T(8,128)S(1)} %get-tuple-element.36.refs_0_), channel_id=1, source_target_pairs={{0,8},{8,0},{16,24},{24,16},{1,9},{9,1},{17,25},{25,17},{2,10},{10... | collective-permute-start | bytes 49160 | tf_op jit(solution)/shard_map/ppermute | solution.py:29
  75.4 3.8 %collective-permute-start.22 = (f32[32,128]{1,0:T(8,128)S(1)}, f32[32,128]{1,0:T(8,128)S(1)}, u32[]{:S(2)}, u32[]{:S(2)}) collective-permute-start(f32[32,128]{1,0:T(8,128)S(1)} %add_whole.2.refs_0_), channel_id=1, source_target_pairs={{0,16},{8,24},{16,0},{24,8},{1,17},{9,25},{17,1},{25,9},{2,18},{10... | collective-permute-start | bytes 49160 | tf_op jit(solution)/shard_map/ppermute | solution.py:29

commit v9 on v8

--- a/solution.py
+++ b/solution.py
@@ -636,15 +636,15 @@
     )(sums, partner)
 
 
-def add_whole(left, right, *earlier):
-    return pl.pallas_call(
-        functools.partial(add_kernel, 2),
-        out_shape=jax.ShapeDtypeStruct(left.shape, f32),
-        in_specs=[vmem] * 2 + [anywhere] * len(earlier),
+def add_whole(*terms):
+    return pl.pallas_call(
+        functools.partial(add_kernel, len(terms)),
+        out_shape=jax.ShapeDtypeStruct(terms[0].shape, f32),
+        in_specs=[vmem] * len(terms),
         out_specs=vmem,
         compiler_params=params(),
         name="add_whole",
-    )(left, right, *earlier)
+    )(*terms)
 
 
 def pass_on(value, *earlier):
@@ -764,11 +764,7 @@
         terms.append(swap(total, "bulk", masks[step]))
     solved = small_call(first_solves_kernel, count, 2, "first_solves", extra)
     following = small_call(next_gram_kernel, count, 3, "next_gram", extra, solved)
-    mask = 1
-    while mask < part_count:
-        partner = swap(gram, "group", mask)
-        gram = add_whole(gram, partner, *([solved] if mask == 1 else []))
-        mask *= 2
+    gram = add_whole(gram, *(swap(gram, "group", mask) for mask in range(1, part_count)))
     return tuple(
         final(gram, solved, following, moving, moved, near, more, new_slot, row, flags, terms)
     )

time: 84.2 us -> 83.7 us (level)
  waiting for transfers between devices: 25.8 us -> 24.8 us
    ppermute x24 -> x25, waiting for transfers between devices: 25.8 us -> 24.8 us  [swap(): return lax.ppermute(value, axis, pairs)]
    ppermute x24 -> x25, starting transfers between devices: 32 us -> 32.4 us  [swap(): return lax.ppermute(value, axis, pairs)]
  transfers between devices with their start and end apart: 24 -> 25, of which waited for: 12 -> 11; matrix products, arithmetic and copies ran while one was open for 0% -> 0% of each run, Pallas kernels for 19% -> 19%
where the time goes in v9:
time: 83.7 us; the launch traced here: 83.5 us
  starting transfers between devices  32.4 us (39%)
  Pallas kernels  25.3 us (30%)
  waiting for transfers between devices  24.8 us (30%)
  between operations  0.92 us (1%)
    ppermute x25, starting transfers between devices, swap(): return lax.ppermute(value, axis, pairs)  32.4 us
    ppermute x25, waiting for transfers between devices, swap(): return lax.ppermute(value, axis, pairs)  24.8 us
    pallas_call x2, Pallas kernels, near_part(): pl.pallas_call(functools.partial(near_kernel, bulk_count, len(panel), sec...  7.36 us
    pallas_call x2, Pallas kernels, returned(): pl.pallas_call(functools.partial(returned_kernel, bulk_count, moved), gri...  5.88 us
    pallas_call x1, Pallas kernels, final(): pl.pallas_call(final_kernel, grid=(1,), out_shape=[jax.ShapeDtypeStruct(n...  4.81 us
    pallas_call x2, Pallas kernels, small_call(): pl.pallas_call(kernel, out_shape=jax.ShapeDtypeStruct((matrices, count, c...  4.33 us
  transfers between devices with their start and end apart: 25, of which 11 were waited for; matrix products, arithmetic and copies ran while one was open for 0% of the time, Pallas kernels for 19%

profile of v9, /device:TPU:0, one launch (start us, length us, event | category | flops | bytes accessed | tf_op | source)
XLA Modules:
  0.0 83.5 jit_solution(1088782270108900479)
XLA Ops:
  0.6 3.6 %returned.1 = (f32[16,64,128]{2,1,0:T(8,128)S(1)}, f32[16,64,128]{2,1,0:T(8,128)S(1)}) custom-call(f32[4,64,128]{2,1,0:T(8,128)} %vectors.3, f32[4,11,128,128]{3,2,1,0:T(8,128)} %refs_6_.3, s32[11,128]{1,0:T(8,128)} %bitcast.16, s32[128]{0:T(128)} %refs_9_.1, s32[128]{0:T(128)} %new_slot.7), custom_call_target="tpu_custom_call" | custom-call | tf_op jit(solution)/shard_map/returned/pallas_call | solution.py:171
  4.2 0.0 copy-start
  4.3 0.0 copy-start.5
  4.3 0.5 collective-permute-start.6
  4.8 3.7 %collective-permute-start.1 = (f32[256,128]{1,0:T(8,128)S(1)}, f32[256,128]{1,0:T(8,128)S(1)}, u32[]{:S(2)}, u32[]{:S(2)}) collective-permute-start(f32[256,128]{1,0:T(8,128)S(1)} %bitcast.4), channel_id=1, source_target_pairs={{0,4},{1,5},{2,6},{3,7},{4,0},{5,1},{6,2},{7,3},{8,12},{9,13},{10,... | collective-permute-start | bytes 393224 | tf_op jit(solution)/shard_map/ppermute | solution.py:29
  8.5 1.3 %collective-permute-start.2 = (f32[256,128]{1,0:T(8,128)S(1)}, f32[256,128]{1,0:T(8,128)S(1)}, u32[]{:S(2)}, u32[]{:S(2)}) collective-permute-start(f32[256,128]{1,0:T(8,128)S(1)} %bitcast.5), channel_id=1, source_target_pairs={{0,6},{1,7},{2,4},{3,5},{4,2},{5,3},{6,0},{7,1},{8,14},{9,15},{10,... | collective-permute-start | bytes 393224 | tf_op jit(solution)/shard_map/ppermute | solution.py:29
  9.8 0.2 collective-permute-start
  10.1 1.9 %collective-permute-start.7 = (f32[8,64,128]{2,1,0:T(8,128)S(1)}, f32[8,64,128]{2,1,0:T(8,128)S(1)}, u32[]{:S(2)}, u32[]{:S(2)}) collective-permute-start(f32[8,64,128]{2,1,0:T(8,128)S(1)} %add_upper.3), channel_id=1, source_target_pairs={{0,2},{1,3},{2,0},{3,1},{4,6},{5,7},{6,4},{7,5},{8,10},{9,11},{10,... | collective-permute-start | bytes 786440 | tf_op jit(solution)/shard_map/ppermute | solution.py:29
  12.0 1.5 %collective-permute-start.4 = (f32[128,128]{1,0:T(8,128)S(1)}, f32[128,128]{1,0:T(8,128)S(1)}, u32[]{:S(2)}, u32[]{:S(2)}) collective-permute-start(f32[128,128]{1,0:T(8,128)S(1)} %bitcast.14), channel_id=1, source_target_pairs={{0,8},{8,0},{16,24},{24,16},{1,9},{9,1},{17,25},{25,17},{2,10},{10... | collective-permute-start | bytes 196616 | tf_op jit(solution)/shard_map/ppermute | solution.py:29
  13.5 2.8 %collective-permute-done.4.other = f32[128,128]{1,0:T(8,128)S(1)} collective-permute-done((f32[128,128]{1,0:T(8,128)S(1)}, f32[128,128]{1,0:T(8,128)S(1)}, u32[]{:S(2)}, u32[]{:S(2)}) %collective-permute-start.4) | collective-permute-done | bytes 65568 | tf_op jit(solution)/shard_map/ppermute | solution.py:29
  16.3 2.2 %collective-permute-done.1.refs_0_.refs_2_ = f32[256,128]{1,0:T(8,128)S(1)} collective-permute-done((f32[256,128]{1,0:T(8,128)S(1)}, f32[256,128]{1,0:T(8,128)S(1)}, u32[]{:S(2)}, u32[]{:S(2)}) %collective-permute-start.1) | collective-permute-done | bytes 131104 | tf_op jit(solution)/shard_map/ppermute | solution.py:29
  18.5 0.1 collective-permute-start.5
  18.6 2.0 %collective-permute-done.refs_1_ = f32[256,128]{1,0:T(8,128)S(1)} collective-permute-done((f32[256,128]{1,0:T(8,128)S(1)}, f32[256,128]{1,0:T(8,128)S(1)}, u32[]{:S(2)}, u32[]{:S(2)}) %collective-permute-start) | collective-permute-done | bytes 131104 | tf_op jit(solution)/shard_map/ppermute | solution.py:29
  20.6 0.1 collective-permute-start.3
  20.7 1.7 %collective-permute-start.9 = (f32[256,128]{1,0:T(8,128)S(1)}, f32[256,128]{1,0:T(8,128)S(1)}, u32[]{:S(2)}, u32[]{:S(2)}) collective-permute-start(f32[256,128]{1,0:T(8,128)S(1)} %merge_side.4.refs_2_.mine), channel_id=1, source_target_pairs={{0,16},{8,24},{16,0},{24,8},{1,17},{9,25},{17,1},{25,9},{2,18},{10... | collective-permute-start | bytes 393224 | tf_op jit(solution)/shard_map/ppermute | solution.py:29
  22.4 2.8 %collective-permute-done.7.refs_2_.refs_1_ = f32[8,64,128]{2,1,0:T(8,128)S(1)} collective-permute-done((f32[8,64,128]{2,1,0:T(8,128)S(1)}, f32[8,64,128]{2,1,0:T(8,128)S(1)}, u32[]{:S(2)}, u32[]{:S(2)}) %collective-permute-start.7) | collective-permute-done | bytes 262176 | tf_op jit(solution)/shard_map/ppermute | solution.py:29
  25.2 3.6 %collective-permute-start.8 = (f32[4,64,128]{2,1,0:T(8,128)S(1)}, f32[4,64,128]{2,1,0:T(8,128)S(1)}, u32[]{:S(2)}, u32[]{:S(2)}) collective-permute-start(f32[4,64,128]{2,1,0:T(8,128)S(1)} %add_upper.4), channel_id=1, source_target_pairs={{0,6},{1,7},{2,4},{3,5},{4,2},{5,3},{6,0},{7,1},{8,14},{9,15},{10,... | collective-permute-start | bytes 393224 | tf_op jit(solution)/shard_map/ppermute | solution.py:29
  28.9 3.4 %near_first.1 = (f32[4,64,128]{2,1,0:T(8,128)S(1)}, f32[4,64,128]{2,1,0:T(8,128)S(1)}, f32[32,128]{1,0:T(8,128)S(1)}, f32[24,128]{1,0:T(8,128)S(1)}) custom-call(f32[256,128]{1,0:T(8,128)S(1)} %bitcast.8, f32[256,128]{1,0:T(8,128)S(1)} %collective-permute-done.refs_1_, f32[256,128]{1,0:T(8,128)S(1)} %collective-permute-done.1.refs_0_.refs_2_, ...), custom_call_target="tpu_custom_call" | custom-call | tf_op jit(solution)/shard_map/near_first/pallas_call | solution.py:264
  32.4 0.9 %gather_first.1 = (f32[4,64,128]{2,1,0:T(8,128)S(1)}, f32[200,128]{1,0:T(8,128)S(1)}) custom-call(f32[4,64,128]{2,1,0:T(8,128)S(1)} %copy-done.1, f32[4,64,128]{2,1,0:T(8,128)S(1)} %get-tuple-element.23.refs_0_.near, f32[16,64,128]{2,1,0:T(8,128)S(1)} %get-tuple-element.24.refs_0_.keep, f32[16,64,128]{2,1,0:T(8,128)S(1)} %collective-permute-done.6.refs_1_.refs_0_, ...), custom_call_target="tpu_custom_call" | custom-call | tf_op jit(solution)/shard_map/gather_first/pallas_call | solution.py:331
  33.3 1.2 %collective-permute-start.10 = (f32[256,128]{1,0:T(8,128)S(1)}, f32[256,128]{1,0:T(8,128)S(1)}, u32[]{:S(2)}, u32[]{:S(2)}) collective-permute-start(f32[256,128]{1,0:T(8,128)S(1)} %bitcast.9), channel_id=1, source_target_pairs={{0,2},{1,3},{2,0},{3,1},{4,6},{5,7},{6,4},{7,5},{8,10},{9,11},{10,... | collective-permute-start | bytes 393224 | tf_op jit(solution)/shard_map/ppermute | solution.py:29
  34.5 2.6 %collective-permute-start.11 = (f32[256,128]{1,0:T(8,128)S(1)}, f32[256,128]{1,0:T(8,128)S(1)}, u32[]{:S(2)}, u32[]{:S(2)}) collective-permute-start(f32[256,128]{1,0:T(8,128)S(1)} %bitcast.10), channel_id=1, source_target_pairs={{0,4},{1,5},{2,6},{3,7},{4,0},{5,1},{6,2},{7,3},{8,12},{9,13},{10,... | collective-permute-start | bytes 393224 | tf_op jit(solution)/shard_map/ppermute | solution.py:29
  37.1 0.6 collective-permute-start.12
  37.7 1.5 %collective-permute-start.13 = (f32[200,128]{1,0:T(8,128)S(1)}, f32[200,128]{1,0:T(8,128)S(1)}, u32[]{:S(2)}, u32[]{:S(2)}) collective-permute-start(f32[200,128]{1,0:T(8,128)S(1)} %get-tuple-element.28.mine), channel_id=1, source_target_pairs={{0,8},{8,0},{16,24},{24,16},{1,9},{9,1},{17,25},{25,17},{2,10},{10... | collective-permute-start | bytes 307208 | tf_op jit(solution)/shard_map/ppermute | solution.py:29
  39.2 2.3 %returned_moved.1 = (f32[16,64,128]{2,1,0:T(8,128)S(1)}, f32[16,64,128]{2,1,0:T(8,128)S(1)}) custom-call(f32[4,64,128]{2,1,0:T(8,128)S(1)} %get-tuple-element.27.vectors.refs_5_.first, f32[4,11,128,128]{3,2,1,0:T(8,128)S(1)} %copy-done, s32[11,128]{1,0:T(8,128)S(1)} %bitcast.18, s32[128]{0:T(128)S(1)} %copy-done.6, s32[128]{0:T(128)S(1)} %copy-done.5), custom_call_target="tpu_custom_call" | custom-call | tf_op jit(solution)/shard_map/returned_moved/pallas_call | solution.py:171
  41.5 0.9 %collective-permute-done.13.other = f32[200,128]{1,0:T(8,128)S(1)} collective-permute-done((f32[200,128]{1,0:T(8,128)S(1)}, f32[200,128]{1,0:T(8,128)S(1)}, u32[]{:S(2)}, u32[]{:S(2)}) %collective-permute-start.13) | collective-permute-done | bytes 102432 | tf_op jit(solution)/shard_map/ppermute | solution.py:29
  42.4 3.2 %collective-permute-done.11.refs_2_ = f32[256,128]{1,0:T(8,128)S(1)} collective-permute-done((f32[256,128]{1,0:T(8,128)S(1)}, f32[256,128]{1,0:T(8,128)S(1)}, u32[]{:S(2)}, u32[]{:S(2)}) %collective-permute-start.11) | collective-permute-done | bytes 131104 | tf_op jit(solution)/shard_map/ppermute | solution.py:29
  45.6 0.1 collective-permute-start.17
  45.7 0.5 collective-permute-start.14
  46.2 1.4 %collective-permute-done.17.refs_1_.refs_3_ = f32[16,64,128]{2,1,0:T(8,128)S(1)} collective-permute-done((f32[16,64,128]{2,1,0:T(8,128)S(1)}, f32[16,64,128]{2,1,0:T(8,128)S(1)}, u32[]{:S(2)}, u32[]{:S(2)}) %collective-permute-start.17) | collective-permute-done | bytes 524320 | tf_op jit(solution)/shard_map/ppermute | solution.py:29
  47.6 2.0 %collective-permute-start.18 = (f32[8,64,128]{2,1,0:T(8,128)S(1)}, f32[8,64,128]{2,1,0:T(8,128)S(1)}, u32[]{:S(2)}, u32[]{:S(2)}) collective-permute-start(f32[8,64,128]{2,1,0:T(8,128)S(1)} %add_upper.5), channel_id=1, source_target_pairs={{0,2},{1,3},{2,0},{3,1},{4,6},{5,7},{6,4},{7,5},{8,10},{9,11},{10,... | collective-permute-start | bytes 786440 | tf_op jit(solution)/shard_map/ppermute | solution.py:29
  49.7 1.5 %collective-permute-start.15 = (f32[328,128]{1,0:T(8,128)S(1)}, f32[328,128]{1,0:T(8,128)S(1)}, u32[]{:S(2)}, u32[]{:S(2)}) collective-permute-start(f32[328,128]{1,0:T(8,128)S(1)} %merge_side.6.refs_4_.mine), channel_id=1, source_target_pairs={{0,16},{8,24},{16,0},{24,8},{1,17},{9,25},{17,1},{25,9},{2,18},{10... | collective-permute-start | bytes 503816 | tf_op jit(solution)/shard_map/ppermute | solution.py:29
  51.2 3.9 %near_second.1 = (f32[4,64,128]{2,1,0:T(8,128)S(1)}, f32[4,64,128]{2,1,0:T(8,128)S(1)}, f32[32,128]{1,0:T(8,128)S(1)}) custom-call(f32[256,128]{1,0:T(8,128)S(1)} %bitcast.13, f32[256,128]{1,0:T(8,128)S(1)} %collective-permute-done.10.refs_1_, f32[256,128]{1,0:T(8,128)S(1)} %collective-permute-done.11.refs_2_, ...), custom_call_target="tpu_custom_call" | custom-call | tf_op jit(solution)/shard_map/near_second/pallas_call | solution.py:264
  55.1 0.6 collective-permute-done.15.other
  55.7 1.5 %edge_second.1 = (f32[2,64,128]{2,1,0:T(8,128)S(1)}, f32[136,128]{1,0:T(8,128)S(1)}) custom-call(f32[4,64,128]{2,1,0:T(8,128)S(1)} %get-tuple-element.27.vectors.refs_5_.first, f32[4,64,128]{2,1,0:T(8,128)S(1)} %get-tuple-element.30.refs_0_.near, f32[32,128]{1,0:T(8,128)S(1)} %get-tuple-element.31.packed, f32[2,4,128,128]{3,2,1,0:T(8,128)S(1)} %copy-done.2, ...), custom_call_target="tpu_custom_call" | custom-call | tf_op jit(solution)/shard_map/edge_second/pallas_call | solution.py:367
  57.2 0.1 collective-permute-start.16
  57.3 1.2 %collective-permute-done.16.partner = f32[136,128]{1,0:T(8,128)S(1)} collective-permute-done((f32[136,128]{1,0:T(8,128)S(1)}, f32[136,128]{1,0:T(8,128)S(1)}, u32[]{:S(2)}, u32[]{:S(2)}) %collective-permute-start.16) | collective-permute-done | bytes 69664 | tf_op jit(solution)/shard_map/ppermute | solution.py:29
  58.6 0.4 collective-permute-start.19
  59.0 4.0 %collective-permute-done.19.partner = f32[136,128]{1,0:T(8,128)S(1)} collective-permute-done((f32[136,128]{1,0:T(8,128)S(1)}, f32[136,128]{1,0:T(8,128)S(1)}, u32[]{:S(2)}, u32[]{:S(2)}) %collective-permute-start.19) | collective-permute-done | bytes 69664 | tf_op jit(solution)/shard_map/ppermute | solution.py:29
  62.9 1.4 %collective-permute-start.20 = (f32[72,128]{1,0:T(8,128)S(1)}, f32[72,128]{1,0:T(8,128)S(1)}, u32[]{:S(2)}, u32[]{:S(2)}) collective-permute-start(f32[72,128]{1,0:T(8,128)S(1)} %get-tuple-element.35.sums), channel_id=1, source_target_pairs={{0,4},{1,5},{2,6},{3,7},{4,0},{5,1},{6,2},{7,3},{8,12},{9,13},{10,... | collective-permute-start | bytes 110600 | tf_op jit(solution)/shard_map/ppermute | solution.py:29
  64.3 3.7 %collective-permute-done.20.partner = f32[72,128]{1,0:T(8,128)S(1)} collective-permute-done((f32[72,128]{1,0:T(8,128)S(1)}, f32[72,128]{1,0:T(8,128)S(1)}, u32[]{:S(2)}, u32[]{:S(2)}) %collective-permute-start.20) | collective-permute-done | bytes 36896 | tf_op jit(solution)/shard_map/ppermute | solution.py:29
  68.1 0.2 last_gram.1
  68.3 2.5 %collective-permute-start.24 = (f32[5,64,128]{2,1,0:T(8,128)S(1)}, f32[5,64,128]{2,1,0:T(8,128)S(1)}, u32[]{:S(2)}, u32[]{:S(2)}) collective-permute-start(f32[5,64,128]{2,1,0:T(8,128)S(1)} %get-tuple-element.43), channel_id=1, source_target_pairs={{0,6},{1,7},{2,4},{3,5},{4,2},{5,3},{6,0},{7,1},{8,14},{9,15},{10,... | collective-permute-start | bytes 491528 | tf_op jit(solution)/shard_map/ppermute | solution.py:29
  70.8 1.5 %collective-permute-start.21 = (f32[32,128]{1,0:T(8,128)S(1)}, f32[32,128]{1,0:T(8,128)S(1)}, u32[]{:S(2)}, u32[]{:S(2)}) collective-permute-start(f32[32,128]{1,0:T(8,128)S(1)} %get-tuple-element.36.refs_0_), channel_id=1, source_target_pairs={{0,8},{8,0},{16,24},{24,16},{1,9},{9,1},{17,25},{25,17},{2,10},{10... | collective-permute-start | bytes 49160 | tf_op jit(solution)/shard_map/ppermute | solution.py:29
  72.3 1.5 %collective-permute-start.22 = (f32[32,128]{1,0:T(8,128)S(1)}, f32[32,128]{1,0:T(8,128)S(1)}, u32[]{:S(2)}, u32[]{:S(2)}) collective-permute-start(f32[32,128]{1,0:T(8,128)S(1)} %get-tuple-element.36.refs_0_), channel_id=1, source_target_pairs={{0,16},{8,24},{16,0},{24,8},{1,17},{9,25},{17,1},{25,9},{2,18},{10... | collective-permute-start | bytes 49160 | tf_op jit(solution)/shard_map/ppermute | solution.py:29
  73.8 0.5 collective-permute-start.23
  74.3 3.0 %first_solves.1.solved = f32[2,64,64]{2,1,0:T(8,128)S(1)} custom-call(f32[72,128]{1,0:T(8,128)S(1)} %get-tuple-element.37.extra.refs_3_), custom_call_target="tpu_custom_call" | custom-call | tf_op jit(solution)/shard_map/first_solves/pallas_call | solution.py:471
  77.3 1.3 %next_gram.1.following = f32[3,64,64]{2,1,0:T(8,128)S(1)} custom-call(f32[72,128]{1,0:T(8,128)S(1)} %get-tuple-element.37.extra.refs_3_, f32[2,64,64]{2,1,0:T(8,128)S(1)} %first_solves.1.solved), custom_call_target="tpu_custom_call" | custom-call | tf_op jit(solution)/shard_map/next_gram/pallas_call | solution.py:471
  78.7 4.8 %final.1 = (f32[4,64,128]{2,1,0:T(8,128)}, f32[4,64,128]{2,1,0:T(8,128)}) custom-call(f32[32,128]{1,0:T(8,128)S(1)} %add_whole.1.gram, f32[2,64,64]{2,1,0:T(8,128)S(1)} %first_solves.1.solved, f32[3,64,64]{2,1,0:T(8,128)S(1)} %next_gram.1.following, f32[4,64,128]{2,1,0:T(8,128)S(1)} %get-tuple-element.38.moving, f32[4,64,128]{2,1,0:T(8,128)S(1)} %get-tuple-element.39.first, ...), custom_call_target="tpu_custom_call" | custom-call | tf_op jit(solution)/shard_map/final/pallas_call | solution.py:516
  (42 shorter events, 0.4 us)
Async XLA Ops:
  0.6 4.2 %copy-start.1 = (f32[4,64,128]{2,1,0:T(8,128)S(1)}, f32[4,64,128]{2,1,0:T(8,128)}, u32[]{:S(2)}) copy-start(f32[4,64,128]{2,1,0:T(8,128)} %vectors.3) | copy-start | bytes 393220
  4.2 24.6 %copy-start = (f32[4,11,128,128]{3,2,1,0:T(8,128)S(1)}, f32[4,11,128,128]{3,2,1,0:T(8,128)}, u32[]{:S(2)}) copy-start(f32[4,11,128,128]{3,2,1,0:T(8,128)} %refs_6_.3) | copy-start | bytes 8650756
  4.3 24.6 %copy-start.3 = (f32[4,128,128]{2,1,0:T(8,128)S(1)}, f32[4,128,128]{2,1,0:T(8,128)}, u32[]{:S(2)}) copy-start(f32[4,128,128]{2,1,0:T(8,128)} %refs_7_.3) | copy-start | bytes 786436
  4.3 24.6 %copy-start.4 = (s32[128,11]{0,1:T(8,128)S(1)}, s32[128,11]{0,1:T(8,128)}, u32[]{:S(2)}) copy-start(s32[128,11]{0,1:T(8,128)} %param.11) | copy-start | bytes 16900
  4.3 24.6 %copy-start.5 = (s32[128]{0:T(128)S(1)}, s32[128]{0:T(128)}, u32[]{:S(2)}) copy-start(s32[128]{0:T(128)} %new_slot.7) | copy-start | bytes 1540
  4.3 24.6 %copy-start.6 = (s32[128]{0:T(128)S(1)}, s32[128]{0:T(128)}, u32[]{:S(2)}) copy-start(s32[128]{0:T(128)} %refs_9_.1) | copy-start | bytes 1540
  4.3 5.8 %collective-permute-start.6 = (f32[16,64,128]{2,1,0:T(8,128)S(1)}, f32[16,64,128]{2,1,0:T(8,128)S(1)}, u32[]{:S(2)}, u32[]{:S(2)}) collective-permute-start(f32[16,64,128]{2,1,0:T(8,128)S(1)} %get-tuple-element.25), channel_id=1, source_target_pairs={{0,1},{1,0},{2,3},{3,2},{4,5},{5,4},{6,7},{7,6},{8,9},{9,8},{10,11... | collective-permute-start | bytes 1572872 | tf_op jit(solution)/shard_map/ppermute | solution.py:29
  4.8 13.7 %collective-permute-start.1 = (f32[256,128]{1,0:T(8,128)S(1)}, f32[256,128]{1,0:T(8,128)S(1)}, u32[]{:S(2)}, u32[]{:S(2)}) collective-permute-start(f32[256,128]{1,0:T(8,128)S(1)} %bitcast.4), channel_id=1, source_target_pairs={{0,4},{1,5},{2,6},{3,7},{4,0},{5,1},{6,2},{7,3},{8,12},{9,13},{10,... | collective-permute-start | bytes 393224 | tf_op jit(solution)/shard_map/ppermute | solution.py:29
  8.5 10.0 %collective-permute-start.2 = (f32[256,128]{1,0:T(8,128)S(1)}, f32[256,128]{1,0:T(8,128)S(1)}, u32[]{:S(2)}, u32[]{:S(2)}) collective-permute-start(f32[256,128]{1,0:T(8,128)S(1)} %bitcast.5), channel_id=1, source_target_pairs={{0,6},{1,7},{2,4},{3,5},{4,2},{5,3},{6,0},{7,1},{8,14},{9,15},{10,... | collective-permute-start | bytes 393224 | tf_op jit(solution)/shard_map/ppermute | solution.py:29
  9.8 10.8 %collective-permute-start = (f32[256,128]{1,0:T(8,128)S(1)}, f32[256,128]{1,0:T(8,128)S(1)}, u32[]{:S(2)}, u32[]{:S(2)}) collective-permute-start(f32[256,128]{1,0:T(8,128)S(1)} %bitcast.6), channel_id=1, source_target_pairs={{0,2},{1,3},{2,0},{3,1},{4,6},{5,7},{6,4},{7,5},{8,10},{9,11},{10,... | collective-permute-start | bytes 393224 | tf_op jit(solution)/shard_map/ppermute | solution.py:29
  10.1 15.1 %collective-permute-start.7 = (f32[8,64,128]{2,1,0:T(8,128)S(1)}, f32[8,64,128]{2,1,0:T(8,128)S(1)}, u32[]{:S(2)}, u32[]{:S(2)}) collective-permute-start(f32[8,64,128]{2,1,0:T(8,128)S(1)} %add_upper.3), channel_id=1, source_target_pairs={{0,2},{1,3},{2,0},{3,1},{4,6},{5,7},{6,4},{7,5},{8,10},{9,11},{10,... | collective-permute-start | bytes 786440 | tf_op jit(solution)/shard_map/ppermute | solution.py:29
  12.0 4.3 %collective-permute-start.4 = (f32[128,128]{1,0:T(8,128)S(1)}, f32[128,128]{1,0:T(8,128)S(1)}, u32[]{:S(2)}, u32[]{:S(2)}) collective-permute-start(f32[128,128]{1,0:T(8,128)S(1)} %bitcast.14), channel_id=1, source_target_pairs={{0,8},{8,0},{16,24},{24,16},{1,9},{9,1},{17,25},{25,17},{2,10},{10... | collective-permute-start | bytes 196616 | tf_op jit(solution)/shard_map/ppermute | solution.py:29
  18.5 10.3 %collective-permute-start.5 = (f32[512,128]{1,0:T(8,128)S(1)}, f32[512,128]{1,0:T(8,128)S(1)}, u32[]{:S(2)}, u32[]{:S(2)}) collective-permute-start(f32[512,128]{1,0:T(8,128)S(1)} %join.4.refs_3_), channel_id=1, source_target_pairs={{0,1},{1,0},{2,3},{3,2},{4,5},{5,4},{6,7},{7,6},{8,9},{9,8},{10,11... | collective-permute-start | bytes 786440 | tf_op jit(solution)/shard_map/ppermute | solution.py:29
  20.6 8.2 %collective-permute-start.3 = (f32[512,128]{1,0:T(8,128)S(1)}, f32[512,128]{1,0:T(8,128)S(1)}, u32[]{:S(2)}, u32[]{:S(2)}) collective-permute-start(f32[512,128]{1,0:T(8,128)S(1)} %join.3), channel_id=1, source_target_pairs={{0,1},{1,0},{2,3},{3,2},{4,5},{5,4},{6,7},{7,6},{8,9},{9,8},{10,11... | collective-permute-start | bytes 786440 | tf_op jit(solution)/shard_map/ppermute | solution.py:29
  20.7 11.6 %collective-permute-start.9 = (f32[256,128]{1,0:T(8,128)S(1)}, f32[256,128]{1,0:T(8,128)S(1)}, u32[]{:S(2)}, u32[]{:S(2)}) collective-permute-start(f32[256,128]{1,0:T(8,128)S(1)} %merge_side.4.refs_2_.mine), channel_id=1, source_target_pairs={{0,16},{8,24},{16,0},{24,8},{1,17},{9,25},{17,1},{25,9},{2,18},{10... | collective-permute-start | bytes 393224 | tf_op jit(solution)/shard_map/ppermute | solution.py:29
  25.2 7.2 %copy-start.2 = (f32[2,4,128,128]{3,2,1,0:T(8,128)S(1)}, f32[2,4,128,128]{3,2,1,0:T(8,128)}, u32[]{:S(2)}) copy-start(f32[2,4,128,128]{3,2,1,0:T(8,128)} %coupling.1) | copy-start | bytes 1572868
  25.2 7.1 %collective-permute-start.8 = (f32[4,64,128]{2,1,0:T(8,128)S(1)}, f32[4,64,128]{2,1,0:T(8,128)S(1)}, u32[]{:S(2)}, u32[]{:S(2)}) collective-permute-start(f32[4,64,128]{2,1,0:T(8,128)S(1)} %add_upper.4), channel_id=1, source_target_pairs={{0,6},{1,7},{2,4},{3,5},{4,2},{5,3},{6,0},{7,1},{8,14},{9,15},{10,... | collective-permute-start | bytes 393224 | tf_op jit(solution)/shard_map/ppermute | solution.py:29
  33.3 9.1 %collective-permute-start.10 = (f32[256,128]{1,0:T(8,128)S(1)}, f32[256,128]{1,0:T(8,128)S(1)}, u32[]{:S(2)}, u32[]{:S(2)}) collective-permute-start(f32[256,128]{1,0:T(8,128)S(1)} %bitcast.9), channel_id=1, source_target_pairs={{0,2},{1,3},{2,0},{3,1},{4,6},{5,7},{6,4},{7,5},{8,10},{9,11},{10,... | collective-permute-start | bytes 393224 | tf_op jit(solution)/shard_map/ppermute | solution.py:29
  34.5 11.0 %collective-permute-start.11 = (f32[256,128]{1,0:T(8,128)S(1)}, f32[256,128]{1,0:T(8,128)S(1)}, u32[]{:S(2)}, u32[]{:S(2)}) collective-permute-start(f32[256,128]{1,0:T(8,128)S(1)} %bitcast.10), channel_id=1, source_target_pairs={{0,4},{1,5},{2,6},{3,7},{4,0},{5,1},{6,2},{7,3},{8,12},{9,13},{10,... | collective-permute-start | bytes 393224 | tf_op jit(solution)/shard_map/ppermute | solution.py:29
  37.1 8.5 %collective-permute-start.12 = (f32[256,128]{1,0:T(8,128)S(1)}, f32[256,128]{1,0:T(8,128)S(1)}, u32[]{:S(2)}, u32[]{:S(2)}) collective-permute-start(f32[256,128]{1,0:T(8,128)S(1)} %bitcast.11), channel_id=1, source_target_pairs={{0,6},{1,7},{2,4},{3,5},{4,2},{5,3},{6,0},{7,1},{8,14},{9,15},{10,... | collective-permute-start | bytes 393224 | tf_op jit(solution)/shard_map/ppermute | solution.py:29
  37.7 4.7 %collective-permute-start.13 = (f32[200,128]{1,0:T(8,128)S(1)}, f32[200,128]{1,0:T(8,128)S(1)}, u32[]{:S(2)}, u32[]{:S(2)}) collective-permute-start(f32[200,128]{1,0:T(8,128)S(1)} %get-tuple-element.28.mine), channel_id=1, source_target_pairs={{0,8},{8,0},{16,24},{24,16},{1,9},{9,1},{17,25},{25,17},{2,10},{10... | collective-permute-start | bytes 307208 | tf_op jit(solution)/shard_map/ppermute | solution.py:29
  45.6 2.0 %collective-permute-start.17 = (f32[16,64,128]{2,1,0:T(8,128)S(1)}, f32[16,64,128]{2,1,0:T(8,128)S(1)}, u32[]{:S(2)}, u32[]{:S(2)}) collective-permute-start(f32[16,64,128]{2,1,0:T(8,128)S(1)} %pass_on.1), channel_id=1, source_target_pairs={{0,1},{1,0},{2,3},{3,2},{4,5},{5,4},{6,7},{7,6},{8,9},{9,8},{10,11... | collective-permute-start | bytes 1572872 | tf_op jit(solution)/shard_map/ppermute | solution.py:29
  45.7 5.5 %collective-permute-start.14 = (f32[1024,128]{1,0:T(8,128)S(1)}, f32[1024,128]{1,0:T(8,128)S(1)}, u32[]{:S(2)}, u32[]{:S(2)}) collective-permute-start(f32[1024,128]{1,0:T(8,128)S(1)} %join.5.refs_1_), channel_id=1, source_target_pairs={{0,1},{1,0},{2,3},{3,2},{4,5},{5,4},{6,7},{7,6},{8,9},{9,8},{10,11... | collective-permute-start | bytes 1572872 | tf_op jit(solution)/shard_map/ppermute | solution.py:29
  47.6 10.9 %collective-permute-start.18 = (f32[8,64,128]{2,1,0:T(8,128)S(1)}, f32[8,64,128]{2,1,0:T(8,128)S(1)}, u32[]{:S(2)}, u32[]{:S(2)}) collective-permute-start(f32[8,64,128]{2,1,0:T(8,128)S(1)} %add_upper.5), channel_id=1, source_target_pairs={{0,2},{1,3},{2,0},{3,1},{4,6},{5,7},{6,4},{7,5},{8,10},{9,11},{10,... | collective-permute-start | bytes 786440 | tf_op jit(solution)/shard_map/ppermute | solution.py:29
  49.7 6.0 %collective-permute-start.15 = (f32[328,128]{1,0:T(8,128)S(1)}, f32[328,128]{1,0:T(8,128)S(1)}, u32[]{:S(2)}, u32[]{:S(2)}) collective-permute-start(f32[328,128]{1,0:T(8,128)S(1)} %merge_side.6.refs_4_.mine), channel_id=1, source_target_pairs={{0,16},{8,24},{16,0},{24,8},{1,17},{9,25},{17,1},{25,9},{2,18},{10... | collective-permute-start | bytes 503816 | tf_op jit(solution)/shard_map/ppermute | solution.py:29
  57.2 1.3 %collective-permute-start.16 = (f32[136,128]{1,0:T(8,128)S(1)}, f32[136,128]{1,0:T(8,128)S(1)}, u32[]{:S(2)}, u32[]{:S(2)}) collective-permute-start(f32[136,128]{1,0:T(8,128)S(1)} %get-tuple-element.32.extra), channel_id=1, source_target_pairs={{0,1},{1,0},{2,3},{3,2},{4,5},{5,4},{6,7},{7,6},{8,9},{9,8},{10,11... | collective-permute-start | bytes 208904 | tf_op jit(solution)/shard_map/ppermute | solution.py:29
  58.6 4.4 %collective-permute-start.19 = (f32[136,128]{1,0:T(8,128)S(1)}, f32[136,128]{1,0:T(8,128)S(1)}, u32[]{:S(2)}, u32[]{:S(2)}) collective-permute-start(f32[136,128]{1,0:T(8,128)S(1)} %settle.1.extra), channel_id=1, source_target_pairs={{0,2},{1,3},{2,0},{3,1},{4,6},{5,7},{6,4},{7,5},{8,10},{9,11},{10,... | collective-permute-start | bytes 208904 | tf_op jit(solution)/shard_map/ppermute | solution.py:29
  62.9 5.1 %collective-permute-start.20 = (f32[72,128]{1,0:T(8,128)S(1)}, f32[72,128]{1,0:T(8,128)S(1)}, u32[]{:S(2)}, u32[]{:S(2)}) collective-permute-start(f32[72,128]{1,0:T(8,128)S(1)} %get-tuple-element.35.sums), channel_id=1, source_target_pairs={{0,4},{1,5},{2,6},{3,7},{4,0},{5,1},{6,2},{7,3},{8,12},{9,13},{10,... | collective-permute-start | bytes 110600 | tf_op jit(solution)/shard_map/ppermute | solution.py:29
  68.3 10.4 %collective-permute-start.24 = (f32[5,64,128]{2,1,0:T(8,128)S(1)}, f32[5,64,128]{2,1,0:T(8,128)S(1)}, u32[]{:S(2)}, u32[]{:S(2)}) collective-permute-start(f32[5,64,128]{2,1,0:T(8,128)S(1)} %get-tuple-element.43), channel_id=1, source_target_pairs={{0,6},{1,7},{2,4},{3,5},{4,2},{5,3},{6,0},{7,1},{8,14},{9,15},{10,... | collective-permute-start | bytes 491528 | tf_op jit(solution)/shard_map/ppermute | solution.py:29
  70.8 7.8 %collective-permute-start.21 = (f32[32,128]{1,0:T(8,128)S(1)}, f32[32,128]{1,0:T(8,128)S(1)}, u32[]{:S(2)}, u32[]{:S(2)}) collective-permute-start(f32[32,128]{1,0:T(8,128)S(1)} %get-tuple-element.36.refs_0_), channel_id=1, source_target_pairs={{0,8},{8,0},{16,24},{24,16},{1,9},{9,1},{17,25},{25,17},{2,10},{10... | collective-permute-start | bytes 49160 | tf_op jit(solution)/shard_map/ppermute | solution.py:29
  72.3 6.3 %collective-permute-start.22 = (f32[32,128]{1,0:T(8,128)S(1)}, f32[32,128]{1,0:T(8,128)S(1)}, u32[]{:S(2)}, u32[]{:S(2)}) collective-permute-start(f32[32,128]{1,0:T(8,128)S(1)} %get-tuple-element.36.refs_0_), channel_id=1, source_target_pairs={{0,16},{8,24},{16,0},{24,8},{1,17},{9,25},{17,1},{25,9},{2,18},{10... | collective-permute-start | bytes 49160 | tf_op jit(solution)/shard_map/ppermute | solution.py:29
  73.8 4.8 %collective-permute-start.23 = (f32[32,128]{1,0:T(8,128)S(1)}, f32[32,128]{1,0:T(8,128)S(1)}, u32[]{:S(2)}, u32[]{:S(2)}) collective-permute-start(f32[32,128]{1,0:T(8,128)S(1)} %get-tuple-element.36.refs_0_), channel_id=1, source_target_pairs={{0,24},{8,16},{16,8},{24,0},{1,25},{9,17},{17,9},{25,1},{2,26},{10... | collective-permute-start | bytes 49160 | tf_op jit(solution)/shard_map/ppermute | solution.py:29

commit v10 on v9

--- a/solution.py
+++ b/solution.py
@@ -467,15 +467,20 @@
     out[2] = dot32(left, jnp.concatenate([upper, lower], axis=0), left_t)
 
 
-def small_call(kernel, count, matrices, name, *operands):
-    return pl.pallas_call(
-        kernel,
-        out_shape=jax.ShapeDtypeStruct((matrices, count, count), f32),
-        in_specs=[vmem] * len(operands),
-        out_specs=vmem,
-        compiler_params=params(),
-        name=name,
-    )(*operands)
+def early_solves_kernel(extra, solved, following):
+    first_solves_kernel(extra, solved)
+    next_gram_kernel(extra, solved, following)
+
+
+def early_solves(extra, count):
+    return pl.pallas_call(
+        early_solves_kernel,
+        out_shape=[jax.ShapeDtypeStruct((matrices, count, count), f32) for matrices in (2, 3)],
+        in_specs=[vmem],
+        out_specs=[vmem] * 2,
+        compiler_params=params(),
+        name="early_solves",
+    )(extra)
 
 
 def final_kernel(gram, solved, following, moving, first, near, more, new_slot, row, *refs):
@@ -762,8 +767,7 @@
         rows //= 2
         total, row = add_with_row(terms, rows, row, flags, step, extra)
         terms.append(swap(total, "bulk", masks[step]))
-    solved = small_call(first_solves_kernel, count, 2, "first_solves", extra)
-    following = small_call(next_gram_kernel, count, 3, "next_gram", extra, solved)
+    solved, following = early_solves(extra, count)
     gram = add_whole(gram, *(swap(gram, "group", mask) for mask in range(1, part_count)))
     return tuple(
         final(gram, solved, following, moving, moved, near, more, new_slot, row, flags, terms)

time: 83.7 us -> 83.6 us (level)
    pallas_call x2 -> x1, Pallas kernels: 4.33 us -> 4.27 us  [early_solves(): pl.pallas_call(early_solves_kernel, out_shape=[jax.ShapeDtypeStruct((matr...]
where the time goes in v10:
time: 83.6 us; the launch traced here: 83.5 us
  starting transfers between devices  32.4 us (39%)
  Pallas kernels  25.2 us (30%)
  waiting for transfers between devices  24.9 us (30%)
  between operations  0.92 us (1%)
    ppermute x25, starting transfers between devices, swap(): return lax.ppermute(value, axis, pairs)  32.4 us
    ppermute x25, waiting for transfers between devices, swap(): return lax.ppermute(value, axis, pairs)  24.9 us
    pallas_call x2, Pallas kernels, near_part(): pl.pallas_call(functools.partial(near_kernel, bulk_count, len(panel), sec...  7.36 us
    pallas_call x2, Pallas kernels, returned(): pl.pallas_call(functools.partial(returned_kernel, bulk_count, moved), gri...  5.88 us
    pallas_call x1, Pallas kernels, final(): pl.pallas_call(final_kernel, grid=(1,), out_shape=[jax.ShapeDtypeStruct(n...  4.81 us
    pallas_call x1, Pallas kernels, early_solves(): pl.pallas_call(early_solves_kernel, out_shape=[jax.ShapeDtypeStruct((matr...  4.27 us
  transfers between devices with their start and end apart: 25, of which 11 were waited for; matrix products, arithmetic and copies ran while one was open for 0% of the time, Pallas kernels for 19%

profile of v10, /device:TPU:0, one launch (start us, length us, event | category | flops | bytes accessed | tf_op | source)
XLA Modules:
  0.0 83.5 jit_solution(11518202490146960667)
XLA Ops:
  0.6 3.6 %returned.1 = (f32[16,64,128]{2,1,0:T(8,128)S(1)}, f32[16,64,128]{2,1,0:T(8,128)S(1)}) custom-call(f32[4,64,128]{2,1,0:T(8,128)} %vectors.3, f32[4,11,128,128]{3,2,1,0:T(8,128)} %refs_6_.3, s32[11,128]{1,0:T(8,128)} %bitcast.16, s32[128]{0:T(128)} %refs_9_.1, s32[128]{0:T(128)} %new_slot.7), custom_call_target="tpu_custom_call" | custom-call | tf_op jit(solution)/shard_map/returned/pallas_call | solution.py:171
  4.3 0.0 copy-start.3
  4.3 0.0 copy-start.4
  4.3 0.5 collective-permute-start.6
  4.8 3.7 %collective-permute-start.1 = (f32[256,128]{1,0:T(8,128)S(1)}, f32[256,128]{1,0:T(8,128)S(1)}, u32[]{:S(2)}, u32[]{:S(2)}) collective-permute-start(f32[256,128]{1,0:T(8,128)S(1)} %bitcast.4), channel_id=1, source_target_pairs={{0,4},{1,5},{2,6},{3,7},{4,0},{5,1},{6,2},{7,3},{8,12},{9,13},{10,... | collective-permute-start | bytes 393224 | tf_op jit(solution)/shard_map/ppermute | solution.py:29
  8.5 1.3 %collective-permute-start.2 = (f32[256,128]{1,0:T(8,128)S(1)}, f32[256,128]{1,0:T(8,128)S(1)}, u32[]{:S(2)}, u32[]{:S(2)}) collective-permute-start(f32[256,128]{1,0:T(8,128)S(1)} %bitcast.5), channel_id=1, source_target_pairs={{0,6},{1,7},{2,4},{3,5},{4,2},{5,3},{6,0},{7,1},{8,14},{9,15},{10,... | collective-permute-start | bytes 393224 | tf_op jit(solution)/shard_map/ppermute | solution.py:29
  9.8 0.2 collective-permute-start
  10.1 1.9 %collective-permute-start.7 = (f32[8,64,128]{2,1,0:T(8,128)S(1)}, f32[8,64,128]{2,1,0:T(8,128)S(1)}, u32[]{:S(2)}, u32[]{:S(2)}) collective-permute-start(f32[8,64,128]{2,1,0:T(8,128)S(1)} %add_upper.3), channel_id=1, source_target_pairs={{0,2},{1,3},{2,0},{3,1},{4,6},{5,7},{6,4},{7,5},{8,10},{9,11},{10,... | collective-permute-start | bytes 786440 | tf_op jit(solution)/shard_map/ppermute | solution.py:29
  12.0 1.5 %collective-permute-start.4 = (f32[128,128]{1,0:T(8,128)S(1)}, f32[128,128]{1,0:T(8,128)S(1)}, u32[]{:S(2)}, u32[]{:S(2)}) collective-permute-start(f32[128,128]{1,0:T(8,128)S(1)} %bitcast.14), channel_id=1, source_target_pairs={{0,8},{8,0},{16,24},{24,16},{1,9},{9,1},{17,25},{25,17},{2,10},{10... | collective-permute-start | bytes 196616 | tf_op jit(solution)/shard_map/ppermute | solution.py:29
  13.5 2.8 %collective-permute-done.4.other = f32[128,128]{1,0:T(8,128)S(1)} collective-permute-done((f32[128,128]{1,0:T(8,128)S(1)}, f32[128,128]{1,0:T(8,128)S(1)}, u32[]{:S(2)}, u32[]{:S(2)}) %collective-permute-start.4) | collective-permute-done | bytes 65568 | tf_op jit(solution)/shard_map/ppermute | solution.py:29
  16.3 2.2 %collective-permute-done.1.refs_0_.refs_2_ = f32[256,128]{1,0:T(8,128)S(1)} collective-permute-done((f32[256,128]{1,0:T(8,128)S(1)}, f32[256,128]{1,0:T(8,128)S(1)}, u32[]{:S(2)}, u32[]{:S(2)}) %collective-permute-start.1) | collective-permute-done | bytes 131104 | tf_op jit(solution)/shard_map/ppermute | solution.py:29
  18.5 0.1 collective-permute-start.5
  18.6 2.0 %collective-permute-done.refs_1_ = f32[256,128]{1,0:T(8,128)S(1)} collective-permute-done((f32[256,128]{1,0:T(8,128)S(1)}, f32[256,128]{1,0:T(8,128)S(1)}, u32[]{:S(2)}, u32[]{:S(2)}) %collective-permute-start) | collective-permute-done | bytes 131104 | tf_op jit(solution)/shard_map/ppermute | solution.py:29
  20.6 0.1 collective-permute-start.3
  20.7 1.7 %collective-permute-start.9 = (f32[256,128]{1,0:T(8,128)S(1)}, f32[256,128]{1,0:T(8,128)S(1)}, u32[]{:S(2)}, u32[]{:S(2)}) collective-permute-start(f32[256,128]{1,0:T(8,128)S(1)} %merge_side.4.refs_2_.mine), channel_id=1, source_target_pairs={{0,16},{8,24},{16,0},{24,8},{1,17},{9,25},{17,1},{25,9},{2,18},{10... | collective-permute-start | bytes 393224 | tf_op jit(solution)/shard_map/ppermute | solution.py:29
  22.4 2.8 %collective-permute-done.7.refs_2_.refs_1_ = f32[8,64,128]{2,1,0:T(8,128)S(1)} collective-permute-done((f32[8,64,128]{2,1,0:T(8,128)S(1)}, f32[8,64,128]{2,1,0:T(8,128)S(1)}, u32[]{:S(2)}, u32[]{:S(2)}) %collective-permute-start.7) | collective-permute-done | bytes 262176 | tf_op jit(solution)/shard_map/ppermute | solution.py:29
  25.2 3.6 %collective-permute-start.8 = (f32[4,64,128]{2,1,0:T(8,128)S(1)}, f32[4,64,128]{2,1,0:T(8,128)S(1)}, u32[]{:S(2)}, u32[]{:S(2)}) collective-permute-start(f32[4,64,128]{2,1,0:T(8,128)S(1)} %add_upper.4), channel_id=1, source_target_pairs={{0,6},{1,7},{2,4},{3,5},{4,2},{5,3},{6,0},{7,1},{8,14},{9,15},{10,... | collective-permute-start | bytes 393224 | tf_op jit(solution)/shard_map/ppermute | solution.py:29
  28.9 3.4 %near_first.1 = (f32[4,64,128]{2,1,0:T(8,128)S(1)}, f32[4,64,128]{2,1,0:T(8,128)S(1)}, f32[32,128]{1,0:T(8,128)S(1)}, f32[24,128]{1,0:T(8,128)S(1)}) custom-call(f32[256,128]{1,0:T(8,128)S(1)} %bitcast.8, f32[256,128]{1,0:T(8,128)S(1)} %collective-permute-done.refs_1_, f32[256,128]{1,0:T(8,128)S(1)} %collective-permute-done.1.refs_0_.refs_2_, ...), custom_call_target="tpu_custom_call" | custom-call | tf_op jit(solution)/shard_map/near_first/pallas_call | solution.py:264
  32.4 0.9 %gather_first.1 = (f32[4,64,128]{2,1,0:T(8,128)S(1)}, f32[200,128]{1,0:T(8,128)S(1)}) custom-call(f32[4,64,128]{2,1,0:T(8,128)S(1)} %copy-done.1, f32[4,64,128]{2,1,0:T(8,128)S(1)} %get-tuple-element.25.refs_0_.near, f32[16,64,128]{2,1,0:T(8,128)S(1)} %get-tuple-element.26.refs_0_.keep, f32[16,64,128]{2,1,0:T(8,128)S(1)} %collective-permute-done.6.refs_1_.refs_0_, ...), custom_call_target="tpu_custom_call" | custom-call | tf_op jit(solution)/shard_map/gather_first/pallas_call | solution.py:331
  33.3 1.2 %collective-permute-start.10 = (f32[256,128]{1,0:T(8,128)S(1)}, f32[256,128]{1,0:T(8,128)S(1)}, u32[]{:S(2)}, u32[]{:S(2)}) collective-permute-start(f32[256,128]{1,0:T(8,128)S(1)} %bitcast.9), channel_id=1, source_target_pairs={{0,2},{1,3},{2,0},{3,1},{4,6},{5,7},{6,4},{7,5},{8,10},{9,11},{10,... | collective-permute-start | bytes 393224 | tf_op jit(solution)/shard_map/ppermute | solution.py:29
  34.5 2.6 %collective-permute-start.11 = (f32[256,128]{1,0:T(8,128)S(1)}, f32[256,128]{1,0:T(8,128)S(1)}, u32[]{:S(2)}, u32[]{:S(2)}) collective-permute-start(f32[256,128]{1,0:T(8,128)S(1)} %bitcast.10), channel_id=1, source_target_pairs={{0,4},{1,5},{2,6},{3,7},{4,0},{5,1},{6,2},{7,3},{8,12},{9,13},{10,... | collective-permute-start | bytes 393224 | tf_op jit(solution)/shard_map/ppermute | solution.py:29
  37.1 0.6 collective-permute-start.12
  37.7 1.5 %collective-permute-start.13 = (f32[200,128]{1,0:T(8,128)S(1)}, f32[200,128]{1,0:T(8,128)S(1)}, u32[]{:S(2)}, u32[]{:S(2)}) collective-permute-start(f32[200,128]{1,0:T(8,128)S(1)} %get-tuple-element.30.mine), channel_id=1, source_target_pairs={{0,8},{8,0},{16,24},{24,16},{1,9},{9,1},{17,25},{25,17},{2,10},{10... | collective-permute-start | bytes 307208 | tf_op jit(solution)/shard_map/ppermute | solution.py:29
  39.2 2.3 %returned_moved.1 = (f32[16,64,128]{2,1,0:T(8,128)S(1)}, f32[16,64,128]{2,1,0:T(8,128)S(1)}) custom-call(f32[4,64,128]{2,1,0:T(8,128)S(1)} %get-tuple-element.29.vectors.refs_5_.first, f32[4,11,128,128]{3,2,1,0:T(8,128)S(1)} %copy-done, s32[11,128]{1,0:T(8,128)S(1)} %bitcast.18, s32[128]{0:T(128)S(1)} %copy-done.6, s32[128]{0:T(128)S(1)} %copy-done.5), custom_call_target="tpu_custom_call" | custom-call | tf_op jit(solution)/shard_map/returned_moved/pallas_call | solution.py:171
  41.5 0.9 %collective-permute-done.13.other = f32[200,128]{1,0:T(8,128)S(1)} collective-permute-done((f32[200,128]{1,0:T(8,128)S(1)}, f32[200,128]{1,0:T(8,128)S(1)}, u32[]{:S(2)}, u32[]{:S(2)}) %collective-permute-start.13) | collective-permute-done | bytes 102432 | tf_op jit(solution)/shard_map/ppermute | solution.py:29
  42.4 3.2 %collective-permute-done.11.refs_2_ = f32[256,128]{1,0:T(8,128)S(1)} collective-permute-done((f32[256,128]{1,0:T(8,128)S(1)}, f32[256,128]{1,0:T(8,128)S(1)}, u32[]{:S(2)}, u32[]{:S(2)}) %collective-permute-start.11) | collective-permute-done | bytes 131104 | tf_op jit(solution)/shard_map/ppermute | solution.py:29
  45.6 0.1 collective-permute-start.17
  45.7 0.5 collective-permute-start.14
  46.2 1.4 %collective-permute-done.17.refs_1_.refs_3_ = f32[16,64,128]{2,1,0:T(8,128)S(1)} collective-permute-done((f32[16,64,128]{2,1,0:T(8,128)S(1)}, f32[16,64,128]{2,1,0:T(8,128)S(1)}, u32[]{:S(2)}, u32[]{:S(2)}) %collective-permute-start.17) | collective-permute-done | bytes 524320 | tf_op jit(solution)/shard_map/ppermute | solution.py:29
  47.6 2.0 %collective-permute-start.18 = (f32[8,64,128]{2,1,0:T(8,128)S(1)}, f32[8,64,128]{2,1,0:T(8,128)S(1)}, u32[]{:S(2)}, u32[]{:S(2)}) collective-permute-start(f32[8,64,128]{2,1,0:T(8,128)S(1)} %add_upper.5), channel_id=1, source_target_pairs={{0,2},{1,3},{2,0},{3,1},{4,6},{5,7},{6,4},{7,5},{8,10},{9,11},{10,... | collective-permute-start | bytes 786440 | tf_op jit(solution)/shard_map/ppermute | solution.py:29
  49.7 1.5 %collective-permute-start.15 = (f32[328,128]{1,0:T(8,128)S(1)}, f32[328,128]{1,0:T(8,128)S(1)}, u32[]{:S(2)}, u32[]{:S(2)}) collective-permute-start(f32[328,128]{1,0:T(8,128)S(1)} %merge_side.6.refs_4_.mine), channel_id=1, source_target_pairs={{0,16},{8,24},{16,0},{24,8},{1,17},{9,25},{17,1},{25,9},{2,18},{10... | collective-permute-start | bytes 503816 | tf_op jit(solution)/shard_map/ppermute | solution.py:29
  51.2 3.9 %near_second.1 = (f32[4,64,128]{2,1,0:T(8,128)S(1)}, f32[4,64,128]{2,1,0:T(8,128)S(1)}, f32[32,128]{1,0:T(8,128)S(1)}) custom-call(f32[256,128]{1,0:T(8,128)S(1)} %bitcast.13, f32[256,128]{1,0:T(8,128)S(1)} %collective-permute-done.10.refs_1_, f32[256,128]{1,0:T(8,128)S(1)} %collective-permute-done.11.refs_2_, ...), custom_call_target="tpu_custom_call" | custom-call | tf_op jit(solution)/shard_map/near_second/pallas_call | solution.py:264
  55.1 0.6 collective-permute-done.15.other
  55.7 1.5 %edge_second.1 = (f32[2,64,128]{2,1,0:T(8,128)S(1)}, f32[136,128]{1,0:T(8,128)S(1)}) custom-call(f32[4,64,128]{2,1,0:T(8,128)S(1)} %get-tuple-element.29.vectors.refs_5_.first, f32[4,64,128]{2,1,0:T(8,128)S(1)} %get-tuple-element.32.refs_0_.near, f32[32,128]{1,0:T(8,128)S(1)} %get-tuple-element.33.packed, f32[2,4,128,128]{3,2,1,0:T(8,128)S(1)} %copy-done.2, ...), custom_call_target="tpu_custom_call" | custom-call | tf_op jit(solution)/shard_map/edge_second/pallas_call | solution.py:367
  57.2 0.1 collective-permute-start.16
  57.3 1.2 %collective-permute-done.16.partner = f32[136,128]{1,0:T(8,128)S(1)} collective-permute-done((f32[136,128]{1,0:T(8,128)S(1)}, f32[136,128]{1,0:T(8,128)S(1)}, u32[]{:S(2)}, u32[]{:S(2)}) %collective-permute-start.16) | collective-permute-done | bytes 69664 | tf_op jit(solution)/shard_map/ppermute | solution.py:29
  58.6 0.4 collective-permute-start.19
  59.0 4.0 %collective-permute-done.19.partner = f32[136,128]{1,0:T(8,128)S(1)} collective-permute-done((f32[136,128]{1,0:T(8,128)S(1)}, f32[136,128]{1,0:T(8,128)S(1)}, u32[]{:S(2)}, u32[]{:S(2)}) %collective-permute-start.19) | collective-permute-done | bytes 69664 | tf_op jit(solution)/shard_map/ppermute | solution.py:29
  62.9 1.4 %collective-permute-start.20 = (f32[72,128]{1,0:T(8,128)S(1)}, f32[72,128]{1,0:T(8,128)S(1)}, u32[]{:S(2)}, u32[]{:S(2)}) collective-permute-start(f32[72,128]{1,0:T(8,128)S(1)} %get-tuple-element.37.sums), channel_id=1, source_target_pairs={{0,4},{1,5},{2,6},{3,7},{4,0},{5,1},{6,2},{7,3},{8,12},{9,13},{10,... | collective-permute-start | bytes 110600 | tf_op jit(solution)/shard_map/ppermute | solution.py:29
  64.3 3.7 %collective-permute-done.20.partner = f32[72,128]{1,0:T(8,128)S(1)} collective-permute-done((f32[72,128]{1,0:T(8,128)S(1)}, f32[72,128]{1,0:T(8,128)S(1)}, u32[]{:S(2)}, u32[]{:S(2)}) %collective-permute-start.20) | collective-permute-done | bytes 36896 | tf_op jit(solution)/shard_map/ppermute | solution.py:29
  68.1 0.2 last_gram.1
  68.3 2.5 %collective-permute-start.24 = (f32[5,64,128]{2,1,0:T(8,128)S(1)}, f32[5,64,128]{2,1,0:T(8,128)S(1)}, u32[]{:S(2)}, u32[]{:S(2)}) collective-permute-start(f32[5,64,128]{2,1,0:T(8,128)S(1)} %get-tuple-element.47), channel_id=1, source_target_pairs={{0,6},{1,7},{2,4},{3,5},{4,2},{5,3},{6,0},{7,1},{8,14},{9,15},{10,... | collective-permute-start | bytes 491528 | tf_op jit(solution)/shard_map/ppermute | solution.py:29
  70.8 1.5 %collective-permute-start.21 = (f32[32,128]{1,0:T(8,128)S(1)}, f32[32,128]{1,0:T(8,128)S(1)}, u32[]{:S(2)}, u32[]{:S(2)}) collective-permute-start(f32[32,128]{1,0:T(8,128)S(1)} %get-tuple-element.38.refs_0_), channel_id=1, source_target_pairs={{0,8},{8,0},{16,24},{24,16},{1,9},{9,1},{17,25},{25,17},{2,10},{10... | collective-permute-start | bytes 49160 | tf_op jit(solution)/shard_map/ppermute | solution.py:29
  72.3 1.5 %collective-permute-start.22 = (f32[32,128]{1,0:T(8,128)S(1)}, f32[32,128]{1,0:T(8,128)S(1)}, u32[]{:S(2)}, u32[]{:S(2)}) collective-permute-start(f32[32,128]{1,0:T(8,128)S(1)} %get-tuple-element.38.refs_0_), channel_id=1, source_target_pairs={{0,16},{8,24},{16,0},{24,8},{1,17},{9,25},{17,1},{25,9},{2,18},{10... | collective-permute-start | bytes 49160 | tf_op jit(solution)/shard_map/ppermute | solution.py:29
  73.8 0.5 collective-permute-start.23
  74.3 4.3 %early_solves.1 = (f32[2,64,64]{2,1,0:T(8,128)S(1)}, f32[3,64,64]{2,1,0:T(8,128)S(1)}) custom-call(f32[72,128]{1,0:T(8,128)S(1)} %get-tuple-element.39.extra.refs_3_), custom_call_target="tpu_custom_call" | custom-call | tf_op jit(solution)/shard_map/early_solves/pallas_call | solution.py:476
  78.6 0.0 collective-permute-done.21.refs_1_
  78.7 4.8 %final.1 = (f32[4,64,128]{2,1,0:T(8,128)}, f32[4,64,128]{2,1,0:T(8,128)}) custom-call(f32[32,128]{1,0:T(8,128)S(1)} %add_whole.1.gram, f32[2,64,64]{2,1,0:T(8,128)S(1)} %get-tuple-element.40.solved, f32[3,64,64]{2,1,0:T(8,128)S(1)} %get-tuple-element.41.following, f32[4,64,128]{2,1,0:T(8,128)S(1)} %get-tuple-element.42.moving, ...), custom_call_target="tpu_custom_call" | custom-call | tf_op jit(solution)/shard_map/final/pallas_call | solution.py:521
  (41 shorter events, 0.4 us)
Async XLA Ops:
  0.6 4.2 %copy-start.1 = (f32[4,64,128]{2,1,0:T(8,128)S(1)}, f32[4,64,128]{2,1,0:T(8,128)}, u32[]{:S(2)}) copy-start(f32[4,64,128]{2,1,0:T(8,128)} %vectors.3) | copy-start | bytes 393220
  4.2 24.6 %copy-start = (f32[4,11,128,128]{3,2,1,0:T(8,128)S(1)}, f32[4,11,128,128]{3,2,1,0:T(8,128)}, u32[]{:S(2)}) copy-start(f32[4,11,128,128]{3,2,1,0:T(8,128)} %refs_6_.3) | copy-start | bytes 8650756
  4.3 24.6 %copy-start.3 = (f32[4,128,128]{2,1,0:T(8,128)S(1)}, f32[4,128,128]{2,1,0:T(8,128)}, u32[]{:S(2)}) copy-start(f32[4,128,128]{2,1,0:T(8,128)} %refs_7_.3) | copy-start | bytes 786436
  4.3 24.6 %copy-start.4 = (s32[128,11]{0,1:T(8,128)S(1)}, s32[128,11]{0,1:T(8,128)}, u32[]{:S(2)}) copy-start(s32[128,11]{0,1:T(8,128)} %param.11) | copy-start | bytes 16900
  4.3 24.6 %copy-start.5 = (s32[128]{0:T(128)S(1)}, s32[128]{0:T(128)}, u32[]{:S(2)}) copy-start(s32[128]{0:T(128)} %new_slot.7) | copy-start | bytes 1540
  4.3 24.6 %copy-start.6 = (s32[128]{0:T(128)S(1)}, s32[128]{0:T(128)}, u32[]{:S(2)}) copy-start(s32[128]{0:T(128)} %refs_9_.1) | copy-start | bytes 1540
  4.3 5.8 %collective-permute-start.6 = (f32[16,64,128]{2,1,0:T(8,128)S(1)}, f32[16,64,128]{2,1,0:T(8,128)S(1)}, u32[]{:S(2)}, u32[]{:S(2)}) collective-permute-start(f32[16,64,128]{2,1,0:T(8,128)S(1)} %get-tuple-element.27), channel_id=1, source_target_pairs={{0,1},{1,0},{2,3},{3,2},{4,5},{5,4},{6,7},{7,6},{8,9},{9,8},{10,11... | collective-permute-start | bytes 1572872 | tf_op jit(solution)/shard_map/ppermute | solution.py:29
  4.8 13.7 %collective-permute-start.1 = (f32[256,128]{1,0:T(8,128)S(1)}, f32[256,128]{1,0:T(8,128)S(1)}, u32[]{:S(2)}, u32[]{:S(2)}) collective-permute-start(f32[256,128]{1,0:T(8,128)S(1)} %bitcast.4), channel_id=1, source_target_pairs={{0,4},{1,5},{2,6},{3,7},{4,0},{5,1},{6,2},{7,3},{8,12},{9,13},{10,... | collective-permute-start | bytes 393224 | tf_op jit(solution)/shard_map/ppermute | solution.py:29
  8.5 10.0 %collective-permute-start.2 = (f32[256,128]{1,0:T(8,128)S(1)}, f32[256,128]{1,0:T(8,128)S(1)}, u32[]{:S(2)}, u32[]{:S(2)}) collective-permute-start(f32[256,128]{1,0:T(8,128)S(1)} %bitcast.5), channel_id=1, source_target_pairs={{0,6},{1,7},{2,4},{3,5},{4,2},{5,3},{6,0},{7,1},{8,14},{9,15},{10,... | collective-permute-start | bytes 393224 | tf_op jit(solution)/shard_map/ppermute | solution.py:29
  9.8 10.8 %collective-permute-start = (f32[256,128]{1,0:T(8,128)S(1)}, f32[256,128]{1,0:T(8,128)S(1)}, u32[]{:S(2)}, u32[]{:S(2)}) collective-permute-start(f32[256,128]{1,0:T(8,128)S(1)} %bitcast.6), channel_id=1, source_target_pairs={{0,2},{1,3},{2,0},{3,1},{4,6},{5,7},{6,4},{7,5},{8,10},{9,11},{10,... | collective-permute-start | bytes 393224 | tf_op jit(solution)/shard_map/ppermute | solution.py:29
  10.1 15.1 %collective-permute-start.7 = (f32[8,64,128]{2,1,0:T(8,128)S(1)}, f32[8,64,128]{2,1,0:T(8,128)S(1)}, u32[]{:S(2)}, u32[]{:S(2)}) collective-permute-start(f32[8,64,128]{2,1,0:T(8,128)S(1)} %add_upper.3), channel_id=1, source_target_pairs={{0,2},{1,3},{2,0},{3,1},{4,6},{5,7},{6,4},{7,5},{8,10},{9,11},{10,... | collective-permute-start | bytes 786440 | tf_op jit(solution)/shard_map/ppermute | solution.py:29
  12.0 4.3 %collective-permute-start.4 = (f32[128,128]{1,0:T(8,128)S(1)}, f32[128,128]{1,0:T(8,128)S(1)}, u32[]{:S(2)}, u32[]{:S(2)}) collective-permute-start(f32[128,128]{1,0:T(8,128)S(1)} %bitcast.14), channel_id=1, source_target_pairs={{0,8},{8,0},{16,24},{24,16},{1,9},{9,1},{17,25},{25,17},{2,10},{10... | collective-permute-start | bytes 196616 | tf_op jit(solution)/shard_map/ppermute | solution.py:29
  18.5 10.3 %collective-permute-start.5 = (f32[512,128]{1,0:T(8,128)S(1)}, f32[512,128]{1,0:T(8,128)S(1)}, u32[]{:S(2)}, u32[]{:S(2)}) collective-permute-start(f32[512,128]{1,0:T(8,128)S(1)} %join.4.refs_3_), channel_id=1, source_target_pairs={{0,1},{1,0},{2,3},{3,2},{4,5},{5,4},{6,7},{7,6},{8,9},{9,8},{10,11... | collective-permute-start | bytes 786440 | tf_op jit(solution)/shard_map/ppermute | solution.py:29
  20.6 8.2 %collective-permute-start.3 = (f32[512,128]{1,0:T(8,128)S(1)}, f32[512,128]{1,0:T(8,128)S(1)}, u32[]{:S(2)}, u32[]{:S(2)}) collective-permute-start(f32[512,128]{1,0:T(8,128)S(1)} %join.3), channel_id=1, source_target_pairs={{0,1},{1,0},{2,3},{3,2},{4,5},{5,4},{6,7},{7,6},{8,9},{9,8},{10,11... | collective-permute-start | bytes 786440 | tf_op jit(solution)/shard_map/ppermute | solution.py:29
  20.7 11.6 %collective-permute-start.9 = (f32[256,128]{1,0:T(8,128)S(1)}, f32[256,128]{1,0:T(8,128)S(1)}, u32[]{:S(2)}, u32[]{:S(2)}) collective-permute-start(f32[256,128]{1,0:T(8,128)S(1)} %merge_side.4.refs_2_.mine), channel_id=1, source_target_pairs={{0,16},{8,24},{16,0},{24,8},{1,17},{9,25},{17,1},{25,9},{2,18},{10... | collective-permute-start | bytes 393224 | tf_op jit(solution)/shard_map/ppermute | solution.py:29
  25.2 7.2 %copy-start.2 = (f32[2,4,128,128]{3,2,1,0:T(8,128)S(1)}, f32[2,4,128,128]{3,2,1,0:T(8,128)}, u32[]{:S(2)}) copy-start(f32[2,4,128,128]{3,2,1,0:T(8,128)} %coupling.1) | copy-start | bytes 1572868
  25.2 7.1 %collective-permute-start.8 = (f32[4,64,128]{2,1,0:T(8,128)S(1)}, f32[4,64,128]{2,1,0:T(8,128)S(1)}, u32[]{:S(2)}, u32[]{:S(2)}) collective-permute-start(f32[4,64,128]{2,1,0:T(8,128)S(1)} %add_upper.4), channel_id=1, source_target_pairs={{0,6},{1,7},{2,4},{3,5},{4,2},{5,3},{6,0},{7,1},{8,14},{9,15},{10,... | collective-permute-start | bytes 393224 | tf_op jit(solution)/shard_map/ppermute | solution.py:29
  33.3 9.1 %collective-permute-start.10 = (f32[256,128]{1,0:T(8,128)S(1)}, f32[256,128]{1,0:T(8,128)S(1)}, u32[]{:S(2)}, u32[]{:S(2)}) collective-permute-start(f32[256,128]{1,0:T(8,128)S(1)} %bitcast.9), channel_id=1, source_target_pairs={{0,2},{1,3},{2,0},{3,1},{4,6},{5,7},{6,4},{7,5},{8,10},{9,11},{10,... | collective-permute-start | bytes 393224 | tf_op jit(solution)/shard_map/ppermute | solution.py:29
  34.5 11.0 %collective-permute-start.11 = (f32[256,128]{1,0:T(8,128)S(1)}, f32[256,128]{1,0:T(8,128)S(1)}, u32[]{:S(2)}, u32[]{:S(2)}) collective-permute-start(f32[256,128]{1,0:T(8,128)S(1)} %bitcast.10), channel_id=1, source_target_pairs={{0,4},{1,5},{2,6},{3,7},{4,0},{5,1},{6,2},{7,3},{8,12},{9,13},{10,... | collective-permute-start | bytes 393224 | tf_op jit(solution)/shard_map/ppermute | solution.py:29
  37.1 8.5 %collective-permute-start.12 = (f32[256,128]{1,0:T(8,128)S(1)}, f32[256,128]{1,0:T(8,128)S(1)}, u32[]{:S(2)}, u32[]{:S(2)}) collective-permute-start(f32[256,128]{1,0:T(8,128)S(1)} %bitcast.11), channel_id=1, source_target_pairs={{0,6},{1,7},{2,4},{3,5},{4,2},{5,3},{6,0},{7,1},{8,14},{9,15},{10,... | collective-permute-start | bytes 393224 | tf_op jit(solution)/shard_map/ppermute | solution.py:29
  37.7 4.7 %collective-permute-start.13 = (f32[200,128]{1,0:T(8,128)S(1)}, f32[200,128]{1,0:T(8,128)S(1)}, u32[]{:S(2)}, u32[]{:S(2)}) collective-permute-start(f32[200,128]{1,0:T(8,128)S(1)} %get-tuple-element.30.mine), channel_id=1, source_target_pairs={{0,8},{8,0},{16,24},{24,16},{1,9},{9,1},{17,25},{25,17},{2,10},{10... | collective-permute-start | bytes 307208 | tf_op jit(solution)/shard_map/ppermute | solution.py:29
  45.6 2.0 %collective-permute-start.17 = (f32[16,64,128]{2,1,0:T(8,128)S(1)}, f32[16,64,128]{2,1,0:T(8,128)S(1)}, u32[]{:S(2)}, u32[]{:S(2)}) collective-permute-start(f32[16,64,128]{2,1,0:T(8,128)S(1)} %pass_on.1), channel_id=1, source_target_pairs={{0,1},{1,0},{2,3},{3,2},{4,5},{5,4},{6,7},{7,6},{8,9},{9,8},{10,11... | collective-permute-start | bytes 1572872 | tf_op jit(solution)/shard_map/ppermute | solution.py:29
  45.7 5.5 %collective-permute-start.14 = (f32[1024,128]{1,0:T(8,128)S(1)}, f32[1024,128]{1,0:T(8,128)S(1)}, u32[]{:S(2)}, u32[]{:S(2)}) collective-permute-start(f32[1024,128]{1,0:T(8,128)S(1)} %join.5.refs_1_), channel_id=1, source_target_pairs={{0,1},{1,0},{2,3},{3,2},{4,5},{5,4},{6,7},{7,6},{8,9},{9,8},{10,11... | collective-permute-start | bytes 1572872 | tf_op jit(solution)/shard_map/ppermute | solution.py:29
  47.6 10.9 %collective-permute-start.18 = (f32[8,64,128]{2,1,0:T(8,128)S(1)}, f32[8,64,128]{2,1,0:T(8,128)S(1)}, u32[]{:S(2)}, u32[]{:S(2)}) collective-permute-start(f32[8,64,128]{2,1,0:T(8,128)S(1)} %add_upper.5), channel_id=1, source_target_pairs={{0,2},{1,3},{2,0},{3,1},{4,6},{5,7},{6,4},{7,5},{8,10},{9,11},{10,... | collective-permute-start | bytes 786440 | tf_op jit(solution)/shard_map/ppermute | solution.py:29
  49.7 6.0 %collective-permute-start.15 = (f32[328,128]{1,0:T(8,128)S(1)}, f32[328,128]{1,0:T(8,128)S(1)}, u32[]{:S(2)}, u32[]{:S(2)}) collective-permute-start(f32[328,128]{1,0:T(8,128)S(1)} %merge_side.6.refs_4_.mine), channel_id=1, source_target_pairs={{0,16},{8,24},{16,0},{24,8},{1,17},{9,25},{17,1},{25,9},{2,18},{10... | collective-permute-start | bytes 503816 | tf_op jit(solution)/shard_map/ppermute | solution.py:29
  57.2 1.3 %collective-permute-start.16 = (f32[136,128]{1,0:T(8,128)S(1)}, f32[136,128]{1,0:T(8,128)S(1)}, u32[]{:S(2)}, u32[]{:S(2)}) collective-permute-start(f32[136,128]{1,0:T(8,128)S(1)} %get-tuple-element.34.extra), channel_id=1, source_target_pairs={{0,1},{1,0},{2,3},{3,2},{4,5},{5,4},{6,7},{7,6},{8,9},{9,8},{10,11... | collective-permute-start | bytes 208904 | tf_op jit(solution)/shard_map/ppermute | solution.py:29
  58.6 4.4 %collective-permute-start.19 = (f32[136,128]{1,0:T(8,128)S(1)}, f32[136,128]{1,0:T(8,128)S(1)}, u32[]{:S(2)}, u32[]{:S(2)}) collective-permute-start(f32[136,128]{1,0:T(8,128)S(1)} %settle.1.extra), channel_id=1, source_target_pairs={{0,2},{1,3},{2,0},{3,1},{4,6},{5,7},{6,4},{7,5},{8,10},{9,11},{10,... | collective-permute-start | bytes 208904 | tf_op jit(solution)/shard_map/ppermute | solution.py:29
  62.9 5.1 %collective-permute-start.20 = (f32[72,128]{1,0:T(8,128)S(1)}, f32[72,128]{1,0:T(8,128)S(1)}, u32[]{:S(2)}, u32[]{:S(2)}) collective-permute-start(f32[72,128]{1,0:T(8,128)S(1)} %get-tuple-element.37.sums), channel_id=1, source_target_pairs={{0,4},{1,5},{2,6},{3,7},{4,0},{5,1},{6,2},{7,3},{8,12},{9,13},{10,... | collective-permute-start | bytes 110600 | tf_op jit(solution)/shard_map/ppermute | solution.py:29
  68.3 10.3 %collective-permute-start.24 = (f32[5,64,128]{2,1,0:T(8,128)S(1)}, f32[5,64,128]{2,1,0:T(8,128)S(1)}, u32[]{:S(2)}, u32[]{:S(2)}) collective-permute-start(f32[5,64,128]{2,1,0:T(8,128)S(1)} %get-tuple-element.47), channel_id=1, source_target_pairs={{0,6},{1,7},{2,4},{3,5},{4,2},{5,3},{6,0},{7,1},{8,14},{9,15},{10,... | collective-permute-start | bytes 491528 | tf_op jit(solution)/shard_map/ppermute | solution.py:29
  70.8 7.8 %collective-permute-start.21 = (f32[32,128]{1,0:T(8,128)S(1)}, f32[32,128]{1,0:T(8,128)S(1)}, u32[]{:S(2)}, u32[]{:S(2)}) collective-permute-start(f32[32,128]{1,0:T(8,128)S(1)} %get-tuple-element.38.refs_0_), channel_id=1, source_target_pairs={{0,8},{8,0},{16,24},{24,16},{1,9},{9,1},{17,25},{25,17},{2,10},{10... | collective-permute-start | bytes 49160 | tf_op jit(solution)/shard_map/ppermute | solution.py:29
  72.3 6.3 %collective-permute-start.22 = (f32[32,128]{1,0:T(8,128)S(1)}, f32[32,128]{1,0:T(8,128)S(1)}, u32[]{:S(2)}, u32[]{:S(2)}) collective-permute-start(f32[32,128]{1,0:T(8,128)S(1)} %get-tuple-element.38.refs_0_), channel_id=1, source_target_pairs={{0,16},{8,24},{16,0},{24,8},{1,17},{9,25},{17,1},{25,9},{2,18},{10... | collective-permute-start | bytes 49160 | tf_op jit(solution)/shard_map/ppermute | solution.py:29
  73.8 4.8 %collective-permute-start.23 = (f32[32,128]{1,0:T(8,128)S(1)}, f32[32,128]{1,0:T(8,128)S(1)}, u32[]{:S(2)}, u32[]{:S(2)}) collective-permute-start(f32[32,128]{1,0:T(8,128)S(1)} %get-tuple-element.38.refs_0_), channel_id=1, source_target_pairs={{0,24},{8,16},{16,8},{24,0},{1,25},{9,17},{17,9},{25,1},{2,26},{10... | collective-permute-start | bytes 49160 | tf_op jit(solution)/shard_map/ppermute | solution.py:29
